TPU v7x, 32 devices: a whole 2x2x4 slice. The times are simulated.
32 devices in a mesh: rep: 2 (over y), slab: 4 (over z), col: 2 (over x), pair: 2 (over core).
Axes of the slice: x: 2, y: 2, z: 4, core: 2. Of those that a mesh axis runs over, the one named last changes fastest.
Arguments:
- populations: float32 [19, 128, 32, 256], P(None, ('rep', 'slab'), 'col', 'pair'), parts along dimension 1, as said below
- solid_mask: int32 [128, 32, 256], P(('rep', 'slab'), 'col', 'pair'), parts along dimension 0, may hold values 0 or 1
- bead_owner: int32 [4096], P(('rep', 'slab', 'col', 'pair')), parts along dimension 0, may hold values from 0 to 7, as said below
- bead_base: int32 [3, 4096], P(None, ('rep', 'slab', 'col', 'pair')), parts along dimension 1, may hold values from 0 to 126, as said below
- bead_offset: float32 [3, 4096], P(None, ('rep', 'slab', 'col', 'pair')), parts along dimension 1, may hold values from 0 to 1
- bead_velocity: float32 [3, 4096], P(None, ('rep', 'slab', 'col', 'pair')), parts along dimension 1, may hold values from -0.6 to 0.6
Outputs:
- next_populations: float32 [19, 128, 32, 256], P(None, ('rep', 'slab'), 'col', 'pair'), parts along dimension 1
- bead_force: float32 [3, 4096], P(None, ('rep', 'slab', 'col', 'pair')), parts along dimension 1
There are 2 independent parts, one for each index of `rep`. A program takes and returns all parts, laid end to end along the dimension named above; each array names one. Nothing has to cross between parts.
Inputs may be any that keep to these rules, and one draw needn't show every extreme that they name: `populations`: populations are positive. `bead_owner`: among the beads of one device each owner index appears at most 32 times; in every draw one owner index appears exactly 32 times among the beads of every device. `bead_base`: row 0 lies in 0 to 126, row 1 in 0 to 14, row 2 in 0 to 14; x is local to the x block of the bead's own pair index, y and z to the owner's block.
All inputs are finite; a program needn't handle non-finite values. No bound on the sum of `solid_mask` on one device may be relied on, other than what follows from the above.
Results may differ from a plain program's by a relative error of at most 0.0003.
Values sent between devices are 32-bit elements; how exact they have to be, the bound alone decides.
No kernel may reach another device: no remote copies, remote signals or barrier semaphores. Data moves between devices by JAX's collectives and lax.ppermute only.
A program may use at most 64 MiB of HBM per device.

v0:
```python
import jax
import jax.numpy as jnp
import numpy as np
from jax import lax
from jax.sharding import PartitionSpec as P

CAP = 32


LATTICE_STEP = np.array(
    [
        [0, 0, 0],
        [1, 0, 0],
        [-1, 0, 0],
        [0, 1, 0],
        [0, -1, 0],
        [0, 0, 1],
        [0, 0, -1],
        [1, 1, 0],
        [-1, -1, 0],
        [1, -1, 0],
        [-1, 1, 0],
        [1, 0, 1],
        [-1, 0, -1],
        [1, 0, -1],
        [-1, 0, 1],
        [0, 1, 1],
        [0, -1, -1],
        [0, 1, -1],
        [0, -1, 1],
    ],
    np.int32,
)
LATTICE_VEL = LATTICE_STEP.astype(np.float32)
LATTICE_WT = np.array([1.0 / 3.0] + [1.0 / 18.0] * 6 + [1.0 / 36.0] * 12, np.float32)
OPPOSITE = np.array([0, 2, 1, 4, 3, 6, 5, 8, 7, 10, 9, 12, 11, 14, 13, 16, 15, 18, 17], np.int32)
TAU_PLUS = 0.8
TAU_MINUS = 0.5 + 3.0 / 16.0 / (TAU_PLUS - 0.5)
DRAG_COEF = 2.0


def with_halo(value, sides, width):
    for axis, dim in sides:
        size, length = (lax.axis_size(axis), value.shape[dim])
        up = [(i, (i + 1) % size) for i in range(size)]
        down = [(j, i) for i, j in up]
        last = lax.slice_in_dim(value, length - width, length, axis=dim)
        first = lax.slice_in_dim(value, 0, width, axis=dim)
        before = lax.ppermute(last, axis, up)
        after = lax.ppermute(first, axis, down)
        value = jnp.concatenate([before, value, after], axis=dim)
    return value


def moments(populations):
    density = jnp.sum(populations, axis=0)
    momentum = jnp.einsum(
        "qd,qzyx->dzyx", jnp.asarray(LATTICE_VEL), populations, precision=lax.Precision.HIGHEST
    )
    return (density, momentum)


def collide(populations, density, momentum, solid_mask, force):
    table = jnp.asarray(LATTICE_VEL)
    weights = jnp.asarray(LATTICE_WT)[:, None, None, None]
    speed = (momentum + 0.5 * force) / density
    along = jnp.einsum("qd,dzyx->qzyx", table, speed, precision=lax.Precision.HIGHEST)
    pushed = jnp.einsum("qd,dzyx->qzyx", table, force, precision=lax.Precision.HIGHEST)
    square = jnp.sum(speed * speed, axis=0)
    power = jnp.sum(speed * force, axis=0)
    balance = weights * density * (1.0 + 3.0 * along + 4.5 * along * along - 1.5 * square)
    source = (1.0 - 0.5 / TAU_PLUS) * weights * (3.0 * (pushed - power) + 9.0 * along * pushed)
    mirror = populations[OPPOSITE]
    balance_mirror = balance[OPPOSITE]
    even_part = 0.5 * (populations + mirror) - 0.5 * (balance + balance_mirror)
    odd_part = 0.5 * (populations - mirror) - 0.5 * (balance - balance_mirror)
    relaxed = populations - even_part / TAU_PLUS - odd_part / TAU_MINUS + source
    return jnp.where(solid_mask[None] == 1, mirror, relaxed)


def hat_weights(start, fraction, length):
    cells = jnp.arange(length, dtype=jnp.int32)[None, :]
    lower = (cells == start[:, None]).astype(jnp.float32)
    upper = (cells == start[:, None] + 1).astype(jnp.float32)
    return (1.0 - fraction)[:, None] * lower + fraction[:, None] * upper


def couple(flow, arrived):
    depth, rows, width = (flow.shape[1], flow.shape[2], flow.shape[3])
    slots = arrived.shape[1]
    hat_x = hat_weights(arrived[0].astype(jnp.int32), arrived[3], width)
    hat_y = hat_weights(arrived[1].astype(jnp.int32), arrived[4], rows)
    hat_z = hat_weights(arrived[2].astype(jnp.int32), arrived[5], depth)
    plane_wt = (hat_z.T[:, None, :] * hat_y.T[None, :, :]).reshape(depth * rows, slots)
    across = jnp.dot(
        flow.reshape(3 * depth * rows, width), hat_x.T, precision=lax.Precision.HIGHEST
    )
    sampled = jnp.sum(across.reshape(3, depth * rows, slots) * plane_wt[None], axis=1)
    drag = DRAG_COEF * (sampled - arrived[6:9]) * arrived[9][None, :]
    spread = (plane_wt[None] * (-drag)[:, None, :]).reshape(3 * depth * rows, slots)
    force_grid = jnp.dot(spread, hat_x, precision=lax.Precision.HIGHEST).reshape(
        3, depth, rows, width
    )
    return (drag, force_grid)


def shards(populations, solid_mask, bead_owner, bead_base, bead_offset, bead_velocity):
    density, momentum = moments(populations)
    flow = momentum / density
    count = bead_owner.shape[0]
    slab_count = lax.axis_size("slab")
    col_count = lax.axis_size("col")
    owners = slab_count * col_count
    slots = owners * CAP
    order = jnp.arange(count, dtype=jnp.int32)
    before = (bead_owner[:, None] == bead_owner[None, :]) & (order[None, :] < order[:, None])
    ahead = jnp.sum(before.astype(jnp.int32), axis=1)
    target = bead_owner * CAP + ahead
    placing = (target[:, None] == jnp.arange(slots, dtype=jnp.int32)[None, :]).astype(jnp.float32)
    payload = jnp.concatenate(
        [
            bead_base.astype(jnp.float32),
            bead_offset,
            bead_velocity,
            jnp.ones((1, count), jnp.float32),
        ],
        axis=0,
    )
    packed = jnp.dot(payload, placing, precision=lax.Precision.HIGHEST)
    arrived = lax.all_to_all(
        packed.reshape(10, owners, CAP), ("slab", "col"), split_axis=1, concat_axis=1, tiled=True
    )
    drag, force_grid = couple(flow, arrived.reshape(10, slots))
    relaxed = collide(populations, density, momentum, solid_mask, force_grid)
    returned = lax.all_to_all(
        drag.reshape(3, owners, CAP), ("slab", "col"), split_axis=1, concat_axis=1, tiled=True
    )
    bead_force = jnp.dot(returned.reshape(3, slots), placing.T, precision=lax.Precision.HIGHEST)
    depth, rows, width = (relaxed.shape[1], relaxed.shape[2], relaxed.shape[3])
    padded = with_halo(relaxed, (("slab", 1), ("col", 2), ("pair", 3)), 1)
    moved = []
    for member in range(19):
        step_x = int(LATTICE_STEP[member, 0])
        step_y = int(LATTICE_STEP[member, 1])
        step_z = int(LATTICE_STEP[member, 2])
        moved.append(
            padded[
                member,
                1 - step_z : 1 - step_z + depth,
                1 - step_y : 1 - step_y + rows,
                1 - step_x : 1 - step_x + width,
            ]
        )
    next_populations = jnp.stack(moved)
    return (next_populations, bead_force)


def solution(mesh):
    return jax.shard_map(
        shards,
        mesh=mesh,
        in_specs=(
            P(None, ("rep", "slab"), "col", "pair"),
            P(("rep", "slab"), "col", "pair"),
            P(("rep", "slab", "col", "pair")),
            P(None, ("rep", "slab", "col", "pair")),
            P(None, ("rep", "slab", "col", "pair")),
            P(None, ("rep", "slab", "col", "pair")),
        ),
        out_specs=(
            P(None, ("rep", "slab"), "col", "pair"),
            P(None, ("rep", "slab", "col", "pair")),
        ),
        check_vma=False,
    )
```

profile of v0, /device:TPU:0, one launch (start us, length us, event | category | flops | bytes accessed | tf_op | source)
XLA Modules:
  0.0 123.9 jit_solution(11815051549524191149)
XLA Ops:
  4.8 7.3 %all-to-all-start = ((f32[8,1,320]{2,1,0:T(1,128)}), f32[8,1,320]{2,1,0:T(1,128)S(1)}, u32[]{:S(2)}, u32[]{:S(2)}) async-start(f32[8,1,320]{2,1,0:T(1,128)} %reshape.348), calls=%async_computation | async-start | bytes 24576 | tf_op jit(solution)/shard_map/all_to_all | solution.py:130
  13.6 1.9 %reduce_sum.47 = f32[16,16,128]{2,1,0:T(8,128)S(1)} reduce(f32[19,16,16,128]{3,2,1,0:T(8,128)} %param.11, f32[]{:T(128)} %constant.22.clone.1), dimensions={0}, to_apply=%region_0.0 | reduce | flops 589824 | bytes 2621444 | tf_op jit(solution)/shard_map/reduce_sum | solution.py:56
  15.5 3.8 %broadcast_divide_fusion = (f32[3,16,16,128]{3,0,2,1:T(4,128)}, f32[3,16,16,128]{3,0,2,1:T(4,128)S(1)}) fusion(f32[16,16,128]{2,1,0:T(8,128)S(1)} %reduce_sum.47, f32[19,3,1,1]{0,1,3,2:T(4,128)S(1)} %copy-done.11, f32[19,16,16,128]{3,2,1,0:T(8,128)S(1)} %copy-done.2), kind=kOutput, calls=%fused_computation.39 | convolution fusion | flops 22511616 | bytes 3408100 | tf_op jit(solution)/shard_map/qd,qzyx->dzyx/dot_general | solution.py:57
  19.3 2.2 %gather_fusion = f32[19,16,16,128]{3,2,1,0:T(8,128)} fusion(f32[19,16,16,128]{3,2,1,0:T(8,128)S(1)} %copy-done.2, s32[1024]{0:T(1024)S(1)} %pad_clamp_fusion), kind=kCustom, calls=%fused_computation | custom fusion | bytes 4980812 | tf_op jit(solution)/shard_map/gather | solution.py:73
  23.4 2.0 %fusion.15 = f32[3,256]{1,0:T(4,128)S(1)} fusion(f32[3,256,128]{2,0,1:T(4,128)} %bitcast.25, f32[256,256]{1,0:T(8,128)S(1)} %bitcast.24, f32[256]{0:T(256)S(1)} %squeeze.14, s32[256]{0:T(256)S(1)} %broadcast_add_fusion, f32[256]{0:T(256)S(1)} %broadcast_subtract_fusion, s32[256]{0:T(256)S(1)} %convert_element_type.59), kind=kOutput, calls=%fused_computation.26 | convolution fusion | flops 302546176 | bytes 662528 | tf_op jit(solution)/shard_map/dot_general | solution.py:95
  28.1 5.3 %fusion.14 = (f32[19,16,16,128]{3,0,2,1:T(8,128)S(1)}, f32[19,16,16,128]{3,0,2,1:T(8,128)}) fusion(f32[16,16,128]{2,1,0:T(8,128)S(1)} %broadcast_multiply_fusion.1, f32[16,16,128]{2,1,0:T(8,128)S(1)} %reduce_sum.47, f32[19]{0:T(128)S(1)} %copy-done.16, f32[19,3,1,1]{0,1,3,2:T(4,128)S(1)} %copy-done.12, f32[3,16,16,128]{3,0,2,1:T(4,128)S(1)} %get-tuple-element.23), kind=kOutput, calls=%fused_computation.24 | convolution fusion | flops 27394048 | bytes 5636400 | tf_op jit(solution)/shard_map/qd,dzyx->qzyx/dot_general | solution.py:67
  33.9 2.2 %gather_fusion.1 = f32[19,16,16,128]{3,2,1,0:T(8,128)} fusion(f32[19,16,16,128]{3,2,1,0:T(8,128)S(1)} %copy.87, s32[1024]{0:T(1024)S(1)} %pad_clamp_fusion), kind=kCustom, calls=%fused_computation.1 | custom fusion | bytes 4980812 | tf_op jit(solution)/shard_map/gather | solution.py:74
  36.2 12.8 %copy_select_fusion = f32[19,16,16,128]{3,0,2,1:T(8,128)S(1)} fusion(f32[19,16,16,128]{3,2,1,0:T(8,128)} %gather_fusion, f32[19,16,16,128]{3,2,1,0:T(8,128)} %gather_fusion.1, f32[19,16,16,128]{3,2,1,0:T(8,128)} %param.11, f32[19,16,16,128]{3,0,2,1:T(8,128)} %get-tuple-element.55, f32[19,3,1,1]{0,1,3,2:T(4,128)} %constant.58, ...), kind=kOutput, calls=%fused_computation.9 | convolution fusion | flops 41091072 | bytes 13271420 | tf_op jit(solution)/shard_map/qd,dzyx->qzyx/dot_general | solution.py:68
  49.7 2.0 %collective-permute-start = (f32[19,1,16,128]{3,0,2,1:T(8,128)}, f32[19,1,16,128]{3,0,2,1:T(8,128)S(1)}, u32[]{:S(2)}, u32[]{:S(2)}) collective-permute-start(f32[19,1,16,128]{3,0,2,1:T(8,128)} %get-tuple-element.49), channel_id=1, source_target_pairs={{0,4},{4,8},{8,12},{12,0},{1,5},{5,9},{9,13},{13,1},{2,6},{6,10},{... | collective-permute-start | bytes 466952 | tf_op jit(solution)/shard_map/ppermute | solution.py:49
  51.8 1.8 %collective-permute-start.1 = (f32[19,1,16,128]{3,0,2,1:T(8,128)}, f32[19,1,16,128]{3,0,2,1:T(8,128)S(1)}, u32[]{:S(2)}, u32[]{:S(2)}) collective-permute-start(f32[19,1,16,128]{3,0,2,1:T(8,128)} %get-tuple-element.50), channel_id=1, source_target_pairs={{4,0},{8,4},{12,8},{0,12},{5,1},{9,5},{13,9},{1,13},{6,2},{10,6},{... | collective-permute-start | bytes 466952 | tf_op jit(solution)/shard_map/ppermute | solution.py:50
  53.6 10.6 %all_to_all.10 = f32[3,8,32]{2,0,1:T(4,128)S(1)} all-to-all(f32[3,8,32]{2,0,1:T(4,128)S(1)} %copy.100), channel_id=1, replica_groups=mesh['rep'=2,'slab'=4,'col'=2,'pair'=2] {'slab','col'}, dimensions={1} | all-to-all | bytes 6144 | tf_op jit(solution)/shard_map/all_to_all | solution.py:135
  67.2 5.5 %collective-permute-done.2 = f32[19,18,1,128]{3,0,2,1:T(8,128)S(1)} collective-permute-done((f32[19,18,1,128]{3,0,2,1:T(8,128)S(1)}, f32[19,18,1,128]{3,0,2,1:T(8,128)S(1)}, u32[]{:S(2)}, u32[]{:S(2)}) %collective-permute-start.2) | collective-permute-done | bytes 175136 | tf_op jit(solution)/shard_map/ppermute | solution.py:49
  72.7 2.9 %collective-permute-done.3 = f32[19,18,1,128]{3,0,2,1:T(8,128)S(1)} collective-permute-done((f32[19,18,1,128]{3,0,2,1:T(8,128)S(1)}, f32[19,18,1,128]{3,0,2,1:T(8,128)S(1)}, u32[]{:S(2)}, u32[]{:S(2)}) %collective-permute-start.3) | collective-permute-done | bytes 175136 | tf_op jit(solution)/shard_map/ppermute | solution.py:50
  76.6 4.3 %fusion.57 = (f32[19,18,18,1]{3,0,2,1:T(8,128)}, f32[19,18,18,1]{3,0,2,1:T(8,128)}) fusion(f32[19,18,18,128]{3,0,2,1:T(8,128)S(1)} %pad_maximum_fusion), kind=kLoop, calls=%fused_computation.136 | loop fusion | bytes 98496 | tf_op jit(solution)/shard_map/slice | solution.py:48
  80.9 4.3 %copy.98 = f32[19,18,18,1]{0,3,2,1:T(1,128)} copy(f32[19,18,18,1]{3,0,2,1:T(8,128)} %get-tuple-element.34) | data formatting | bytes 49248 | tf_op jit(solution)/shard_map/slice | solution.py:48
  85.2 4.3 %copy.96 = f32[19,18,18,1]{0,3,2,1:T(1,128)} copy(f32[19,18,18,1]{3,0,2,1:T(8,128)} %get-tuple-element.35) | data formatting | bytes 49248 | tf_op jit(solution)/shard_map/slice | solution.py:47
  90.0 2.4 %pad_maximum_fusion.10 = (f32[1,16,16,128]{3,0,2,1:T(1,128)}, f32[1,16,16,128]{3,0,2,1:T(1,128)}, f32[1,16,16,128]{3,0,2,1:T(1,128)}, f32[1,16,16,128]{3,0,2,1:T(1,128)}, f32[1,16,16,128]{3,0,2,1:T(1,128)}) fusion(f32[19,18,1,128]{3,0,2,1:T(8,128)} %copy-done.6, f32[19,1,16,128]{3,0,2,1:T(8,128)S(1)} %collective-permute-done.1, ...), kind=kLoop, calls=%fused_computation.49 | loop fusion | flops 425984 | bytes 3807232 | tf_op jit(solution)/shard_map/slice | solution.py:147
  92.3 4.3 %copy.97 = f32[19,18,18,1]{3,0,2,1:T(8,128)} copy(f32[19,18,18,1]{0,3,2,1:T(1,128)} %collective-permute-done.4) | data formatting | bytes 49248 | tf_op jit(solution)/shard_map/ppermute | solution.py:49
  96.6 4.4 %pad_maximum_fusion.17 = (f32[1,16,16,128]{3,0,2,1:T(1,128)}, f32[1,16,16,128]{3,0,2,1:T(1,128)}, f32[1,16,16,128]{3,0,2,1:T(1,128)}) fusion(f32[19,18,18,1]{3,0,2,1:T(8,128)} %copy.97, f32[19,18,1,128]{3,0,2,1:T(8,128)} %copy-done.6, f32[19,18,1,128]{3,0,2,1:T(8,128)} %copy-done.3, f32[19,1,16,128]{3,0,2,1:T(8,128)S(1)} %collective-permute-done.1, ...), kind=kLoop, calls=%fused_computation.56 | loop fusion | flops 491520 | bytes 3569712 | tf_op jit(solution)/shard_map/concatenate | solution.py:51
  102.4 4.3 %copy.99 = f32[19,18,18,1]{3,0,2,1:T(8,128)} copy(f32[19,18,18,1]{0,3,2,1:T(1,128)} %collective-permute-done.5) | data formatting | bytes 49248 | tf_op jit(solution)/shard_map/ppermute | solution.py:50
  106.7 5.1 %pad_maximum_fusion.12 = (f32[1,16,16,128]{3,0,2,1:T(1,128)}, f32[1,16,16,128]{3,0,2,1:T(1,128)}, f32[1,16,16,128]{3,0,2,1:T(1,128)}) fusion(f32[19,18,18,1]{3,0,2,1:T(8,128)} %copy.99, f32[19,18,1,128]{3,0,2,1:T(8,128)} %copy-done.6, f32[19,18,1,128]{3,0,2,1:T(8,128)} %copy-done.3, f32[19,1,16,128]{3,0,2,1:T(8,128)S(1)} %collective-permute-done.1, ...), kind=kLoop, calls=%fused_computation.51 | loop fusion | flops 491520 | bytes 3569712 | tf_op jit(solution)/shard_map/concatenate | solution.py:51
  111.9 2.1 %pad_maximum_fusion.26 = (f32[1,16,16,128]{3,0,2,1:T(1,128)}, f32[1,16,16,128]{3,0,2,1:T(1,128)}, f32[1,16,16,128]{3,0,2,1:T(1,128)}, f32[1,16,16,128]{3,0,2,1:T(1,128)}, f32[1,16,16,128]{3,0,2,1:T(1,128)}) fusion(f32[19,18,18,1]{3,0,2,1:T(8,128)S(1)} %copy-done, f32[19,18,1,128]{3,0,2,1:T(8,128)S(1)} %copy-done.8, f32[19,18,1,128]{3,0,2,1:T(8,128)S(1)} %copy-done.5, ...), kind=kLoop, calls=%fused_computation.65 | loop fusion | flops 458752 | bytes 8749056 | tf_op jit(solution)/shard_map/slice | solution.py:147
  114.0 7.9 %stack.3 = f32[19,16,16,128]{3,0,2,1:T(8,128)S(1)} concatenate(f32[1,16,16,128]{3,0,2,1:T(1,128)} %get-tuple-element.48, f32[1,16,16,128]{3,0,2,1:T(1,128)} %get-tuple-element.33, f32[1,16,16,128]{3,0,2,1:T(1,128)} %get-tuple-element.31, f32[1,16,16,128]{3,0,2,1:T(1,128)} %get-tuple-element.42, f32[1,16,16,128]{3,0,2,1:T(1,128)} %get-tuple-element.39, ...), dimensions={0} | concatenate | bytes 4980736 | tf_op jit(solution)/shard_map/stack | solution.py:154
  122.0 1.9 %copy.102 = f32[19,16,16,128]{3,2,1,0:T(8,128)} copy(f32[19,16,16,128]{3,0,2,1:T(8,128)S(1)} %stack.3) | data formatting | bytes 4980736
  (90 shorter events, 17.4 us)
Async XLA Ops:
  0.6 14.8 %copy-start.11 = (f32[19,3,1,1]{0,1,3,2:T(4,128)S(1)}, f32[19,3,1,1]{0,1,3,2:T(4,128)}, u32[]{:S(2)}) copy-start(f32[19,3,1,1]{0,1,3,2:T(4,128)} %constant.58) | copy-start | bytes 688
  0.6 14.8 %copy-start.2 = (f32[19,16,16,128]{3,2,1,0:T(8,128)S(1)}, f32[19,16,16,128]{3,2,1,0:T(8,128)}, u32[]{:S(2)}) copy-start(f32[19,16,16,128]{3,2,1,0:T(8,128)} %param.11) | copy-start | bytes 7471108
  2.3 1.7 %copy-start.14 = (s32[128]{0:T(128)}, s32[128]{0:T(128)S(1)}, u32[]{:S(2)}) copy-start(s32[128]{0:T(128)S(1)} %multiply_add_fusion) | copy-start | bytes 1540
  4.8 16.7 %all-to-all-start = ((f32[8,1,320]{2,1,0:T(1,128)}), f32[8,1,320]{2,1,0:T(1,128)S(1)}, u32[]{:S(2)}, u32[]{:S(2)}) async-start(f32[8,1,320]{2,1,0:T(1,128)} %reshape.348), calls=%async_computation | async-start | bytes 24576 | tf_op jit(solution)/shard_map/all_to_all | solution.py:130
  13.6 5.7 %copy-start.13 = (s32[19]{0:T(128)S(1)}, s32[19]{0:T(128)}, u32[]{:S(2)}) copy-start(s32[19]{0:T(128)} %constant.56) | copy-start | bytes 232
  15.5 12.6 %copy-start.9 = (f32[16,16,128]{2,1,0:T(8,128)}, f32[16,16,128]{2,1,0:T(8,128)S(1)}, u32[]{:S(2)}) copy-start(f32[16,16,128]{2,1,0:T(8,128)S(1)} %reduce_sum.47) | copy-start | bytes 393220
  21.5 6.6 %copy-start.12 = (f32[19,3,1,1]{0,1,3,2:T(4,128)S(1)}, f32[19,3,1,1]{0,1,3,2:T(4,128)}, u32[]{:S(2)}) copy-start(f32[19,3,1,1]{0,1,3,2:T(4,128)} %constant.58) | copy-start | bytes 688
  21.5 6.6 %copy-start.16 = (f32[19]{0:T(128)S(1)}, f32[19]{0:T(128)}, u32[]{:S(2)}) copy-start(f32[19]{0:T(128)} %constant.51.clone) | copy-start | bytes 232
  28.1 5.4 %copy-start.10 = (f32[16,16,128]{2,1,0:T(8,128)}, f32[16,16,128]{2,1,0:T(8,128)S(1)}, u32[]{:S(2)}) copy-start(f32[16,16,128]{2,1,0:T(8,128)S(1)} %broadcast_multiply_fusion.1) | copy-start | bytes 393220
  49.7 14.5 %collective-permute-start = (f32[19,1,16,128]{3,0,2,1:T(8,128)}, f32[19,1,16,128]{3,0,2,1:T(8,128)S(1)}, u32[]{:S(2)}, u32[]{:S(2)}) collective-permute-start(f32[19,1,16,128]{3,0,2,1:T(8,128)} %get-tuple-element.49), channel_id=1, source_target_pairs={{0,4},{4,8},{8,12},{12,0},{1,5},{5,9},{9,13},{13,1},{2,6},{6,10},{... | collective-permute-start | bytes 466952 | tf_op jit(solution)/shard_map/ppermute | solution.py:49
  51.8 12.5 %collective-permute-start.1 = (f32[19,1,16,128]{3,0,2,1:T(8,128)}, f32[19,1,16,128]{3,0,2,1:T(8,128)S(1)}, u32[]{:S(2)}, u32[]{:S(2)}) collective-permute-start(f32[19,1,16,128]{3,0,2,1:T(8,128)} %get-tuple-element.50), channel_id=1, source_target_pairs={{4,0},{8,4},{12,8},{0,12},{5,1},{9,5},{13,9},{1,13},{6,2},{10,6},{... | collective-permute-start | bytes 466952 | tf_op jit(solution)/shard_map/ppermute | solution.py:50
  64.2 2.1 %copy-start.15 = (s32[128]{0:T(128)S(1)}, s32[128]{0:T(128)}, u32[]{:S(2)}) copy-start(s32[128]{0:T(128)} %copy-done.14) | copy-start | bytes 1540
  64.3 8.4 %collective-permute-start.2 = (f32[19,18,1,128]{3,0,2,1:T(8,128)S(1)}, f32[19,18,1,128]{3,0,2,1:T(8,128)S(1)}, u32[]{:S(2)}, u32[]{:S(2)}) collective-permute-start(f32[19,18,1,128]{3,0,2,1:T(8,128)S(1)} %get-tuple-element.44), channel_id=1, source_target_pairs={{0,2},{2,0},{1,3},{3,1},{4,6},{6,4},{5,7},{7,5},{8,10},{10,8},{9,1... | collective-permute-start | bytes 525320 | tf_op jit(solution)/shard_map/ppermute | solution.py:49
  64.9 10.8 %collective-permute-start.3 = (f32[19,18,1,128]{3,0,2,1:T(8,128)S(1)}, f32[19,18,1,128]{3,0,2,1:T(8,128)S(1)}, u32[]{:S(2)}, u32[]{:S(2)}) collective-permute-start(f32[19,18,1,128]{3,0,2,1:T(8,128)S(1)} %get-tuple-element.45), channel_id=1, source_target_pairs={{2,0},{0,2},{3,1},{1,3},{6,4},{4,6},{7,5},{5,7},{10,8},{8,10},{11,... | collective-permute-start | bytes 525320 | tf_op jit(solution)/shard_map/ppermute | solution.py:50
  72.7 2.9 %copy-start.3 = (f32[19,18,1,128]{3,0,2,1:T(8,128)}, f32[19,18,1,128]{3,0,2,1:T(8,128)S(1)}, u32[]{:S(2)}) copy-start(f32[19,18,1,128]{3,0,2,1:T(8,128)S(1)} %collective-permute-done.2) | copy-start | bytes 525316
  75.6 0.7 copy-start.6
  85.2 17.2 %collective-permute-start.5 = (f32[19,18,18,1]{0,3,2,1:T(1,128)}, f32[19,18,18,1]{0,3,2,1:T(1,128)}, u32[]{:S(2)}, u32[]{:S(2)}) collective-permute-start(f32[19,18,18,1]{0,3,2,1:T(1,128)} %copy.98), channel_id=1, source_target_pairs={{1,0},{0,1},{3,2},{2,3},{5,4},{4,5},{7,6},{6,7},{9,8},{8,9},{11,10... | collective-permute-start | bytes 73880 | tf_op jit(solution)/shard_map/ppermute | solution.py:50
  89.5 2.9 %collective-permute-start.4 = (f32[19,18,18,1]{0,3,2,1:T(1,128)}, f32[19,18,18,1]{0,3,2,1:T(1,128)}, u32[]{:S(2)}, u32[]{:S(2)}) collective-permute-start(f32[19,18,18,1]{0,3,2,1:T(1,128)} %copy.96), channel_id=1, source_target_pairs={{0,1},{1,0},{2,3},{3,2},{4,5},{5,4},{6,7},{7,6},{8,9},{9,8},{10,11... | collective-permute-start | bytes 73880 | tf_op jit(solution)/shard_map/ppermute | solution.py:49
  96.6 4.4 %copy-start.1 = (f32[19,18,18,1]{3,0,2,1:T(8,128)S(1)}, f32[19,18,18,1]{3,0,2,1:T(8,128)}, u32[]{:S(2)}) copy-start(f32[19,18,18,1]{3,0,2,1:T(8,128)} %copy.97) | copy-start | bytes 73876
  96.6 4.4 %copy-start.4 = (f32[19,18,1,128]{3,0,2,1:T(8,128)S(1)}, f32[19,18,1,128]{3,0,2,1:T(8,128)}, u32[]{:S(2)}) copy-start(f32[19,18,1,128]{3,0,2,1:T(8,128)} %copy-done.3) | copy-start | bytes 525316
  96.6 4.4 %copy-start.7 = (f32[19,18,1,128]{3,0,2,1:T(8,128)S(1)}, f32[19,18,1,128]{3,0,2,1:T(8,128)}, u32[]{:S(2)}) copy-start(f32[19,18,1,128]{3,0,2,1:T(8,128)} %copy-done.6) | copy-start | bytes 525316
  106.7 5.1 %copy-start = (f32[19,18,18,1]{3,0,2,1:T(8,128)S(1)}, f32[19,18,18,1]{3,0,2,1:T(8,128)}, u32[]{:S(2)}) copy-start(f32[19,18,18,1]{3,0,2,1:T(8,128)} %copy.99) | copy-start | bytes 73876
  106.7 5.1 %copy-start.5 = (f32[19,18,1,128]{3,0,2,1:T(8,128)S(1)}, f32[19,18,1,128]{3,0,2,1:T(8,128)}, u32[]{:S(2)}) copy-start(f32[19,18,1,128]{3,0,2,1:T(8,128)} %copy-done.3) | copy-start | bytes 525316
  106.7 5.1 %copy-start.8 = (f32[19,18,1,128]{3,0,2,1:T(8,128)S(1)}, f32[19,18,1,128]{3,0,2,1:T(8,128)}, u32[]{:S(2)}) copy-start(f32[19,18,1,128]{3,0,2,1:T(8,128)} %copy-done.6) | copy-start | bytes 525316
where the time goes:
time: 125 us; the launch traced here: 124 us
  local copies, waits for them, and re-layouts  39.9 us (32%)
  matrix products  26.7 us (21%)
  other arithmetic  23.7 us (19%)
  starting transfers between devices  13.7 us (11%)
  blocking collectives  10.6 us (8%)
  waiting for transfers between devices  8.44 us (7%)
    dot_general x1, matrix products, collide(): jnp.einsum('qd,dzyx->qzyx', table, force, precision=lax.Precision.HIGHEST)  12.8 us
    all_to_all x1, blocking collectives, shards(): lax.all_to_all(drag.reshape(3, owners, CAP), ('slab', 'col'), split_axis=...  10.6 us
    concatenate x3, other arithmetic, with_halo(): value = jnp.concatenate([before, value, after], axis=dim)  9.77 us
    slice x2, local copies, waits for them, and re-layouts, with_halo(): first = lax.slice_in_dim(value, 0, width, axis=dim)  8.6 us
    another operation x1, local copies, waits for them, and re-layouts, shards(): next_populations = jnp.stack(moved)  7.94 us
    all_to_all x1, starting transfers between devices, shards(): lax.all_to_all(packed.reshape(10, owners, CAP), ('slab', 'col'), split_ax...  7.25 us
    slice x3, other arithmetic, shards(): padded[member, 1 - step_z:1 - step_z + depth, 1 - step_y:1 - step_y + row...  5.9 us
    ppermute x3, waiting for transfers between devices, with_halo(): before = lax.ppermute(last, axis, up)  5.51 us
  transfers between devices with their start and end apart: 7, of which 2 were waited for; matrix products, arithmetic and copies ran while one was open for 22% of the time, Pallas kernels for 0%

commit v1 on v0

v1 whole, which is shorter than its diff:
```python
import functools

import jax
import jax.numpy as jnp
import numpy as np
from jax import lax
from jax.experimental import pallas as pl
from jax.experimental.pallas import tpu as pltpu
from jax.sharding import PartitionSpec as P

CAP = 32
GROUP = 8

STEP = np.array(
    [
        [0, 0, 0],
        [1, 0, 0],
        [-1, 0, 0],
        [0, 1, 0],
        [0, -1, 0],
        [0, 0, 1],
        [0, 0, -1],
        [1, 1, 0],
        [-1, -1, 0],
        [1, -1, 0],
        [-1, 1, 0],
        [1, 0, 1],
        [-1, 0, -1],
        [1, 0, -1],
        [-1, 0, 1],
        [0, 1, 1],
        [0, -1, -1],
        [0, 1, -1],
        [0, -1, 1],
    ],
    np.int32,
)
TAU_PLUS = 0.8
TAU_MINUS = 0.5 + (3.0 / 16.0) / (TAU_PLUS - 0.5)
KEEP_EVEN = 1.0 - 1.0 / TAU_PLUS
KEEP_ODD = 1.0 - 1.0 / TAU_MINUS
FORCE_GAIN = 1.0 - 0.5 / TAU_PLUS
DRAG_COEF = 2.0
F32 = jnp.float32
BF16 = jnp.bfloat16

X_PLUS = [i for i in range(19) if STEP[i, 0] == 1]
X_MINUS = [i for i in range(19) if STEP[i, 0] == -1]
NT = (((1,), (1,)), ((), ()))
NN = (((1,), (0,)), ((), ()))


def iota(shape, dim):
    return lax.broadcasted_iota(jnp.int32, shape, dim)


def high_low(value):
    high = value.astype(BF16)
    return high, (value - high.astype(F32)).astype(BF16)


def dot_split(left, right, dims):
    a, b = high_low(left)
    c, d = high_low(right)
    mul = functools.partial(lax.dot_general, dimension_numbers=dims, preferred_element_type=F32)
    return mul(a, c) + (mul(a, d) + mul(b, c))


def dot_select(value, choose, dims):
    first = value.astype(BF16).astype(F32)
    rest = value - first
    second = rest.astype(BF16).astype(F32)
    stacked = jnp.concatenate([first, second, rest - second], axis=0).astype(BF16)
    got = lax.dot_general(stacked, choose, dimension_numbers=dims, preferred_element_type=F32)
    rows = value.shape[0]
    return got[0:rows] + got[rows : 2 * rows] + got[2 * rows : 3 * rows]


def density_momentum(pops):
    momentum = []
    for axis in range(3):
        plus = [pops[i] for i in range(19) if STEP[i, axis] == 1]
        minus = [pops[i] for i in range(19) if STEP[i, axis] == -1]
        momentum.append(sum(plus[1:], plus[0]) - sum(minus[1:], minus[0]))
    return sum(pops[1:], pops[0]), momentum


def along(step, vector):
    terms = None
    for axis in range(3):
        if step[axis] == 0:
            continue
        if terms is None:
            terms = vector[axis] if step[axis] == 1 else -vector[axis]
        else:
            terms = terms + vector[axis] if step[axis] == 1 else terms - vector[axis]
    return terms


def collide(pops, solid, force):
    density, momentum = density_momentum(pops)
    inverse = 1.0 / density
    carried = [m + 0.5 * f for m, f in zip(momentum, force)]
    speed = [m * inverse for m in carried]
    w = 1.0 / 36.0
    bend = [(4.5 * w / TAU_PLUS) * m + (9.0 * w * FORCE_GAIN) * f for m, f in zip(carried, force)]
    push = [(3.0 * w / TAU_MINUS) * m + (3.0 * w * FORCE_GAIN) * f for m, f in zip(carried, force)]
    drop = [(1.5 * w / TAU_PLUS) * m + (3.0 * w * FORCE_GAIN) * f for m, f in zip(carried, force)]
    rest = (w / TAU_PLUS) * density - sum(
        [u * d for u, d in zip(speed[1:], drop[1:])], speed[0] * drop[0]
    )
    wall = solid == 1
    out = [None] * 19
    out[0] = jnp.where(wall, pops[0], KEEP_EVEN * pops[0] + 12.0 * rest)
    for i in range(1, 19, 2):
        a, b = pops[i], pops[i + 1]
        step = STEP[i]
        even = rest + along(step, speed) * along(step, bend)
        odd = along(step, push)
        if i < 7:
            even = even + even
            odd = odd + odd
        even = (0.5 * KEEP_EVEN) * (a + b) + even
        odd = (0.5 * KEEP_ODD) * (a - b) + odd
        out[i] = jnp.where(wall, b, even + odd)
        out[i + 1] = jnp.where(wall, a, even - odd)
    return out


def turn(value, amount, axis):
    if amount == 0:
        return value
    return pltpu.roll(value, int(amount) % value.shape[axis], axis)


def message_plan(shape):
    plan = {}
    for i in range(1, 19):
        moving = [a for a in (2, 1, 0) if STEP[i, a] != 0]
        subsets = [[a] for a in moving] + ([moving] if len(moving) == 2 else [])
        for axes in subsets:
            if axes == [0]:
                continue
            key = tuple(
                int(STEP[i, a]) % shape[k] if a in axes else 0 for k, a in enumerate((2, 1, 0))
            )
            plan.setdefault(key, []).append((i, tuple(axes)))
    return plan


def part_rows(part, span):
    return 8 if part[1] == (2, 1) else span


def message_rows(parts, span, with_drag):
    rows = 8 if with_drag else 0
    places = {}
    for part in parts:
        places[part] = rows
        rows += part_rows(part, span)
    return rows, places


def send(value, shape, offset):
    slabs, cols, pairs = shape
    perm = []
    for s in range(slabs):
        for c in range(cols):
            for p in range(pairs):
                there = (
                    ((s + offset[0]) % slabs) * cols + (c + offset[1]) % cols
                ) * pairs + (p + offset[2]) % pairs
                perm.append(((s * cols + c) * pairs + p, there))
    return lax.ppermute(value, ("slab", "col", "pair"), perm)


def wrap(value, size):
    return jnp.where(value < 0, value + size, value)


def pack_kernel(slabs, cols, count, single, owner_ref, base_ref, offset_ref, velocity_ref, target_ref, *rest):
    outs, table = rest[:-1], rest[-1]
    owner = owner_ref[...]
    owner_slab = lax.shift_right_logical(owner, cols.bit_length() - 1)
    owner_col = owner - owner_slab * cols
    relative = wrap(owner_slab - lax.axis_index("slab"), slabs) * cols + wrap(
        owner_col - lax.axis_index("col"), cols
    )
    first = 0 if single else pl.program_id(0) * GROUP
    local = relative - first
    member = (iota((GROUP, count), 0) == local).astype(F32)
    earlier = (iota((count, count), 0) < iota((count, count), 1)).astype(F32).astype(BF16)
    ahead = lax.dot_general(member.astype(BF16), earlier, NN, preferred_element_type=F32)
    rank = jnp.sum(member * ahead, axis=0, keepdims=True).astype(jnp.int32)
    inside = (local >= 0) & (local < GROUP)
    target = jnp.where(inside, local * CAP + rank, -1)
    whole_target = jnp.where(inside, relative * CAP + rank, -1)
    if single:
        target_ref[...] = whole_target
    else:

        @pl.when(pl.program_id(0) == 0)
        def _():
            target_ref[...] = whole_target

        @pl.when(pl.program_id(0) > 0)
        def _():
            target_ref[...] = jnp.maximum(target_ref[...], whole_target)

    choose = (iota((GROUP * CAP, count), 0) == target).astype(F32).astype(BF16)
    table[...] = jnp.zeros_like(table)
    table[0:3] = base_ref[...].astype(F32) + 1.0
    table[8:11] = offset_ref[...]
    table[16:19] = velocity_ref[...]
    packed = dot_select(table[...], choose, NT)
    blank = jnp.zeros((8, CAP), F32)
    for r in range(GROUP):
        lanes = slice(r * CAP, (r + 1) * CAP)
        tile = jnp.concatenate(
            [packed[0:8, lanes], packed[8:16, lanes], packed[16:24, lanes], blank], axis=1
        )
        if single:
            outs[r][...] = tile
        else:
            outs[0][r] = tile


def pack(slabs, cols, owner, base, offset, velocity):
    owners, count = slabs * cols, owner.shape[0]
    single = owners == GROUP
    tile = jax.ShapeDtypeStruct((8, 128), F32)
    target = jax.ShapeDtypeStruct((1, count), jnp.int32)
    kernel = functools.partial(pack_kernel, slabs, cols, count, single)
    scratch = [pltpu.VMEM((24, count), F32)]
    args = (owner.reshape(1, count), base, offset, velocity)
    if single:
        target, *tiles = pl.pallas_call(
            kernel, out_shape=[target] + [tile] * owners, scratch_shapes=scratch, name="pack"
        )(*args)
        return target, tiles
    return pl.pallas_call(
        kernel,
        out_shape=[target, jax.ShapeDtypeStruct((owners, 8, 128), F32)],
        grid=(owners // GROUP,),
        in_specs=[pl.BlockSpec(a.shape, lambda k: (0, 0)) for a in args],
        out_specs=[
            pl.BlockSpec((1, count), lambda k: (0, 0)),
            pl.BlockSpec((GROUP, 8, 128), lambda k: (k, 0, 0)),
        ],
        scratch_shapes=scratch,
        compiler_params=pltpu.CompilerParams(vmem_limit_bytes=48 << 20),
        name="pack",
    )(*args)


def moments_kernel(pops_ref, solid_ref, flow_ref, edge_ref, edge_solid_ref):
    depth, rows = pops_ref.shape[1], pops_ref.shape[2]

    def plane(z, carry):
        pops = [pops_ref[i, z] for i in range(19)]
        density, momentum = density_momentum(pops)
        inverse = 1.0 / density
        for axis in range(3):
            flow_ref[axis, pl.ds(pl.multiple_of(z * rows, rows), rows)] = momentum[axis] * inverse
        return carry

    lax.fori_loop(0, depth, plane, 0)
    for i in range(19):
        edge_ref[i, 0] = pops_ref[i, 0]
        edge_ref[i, 1] = pops_ref[i, depth - 1]
        edge_ref[i, 2] = pops_ref[i, :, 0, :]
        edge_ref[i, 3] = pops_ref[i, :, rows - 1, :]
    edge_solid_ref[0] = solid_ref[0]
    edge_solid_ref[1] = solid_ref[depth - 1]
    edge_solid_ref[2] = solid_ref[:, 0, :]
    edge_solid_ref[3] = solid_ref[:, rows - 1, :]


def moments(pops, solid):
    _, depth, rows, width = pops.shape
    return pl.pallas_call(
        moments_kernel,
        out_shape=[
            jax.ShapeDtypeStruct((3, depth * rows, width), F32),
            jax.ShapeDtypeStruct((19, 4, rows, width), F32),
            jax.ShapeDtypeStruct((4, rows, width), jnp.int32),
        ],
        compiler_params=pltpu.CompilerParams(vmem_limit_bytes=16 << 20),
        cost_estimate=pl.CostEstimate(flops=3000000, bytes_accessed=4000000, transcendentals=0),
        name="moments",
    )(pops, solid)


def couple_group(tiles, flow, depth, rows):
    width, slots = flow.shape[1], GROUP * CAP
    base = jnp.concatenate([t[:, 0:CAP] for t in tiles], axis=1)
    part = jnp.concatenate([t[:, CAP : 2 * CAP] for t in tiles], axis=1)
    velocity = jnp.concatenate([t[:, 2 * CAP : 3 * CAP] for t in tiles], axis=1)
    start = base.astype(jnp.int32) - 1

    def hat(axis, length):
        cell = iota((length, slots), 0)
        low, share = start[axis : axis + 1], part[axis : axis + 1]
        return jnp.where(cell == low, 1.0 - share, 0.0) + jnp.where(cell == low + 1, share, 0.0)

    hat_x, hat_y, hat_z = hat(0, width), hat(1, rows), hat(2, depth)
    weight = (hat_z[:, None, :] * hat_y[None, :, :]).reshape(depth * rows, slots)
    across = dot_split(flow, hat_x, NN)
    cells = depth * rows
    sampled = [
        jnp.sum(across[d * cells : (d + 1) * cells] * weight, axis=0, keepdims=True)
        for d in range(3)
    ]
    drag = [DRAG_COEF * (sampled[d] - velocity[d : d + 1]) for d in range(3)]
    spread = jnp.concatenate([weight * (-drag[d]) for d in range(3)], axis=0)
    return drag, dot_split(spread, hat_x, NT)


def couple_kernel(
    single, shape, plan, depth, rows, n_in, flow_ref, edge_ref, edge_solid_ref, *refs
):
    ins, force_ref, refs = refs[:n_in], refs[n_in], refs[n_in + 1 :]
    width = flow_ref.shape[2]
    flow = flow_ref[...].reshape(3 * depth * rows, width)
    blank = jnp.zeros((8, 128 - CAP), F32)
    hollow = jnp.zeros((5, GROUP * CAP), F32)

    def drag_tiles(drag):
        stacked = jnp.concatenate(drag + [hollow], axis=0)
        return [
            jnp.concatenate([stacked[:, r * CAP : (r + 1) * CAP], blank], axis=1)
            for r in range(GROUP)
        ]

    if single:
        drag, force = couple_group([t[...] for t in ins], flow, depth, rows)
        force_ref[...] = force.reshape(3, depth, rows, width)
        tiles = drag_tiles(drag)
        refs[0][...] = tiles[0]
        messages = dict(zip(sorted(plan), refs[1:]))
        for r in range(1, GROUP):
            dz, dy = divmod(r, shape[1])
            messages[((-dz) % shape[0], (-dy) % shape[1], 0)][0:8] = tiles[r]
    else:
        force_ref[...] = jnp.zeros_like(force_ref)

        def group(k, carry):
            got = [ins[0][k * GROUP + r] for r in range(GROUP)]
            drag, force = couple_group(got, flow, depth, rows)
            force_ref[...] += force.reshape(3, depth, rows, width)
            for r, tile in enumerate(drag_tiles(drag)):
                refs[0][k * GROUP + r] = tile
            return carry

        lax.fori_loop(0, ins[0].shape[0] // GROUP, group, 0)
        messages = dict(zip(sorted(plan), refs[1:]))

    places = {
        key: message_rows(parts, rows, single and key[2] == 0)[1] for key, parts in plan.items()
    }
    for side in range(4):
        pops = [edge_ref[i, side] for i in range(19)]
        if side < 2:
            force = [force_ref[d, (0, depth - 1)[side]] for d in range(3)]
        else:
            force = [force_ref[d, :, (0, rows - 1)[side - 2], :] for d in range(3)]
        out = collide(pops, edge_solid_ref[side], force)
        axis = 2 if side < 2 else 1
        leaving = -1 if side % 2 == 0 else 1
        for i in range(19):
            if STEP[i, axis] != leaving:
                continue
            moved = turn(out[i], STEP[i, 1 if axis == 2 else 2], 0)
            moved = turn(moved, STEP[i, 0], 1)
            for key, parts in plan.items():
                for part in parts:
                    if part[0] != i or part[1][0] != axis:
                        continue
                    row = places[key][part]
                    if part[1] == (2, 1):
                        kept = 0 if STEP[i, 1] == 1 else rows - 1
                        messages[key][row : row + 8] = jnp.broadcast_to(
                            moved[kept : kept + 1], (8, width)
                        )
                    else:
                        messages[key][row : row + rows] = moved


def couple(shape, plan, tiles, flow, edge, edge_solid, depth, rows, single):
    width = flow.shape[2]
    sizes = [
        message_rows(plan[key], rows, single and key[2] == 0)[0] for key in sorted(plan)
    ]
    own = (8, 128) if single else tiles[0].shape
    out_shape = [
        jax.ShapeDtypeStruct((3, depth, rows, width), F32),
        jax.ShapeDtypeStruct(own, F32),
    ] + [jax.ShapeDtypeStruct((n, width), F32) for n in sizes]
    force, drag, *messages = pl.pallas_call(
        functools.partial(couple_kernel, single, shape, plan, depth, rows, len(tiles)),
        out_shape=out_shape,
        compiler_params=pltpu.CompilerParams(vmem_limit_bytes=24 << 20),
        name="couple",
    )(flow, edge, edge_solid, *tiles)
    return force, drag, dict(zip(sorted(plan), messages))


def stream_kernel(pops_ref, solid_ref, force_ref, out_ref, column_ref):
    depth, rows, width = pops_ref.shape[1:]
    lane = iota((rows, width), 1)

    def plane(z, columns):
        pops = [pops_ref[i, z] for i in range(19)]
        out = collide(pops, solid_ref[z], [force_ref[d, z] for d in range(3)])
        columns = list(columns)
        for i in range(19):
            moved = turn(turn(out[i], STEP[i, 1], 0), STEP[i, 0], 1)
            there = z + int(STEP[i, 2])
            there = jnp.where(there < 0, depth - 1, jnp.where(there == depth, 0, there))
            out_ref[i, there] = moved
            for side, group, edge in ((0, X_PLUS, 0), (1, X_MINUS, width - 1)):
                if i in group:
                    place = group.index(i) * depth + there
                    column = jnp.broadcast_to(moved[:, edge : edge + 1], (rows, width))
                    columns[side] = jnp.where(lane == place, column, columns[side])
        return tuple(columns)

    zero = jnp.zeros((rows, width), F32)
    columns = lax.fori_loop(0, depth, plane, (zero, zero))
    column_ref[0] = columns[0]
    column_ref[1] = columns[1]


def stream(pops, solid, force):
    _, depth, rows, width = pops.shape
    return pl.pallas_call(
        stream_kernel,
        out_shape=[
            jax.ShapeDtypeStruct(pops.shape, F32),
            jax.ShapeDtypeStruct((2, rows, width), F32),
        ],
        compiler_params=pltpu.CompilerParams(vmem_limit_bytes=16 << 20),
        cost_estimate=pl.CostEstimate(flops=10000000, bytes_accessed=6000000, transcendentals=0),
        name="stream",
    )(pops, solid, force)


def finish_kernel(
    single, shape, plan, n_back, target_ref, local_ref, column_ref, *refs
):
    backs, refs = refs[:n_back], refs[n_back:]
    keys = sorted(plan)
    messages, refs = dict(zip(keys, refs[: len(keys)])), refs[len(keys) :]
    out_ref, bead_ref, held, sem = refs
    depth, rows, width = local_ref.shape[1:]
    lane = iota((rows, width), 1)
    places = {}
    for key in keys:
        for part, row in message_rows(plan[key], rows, single and key[2] == 0)[1].items():
            places[part] = (messages[key], row)

    def arrived(part):
        ref, row = places[part]
        return ref[row : row + part_rows(part, rows)]

    copies = []
    for i in range(19):
        step = STEP[i]
        side = 0 if step[0] == 1 else width - 1
        enter_z = 0 if step[2] == 1 else depth - 1
        enter_y = 0 if step[1] == 1 else rows - 1
        if step[0] != 0:
            group, which = (X_PLUS, 0) if step[0] == 1 else (X_MINUS, 1)
            columns = column_ref[which]
            for z in range(depth):
                place = group.index(i) * depth + z
                column = jnp.broadcast_to(columns[:, place : place + 1], (rows, width))
                held[i, z] = jnp.where(lane == side, column, local_ref[i, z])
        else:
            held[i] = local_ref[i]
        for axis in (2, 1):
            if step[axis] == 0:
                continue
            value = arrived((i, (axis,)))
            if step[0] != 0:
                value = jnp.where(lane == side, arrived((i, (axis, 0))), value)
            if axis == 2:
                held[i, enter_z] = value
            else:
                held[i, :, enter_y, :] = value
        if step[1] != 0 and step[2] != 0:
            held[i, enter_z, enter_y : enter_y + 1, :] = arrived((i, (2, 1)))[0:1]
        copy = pltpu.make_async_copy(held.at[i], out_ref.at[i], sem.at[i])
        copy.start()
        copies.append(copy)

    count = target_ref.shape[1]

    def gathered(tiles, first):
        slots = jnp.concatenate([t[:, 0:CAP] for t in tiles], axis=1)
        choose = (iota((GROUP * CAP, count), 0) + first == target_ref[...]).astype(F32)
        return dot_select(slots, choose.astype(BF16), NN)[0:3]

    if single:
        tiles = [backs[0][...]]
        for r in range(1, GROUP):
            dz, dy = divmod(r, shape[1])
            tiles.append(messages[((-dz) % shape[0], (-dy) % shape[1], 0)][0:8])
        bead_ref[...] = gathered(tiles, 0)
    else:

        def group(k, total):
            tiles = [backs[0][k * GROUP + r] for r in range(GROUP)]
            return total + gathered(tiles, k * (GROUP * CAP))

        bead_ref[...] = lax.fori_loop(
            0, backs[0].shape[0] // GROUP, group, jnp.zeros((3, count), F32)
        )
    for copy in copies:
        copy.wait()


def finish(shape, plan, target, local, columns, backs, messages, single):
    vmem = pl.BlockSpec(memory_space=pltpu.VMEM)
    args = [target, local, columns, *backs, *[messages[key] for key in sorted(plan)]]
    return pl.pallas_call(
        functools.partial(finish_kernel, single, shape, plan, len(backs)),
        out_shape=[
            jax.ShapeDtypeStruct(local.shape, F32),
            jax.ShapeDtypeStruct((3, target.shape[1]), F32),
        ],
        in_specs=[vmem] * len(args),
        out_specs=[pl.BlockSpec(memory_space=pl.ANY), vmem],
        scratch_shapes=[pltpu.VMEM(local.shape, F32), pltpu.SemaphoreType.DMA((19,))],
        compiler_params=pltpu.CompilerParams(vmem_limit_bytes=24 << 20),
        name="finish",
    )(*args)


def shards(populations, solid_mask, bead_owner, bead_base, bead_offset, bead_velocity):
    slabs, cols, pairs = shape = tuple(lax.axis_size(a) for a in ("slab", "col", "pair"))
    owners = slabs * cols
    depth, rows = populations.shape[1:3]
    single = owners == GROUP
    plan = message_plan(shape)
    if single:
        for r in range(1, owners):
            plan.setdefault(divmod(r, cols) + (0,), [])

    target, tiles = pack(slabs, cols, bead_owner, bead_base, bead_offset, bead_velocity)
    if single:
        tiles = [tiles[0]] + [
            send(tiles[r], shape, divmod(r, cols) + (0,)) for r in range(1, owners)
        ]
    else:
        slab, col = lax.axis_index("slab"), lax.axis_index("col")
        index = jnp.arange(owners, dtype=jnp.int32)
        away = ((index // cols - slab) % slabs) * cols + (index % cols - col) % cols
        back = ((index // cols + slab) % slabs) * cols + (index % cols + col) % cols
        swap = functools.partial(
            lax.all_to_all, axis_name=("slab", "col"), split_axis=0, concat_axis=0, tiled=True
        )
        tiles = [swap(tiles[away])]
    flow, edge, edge_solid = moments(populations, solid_mask)
    force, drag, messages = couple(
        shape, plan, tiles, flow, edge, edge_solid, depth, rows, single
    )
    messages = {key: send(value, shape, key) for key, value in messages.items()}
    if not single:
        drag = swap(drag)[back]
    local, columns = stream(populations, solid_mask, force)
    columns = send(columns, shape, (0, 0, 1))
    return finish(shape, plan, target, local, columns, [drag], messages, single)


def solution(mesh):
    return jax.shard_map(
        shards,
        mesh=mesh,
        in_specs=(
            P(None, ("rep", "slab"), "col", "pair"),
            P(("rep", "slab"), "col", "pair"),
            P(("rep", "slab", "col", "pair")),
            P(None, ("rep", "slab", "col", "pair")),
            P(None, ("rep", "slab", "col", "pair")),
            P(None, ("rep", "slab", "col", "pair")),
        ),
        out_specs=(
            P(None, ("rep", "slab"), "col", "pair"),
            P(None, ("rep", "slab", "col", "pair")),
        ),
        check_vma=False,
    )
```

time: 125 us -> 44.7 us (0.36)
  local copies, waits for them, and re-layouts: 39.9 us -> 2.62 us
  matrix products: 26.7 us -> 0 us
  other arithmetic: 23.7 us -> 0 us
  starting transfers between devices: 13.7 us -> 28.3 us
  blocking collectives: 10.6 us -> 0 us
  Pallas kernels: 0 us -> 9.79 us
  waiting for transfers between devices: 8.44 us -> 3.06 us
    dot_general x7 -> x0, matrix products: 26.7 us -> none  [the longest x1 12.8 us: collide(): jnp.einsum('qd,dzyx->qzyx', table, force, precision=lax.Precision.HIGHEST)]
    ppermute x6 -> x18, starting transfers between devices: 6.43 us -> 28.3 us  [send(): return lax.ppermute(value, ('slab', 'col', 'pair'), perm)]
    slice x6 -> x0, local copies, waits for them, and re-layouts: 13.7 us -> none  [the longest x2 8.6 us: with_halo(): first = lax.slice_in_dim(value, 0, width, axis=dim)]
    all_to_all x1 -> x0, blocking collectives: 10.6 us -> none  [shards(): lax.all_to_all(drag.reshape(3, owners, CAP), ('slab', 'col'), split_axis=...]
    pallas_call x0 -> x5, Pallas kernels: none -> 9.79 us  [the longest x1 3.51 us: stream(): pl.pallas_call(stream_kernel, out_shape=[jax.ShapeDtypeStruct(pops.shape,...]
    concatenate x3 -> x0, other arithmetic: 9.77 us -> none  [with_halo(): value = jnp.concatenate([before, value, after], axis=dim)]
    ppermute x2 -> x0, local copies, waits for them, and re-layouts: 8.57 us -> none  [the longest x1 4.29 us: with_halo(): after = lax.ppermute(first, axis, down)]
    another operation x1 -> x0, local copies, waits for them, and re-layouts: 7.94 us -> none  [shards(): next_populations = jnp.stack(moved)]
  transfers between devices with their start and end apart: 7 -> 18, of which waited for: 2 -> 3; matrix products, arithmetic and copies ran while one was open for 22% -> 0% of each run, Pallas kernels for 0% -> 9%
where the time goes in v1:
time: 44.7 us; the launch traced here: 44.5 us
  starting transfers between devices  28.3 us (63%)
  Pallas kernels  9.79 us (22%)
  waiting for transfers between devices  3.06 us (7%)
  local copies, waits for them, and re-layouts  2.62 us (6%)
  between operations  0.74 us (2%)
    ppermute x18, starting transfers between devices, send(): return lax.ppermute(value, ('slab', 'col', 'pair'), perm)  28.3 us
    pallas_call x1, Pallas kernels, stream(): pl.pallas_call(stream_kernel, out_shape=[jax.ShapeDtypeStruct(pops.shape,...  3.51 us
    ppermute x18, waiting for transfers between devices, send(): return lax.ppermute(value, ('slab', 'col', 'pair'), perm)  3.06 us
    unnamed x12, local copies, waits for them, and re-layouts  2.62 us
    pallas_call x1, Pallas kernels, finish(): pl.pallas_call(functools.partial(finish_kernel, single, shape, plan, len(...  2.26 us
    pallas_call x1, Pallas kernels, pack(): pl.pallas_call(kernel, out_shape=[target] + [tile] * owners, scratch_shap...  1.74 us
    pallas_call x1, Pallas kernels, couple(): pl.pallas_call(functools.partial(couple_kernel, single, shape, plan, dept...  1.65 us
  transfers between devices with their start and end apart: 18, of which 3 were waited for; matrix products, arithmetic and copies ran while one was open for 0% of the time, Pallas kernels for 9%

profile of v1, /device:TPU:0, one launch (start us, length us, event | category | flops | bytes accessed | tf_op | source)
XLA Modules:
  0.0 44.5 jit_solution(7503784662286036936)
XLA Ops:
  0.6 1.7 %pack.1 = (s32[1,128]{1,0:T(1,128)}, f32[8,128]{1,0:T(8,128)}, f32[8,128]{1,0:T(8,128)}, f32[8,128]{1,0:T(8,128)}, f32[8,128]{1,0:T(8,128)}, /*index=5*/f32[8,12...) custom-call(s32[1,128]{1,0:T(1,128)} %bitcast.1, s32[3,128]{1,0:T(4,128)} %base_ref.1, ...), custom_call_target="tpu_custom_call" | custom-call | tf_op jit(solution)/shard_map/pack/pallas_call | solution.py:237
  2.4 3.0 %collective-permute-start = (f32[8,128]{1,0:T(8,128)}, f32[8,128]{1,0:T(8,128)S(1)}, u32[]{:S(2)}, u32[]{:S(2)}) collective-permute-start(f32[8,128]{1,0:T(8,128)} %get-tuple-element.33), channel_id=1, source_target_pairs={{0,2},{1,3},{2,0},{3,1},{4,6},{5,7},{6,4},{7,5},{8,10},{9,11},{10,... | collective-permute-start | bytes 12296 | tf_op jit(solution)/shard_map/ppermute | solution.py:174
  5.4 1.6 %collective-permute-start.1 = (f32[8,128]{1,0:T(8,128)}, f32[8,128]{1,0:T(8,128)S(1)}, u32[]{:S(2)}, u32[]{:S(2)}) collective-permute-start(f32[8,128]{1,0:T(8,128)} %get-tuple-element.34), channel_id=1, source_target_pairs={{0,4},{1,5},{2,6},{3,7},{4,8},{5,9},{6,10},{7,11},{8,12},{9,13},{1... | collective-permute-start | bytes 12296 | tf_op jit(solution)/shard_map/ppermute | solution.py:174
  6.9 1.5 %collective-permute-start.2 = (f32[8,128]{1,0:T(8,128)}, f32[8,128]{1,0:T(8,128)S(1)}, u32[]{:S(2)}, u32[]{:S(2)}) collective-permute-start(f32[8,128]{1,0:T(8,128)} %get-tuple-element.35), channel_id=1, source_target_pairs={{0,6},{1,7},{2,4},{3,5},{4,10},{5,11},{6,8},{7,9},{8,14},{9,15},{1... | collective-permute-start | bytes 12296 | tf_op jit(solution)/shard_map/ppermute | solution.py:174
  8.5 1.0 %collective-permute-start.3 = (f32[8,128]{1,0:T(8,128)}, f32[8,128]{1,0:T(8,128)S(1)}, u32[]{:S(2)}, u32[]{:S(2)}) collective-permute-start(f32[8,128]{1,0:T(8,128)} %get-tuple-element.36), channel_id=1, source_target_pairs={{0,8},{1,9},{2,10},{3,11},{4,12},{5,13},{6,14},{7,15},{8,0},{9,1},... | collective-permute-start | bytes 12296 | tf_op jit(solution)/shard_map/ppermute | solution.py:174
  9.5 2.8 %collective-permute-start.4 = (f32[8,128]{1,0:T(8,128)}, f32[8,128]{1,0:T(8,128)S(1)}, u32[]{:S(2)}, u32[]{:S(2)}) collective-permute-start(f32[8,128]{1,0:T(8,128)} %get-tuple-element.37), channel_id=1, source_target_pairs={{0,10},{1,11},{2,8},{3,9},{4,14},{5,15},{6,12},{7,13},{8,2},{9,3},... | collective-permute-start | bytes 12296 | tf_op jit(solution)/shard_map/ppermute | solution.py:174
  12.4 2.2 %collective-permute-start.5 = (f32[8,128]{1,0:T(8,128)}, f32[8,128]{1,0:T(8,128)S(1)}, u32[]{:S(2)}, u32[]{:S(2)}) collective-permute-start(f32[8,128]{1,0:T(8,128)} %get-tuple-element.38), channel_id=1, source_target_pairs={{0,12},{1,13},{2,14},{3,15},{4,0},{5,1},{6,2},{7,3},{8,4},{9,5},{1... | collective-permute-start | bytes 12296 | tf_op jit(solution)/shard_map/ppermute | solution.py:174
  14.8 1.7 %copy-done = f32[19,16,16,128]{3,2,1,0:T(8,128)S(1)} copy-done((f32[19,16,16,128]{3,2,1,0:T(8,128)S(1)}, f32[19,16,16,128]{3,2,1,0:T(8,128)}, u32[]{:S(2)}) %copy-start) | copy-done | bytes 2490392
  16.5 0.9 %copy-done.2 = s32[16,16,128]{2,1,0:T(8,128)S(1)} copy-done((s32[16,16,128]{2,1,0:T(8,128)S(1)}, s32[16,16,128]{2,1,0:T(8,128)}, u32[]{:S(2)}) %copy-start.2) | copy-done | bytes 131096
  17.4 0.6 %moments.1 = (f32[3,256,128]{2,1,0:T(8,128)S(1)}, f32[19,4,16,128]{3,2,1,0:T(8,128)S(1)}, s32[4,16,128]{2,1,0:T(8,128)S(1)}) custom-call(f32[19,16,16,128]{3,2,1,0:T(8,128)S(1)} %copy-done, s32[16,16,128]{2,1,0:T(8,128)S(1)} %copy-done.2), custom_call_target="tpu_custom_call" | custom-call | flops 3000000 | bytes 4000000 | tf_op jit(solution)/shard_map/moments/pallas_call | solution.py:281
  18.1 1.2 %collective-permute-done.6.refs_7_ = f32[8,128]{1,0:T(8,128)S(1)} collective-permute-done((f32[8,128]{1,0:T(8,128)}, f32[8,128]{1,0:T(8,128)S(1)}, u32[]{:S(2)}, u32[]{:S(2)}) %collective-permute-start.6) | collective-permute-done | bytes 4128 | tf_op jit(solution)/shard_map/ppermute | solution.py:174
  19.3 1.7 %couple.1 = (f32[3,16,16,128]{3,2,1,0:T(8,128)S(1)}, f32[8,128]{1,0:T(8,128)S(1)}, f32[168,128]{1,0:T(8,128)S(1)}, f32[64,128]{1,0:T(8,128)S(1)}, f32[88,128]{1,...) custom-call(f32[3,256,128]{2,1,0:T(8,128)S(1)} %get-tuple-element.29, ...), custom_call_target="tpu_custom_call" | custom-call | tf_op jit(solution)/shard_map/couple/pallas_call | solution.py:399
  21.5 1.5 %collective-permute-start.12 = (f32[24,128]{1,0:T(8,128)S(1)}, f32[24,128]{1,0:T(8,128)S(1)}, u32[]{:S(2)}, u32[]{:S(2)}) collective-permute-start(f32[24,128]{1,0:T(8,128)S(1)} %get-tuple-element.48), channel_id=1, source_target_pairs={{0,6},{1,7},{2,4},{3,5},{4,10},{5,11},{6,8},{7,9},{8,14},{9,15},{1... | collective-permute-start | bytes 36872 | tf_op jit(solution)/shard_map/ppermute | solution.py:174
  23.1 2.2 %collective-permute-start.13 = (f32[8,128]{1,0:T(8,128)S(1)}, f32[8,128]{1,0:T(8,128)S(1)}, u32[]{:S(2)}, u32[]{:S(2)}) collective-permute-start(f32[8,128]{1,0:T(8,128)S(1)} %get-tuple-element.49), channel_id=1, source_target_pairs={{0,8},{1,9},{2,10},{3,11},{4,12},{5,13},{6,14},{7,15},{8,0},{9,1},... | collective-permute-start | bytes 12296 | tf_op jit(solution)/shard_map/ppermute | solution.py:174
  25.3 1.6 %collective-permute-start.14 = (f32[8,128]{1,0:T(8,128)S(1)}, f32[8,128]{1,0:T(8,128)S(1)}, u32[]{:S(2)}, u32[]{:S(2)}) collective-permute-start(f32[8,128]{1,0:T(8,128)S(1)} %get-tuple-element.50), channel_id=1, source_target_pairs={{0,10},{1,11},{2,8},{3,9},{4,14},{5,15},{6,12},{7,13},{8,2},{9,3},... | collective-permute-start | bytes 12296 | tf_op jit(solution)/shard_map/ppermute | solution.py:174
  26.9 0.6 %collective-permute-done.13.refs_6_ = f32[8,128]{1,0:T(8,128)S(1)} collective-permute-done((f32[8,128]{1,0:T(8,128)S(1)}, f32[8,128]{1,0:T(8,128)S(1)}, u32[]{:S(2)}, u32[]{:S(2)}) %collective-permute-start.13) | collective-permute-done | bytes 4128 | tf_op jit(solution)/shard_map/ppermute | solution.py:174
  27.6 3.2 %collective-permute-start.17 = (f32[24,128]{1,0:T(8,128)S(1)}, f32[24,128]{1,0:T(8,128)S(1)}, u32[]{:S(2)}, u32[]{:S(2)}) collective-permute-start(f32[24,128]{1,0:T(8,128)S(1)} %get-tuple-element.53), channel_id=1, source_target_pairs={{0,14},{1,15},{2,12},{3,13},{4,2},{5,3},{6,0},{7,1},{8,6},{9,7},{1... | collective-permute-start | bytes 36872 | tf_op jit(solution)/shard_map/ppermute | solution.py:174
  30.8 1.6 %collective-permute-start.10 = (f32[88,128]{1,0:T(8,128)S(1)}, f32[88,128]{1,0:T(8,128)S(1)}, u32[]{:S(2)}, u32[]{:S(2)}) collective-permute-start(f32[88,128]{1,0:T(8,128)S(1)} %get-tuple-element.46), channel_id=1, source_target_pairs={{0,4},{1,5},{2,6},{3,7},{4,8},{5,9},{6,10},{7,11},{8,12},{9,13},{1... | collective-permute-start | bytes 135176 | tf_op jit(solution)/shard_map/ppermute | solution.py:174
  32.4 2.2 %collective-permute-start.15 = (f32[88,128]{1,0:T(8,128)S(1)}, f32[88,128]{1,0:T(8,128)S(1)}, u32[]{:S(2)}, u32[]{:S(2)}) collective-permute-start(f32[88,128]{1,0:T(8,128)S(1)} %get-tuple-element.51), channel_id=1, source_target_pairs={{0,12},{1,13},{2,14},{3,15},{4,0},{5,1},{6,2},{7,3},{8,4},{9,5},{1... | collective-permute-start | bytes 135176 | tf_op jit(solution)/shard_map/ppermute | solution.py:174
  34.6 1.1 %collective-permute-start.16 = (f32[32,128]{1,0:T(8,128)S(1)}, f32[32,128]{1,0:T(8,128)S(1)}, u32[]{:S(2)}, u32[]{:S(2)}) collective-permute-start(f32[32,128]{1,0:T(8,128)S(1)} %get-tuple-element.52), channel_id=1, source_target_pairs={{0,13},{1,12},{2,15},{3,14},{4,1},{5,0},{6,3},{7,2},{8,5},{9,4},{1... | collective-permute-start | bytes 49160 | tf_op jit(solution)/shard_map/ppermute | solution.py:174
  35.7 1.7 %collective-permute-start.9 = (f32[64,128]{1,0:T(8,128)S(1)}, f32[64,128]{1,0:T(8,128)S(1)}, u32[]{:S(2)}, u32[]{:S(2)}) collective-permute-start(f32[64,128]{1,0:T(8,128)S(1)} %get-tuple-element.45), channel_id=1, source_target_pairs={{0,3},{1,2},{2,1},{3,0},{4,7},{5,6},{6,5},{7,4},{8,11},{9,10},{10,... | collective-permute-start | bytes 98312 | tf_op jit(solution)/shard_map/ppermute | solution.py:174
  37.4 3.5 %stream.1 = (f32[19,16,16,128]{3,2,1,0:T(8,128)S(1)}, f32[2,16,128]{2,1,0:T(8,128)S(1)}) custom-call(f32[19,16,16,128]{3,2,1,0:T(8,128)S(1)} %copy-done.1, s32[16,16,128]{2,1,0:T(8,128)S(1)} %copy-done.3, f32[3,16,16,128]{3,2,1,0:T(8,128)S(1)} %get-tuple-element.40.force_ref), custom_call_target="tpu_custom_call" | custom-call | flops 10000000 | bytes 6000000 | tf_op jit(solution)/shard_map/stream/pallas_call | solution.py:436
  41.1 1.2 %collective-permute-done.7.column_ref = f32[2,16,128]{2,1,0:T(8,128)S(1)} collective-permute-done((f32[2,16,128]{2,1,0:T(8,128)S(1)}, f32[2,16,128]{2,1,0:T(8,128)S(1)}, u32[]{:S(2)}, u32[]{:S(2)}) %collective-permute-start.7) | collective-permute-done | bytes 16416 | tf_op jit(solution)/shard_map/ppermute | solution.py:174
  42.3 2.3 %finish.1 = (f32[19,16,16,128]{3,2,1,0:T(8,128)}, f32[3,128]{1,0:T(4,128)}) custom-call(s32[1,128]{1,0:T(1,128)S(1)} %copy-done.5, f32[19,16,16,128]{3,2,1,0:T(8,128)S(1)} %get-tuple-element.41.local_ref, f32[2,16,128]{2,1,0:T(8,128)S(1)} %collective-permute-done.7.column_ref, f32[8,128]{1,0:T(8,128)S(1)} %get-tuple-element.43.refs_0_, ...), custom_call_target="tpu_custom_call" | custom-call | tf_op jit(solution)/shard_map/finish/pallas_call | solution.py:526
  (29 shorter events, 0.9 us)
Async XLA Ops:
  2.4 16.9 %copy-start.4 = (f32[8,128]{1,0:T(8,128)S(1)}, f32[8,128]{1,0:T(8,128)}, u32[]{:S(2)}) copy-start(f32[8,128]{1,0:T(8,128)} %get-tuple-element.32.refs_0_) | copy-start | bytes 12292
  2.4 10.0 %collective-permute-start = (f32[8,128]{1,0:T(8,128)}, f32[8,128]{1,0:T(8,128)S(1)}, u32[]{:S(2)}, u32[]{:S(2)}) collective-permute-start(f32[8,128]{1,0:T(8,128)} %get-tuple-element.33), channel_id=1, source_target_pairs={{0,2},{1,3},{2,0},{3,1},{4,6},{5,7},{6,4},{7,5},{8,10},{9,11},{10,... | collective-permute-start | bytes 12296 | tf_op jit(solution)/shard_map/ppermute | solution.py:174
  5.4 9.2 %collective-permute-start.1 = (f32[8,128]{1,0:T(8,128)}, f32[8,128]{1,0:T(8,128)S(1)}, u32[]{:S(2)}, u32[]{:S(2)}) collective-permute-start(f32[8,128]{1,0:T(8,128)} %get-tuple-element.34), channel_id=1, source_target_pairs={{0,4},{1,5},{2,6},{3,7},{4,8},{5,9},{6,10},{7,11},{8,12},{9,13},{1... | collective-permute-start | bytes 12296 | tf_op jit(solution)/shard_map/ppermute | solution.py:174
  6.9 11.1 %collective-permute-start.2 = (f32[8,128]{1,0:T(8,128)}, f32[8,128]{1,0:T(8,128)S(1)}, u32[]{:S(2)}, u32[]{:S(2)}) collective-permute-start(f32[8,128]{1,0:T(8,128)} %get-tuple-element.35), channel_id=1, source_target_pairs={{0,6},{1,7},{2,4},{3,5},{4,10},{5,11},{6,8},{7,9},{8,14},{9,15},{1... | collective-permute-start | bytes 12296 | tf_op jit(solution)/shard_map/ppermute | solution.py:174
  8.5 9.6 %collective-permute-start.3 = (f32[8,128]{1,0:T(8,128)}, f32[8,128]{1,0:T(8,128)S(1)}, u32[]{:S(2)}, u32[]{:S(2)}) collective-permute-start(f32[8,128]{1,0:T(8,128)} %get-tuple-element.36), channel_id=1, source_target_pairs={{0,8},{1,9},{2,10},{3,11},{4,12},{5,13},{6,14},{7,15},{8,0},{9,1},... | collective-permute-start | bytes 12296 | tf_op jit(solution)/shard_map/ppermute | solution.py:174
  9.5 8.6 %collective-permute-start.4 = (f32[8,128]{1,0:T(8,128)}, f32[8,128]{1,0:T(8,128)S(1)}, u32[]{:S(2)}, u32[]{:S(2)}) collective-permute-start(f32[8,128]{1,0:T(8,128)} %get-tuple-element.37), channel_id=1, source_target_pairs={{0,10},{1,11},{2,8},{3,9},{4,14},{5,15},{6,12},{7,13},{8,2},{9,3},... | collective-permute-start | bytes 12296 | tf_op jit(solution)/shard_map/ppermute | solution.py:174
  12.4 5.8 %collective-permute-start.5 = (f32[8,128]{1,0:T(8,128)}, f32[8,128]{1,0:T(8,128)S(1)}, u32[]{:S(2)}, u32[]{:S(2)}) collective-permute-start(f32[8,128]{1,0:T(8,128)} %get-tuple-element.38), channel_id=1, source_target_pairs={{0,12},{1,13},{2,14},{3,15},{4,0},{5,1},{6,2},{7,3},{8,4},{9,5},{1... | collective-permute-start | bytes 12296 | tf_op jit(solution)/shard_map/ppermute | solution.py:174
  14.6 4.7 %collective-permute-start.6 = (f32[8,128]{1,0:T(8,128)}, f32[8,128]{1,0:T(8,128)S(1)}, u32[]{:S(2)}, u32[]{:S(2)}) collective-permute-start(f32[8,128]{1,0:T(8,128)} %get-tuple-element.39), channel_id=1, source_target_pairs={{0,14},{1,15},{2,12},{3,13},{4,2},{5,3},{6,0},{7,1},{8,6},{9,7},{1... | collective-permute-start | bytes 12296 | tf_op jit(solution)/shard_map/ppermute | solution.py:174
  14.8 1.7 %copy-start = (f32[19,16,16,128]{3,2,1,0:T(8,128)S(1)}, f32[19,16,16,128]{3,2,1,0:T(8,128)}, u32[]{:S(2)}) copy-start(f32[19,16,16,128]{3,2,1,0:T(8,128)} %pops_ref.3) | copy-start | bytes 7471108
  16.5 0.9 %copy-start.2 = (s32[16,16,128]{2,1,0:T(8,128)S(1)}, s32[16,16,128]{2,1,0:T(8,128)}, u32[]{:S(2)}) copy-start(s32[16,16,128]{2,1,0:T(8,128)} %solid_ref.3) | copy-start | bytes 393220
  17.4 20.0 %copy-start.1 = (f32[19,16,16,128]{3,2,1,0:T(8,128)S(1)}, f32[19,16,16,128]{3,2,1,0:T(8,128)}, u32[]{:S(2)}) copy-start(f32[19,16,16,128]{3,2,1,0:T(8,128)} %pops_ref.3) | copy-start | bytes 7471108
  17.4 20.0 %copy-start.3 = (s32[16,16,128]{2,1,0:T(8,128)S(1)}, s32[16,16,128]{2,1,0:T(8,128)}, u32[]{:S(2)}) copy-start(s32[16,16,128]{2,1,0:T(8,128)} %solid_ref.3) | copy-start | bytes 393220
  18.1 24.2 %copy-start.5 = (s32[1,128]{1,0:T(1,128)S(1)}, s32[1,128]{1,0:T(1,128)}, u32[]{:S(2)}) copy-start(s32[1,128]{1,0:T(1,128)} %get-tuple-element.28.target_ref) | copy-start | bytes 1540
  21.0 21.3 %collective-permute-start.8 = (f32[168,128]{1,0:T(8,128)S(1)}, f32[168,128]{1,0:T(8,128)S(1)}, u32[]{:S(2)}, u32[]{:S(2)}) collective-permute-start(f32[168,128]{1,0:T(8,128)S(1)} %get-tuple-element.44), channel_id=1, source_target_pairs={{0,2},{1,3},{2,0},{3,1},{4,6},{5,7},{6,4},{7,5},{8,10},{9,11},{10,... | collective-permute-start | bytes 258056 | tf_op jit(solution)/shard_map/ppermute | solution.py:174
  21.5 10.8 %collective-permute-start.12 = (f32[24,128]{1,0:T(8,128)S(1)}, f32[24,128]{1,0:T(8,128)S(1)}, u32[]{:S(2)}, u32[]{:S(2)}) collective-permute-start(f32[24,128]{1,0:T(8,128)S(1)} %get-tuple-element.48), channel_id=1, source_target_pairs={{0,6},{1,7},{2,4},{3,5},{4,10},{5,11},{6,8},{7,9},{8,14},{9,15},{1... | collective-permute-start | bytes 36872 | tf_op jit(solution)/shard_map/ppermute | solution.py:174
  23.1 4.5 %collective-permute-start.13 = (f32[8,128]{1,0:T(8,128)S(1)}, f32[8,128]{1,0:T(8,128)S(1)}, u32[]{:S(2)}, u32[]{:S(2)}) collective-permute-start(f32[8,128]{1,0:T(8,128)S(1)} %get-tuple-element.49), channel_id=1, source_target_pairs={{0,8},{1,9},{2,10},{3,11},{4,12},{5,13},{6,14},{7,15},{8,0},{9,1},... | collective-permute-start | bytes 12296 | tf_op jit(solution)/shard_map/ppermute | solution.py:174
  25.3 5.5 %collective-permute-start.14 = (f32[8,128]{1,0:T(8,128)S(1)}, f32[8,128]{1,0:T(8,128)S(1)}, u32[]{:S(2)}, u32[]{:S(2)}) collective-permute-start(f32[8,128]{1,0:T(8,128)S(1)} %get-tuple-element.50), channel_id=1, source_target_pairs={{0,10},{1,11},{2,8},{3,9},{4,14},{5,15},{6,12},{7,13},{8,2},{9,3},... | collective-permute-start | bytes 12296 | tf_op jit(solution)/shard_map/ppermute | solution.py:174
  26.9 8.8 %collective-permute-start.11 = (f32[32,128]{1,0:T(8,128)S(1)}, f32[32,128]{1,0:T(8,128)S(1)}, u32[]{:S(2)}, u32[]{:S(2)}) collective-permute-start(f32[32,128]{1,0:T(8,128)S(1)} %get-tuple-element.47), channel_id=1, source_target_pairs={{0,5},{1,4},{2,7},{3,6},{4,9},{5,8},{6,11},{7,10},{8,13},{9,12},{1... | collective-permute-start | bytes 49160 | tf_op jit(solution)/shard_map/ppermute | solution.py:174
  27.6 7.0 %collective-permute-start.17 = (f32[24,128]{1,0:T(8,128)S(1)}, f32[24,128]{1,0:T(8,128)S(1)}, u32[]{:S(2)}, u32[]{:S(2)}) collective-permute-start(f32[24,128]{1,0:T(8,128)S(1)} %get-tuple-element.53), channel_id=1, source_target_pairs={{0,14},{1,15},{2,12},{3,13},{4,2},{5,3},{6,0},{7,1},{8,6},{9,7},{1... | collective-permute-start | bytes 36872 | tf_op jit(solution)/shard_map/ppermute | solution.py:174
  30.8 11.5 %collective-permute-start.10 = (f32[88,128]{1,0:T(8,128)S(1)}, f32[88,128]{1,0:T(8,128)S(1)}, u32[]{:S(2)}, u32[]{:S(2)}) collective-permute-start(f32[88,128]{1,0:T(8,128)S(1)} %get-tuple-element.46), channel_id=1, source_target_pairs={{0,4},{1,5},{2,6},{3,7},{4,8},{5,9},{6,10},{7,11},{8,12},{9,13},{1... | collective-permute-start | bytes 135176 | tf_op jit(solution)/shard_map/ppermute | solution.py:174
  32.4 9.9 %collective-permute-start.15 = (f32[88,128]{1,0:T(8,128)S(1)}, f32[88,128]{1,0:T(8,128)S(1)}, u32[]{:S(2)}, u32[]{:S(2)}) collective-permute-start(f32[88,128]{1,0:T(8,128)S(1)} %get-tuple-element.51), channel_id=1, source_target_pairs={{0,12},{1,13},{2,14},{3,15},{4,0},{5,1},{6,2},{7,3},{8,4},{9,5},{1... | collective-permute-start | bytes 135176 | tf_op jit(solution)/shard_map/ppermute | solution.py:174
  34.6 6.4 %collective-permute-start.16 = (f32[32,128]{1,0:T(8,128)S(1)}, f32[32,128]{1,0:T(8,128)S(1)}, u32[]{:S(2)}, u32[]{:S(2)}) collective-permute-start(f32[32,128]{1,0:T(8,128)S(1)} %get-tuple-element.52), channel_id=1, source_target_pairs={{0,13},{1,12},{2,15},{3,14},{4,1},{5,0},{6,3},{7,2},{8,5},{9,4},{1... | collective-permute-start | bytes 49160 | tf_op jit(solution)/shard_map/ppermute | solution.py:174
  35.7 6.5 %collective-permute-start.9 = (f32[64,128]{1,0:T(8,128)S(1)}, f32[64,128]{1,0:T(8,128)S(1)}, u32[]{:S(2)}, u32[]{:S(2)}) collective-permute-start(f32[64,128]{1,0:T(8,128)S(1)} %get-tuple-element.45), channel_id=1, source_target_pairs={{0,3},{1,2},{2,1},{3,0},{4,7},{5,6},{6,5},{7,4},{8,11},{9,10},{10,... | collective-permute-start | bytes 98312 | tf_op jit(solution)/shard_map/ppermute | solution.py:174
  41.0 1.2 %collective-permute-start.7 = (f32[2,16,128]{2,1,0:T(8,128)S(1)}, f32[2,16,128]{2,1,0:T(8,128)S(1)}, u32[]{:S(2)}, u32[]{:S(2)}) collective-permute-start(f32[2,16,128]{2,1,0:T(8,128)S(1)} %get-tuple-element.42), channel_id=1, source_target_pairs={{0,1},{1,0},{2,3},{3,2},{4,5},{5,4},{6,7},{7,6},{8,9},{9,8},{10,11... | collective-permute-start | bytes 49160 | tf_op jit(solution)/shard_map/ppermute | solution.py:174

commit v2 on v1

--- a/solution.py
+++ b/solution.py
@@ -152,8 +152,8 @@
     return 8 if part[1] == (2, 1) else span
 
 
-def message_rows(parts, span, with_drag):
-    rows = 8 if with_drag else 0
+def message_rows(parts, span):
+    rows = 0
     places = {}
     for part in parts:
         places[part] = rows
@@ -178,34 +178,27 @@
     return jnp.where(value < 0, value + size, value)
 
 
-def pack_kernel(slabs, cols, count, single, owner_ref, base_ref, offset_ref, velocity_ref, target_ref, *rest):
-    outs, table = rest[:-1], rest[-1]
+def pack_kernel(slabs, cols, count, owner_ref, base_ref, offset_ref, velocity_ref, target_ref, out_ref, table):
     owner = owner_ref[...]
     owner_slab = lax.shift_right_logical(owner, cols.bit_length() - 1)
     owner_col = owner - owner_slab * cols
     relative = wrap(owner_slab - lax.axis_index("slab"), slabs) * cols + wrap(
         owner_col - lax.axis_index("col"), cols
     )
-    first = 0 if single else pl.program_id(0) * GROUP
-    local = relative - first
+    local = relative - pl.program_id(0) * GROUP
     member = (iota((GROUP, count), 0) == local).astype(F32)
-    earlier = (iota((count, count), 0) < iota((count, count), 1)).astype(F32).astype(BF16)
-    ahead = lax.dot_general(member.astype(BF16), earlier, NN, preferred_element_type=F32)
-    rank = jnp.sum(member * ahead, axis=0, keepdims=True).astype(jnp.int32)
+    rank = jnp.sum(member * rank_among(member), axis=0, keepdims=True).astype(jnp.int32)
     inside = (local >= 0) & (local < GROUP)
     target = jnp.where(inside, local * CAP + rank, -1)
     whole_target = jnp.where(inside, relative * CAP + rank, -1)
-    if single:
+
+    @pl.when(pl.program_id(0) == 0)
+    def _():
         target_ref[...] = whole_target
-    else:
-
-        @pl.when(pl.program_id(0) == 0)
-        def _():
-            target_ref[...] = whole_target
-
-        @pl.when(pl.program_id(0) > 0)
-        def _():
-            target_ref[...] = jnp.maximum(target_ref[...], whole_target)
+
+    @pl.when(pl.program_id(0) > 0)
+    def _():
+        target_ref[...] = jnp.maximum(target_ref[...], whole_target)
 
     choose = (iota((GROUP * CAP, count), 0) == target).astype(F32).astype(BF16)
     table[...] = jnp.zeros_like(table)
@@ -216,41 +209,63 @@
     blank = jnp.zeros((8, CAP), F32)
     for r in range(GROUP):
         lanes = slice(r * CAP, (r + 1) * CAP)
-        tile = jnp.concatenate(
+        out_ref[r] = jnp.concatenate(
             [packed[0:8, lanes], packed[8:16, lanes], packed[16:24, lanes], blank], axis=1
         )
-        if single:
-            outs[r][...] = tile
-        else:
-            outs[0][r] = tile
 
 
 def pack(slabs, cols, owner, base, offset, velocity):
     owners, count = slabs * cols, owner.shape[0]
-    single = owners == GROUP
-    tile = jax.ShapeDtypeStruct((8, 128), F32)
-    target = jax.ShapeDtypeStruct((1, count), jnp.int32)
-    kernel = functools.partial(pack_kernel, slabs, cols, count, single)
-    scratch = [pltpu.VMEM((24, count), F32)]
     args = (owner.reshape(1, count), base, offset, velocity)
-    if single:
-        target, *tiles = pl.pallas_call(
-            kernel, out_shape=[target] + [tile] * owners, scratch_shapes=scratch, name="pack"
-        )(*args)
-        return target, tiles
     return pl.pallas_call(
-        kernel,
-        out_shape=[target, jax.ShapeDtypeStruct((owners, 8, 128), F32)],
+        functools.partial(pack_kernel, slabs, cols, count),
+        out_shape=[
+            jax.ShapeDtypeStruct((1, count), jnp.int32),
+            jax.ShapeDtypeStruct((owners, 8, 128), F32),
+        ],
         grid=(owners // GROUP,),
         in_specs=[pl.BlockSpec(a.shape, lambda k: (0, 0)) for a in args],
         out_specs=[
             pl.BlockSpec((1, count), lambda k: (0, 0)),
             pl.BlockSpec((GROUP, 8, 128), lambda k: (k, 0, 0)),
         ],
-        scratch_shapes=scratch,
+        scratch_shapes=[pltpu.VMEM((24, count), F32)],
         compiler_params=pltpu.CompilerParams(vmem_limit_bytes=48 << 20),
         name="pack",
     )(*args)
+
+
+def publish_kernel(owner_ref, base_ref, offset_ref, velocity_ref, out_ref):
+    out_ref[0:1] = owner_ref[...].astype(F32)
+    out_ref[1:4] = base_ref[...].astype(F32) + 1.0
+    out_ref[4:7] = offset_ref[...]
+    out_ref[7:10] = velocity_ref[...]
+    out_ref[10:16] = jnp.zeros((6, out_ref.shape[1]), F32)
+
+
+def publish(owner, base, offset, velocity):
+    count = owner.shape[0]
+    return pl.pallas_call(
+        publish_kernel, out_shape=jax.ShapeDtypeStruct((16, count), F32), name="publish"
+    )(owner.reshape(1, count), base, offset, velocity)
+
+
+def rank_among(member):
+    count = member.shape[1]
+    earlier = (iota((count, count), 0) < iota((count, count), 1)).astype(F32).astype(BF16)
+    return lax.dot_general(member.astype(BF16), earlier, NN, preferred_element_type=F32)
+
+
+def own_slots(all_ref, me):
+    owner = jnp.concatenate([all_ref[k, 0:1] for k in range(GROUP)], axis=0)
+    member = (owner == me.astype(F32)).astype(F32)
+    place = jnp.where(member > 0.0, rank_among(member), -1.0).astype(jnp.int32)
+    count = owner.shape[1]
+    slots = []
+    for k in range(GROUP):
+        choose = (iota((CAP, count), 0) == place[k : k + 1]).astype(F32).astype(BF16)
+        slots.append(dot_select(all_ref[k], choose, NT))
+    return jnp.concatenate(slots, axis=1)
 
 
 def moments_kernel(pops_ref, solid_ref, flow_ref, edge_ref, edge_solid_ref):
@@ -291,11 +306,15 @@
     )(pops, solid)
 
 
-def couple_group(tiles, flow, depth, rows):
+def unpack(tiles):
+    return [
+        jnp.concatenate([t[0:3, g * CAP : (g + 1) * CAP] for t in tiles], axis=1)
+        for g in range(3)
+    ]
+
+
+def couple_group(base, part, velocity, flow, depth, rows):
     width, slots = flow.shape[1], GROUP * CAP
-    base = jnp.concatenate([t[:, 0:CAP] for t in tiles], axis=1)
-    part = jnp.concatenate([t[:, CAP : 2 * CAP] for t in tiles], axis=1)
-    velocity = jnp.concatenate([t[:, 2 * CAP : 3 * CAP] for t in tiles], axis=1)
     start = base.astype(jnp.int32) - 1
 
     def hat(axis, length):
@@ -317,47 +336,41 @@
 
 
 def couple_kernel(
-    single, shape, plan, depth, rows, n_in, flow_ref, edge_ref, edge_solid_ref, *refs
+    single, shape, plan, depth, rows, beads_ref, flow_ref, edge_ref, edge_solid_ref, force_ref, drag_ref, *refs
 ):
-    ins, force_ref, refs = refs[:n_in], refs[n_in], refs[n_in + 1 :]
     width = flow_ref.shape[2]
     flow = flow_ref[...].reshape(3 * depth * rows, width)
+    messages = dict(zip(sorted(plan), refs))
     blank = jnp.zeros((8, 128 - CAP), F32)
     hollow = jnp.zeros((5, GROUP * CAP), F32)
 
-    def drag_tiles(drag):
-        stacked = jnp.concatenate(drag + [hollow], axis=0)
-        return [
-            jnp.concatenate([stacked[:, r * CAP : (r + 1) * CAP], blank], axis=1)
-            for r in range(GROUP)
+    if single:
+        me = lax.axis_index("slab") * shape[1] + lax.axis_index("col")
+        slots = own_slots(beads_ref, me)
+        drag, force = couple_group(slots[1:4], slots[4:7], slots[7:10], flow, depth, rows)
+        force_ref[...] = force.reshape(3, depth, rows, width)
+        pieces = [
+            jnp.concatenate([d[:, k * CAP : (k + 1) * CAP] for k in range(GROUP)], axis=0)
+            for d in drag
         ]
-
-    if single:
-        drag, force = couple_group([t[...] for t in ins], flow, depth, rows)
-        force_ref[...] = force.reshape(3, depth, rows, width)
-        tiles = drag_tiles(drag)
-        refs[0][...] = tiles[0]
-        messages = dict(zip(sorted(plan), refs[1:]))
-        for r in range(1, GROUP):
-            dz, dy = divmod(r, shape[1])
-            messages[((-dz) % shape[0], (-dy) % shape[1], 0)][0:8] = tiles[r]
+        drag_ref[...] = jnp.concatenate(pieces + [jnp.zeros((GROUP, CAP), F32)], axis=1)
     else:
         force_ref[...] = jnp.zeros_like(force_ref)
 
         def group(k, carry):
-            got = [ins[0][k * GROUP + r] for r in range(GROUP)]
-            drag, force = couple_group(got, flow, depth, rows)
+            got = [beads_ref[k * GROUP + r] for r in range(GROUP)]
+            drag, force = couple_group(*unpack(got), flow, depth, rows)
             force_ref[...] += force.reshape(3, depth, rows, width)
-            for r, tile in enumerate(drag_tiles(drag)):
-                refs[0][k * GROUP + r] = tile
+            stacked = jnp.concatenate(drag + [hollow], axis=0)
+            for r in range(GROUP):
+                drag_ref[k * GROUP + r] = jnp.concatenate(
+                    [stacked[:, r * CAP : (r + 1) * CAP], blank], axis=1
+                )
             return carry
 
-        lax.fori_loop(0, ins[0].shape[0] // GROUP, group, 0)
-        messages = dict(zip(sorted(plan), refs[1:]))
-
-    places = {
-        key: message_rows(parts, rows, single and key[2] == 0)[1] for key, parts in plan.items()
-    }
+        lax.fori_loop(0, beads_ref.shape[0] // GROUP, group, 0)
+
+    places = {key: message_rows(parts, rows)[1] for key, parts in plan.items()}
     for side in range(4):
         pops = [edge_ref[i, side] for i in range(19)]
         if side < 2:
@@ -386,22 +399,20 @@
                         messages[key][row : row + rows] = moved
 
 
-def couple(shape, plan, tiles, flow, edge, edge_solid, depth, rows, single):
+def couple(single, shape, plan, beads, flow, edge, edge_solid, depth, rows):
     width = flow.shape[2]
-    sizes = [
-        message_rows(plan[key], rows, single and key[2] == 0)[0] for key in sorted(plan)
-    ]
-    own = (8, 128) if single else tiles[0].shape
+    sizes = [message_rows(plan[key], rows)[0] for key in sorted(plan)]
+    own = (8, 128) if single else beads.shape
     out_shape = [
         jax.ShapeDtypeStruct((3, depth, rows, width), F32),
         jax.ShapeDtypeStruct(own, F32),
     ] + [jax.ShapeDtypeStruct((n, width), F32) for n in sizes]
     force, drag, *messages = pl.pallas_call(
-        functools.partial(couple_kernel, single, shape, plan, depth, rows, len(tiles)),
+        functools.partial(couple_kernel, single, shape, plan, depth, rows),
         out_shape=out_shape,
         compiler_params=pltpu.CompilerParams(vmem_limit_bytes=24 << 20),
         name="couple",
-    )(flow, edge, edge_solid, *tiles)
+    )(beads, flow, edge, edge_solid)
     return force, drag, dict(zip(sorted(plan), messages))
 
 
@@ -445,10 +456,7 @@
     )(pops, solid, force)
 
 
-def finish_kernel(
-    single, shape, plan, n_back, target_ref, local_ref, column_ref, *refs
-):
-    backs, refs = refs[:n_back], refs[n_back:]
+def finish_kernel(single, shape, plan, target_ref, local_ref, column_ref, back_ref, *refs):
     keys = sorted(plan)
     messages, refs = dict(zip(keys, refs[: len(keys)])), refs[len(keys) :]
     out_ref, bead_ref, held, sem = refs
@@ -456,7 +464,7 @@
     lane = iota((rows, width), 1)
     places = {}
     for key in keys:
-        for part, row in message_rows(plan[key], rows, single and key[2] == 0)[1].items():
+        for part, row in message_rows(plan[key], rows)[1].items():
             places[part] = (messages[key], row)
 
     def arrived(part):
@@ -495,36 +503,37 @@
         copies.append(copy)
 
     count = target_ref.shape[1]
-
-    def gathered(tiles, first):
-        slots = jnp.concatenate([t[:, 0:CAP] for t in tiles], axis=1)
-        choose = (iota((GROUP * CAP, count), 0) + first == target_ref[...]).astype(F32)
-        return dot_select(slots, choose.astype(BF16), NN)[0:3]
-
     if single:
-        tiles = [backs[0][...]]
-        for r in range(1, GROUP):
-            dz, dy = divmod(r, shape[1])
-            tiles.append(messages[((-dz) % shape[0], (-dy) % shape[1], 0)][0:8])
-        bead_ref[...] = gathered(tiles, 0)
+        me = lax.axis_index("slab") * shape[1] + lax.axis_index("col")
+        mine = jnp.concatenate([back_ref[k, pl.ds(me, 1), :] for k in range(GROUP)], axis=0)
+        owner = target_ref[...]
+        member = (iota((GROUP, count), 0) == owner).astype(F32)
+        slot = jnp.sum(member * rank_among(member), axis=0, keepdims=True).astype(jnp.int32)
+        for d in range(3):
+            choose = (iota((128, count), 0) == slot + d * CAP).astype(F32).astype(BF16)
+            picked = dot_select(mine, choose, NN)
+            bead_ref[d : d + 1] = jnp.sum(member * picked, axis=0, keepdims=True)
     else:
 
         def group(k, total):
-            tiles = [backs[0][k * GROUP + r] for r in range(GROUP)]
-            return total + gathered(tiles, k * (GROUP * CAP))
+            tiles = [back_ref[k * GROUP + r] for r in range(GROUP)]
+            slots = jnp.concatenate([t[:, 0:CAP] for t in tiles], axis=1)
+            first = k * (GROUP * CAP)
+            choose = (iota((GROUP * CAP, count), 0) + first == target_ref[...]).astype(F32)
+            return total + dot_select(slots, choose.astype(BF16), NN)[0:3]
 
         bead_ref[...] = lax.fori_loop(
-            0, backs[0].shape[0] // GROUP, group, jnp.zeros((3, count), F32)
+            0, back_ref.shape[0] // GROUP, group, jnp.zeros((3, count), F32)
         )
     for copy in copies:
         copy.wait()
 
 
-def finish(shape, plan, target, local, columns, backs, messages, single):
+def finish(single, shape, plan, target, local, columns, back, messages):
     vmem = pl.BlockSpec(memory_space=pltpu.VMEM)
-    args = [target, local, columns, *backs, *[messages[key] for key in sorted(plan)]]
+    args = [target, local, columns, back, *[messages[key] for key in sorted(plan)]]
     return pl.pallas_call(
-        functools.partial(finish_kernel, single, shape, plan, len(backs)),
+        functools.partial(finish_kernel, single, shape, plan),
         out_shape=[
             jax.ShapeDtypeStruct(local.shape, F32),
             jax.ShapeDtypeStruct((3, target.shape[1]), F32),
@@ -543,34 +552,31 @@
     depth, rows = populations.shape[1:3]
     single = owners == GROUP
     plan = message_plan(shape)
+    beads = (bead_owner, bead_base, bead_offset, bead_velocity)
+    group = ("slab", "col")
+
     if single:
-        for r in range(1, owners):
-            plan.setdefault(divmod(r, cols) + (0,), [])
-
-    target, tiles = pack(slabs, cols, bead_owner, bead_base, bead_offset, bead_velocity)
-    if single:
-        tiles = [tiles[0]] + [
-            send(tiles[r], shape, divmod(r, cols) + (0,)) for r in range(1, owners)
-        ]
+        tiles = lax.all_gather(publish(*beads), group)
+        target = bead_owner.reshape(1, -1)
     else:
+        target, tiles = pack(slabs, cols, *beads)
         slab, col = lax.axis_index("slab"), lax.axis_index("col")
         index = jnp.arange(owners, dtype=jnp.int32)
         away = ((index // cols - slab) % slabs) * cols + (index % cols - col) % cols
         back = ((index // cols + slab) % slabs) * cols + (index % cols + col) % cols
         swap = functools.partial(
-            lax.all_to_all, axis_name=("slab", "col"), split_axis=0, concat_axis=0, tiled=True
+            lax.all_to_all, axis_name=group, split_axis=0, concat_axis=0, tiled=True
         )
-        tiles = [swap(tiles[away])]
+        tiles = swap(tiles[away])
     flow, edge, edge_solid = moments(populations, solid_mask)
     force, drag, messages = couple(
-        shape, plan, tiles, flow, edge, edge_solid, depth, rows, single
+        single, shape, plan, tiles, flow, edge, edge_solid, depth, rows
     )
+    drag = lax.all_gather(drag, group) if single else swap(drag)[back]
     messages = {key: send(value, shape, key) for key, value in messages.items()}
-    if not single:
-        drag = swap(drag)[back]
     local, columns = stream(populations, solid_mask, force)
     columns = send(columns, shape, (0, 0, 1))
-    return finish(shape, plan, target, local, columns, [drag], messages, single)
+    return finish(single, shape, plan, target, local, columns, drag, messages)
 
 
 def solution(mesh):

time: 44.7 us -> 89.2 us (2.00)
  blocking collectives: 0 us -> 62.9 us
  starting transfers between devices: 28.3 us -> 11.4 us
  waiting for transfers between devices: 3.06 us -> 1.65 us
    all_gather x0 -> x2, blocking collectives: none -> 62.9 us  [the longest x1 32.5 us: shards(): tiles = lax.all_gather(publish(*beads), group)]
    ppermute x18 -> x9, starting transfers between devices: 28.3 us -> 11.4 us  [send(): return lax.ppermute(value, ('slab', 'col', 'pair'), perm)]
    ppermute x18 -> x9, waiting for transfers between devices: 3.06 us -> 1.65 us  [send(): return lax.ppermute(value, ('slab', 'col', 'pair'), perm)]
    unnamed x12 -> x10, local copies, waits for them, and re-layouts: 2.62 us -> 2.62 us
  transfers between devices with their start and end apart: 18 -> 9, of which waited for: 3 -> 1; matrix products, arithmetic and copies ran while one was open for 0% -> 0% of each run, Pallas kernels for 9% -> 4%
where the time goes in v2:
time: 89.2 us; the launch traced here: 89 us
  blocking collectives  62.9 us (71%)
  starting transfers between devices  11.4 us (13%)
  Pallas kernels  9.72 us (11%)
  local copies, waits for them, and re-layouts  2.62 us (3%)
  waiting for transfers between devices  1.65 us (2%)
    all_gather x1, blocking collectives, shards(): tiles = lax.all_gather(publish(*beads), group)  32.5 us
    all_gather x1, blocking collectives, shards(): drag = lax.all_gather(drag, group) if single else swap(drag)[back]  30.4 us
    ppermute x9, starting transfers between devices, send(): return lax.ppermute(value, ('slab', 'col', 'pair'), perm)  11.4 us
    pallas_call x1, Pallas kernels, stream(): pl.pallas_call(stream_kernel, out_shape=[jax.ShapeDtypeStruct(pops.shape,...  3.52 us
    unnamed x10, local copies, waits for them, and re-layouts  2.62 us
    pallas_call x1, Pallas kernels, finish(): pl.pallas_call(functools.partial(finish_kernel, single, shape, plan), out...  2.26 us
    pallas_call x1, Pallas kernels, couple(): pl.pallas_call(functools.partial(couple_kernel, single, shape, plan, dept...  1.98 us
  transfers between devices with their start and end apart: 9, of which 1 were waited for; matrix products, arithmetic and copies ran while one was open for 0% of the time, Pallas kernels for 4%

profile of v2, /device:TPU:0, one launch (start us, length us, event | category | flops | bytes accessed | tf_op | source)
XLA Modules:
  0.0 89.0 jit_solution(5818984440726026001)
XLA Ops:
  0.6 1.3 %publish.1 = f32[16,128]{1,0:T(8,128)} custom-call(s32[1,128]{1,0:T(1,128)} %bitcast.5, s32[3,128]{1,0:T(4,128)} %base_ref.1, f32[3,128]{1,0:T(4,128)} %offset_ref.1, f32[3,128]{1,0:T(4,128)} %velocity_ref.1), custom_call_target="tpu_custom_call" | custom-call | tf_op jit(solution)/shard_map/publish/pallas_call | solution.py:248
  2.0 32.5 %all-gather = f32[128,128]{1,0:T(8,128)S(1)} all-gather(f32[16,128]{1,0:T(8,128)} %publish.1), channel_id=2, replica_groups=mesh['rep'=2,'slab'=4,'col'=2,'pair'=2] {'slab','col'}, dimensions={0}, use_global_device_ids=true | all-gather | bytes 73728 | tf_op jit(solution)/shard_map/all_gather | solution.py:559
  34.5 1.7 %copy-done = f32[19,16,16,128]{3,2,1,0:T(8,128)S(1)} copy-done((f32[19,16,16,128]{3,2,1,0:T(8,128)S(1)}, f32[19,16,16,128]{3,2,1,0:T(8,128)}, u32[]{:S(2)}) %copy-start) | copy-done | bytes 2490392
  36.2 0.9 %copy-done.2 = s32[16,16,128]{2,1,0:T(8,128)S(1)} copy-done((s32[16,16,128]{2,1,0:T(8,128)S(1)}, s32[16,16,128]{2,1,0:T(8,128)}, u32[]{:S(2)}) %copy-start.2) | copy-done | bytes 131096
  37.1 0.6 moments.1
  37.7 0.0 copy-start.4
  37.7 2.0 %couple.1 = (f32[3,16,16,128]{3,2,1,0:T(8,128)S(1)}, f32[8,128]{1,0:T(8,128)S(1)}, f32[160,128]{1,0:T(8,128)S(1)}, f32[64,128]{1,0:T(8,128)S(1)}, f32[80,128]{1,...) custom-call(f32[8,16,128]{2,1,0:T(8,128)S(1)} %bitcast.3, ...), custom_call_target="tpu_custom_call" | custom-call | tf_op jit(solution)/shard_map/couple/pallas_call | solution.py:410
  39.7 1.5 %collective-permute-start.1 = (f32[160,128]{1,0:T(8,128)S(1)}, f32[160,128]{1,0:T(8,128)S(1)}, u32[]{:S(2)}, u32[]{:S(2)}) collective-permute-start(f32[160,128]{1,0:T(8,128)S(1)} %get-tuple-element.24), channel_id=1, source_target_pairs={{0,2},{1,3},{2,0},{3,1},{4,6},{5,7},{6,4},{7,5},{8,10},{9,11},{10,... | collective-permute-start | bytes 245768 | tf_op jit(solution)/shard_map/ppermute | solution.py:174
  41.2 0.0 collective-permute-start.4
  41.2 0.0 collective-permute-start.5
  41.2 4.7 %collective-permute-start.8 = (f32[16,128]{1,0:T(8,128)S(1)}, f32[16,128]{1,0:T(8,128)S(1)}, u32[]{:S(2)}, u32[]{:S(2)}) collective-permute-start(f32[16,128]{1,0:T(8,128)S(1)} %get-tuple-element.31), channel_id=1, source_target_pairs={{0,14},{1,15},{2,12},{3,13},{4,2},{5,3},{6,0},{7,1},{8,6},{9,7},{1... | collective-permute-start | bytes 24584 | tf_op jit(solution)/shard_map/ppermute | solution.py:174
  45.9 0.0 collective-permute-start.3
  45.9 1.6 %collective-permute-done.5.refs_4_ = f32[16,128]{1,0:T(8,128)S(1)} collective-permute-done((f32[16,128]{1,0:T(8,128)S(1)}, f32[16,128]{1,0:T(8,128)S(1)}, u32[]{:S(2)}, u32[]{:S(2)}) %collective-permute-start.5) | collective-permute-done | bytes 8224 | tf_op jit(solution)/shard_map/ppermute | solution.py:174
  47.6 2.2 %collective-permute-start.6 = (f32[80,128]{1,0:T(8,128)S(1)}, f32[80,128]{1,0:T(8,128)S(1)}, u32[]{:S(2)}, u32[]{:S(2)}) collective-permute-start(f32[80,128]{1,0:T(8,128)S(1)} %get-tuple-element.29), channel_id=1, source_target_pairs={{0,12},{1,13},{2,14},{3,15},{4,0},{5,1},{6,2},{7,3},{8,4},{9,5},{1... | collective-permute-start | bytes 122888 | tf_op jit(solution)/shard_map/ppermute | solution.py:174
  49.8 0.0 collective-permute-done.8.refs_7_
  49.8 0.3 collective-permute-start.7
  50.1 0.0 collective-permute-done.4.refs_3_
  50.1 2.6 %collective-permute-start.2 = (f32[64,128]{1,0:T(8,128)S(1)}, f32[64,128]{1,0:T(8,128)S(1)}, u32[]{:S(2)}, u32[]{:S(2)}) collective-permute-start(f32[64,128]{1,0:T(8,128)S(1)} %get-tuple-element.25), channel_id=1, source_target_pairs={{0,3},{1,2},{2,1},{3,0},{4,7},{5,6},{6,5},{7,4},{8,11},{9,10},{10,... | collective-permute-start | bytes 98312 | tf_op jit(solution)/shard_map/ppermute | solution.py:174
  52.7 3.5 %stream.1 = (f32[19,16,16,128]{3,2,1,0:T(8,128)S(1)}, f32[2,16,128]{2,1,0:T(8,128)S(1)}) custom-call(f32[19,16,16,128]{3,2,1,0:T(8,128)S(1)} %copy-done.1, s32[16,16,128]{2,1,0:T(8,128)S(1)} %copy-done.3, f32[3,16,16,128]{3,2,1,0:T(8,128)S(1)} %get-tuple-element.20.force_ref), custom_call_target="tpu_custom_call" | custom-call | flops 10000000 | bytes 6000000 | tf_op jit(solution)/shard_map/stream/pallas_call | solution.py:447
  56.2 0.0 collective-permute-done.7.refs_6_
  56.2 0.1 collective-permute-start
  56.3 30.4 %all-gather.1 = f32[64,128]{1,0:T(8,128)S(1)} all-gather(f32[8,128]{1,0:T(8,128)S(1)} %get-tuple-element.23), channel_id=3, replica_groups=mesh['rep'=2,'slab'=4,'col'=2,'pair'=2] {'slab','col'}, dimensions={0}, use_global_device_ids=true | all-gather | bytes 36864 | tf_op jit(solution)/shard_map/all_gather | solution.py:575
  86.7 0.0 collective-permute-done.column_ref
  86.7 2.3 %finish.1 = (f32[19,16,16,128]{3,2,1,0:T(8,128)}, f32[3,128]{1,0:T(4,128)}) custom-call(s32[1,128]{1,0:T(1,128)S(1)} %bitcast.6, f32[19,16,16,128]{3,2,1,0:T(8,128)S(1)} %get-tuple-element.21.local_ref, f32[2,16,128]{2,1,0:T(8,128)S(1)} %collective-permute-done.column_ref, f32[8,8,128]{2,1,0:T(8,128)S(1)} %bitcast.4, ...), custom_call_target="tpu_custom_call" | custom-call | tf_op jit(solution)/shard_map/finish/pallas_call | solution.py:535
  (11 shorter events, 0.0 us)
Async XLA Ops:
  34.4 1.7 %copy-start = (f32[19,16,16,128]{3,2,1,0:T(8,128)S(1)}, f32[19,16,16,128]{3,2,1,0:T(8,128)}, u32[]{:S(2)}) copy-start(f32[19,16,16,128]{3,2,1,0:T(8,128)} %pops_ref.3) | copy-start | bytes 7471108
  36.2 0.9 %copy-start.2 = (s32[16,16,128]{2,1,0:T(8,128)S(1)}, s32[16,16,128]{2,1,0:T(8,128)}, u32[]{:S(2)}) copy-start(s32[16,16,128]{2,1,0:T(8,128)} %solid_ref.3) | copy-start | bytes 393220
  37.1 15.6 %copy-start.1 = (f32[19,16,16,128]{3,2,1,0:T(8,128)S(1)}, f32[19,16,16,128]{3,2,1,0:T(8,128)}, u32[]{:S(2)}) copy-start(f32[19,16,16,128]{3,2,1,0:T(8,128)} %pops_ref.3) | copy-start | bytes 7471108
  37.1 15.6 %copy-start.3 = (s32[16,16,128]{2,1,0:T(8,128)S(1)}, s32[16,16,128]{2,1,0:T(8,128)}, u32[]{:S(2)}) copy-start(s32[16,16,128]{2,1,0:T(8,128)} %solid_ref.3) | copy-start | bytes 393220
  37.7 49.0 %copy-start.4 = (s32[128]{0:T(128)S(1)}, s32[128]{0:T(128)}, u32[]{:S(2)}) copy-start(s32[128]{0:T(128)} %param.8) | copy-start | bytes 1540
  39.7 47.0 %collective-permute-start.1 = (f32[160,128]{1,0:T(8,128)S(1)}, f32[160,128]{1,0:T(8,128)S(1)}, u32[]{:S(2)}, u32[]{:S(2)}) collective-permute-start(f32[160,128]{1,0:T(8,128)S(1)} %get-tuple-element.24), channel_id=1, source_target_pairs={{0,2},{1,3},{2,0},{3,1},{4,6},{5,7},{6,4},{7,5},{8,10},{9,11},{10,... | collective-permute-start | bytes 245768 | tf_op jit(solution)/shard_map/ppermute | solution.py:174
  41.2 8.9 %collective-permute-start.4 = (f32[32,128]{1,0:T(8,128)S(1)}, f32[32,128]{1,0:T(8,128)S(1)}, u32[]{:S(2)}, u32[]{:S(2)}) collective-permute-start(f32[32,128]{1,0:T(8,128)S(1)} %get-tuple-element.27), channel_id=1, source_target_pairs={{0,5},{1,4},{2,7},{3,6},{4,9},{5,8},{6,11},{7,10},{8,13},{9,12},{1... | collective-permute-start | bytes 49160 | tf_op jit(solution)/shard_map/ppermute | solution.py:174
  41.2 6.4 %collective-permute-start.5 = (f32[16,128]{1,0:T(8,128)S(1)}, f32[16,128]{1,0:T(8,128)S(1)}, u32[]{:S(2)}, u32[]{:S(2)}) collective-permute-start(f32[16,128]{1,0:T(8,128)S(1)} %get-tuple-element.28), channel_id=1, source_target_pairs={{0,6},{1,7},{2,4},{3,5},{4,10},{5,11},{6,8},{7,9},{8,14},{9,15},{1... | collective-permute-start | bytes 24584 | tf_op jit(solution)/shard_map/ppermute | solution.py:174
  41.2 8.6 %collective-permute-start.8 = (f32[16,128]{1,0:T(8,128)S(1)}, f32[16,128]{1,0:T(8,128)S(1)}, u32[]{:S(2)}, u32[]{:S(2)}) collective-permute-start(f32[16,128]{1,0:T(8,128)S(1)} %get-tuple-element.31), channel_id=1, source_target_pairs={{0,14},{1,15},{2,12},{3,13},{4,2},{5,3},{6,0},{7,1},{8,6},{9,7},{1... | collective-permute-start | bytes 24584 | tf_op jit(solution)/shard_map/ppermute | solution.py:174
  45.9 40.8 %collective-permute-start.3 = (f32[80,128]{1,0:T(8,128)S(1)}, f32[80,128]{1,0:T(8,128)S(1)}, u32[]{:S(2)}, u32[]{:S(2)}) collective-permute-start(f32[80,128]{1,0:T(8,128)S(1)} %get-tuple-element.26), channel_id=1, source_target_pairs={{0,4},{1,5},{2,6},{3,7},{4,8},{5,9},{6,10},{7,11},{8,12},{9,13},{1... | collective-permute-start | bytes 122888 | tf_op jit(solution)/shard_map/ppermute | solution.py:174
  47.6 39.2 %collective-permute-start.6 = (f32[80,128]{1,0:T(8,128)S(1)}, f32[80,128]{1,0:T(8,128)S(1)}, u32[]{:S(2)}, u32[]{:S(2)}) collective-permute-start(f32[80,128]{1,0:T(8,128)S(1)} %get-tuple-element.29), channel_id=1, source_target_pairs={{0,12},{1,13},{2,14},{3,15},{4,0},{5,1},{6,2},{7,3},{8,4},{9,5},{1... | collective-permute-start | bytes 122888 | tf_op jit(solution)/shard_map/ppermute | solution.py:174
  49.8 6.4 %collective-permute-start.7 = (f32[32,128]{1,0:T(8,128)S(1)}, f32[32,128]{1,0:T(8,128)S(1)}, u32[]{:S(2)}, u32[]{:S(2)}) collective-permute-start(f32[32,128]{1,0:T(8,128)S(1)} %get-tuple-element.30), channel_id=1, source_target_pairs={{0,13},{1,12},{2,15},{3,14},{4,1},{5,0},{6,3},{7,2},{8,5},{9,4},{1... | collective-permute-start | bytes 49160 | tf_op jit(solution)/shard_map/ppermute | solution.py:174
  50.1 36.7 %collective-permute-start.2 = (f32[64,128]{1,0:T(8,128)S(1)}, f32[64,128]{1,0:T(8,128)S(1)}, u32[]{:S(2)}, u32[]{:S(2)}) collective-permute-start(f32[64,128]{1,0:T(8,128)S(1)} %get-tuple-element.25), channel_id=1, source_target_pairs={{0,3},{1,2},{2,1},{3,0},{4,7},{5,6},{6,5},{7,4},{8,11},{9,10},{10,... | collective-permute-start | bytes 98312 | tf_op jit(solution)/shard_map/ppermute | solution.py:174
  56.2 30.5 %collective-permute-start = (f32[2,16,128]{2,1,0:T(8,128)S(1)}, f32[2,16,128]{2,1,0:T(8,128)S(1)}, u32[]{:S(2)}, u32[]{:S(2)}) collective-permute-start(f32[2,16,128]{2,1,0:T(8,128)S(1)} %get-tuple-element.22), channel_id=1, source_target_pairs={{0,1},{1,0},{2,3},{3,2},{4,5},{5,4},{6,7},{7,6},{8,9},{9,8},{10,11... | collective-permute-start | bytes 49160 | tf_op jit(solution)/shard_map/ppermute | solution.py:174

commit v3 on v2

v3 whole, which is shorter than its diff:
```python
import functools

import jax
import jax.numpy as jnp
import numpy as np
from jax import lax
from jax.experimental import pallas as pl
from jax.experimental.pallas import tpu as pltpu
from jax.sharding import PartitionSpec as P

CAP = 32
GROUP = 8

STEP = np.array(
    [
        [0, 0, 0],
        [1, 0, 0],
        [-1, 0, 0],
        [0, 1, 0],
        [0, -1, 0],
        [0, 0, 1],
        [0, 0, -1],
        [1, 1, 0],
        [-1, -1, 0],
        [1, -1, 0],
        [-1, 1, 0],
        [1, 0, 1],
        [-1, 0, -1],
        [1, 0, -1],
        [-1, 0, 1],
        [0, 1, 1],
        [0, -1, -1],
        [0, 1, -1],
        [0, -1, 1],
    ],
    np.int32,
)
TAU_PLUS = 0.8
TAU_MINUS = 0.5 + (3.0 / 16.0) / (TAU_PLUS - 0.5)
KEEP_EVEN = 1.0 - 1.0 / TAU_PLUS
KEEP_ODD = 1.0 - 1.0 / TAU_MINUS
FORCE_GAIN = 1.0 - 0.5 / TAU_PLUS
DRAG_COEF = 2.0
F32 = jnp.float32
BF16 = jnp.bfloat16

ENTER = [[[i for i in range(19) if STEP[i, a] == sign] for sign in (1, -1)] for a in range(3)]
NT = (((1,), (1,)), ((), ()))
NN = (((1,), (0,)), ((), ()))


def iota(shape, dim):
    return lax.broadcasted_iota(jnp.int32, shape, dim)


def high_low(value):
    high = value.astype(BF16)
    return high, (value - high.astype(F32)).astype(BF16)


def dot_split(left, right, dims):
    a, b = high_low(left)
    c, d = high_low(right)
    mul = functools.partial(lax.dot_general, dimension_numbers=dims, preferred_element_type=F32)
    return mul(a, c) + (mul(a, d) + mul(b, c))


def dot_select(value, choose, dims):
    first = value.astype(BF16).astype(F32)
    rest = value - first
    second = rest.astype(BF16).astype(F32)
    stacked = jnp.concatenate([first, second, rest - second], axis=0).astype(BF16)
    got = lax.dot_general(stacked, choose, dimension_numbers=dims, preferred_element_type=F32)
    rows = value.shape[0]
    return got[0:rows] + got[rows : 2 * rows] + got[2 * rows : 3 * rows]


def density_momentum(pops):
    momentum = []
    for axis in range(3):
        plus = [pops[i] for i in range(19) if STEP[i, axis] == 1]
        minus = [pops[i] for i in range(19) if STEP[i, axis] == -1]
        momentum.append(sum(plus[1:], plus[0]) - sum(minus[1:], minus[0]))
    return sum(pops[1:], pops[0]), momentum


def along(step, vector):
    terms = None
    for axis in range(3):
        if step[axis] == 0:
            continue
        if terms is None:
            terms = vector[axis] if step[axis] == 1 else -vector[axis]
        else:
            terms = terms + vector[axis] if step[axis] == 1 else terms - vector[axis]
    return terms


def collide(pops, wall, force):
    density, momentum = density_momentum(pops)
    inverse = 1.0 / density
    carried = [m + 0.5 * f for m, f in zip(momentum, force)]
    speed = [m * inverse for m in carried]
    w = 1.0 / 36.0
    bend = [(4.5 * w / TAU_PLUS) * m + (9.0 * w * FORCE_GAIN) * f for m, f in zip(carried, force)]
    push = [(3.0 * w / TAU_MINUS) * m + (3.0 * w * FORCE_GAIN) * f for m, f in zip(carried, force)]
    drop = [(1.5 * w / TAU_PLUS) * m + (3.0 * w * FORCE_GAIN) * f for m, f in zip(carried, force)]
    rest = (w / TAU_PLUS) * density - sum(
        [u * d for u, d in zip(speed[1:], drop[1:])], speed[0] * drop[0]
    )
    out = [None] * 19
    out[0] = jnp.where(wall, pops[0], KEEP_EVEN * pops[0] + 12.0 * rest)
    for i in range(1, 19, 2):
        a, b = pops[i], pops[i + 1]
        step = STEP[i]
        even = rest + along(step, speed) * along(step, bend)
        odd = along(step, push)
        if i < 7:
            even = even + even
            odd = odd + odd
        even = (0.5 * KEEP_EVEN) * (a + b) + even
        odd = (0.5 * KEEP_ODD) * (a - b) + odd
        out[i] = jnp.where(wall, b, even + odd)
        out[i + 1] = jnp.where(wall, a, even - odd)
    return out


def turn(value, amount, axis):
    if amount == 0:
        return value
    return pltpu.roll(value, int(amount) % value.shape[axis], axis)


def send(value, shape, offset):
    slabs, cols, pairs = shape
    perm = []
    for s in range(slabs):
        for c in range(cols):
            for p in range(pairs):
                there = (
                    ((s + offset[0]) % slabs) * cols + (c + offset[1]) % cols
                ) * pairs + (p + offset[2]) % pairs
                perm.append(((s * cols + c) * pairs + p, there))
    return lax.ppermute(value, ("slab", "col", "pair"), perm)


def rank_among(member):
    count = member.shape[1]
    earlier = (iota((count, count), 0) < iota((count, count), 1)).astype(F32).astype(BF16)
    return lax.dot_general(member.astype(BF16), earlier, NN, preferred_element_type=F32)


def spread_column(tile, lane):
    return jnp.broadcast_to(tile[:, lane : lane + 1], tile.shape)


def enter_x(value, i, column):
    step = STEP[i, 0]
    if step == 0:
        return value
    side = 0 if step == 1 else value.shape[1] - 1
    return jnp.where(iota(value.shape, 1) == side, column, turn(value, step, 1))


def x_place(i):
    group = 0 if STEP[i, 0] == 1 else 1
    return group, ENTER[0][group].index(i)


def pack_kernel(owner_ref, base_ref, offset_ref, velocity_ref, target_ref, out_ref, table):
    count = owner_ref.shape[1]
    local = owner_ref[...] - pl.program_id(0) * GROUP
    member = (iota((GROUP, count), 0) == local).astype(F32)
    rank = jnp.sum(member * rank_among(member), axis=0, keepdims=True).astype(jnp.int32)
    inside = (local >= 0) & (local < GROUP)
    target = jnp.where(inside, local * CAP + rank, -1)
    whole_target = jnp.where(inside, owner_ref[...] * CAP + rank, -1)

    @pl.when(pl.program_id(0) == 0)
    def _():
        target_ref[...] = whole_target

    @pl.when(pl.program_id(0) > 0)
    def _():
        target_ref[...] = jnp.maximum(target_ref[...], whole_target)

    choose = (iota((GROUP * CAP, count), 0) == target).astype(F32).astype(BF16)
    table[...] = jnp.zeros_like(table)
    table[0:3] = base_ref[...].astype(F32) + 1.0
    table[8:11] = offset_ref[...]
    table[16:19] = velocity_ref[...]
    packed = dot_select(table[...], choose, NT)
    blank = jnp.zeros((8, CAP), F32)
    for r in range(GROUP):
        lanes = slice(r * CAP, (r + 1) * CAP)
        out_ref[r] = jnp.concatenate(
            [packed[0:8, lanes], packed[8:16, lanes], packed[16:24, lanes], blank], axis=1
        )


def pack(owners, owner, base, offset, velocity):
    count = owner.shape[0]
    args = (owner.reshape(1, count), base, offset, velocity)
    return pl.pallas_call(
        pack_kernel,
        out_shape=[
            jax.ShapeDtypeStruct((1, count), jnp.int32),
            jax.ShapeDtypeStruct((owners, 8, 128), F32),
        ],
        grid=(owners // GROUP,),
        in_specs=[pl.BlockSpec(a.shape, lambda k: (0, 0)) for a in args],
        out_specs=[
            pl.BlockSpec((1, count), lambda k: (0, 0)),
            pl.BlockSpec((GROUP, 8, 128), lambda k: (k, 0, 0)),
        ],
        scratch_shapes=[pltpu.VMEM((24, count), F32)],
        compiler_params=pltpu.CompilerParams(
            vmem_limit_bytes=(4 << 20) if owners == GROUP else (48 << 20)
        ),
        name="pack",
    )(*args)


def moments_kernel(
    pops_ref, solid_ref, flow_ref, edge_ref, edge_solid_ref, column_ref, held, held_solid, sem
):
    depth, rows, width = pops_ref.shape[1:]
    chunks = 4
    span = depth // chunks
    copies = [pltpu.make_async_copy(solid_ref, held_solid, sem.at[chunks])]
    for k in range(chunks):
        part = pl.ds(k * span, span)
        copies.append(
            pltpu.make_async_copy(pops_ref.at[:, part], held.at[:, part], sem.at[k])
        )
    for copy in copies:
        copy.start()

    def plane(z, carry):
        pops = [held[i, z] for i in range(19)]
        density, momentum = density_momentum(pops)
        inverse = 1.0 / density
        for axis in range(3):
            flow_ref[axis, pl.ds(pl.multiple_of(z * rows, rows), rows)] = momentum[axis] * inverse
        return carry

    for k in range(chunks):
        copies[1 + k].wait()
        lax.fori_loop(k * span, (k + 1) * span, plane, 0)
    copies[0].wait()
    edge_solid_ref[0] = held_solid[0]
    edge_solid_ref[1] = held_solid[depth - 1]
    edge_solid_ref[2] = held_solid[:, 0, :]
    edge_solid_ref[3] = held_solid[:, rows - 1, :]
    lane = iota((rows, 128), 1)

    def ends(planes):
        tile = jnp.ones((rows, 128), F32)
        for z, value in enumerate(planes):
            tile = jnp.where(lane == z, spread_column(value, 0), tile)
            tile = jnp.where(lane == depth + z, spread_column(value, width - 1), tile)
        return tile

    def population(i, carry):
        edge_ref[i, 0] = held[i, 0]
        edge_ref[i, 1] = held[i, depth - 1]
        edge_ref[i, 2] = held[i, :, 0, :]
        edge_ref[i, 3] = held[i, :, rows - 1, :]
        column_ref[i] = ends([held[i, z] for z in range(depth)])
        return carry

    lax.fori_loop(0, 19, population, 0)
    column_ref[19] = ends([held_solid[z].astype(F32) for z in range(depth)])


def moments(pops, solid):
    _, depth, rows, width = pops.shape
    hbm = pl.BlockSpec(memory_space=pltpu.HBM)
    return pl.pallas_call(
        moments_kernel,
        out_shape=[
            jax.ShapeDtypeStruct((3, depth * rows, width), F32),
            jax.ShapeDtypeStruct((19, 4, rows, width), F32),
            jax.ShapeDtypeStruct((4, rows, width), jnp.int32),
            jax.ShapeDtypeStruct((20, rows, 128), F32),
        ],
        in_specs=[hbm, hbm],
        scratch_shapes=[
            pltpu.VMEM(pops.shape, F32),
            pltpu.VMEM(solid.shape, jnp.int32),
            pltpu.SemaphoreType.DMA((5,)),
        ],
        compiler_params=pltpu.CompilerParams(vmem_limit_bytes=12 << 20),
        cost_estimate=pl.CostEstimate(flops=3000000, bytes_accessed=4000000, transcendentals=0),
        name="moments",
    )(pops, solid)


def unpack(tiles):
    return [
        jnp.concatenate([t[:, g * CAP : (g + 1) * CAP] for t in tiles], axis=1) for g in range(3)
    ]


def couple_group(base, part, velocity, flow, depth, rows):
    width, slots = flow.shape[1], GROUP * CAP
    start = base.astype(jnp.int32) - 1

    def hat(axis, length):
        cell = iota((length, slots), 0)
        low, share = start[axis : axis + 1], part[axis : axis + 1]
        return jnp.where(cell == low, 1.0 - share, 0.0) + jnp.where(cell == low + 1, share, 0.0)

    hat_x, hat_y, hat_z = hat(0, width), hat(1, rows), hat(2, depth)
    weight = (hat_z[:, None, :] * hat_y[None, :, :]).reshape(depth * rows, slots)
    across = dot_split(flow, hat_x, NN)
    cells = depth * rows
    sampled = [
        jnp.sum(across[d * cells : (d + 1) * cells] * weight, axis=0, keepdims=True)
        for d in range(3)
    ]
    drag = [DRAG_COEF * (sampled[d] - velocity[d : d + 1]) for d in range(3)]
    spread = jnp.concatenate([weight * (-drag[d]) for d in range(3)], axis=0)
    return drag, dot_split(spread, hat_x, NT)


def couple_kernel(shape, depth, rows, beads_ref, flow_ref, column_ref, force_ref, face_ref, *drag_refs):
    slabs, cols, _ = shape
    width = flow_ref.shape[2]
    flow = flow_ref[...].reshape(3 * depth * rows, width)
    hollow = jnp.zeros((5, GROUP * CAP), F32)

    if len(drag_refs) == 2:
        slab, col = lax.axis_index("slab"), lax.axis_index("col")
        got = []
        for r in range(GROUP):
            there = [a - b for a, b in zip((slab, col), divmod(r, cols))]
            there = [jnp.where(a < 0, a + n, a) for a, n in zip(there, (slabs, cols))]
            got.append(beads_ref[there[0] * cols + there[1]])
        drag, force = couple_group(*unpack(got), flow, depth, rows)
        force_ref[...] = force.reshape(3, depth, rows, width)
        stacked = jnp.concatenate(drag + [hollow], axis=0)
        lanes = cols * CAP
        blank = jnp.zeros((8, 128 - lanes), F32)
        for dz in range(slabs):
            tile = jnp.concatenate([stacked[:, dz * lanes : (dz + 1) * lanes], blank], axis=1)
            drag_refs[0][dz] = tile
            if dz == 2:
                drag_refs[1][...] = tile
    else:
        force_ref[...] = jnp.zeros_like(force_ref)
        blank = jnp.zeros((8, 128 - CAP), F32)

        def group(k, carry):
            got = [beads_ref[k * GROUP + r] for r in range(GROUP)]
            drag, force = couple_group(*unpack(got), flow, depth, rows)
            force_ref[...] += force.reshape(3, depth, rows, width)
            stacked = jnp.concatenate(drag + [hollow], axis=0)
            for r in range(GROUP):
                drag_refs[0][k * GROUP + r] = jnp.concatenate(
                    [stacked[:, r * CAP : (r + 1) * CAP], blank], axis=1
                )
            return carry

        lax.fori_loop(0, beads_ref.shape[0] // GROUP, group, 0)

    lane = iota((rows, 128), 1)
    force = []
    for d in range(3):
        tile = jnp.zeros((rows, 128), F32)
        for z in range(depth):
            plane = force_ref[d, z]
            tile = jnp.where(lane == z, spread_column(plane, 0), tile)
            tile = jnp.where(lane == depth + z, spread_column(plane, width - 1), tile)
        force.append(tile)
    out = collide([column_ref[i] for i in range(19)], column_ref[19] == 1.0, force)
    blank = jnp.zeros((rows, 128 - 5 * depth), F32)
    for group in range(2):
        side = slice(depth, 2 * depth) if group == 0 else slice(0, depth)
        face_ref[group] = jnp.concatenate(
            [out[i][:, side] for i in ENTER[0][group]] + [blank], axis=1
        )


def couple(shape, beads, flow, columns, depth, rows):
    width = flow.shape[2]
    single = beads.shape[0] == GROUP
    tile = jax.ShapeDtypeStruct((8, 128), F32)
    drags = [jax.ShapeDtypeStruct((shape[0], 8, 128), F32), tile] if single else [beads]
    return pl.pallas_call(
        functools.partial(couple_kernel, shape, depth, rows),
        out_shape=[
            jax.ShapeDtypeStruct((3, depth, rows, width), F32),
            jax.ShapeDtypeStruct((2, rows, 128), F32),
        ]
        + [jax.ShapeDtypeStruct(d.shape, F32) for d in drags],
        compiler_params=pltpu.CompilerParams(vmem_limit_bytes=24 << 20),
        name="couple",
    )(beads, flow, columns)


def faces_kernel(force_ref, edge_ref, edge_solid_ref, face_ref, drag_ref, up_ref, down_ref, draft_ref):
    depth, rows, width = force_ref.shape[1:]
    faces = [face_ref[0], face_ref[1]]
    turned = [f.T for f in faces]
    for side in range(4):
        pops = [edge_ref[i, side] for i in range(19)]
        first = side % 2 == 0
        if side < 2:
            force = [force_ref[d, 0 if first else depth - 1] for d in range(3)]
        else:
            force = [force_ref[d, :, 0 if first else rows - 1, :] for d in range(3)]
        out = collide(pops, edge_solid_ref[side] == 1, force)
        axis = 2 if side < 2 else 1
        group = 1 if first else 0
        for k, i in enumerate(ENTER[axis][group]):
            value = out[i]
            if STEP[i, 0] != 0:
                which, place = x_place(i)
                if axis == 2:
                    z = 0 if first else depth - 1
                    column = spread_column(faces[which], place * depth + z)
                else:
                    y = 0 if first else rows - 1
                    block = turned[which][place * depth : (place + 1) * depth]
                    column = jnp.broadcast_to(block[:, y : y + 1], (depth, width))
                value = enter_x(value, i, column)
            if axis == 2:
                (down_ref if first else up_ref)[k * rows : (k + 1) * rows] = value
            else:
                at = (group * 5 + k) * depth
                draft_ref[at : at + depth] = turn(value, STEP[i, 2], 0)
    if up_ref.shape[0] > 5 * rows:
        up_ref[5 * rows : 5 * rows + 8] = drag_ref[drag_ref.shape[0] - 1]
        down_ref[5 * rows : 5 * rows + 8] = drag_ref[1]


def faces(single, force, edge, edge_solid, face, drag):
    _, depth, rows, width = force.shape
    message = jax.ShapeDtypeStruct((5 * rows + (8 if single else 0), width), F32)
    return pl.pallas_call(
        faces_kernel,
        out_shape=[message, message, jax.ShapeDtypeStruct((10 * depth, width), F32)],
        compiler_params=pltpu.CompilerParams(vmem_limit_bytes=8 << 20),
        name="faces",
    )(force, edge, edge_solid, face, drag)


def rows_kernel(depth, rows, draft_ref, up_ref, down_ref, *refs):
    outs = refs[-1:] if len(refs) == 3 else refs
    for group in range(2):
        out_ref = outs[0] if len(outs) == 1 else outs[group]
        base = group * 5 * depth if len(outs) == 1 else 0
        y = rows - 1 if group == 0 else 0
        for k, i in enumerate(ENTER[1][group]):
            at = base + k * depth
            out_ref[at : at + depth] = draft_ref[(group * 5 + k) * depth : (group * 5 + k + 1) * depth]
            if STEP[i, 2] != 0:
                side = 0 if STEP[i, 2] == 1 else 1
                z = 0 if side == 0 else depth - 1
                row = ENTER[2][side].index(i) * rows + y
                out_ref[at + z : at + z + 1] = (up_ref, down_ref)[side][row : row + 1]
    if len(refs) == 3:
        own_ref, far_ref, out_ref = refs
        at, tail = 10 * depth, 5 * rows
        out_ref[at : at + 8] = own_ref[0]
        out_ref[at + 8 : at + 16] = down_ref[tail : tail + 8]
        out_ref[at + 16 : at + 24] = far_ref[...]
        out_ref[at + 24 : at + 32] = up_ref[tail : tail + 8]


def leaving_rows(shape, depth, rows, draft, up, down, drags):
    width = draft.shape[1]
    if drags:
        sizes = [10 * depth + 8 * shape[0]]
    else:
        sizes = [5 * depth] * 2
    return pl.pallas_call(
        functools.partial(rows_kernel, depth, rows),
        out_shape=[jax.ShapeDtypeStruct((n, width), F32) for n in sizes],
        compiler_params=pltpu.CompilerParams(vmem_limit_bytes=4 << 20),
        name="rows",
    )(draft, up, down, *drags)


def stream_kernel(pops_ref, solid_ref, force_ref, face_ref, out_ref, tile_ref, held, sem):
    depth, rows, width = pops_ref.shape[1:]
    chunks = 4
    span = depth // chunks

    def plane(z, faces):
        out = collide(
            [pops_ref[i, z] for i in range(19)],
            solid_ref[z] == 1,
            [force_ref[d, z] for d in range(3)],
        )
        for i in range(19):
            value = out[i]
            if STEP[i, 0] != 0:
                which, place = x_place(i)
                value = enter_x(value, i, spread_column(faces[which], place * depth))
            held[i, z + 1 + int(STEP[i, 2])] = turn(value, STEP[i, 1], 0)
        return tuple(pltpu.roll(f, 127, 1) for f in faces)

    runs = [(0, 5), (5, 6), (6, 7), (7, 11)] + [(i, i + 1) for i in range(11, 19)]
    copies = []
    carry = (face_ref[0], face_ref[1])
    for k in range(chunks):
        carry = lax.fori_loop(k * span, (k + 1) * span, plane, carry)
        for n, (a, b) in enumerate(runs):
            step = int(STEP[a, 2])
            low = max(k * span + step, 0)
            high = min((k + 1) * span + step, depth)
            copy = pltpu.make_async_copy(
                held.at[a:b, low + 1 : high + 1], out_ref.at[a:b, low:high], sem.at[k, n]
            )
            copy.start()
            copies.append(copy)
    for group in range(2):
        first = 0 if group == 0 else rows - 8
        for k, i in enumerate(ENTER[1][group]):
            tile_ref[group * 5 + k] = held[i, 1 : depth + 1, first : first + 8, :]
    for copy in copies:
        copy.wait()


def stream(pops, solid, force, face):
    _, depth, rows, width = pops.shape
    vmem = pl.BlockSpec(memory_space=pltpu.VMEM)
    return pl.pallas_call(
        stream_kernel,
        out_shape=[
            jax.ShapeDtypeStruct(pops.shape, F32),
            jax.ShapeDtypeStruct((10, depth, 8, width), F32),
        ],
        in_specs=[vmem] * 4,
        out_specs=[pl.BlockSpec(memory_space=pltpu.HBM), vmem],
        scratch_shapes=[
            pltpu.VMEM((19, depth + 2, rows, width), F32),
            pltpu.SemaphoreType.DMA((4, 12)),
        ],
        compiler_params=pltpu.CompilerParams(vmem_limit_bytes=16 << 20),
        cost_estimate=pl.CostEstimate(flops=10000000, bytes_accessed=6000000, transcendentals=0),
        name="stream",
    )(pops, solid, force, face)


def finish_kernel(shape, n_rows, whole_ref, target_ref, tile_ref, up_ref, down_ref, *refs):
    row_refs, refs = refs[:n_rows], refs[n_rows:]
    drag_refs, (out_ref, bead_ref, planes, tiles, sem) = refs[:-5], refs[-5:]
    depth, rows, width = whole_ref.shape[1:]

    def entering(group, k):
        if n_rows == 1:
            at = (group * 5 + k) * depth
            return row_refs[0][at : at + depth]
        return row_refs[group][k * depth : (k + 1) * depth]

    copies = []

    def leave(source, target):
        copy = pltpu.make_async_copy(source, target, sem.at[len(copies)])
        copy.start()
        copies.append(copy)

    for group in range(2):
        z = 0 if group == 0 else depth - 1
        for k, i in enumerate(ENTER[2][group]):
            value = (up_ref, down_ref)[group][k * rows : (k + 1) * rows]
            if STEP[i, 1] != 0:
                side = 0 if STEP[i, 1] == 1 else 1
                row = entering(side, ENTER[1][side].index(i))[z : z + 1]
                y = 0 if side == 0 else rows - 1
                value = jnp.where(
                    iota((rows, width), 0) == y,
                    jnp.broadcast_to(row, (rows, width)),
                    turn(value, STEP[i, 1], 0),
                )
            n = group * 5 + k
            planes[n] = value
            leave(planes.at[n], out_ref.at[i, z])
    for group in range(2):
        first = 0 if group == 0 else rows - 8
        for k, i in enumerate(ENTER[1][group]):
            n = group * 5 + k
            tiles[n] = tile_ref[n]
            tiles[n, :, 0 if group == 0 else 7, :] = entering(group, k)
            low, high = (1 if STEP[i, 2] == 1 else 0), (depth - 1 if STEP[i, 2] == -1 else depth)
            leave(tiles.at[n, low:high], out_ref.at[i, low:high, first : first + 8])

    count = target_ref.shape[1]
    target = target_ref[...]
    if n_rows == 1:
        own_ref, far_ref = drag_refs
        slabs, cols, _ = shape
        at, tail = 10 * depth, 5 * rows
        direct = jnp.concatenate(
            [own_ref[0], down_ref[tail : tail + 8], far_ref[...], up_ref[tail : tail + 8]], axis=0
        )
        passed = row_refs[0][at : at + 8 * slabs]
        table = jnp.where(iota(direct.shape, 1) < CAP, direct, passed)
        owner = lax.shift_right_logical(target, 5)
        slot = target - owner * CAP
        owner_slab = lax.shift_right_logical(owner, cols.bit_length() - 1)
        away_col = owner - owner_slab * cols - lax.axis_index("col")
        away_col = jnp.where(away_col < 0, away_col + cols, away_col)
        away_slab = owner_slab - lax.axis_index("slab")
        away_slab = jnp.where(away_slab < 0, away_slab + slabs, away_slab)
        choose = (iota((128, count), 0) == away_col * CAP + slot).astype(F32).astype(BF16)
        picked = dot_select(table, choose, NN)
        total = jnp.where(away_slab == 0, picked[0:8], 0.0)
        for dz in range(1, slabs):
            total = total + jnp.where(away_slab == dz, picked[8 * dz : 8 * dz + 8], 0.0)
        bead_ref[...] = total[0:3]
    else:
        back_ref = drag_refs[0]

        def group(k, total):
            got = [back_ref[k * GROUP + r] for r in range(GROUP)]
            slots = jnp.concatenate([t[:, 0:CAP] for t in got], axis=1)
            first = k * (GROUP * CAP)
            choose = (iota((GROUP * CAP, count), 0) + first == target).astype(F32)
            return total + dot_select(slots, choose.astype(BF16), NN)

        total = lax.fori_loop(
            0, back_ref.shape[0] // GROUP, group, jnp.zeros((8, count), F32)
        )
        bead_ref[...] = total[0:3]
    for copy in copies:
        copy.wait()


def finish(shape, whole, target, tiles, up, down, entered, drags):
    _, depth, rows, width = whole.shape
    vmem = pl.BlockSpec(memory_space=pltpu.VMEM)
    hbm = pl.BlockSpec(memory_space=pltpu.HBM)
    args = [whole, target, tiles, up, down, *entered, *drags]
    return pl.pallas_call(
        functools.partial(finish_kernel, shape, len(entered)),
        out_shape=[
            jax.ShapeDtypeStruct(whole.shape, F32),
            jax.ShapeDtypeStruct((3, target.shape[1]), F32),
        ],
        in_specs=[hbm] + [vmem] * (len(args) - 1),
        out_specs=[hbm, vmem],
        scratch_shapes=[
            pltpu.VMEM((10, rows, width), F32),
            pltpu.VMEM((10, depth, 8, width), F32),
            pltpu.SemaphoreType.DMA((20,)),
        ],
        input_output_aliases={0: 0},
        compiler_params=pltpu.CompilerParams(vmem_limit_bytes=24 << 20),
        name="finish",
    )(*args)


def shards(populations, solid_mask, bead_owner, bead_base, bead_offset, bead_velocity):
    slabs, cols, pairs = shape = tuple(lax.axis_size(a) for a in ("slab", "col", "pair"))
    owners = slabs * cols
    depth, rows = populations.shape[1:3]
    single = owners == GROUP and slabs == 4
    swap = functools.partial(
        lax.all_to_all, axis_name=("slab", "col"), split_axis=0, concat_axis=0, tiled=True
    )

    target, beads = pack(owners, bead_owner, bead_base, bead_offset, bead_velocity)
    beads = swap(beads)
    flow, edge, edge_solid, columns = moments(populations, solid_mask)
    force, face, drag, *far = couple(shape, beads, flow, columns, depth, rows)
    face = send(face, shape, (0, 0, 1))
    if single:
        far = send(far[0], shape, (2, 0, 0))
    else:
        drag = swap(drag)
    up, down, draft = faces(single, force, edge, edge_solid, face, drag)
    up = send(up, shape, (1, 0, 0))
    down = send(down, shape, (-1, 0, 0))
    whole, tiles = stream(populations, solid_mask, force, face)
    drags = [drag, far] if single else []
    leaving = leaving_rows(shape, depth, rows, draft, up, down, drags)
    entered = [send(value, shape, (0, sign, 0)) for value, sign in zip(leaving, (1, -1))]
    return tuple(finish(shape, whole, target, tiles, up, down, entered, drags or [drag]))


def solution(mesh):
    return jax.shard_map(
        shards,
        mesh=mesh,
        in_specs=(
            P(None, ("rep", "slab"), "col", "pair"),
            P(("rep", "slab"), "col", "pair"),
            P(("rep", "slab", "col", "pair")),
            P(None, ("rep", "slab", "col", "pair")),
            P(None, ("rep", "slab", "col", "pair")),
            P(None, ("rep", "slab", "col", "pair")),
        ),
        out_specs=(
            P(None, ("rep", "slab"), "col", "pair"),
            P(None, ("rep", "slab", "col", "pair")),
        ),
        check_vma=False,
    )
```

time: 89.2 us -> 39.5 us (0.44)
  blocking collectives: 62.9 us -> 0 us
  local copies, waits for them, and re-layouts: 2.62 us -> 7.04 us
  waiting for transfers between devices: 1.65 us -> 4.62 us
  starting transfers between devices: 11.4 us -> 14.3 us
  Pallas kernels: 9.72 us -> 12.5 us
    all_gather x2 -> x0, blocking collectives: 62.9 us -> none  [the longest x1 32.5 us: shards(): tiles = lax.all_gather(publish(*beads), group)]
    all_to_all x0 -> x1, starting transfers between devices: none -> 7.25 us  [shards(): beads = swap(beads)]
    unnamed x10 -> x20, local copies, waits for them, and re-layouts: 2.62 us -> 7.04 us
    ppermute x9 -> x5, starting transfers between devices: 11.4 us -> 7.05 us  [send(): return lax.ppermute(value, ('slab', 'col', 'pair'), perm)]
    pallas_call x1, Pallas kernels: 0.63 us -> 4.15 us  [moments(): pl.pallas_call(moments_kernel, out_shape=[jax.ShapeDtypeStruct((3, depth...]
    ppermute x9 -> x5, waiting for transfers between devices: 1.65 us -> 4.62 us  [send(): return lax.ppermute(value, ('slab', 'col', 'pair'), perm)]
    pallas_call x3 -> x5, Pallas kernels: 5.57 us -> 4.66 us  [the longest x1 1.68 us: couple(): pl.pallas_call(functools.partial(couple_kernel, shape, depth, rows), out_...]
  transfers between devices with their start and end apart: 9 -> 6, of which waited for: 1 -> 2; matrix products, arithmetic and copies ran while one was open for 0% -> 0% of each run, Pallas kernels for 4% -> 20%
where the time goes in v3:
time: 39.5 us; the launch traced here: 39.2 us
  starting transfers between devices  14.3 us (36%)
  Pallas kernels  12.5 us (32%)
  local copies, waits for them, and re-layouts  7.04 us (18%)
  waiting for transfers between devices  4.62 us (12%)
  between operations  0.71 us (2%)
    all_to_all x1, starting transfers between devices, shards(): beads = swap(beads)  7.25 us
    ppermute x5, starting transfers between devices, send(): return lax.ppermute(value, ('slab', 'col', 'pair'), perm)  7.05 us
    unnamed x20, local copies, waits for them, and re-layouts  7.04 us
    ppermute x5, waiting for transfers between devices, send(): return lax.ppermute(value, ('slab', 'col', 'pair'), perm)  4.62 us
    pallas_call x1, Pallas kernels, moments(): pl.pallas_call(moments_kernel, out_shape=[jax.ShapeDtypeStruct((3, depth...  4.15 us
    pallas_call x1, Pallas kernels, stream(): pl.pallas_call(stream_kernel, out_shape=[jax.ShapeDtypeStruct(pops.shape,...  3.7 us
    pallas_call x1, Pallas kernels, couple(): pl.pallas_call(functools.partial(couple_kernel, shape, depth, rows), out_...  1.68 us
    pallas_call x1, Pallas kernels, finish(): pl.pallas_call(functools.partial(finish_kernel, shape, len(entered)), out...  1.62 us
  transfers between devices with their start and end apart: 6, of which 2 were waited for; matrix products, arithmetic and copies ran while one was open for 0% of the time, Pallas kernels for 20%

profile of v3, /device:TPU:0, one launch (start us, length us, event | category | flops | bytes accessed | tf_op | source)
XLA Modules:
  0.0 39.2 jit_solution(14688581114442488764)
XLA Ops:
  0.6 0.7 %copy-done.6 = s32[3,128]{1,0:T(4,128)S(1)} copy-done((s32[3,128]{1,0:T(4,128)S(1)}, s32[3,128]{1,0:T(4,128)}, u32[]{:S(2)}) %copy-start.6) | copy-done | bytes 1560
  1.3 0.7 %copy-done.7 = f32[3,128]{1,0:T(4,128)S(1)} copy-done((f32[3,128]{1,0:T(4,128)S(1)}, f32[3,128]{1,0:T(4,128)}, u32[]{:S(2)}) %copy-start.7) | copy-done | bytes 1560
  2.0 0.7 %copy-done.8 = f32[3,128]{1,0:T(4,128)S(1)} copy-done((f32[3,128]{1,0:T(4,128)S(1)}, f32[3,128]{1,0:T(4,128)}, u32[]{:S(2)}) %copy-start.8) | copy-done | bytes 1560
  2.7 0.7 %copy-done.9 = s32[128]{0:T(128)S(1)} copy-done((s32[128]{0:T(128)S(1)}, s32[128]{0:T(128)}, u32[]{:S(2)}) %copy-start.9) | copy-done | bytes 536
  3.3 1.0 %pack.1 = (s32[1,128]{1,0:T(1,128)S(1)}, f32[8,8,128]{2,1,0:T(8,128)}) custom-call(s32[1,128]{1,0:T(1,128)S(1)} %bitcast.1, s32[3,128]{1,0:T(4,128)S(1)} %copy-done.6, f32[3,128]{1,0:T(4,128)S(1)} %copy-done.7, f32[3,128]{1,0:T(4,128)S(1)} %copy-done.8), custom_call_target="tpu_custom_call" | custom-call | tf_op jit(solution)/shard_map/pack/pallas_call | solution.py:204
  4.3 7.3 %all-to-all-start = ((f32[8,8,128]{2,1,0:T(8,128)}), f32[8,8,128]{2,1,0:T(8,128)S(1)}, u32[]{:S(2)}, u32[]{:S(2)}) async-start(f32[8,8,128]{2,1,0:T(8,128)} %get-tuple-element.17), calls=%async_computation | async-start | bytes 65536 | tf_op jit(solution)/shard_map/all_to_all | solution.py:667
  11.6 1.7 %copy-done = f32[19,16,16,128]{3,2,1,0:T(8,128)S(1)} copy-done((f32[19,16,16,128]{3,2,1,0:T(8,128)S(1)}, f32[19,16,16,128]{3,2,1,0:T(8,128)}, u32[]{:S(2)}) %copy-start) | copy-done | bytes 2490392
  13.3 0.9 %copy-done.2 = s32[16,16,128]{2,1,0:T(8,128)S(1)} copy-done((s32[16,16,128]{2,1,0:T(8,128)S(1)}, s32[16,16,128]{2,1,0:T(8,128)}, u32[]{:S(2)}) %copy-start.2) | copy-done | bytes 131096
  14.2 4.1 %moments.1 = (f32[3,256,128]{2,1,0:T(8,128)S(1)}, f32[19,4,16,128]{3,2,1,0:T(8,128)S(1)}, s32[4,16,128]{2,1,0:T(8,128)S(1)}, f32[20,16,128]{2,1,0:T(8,128)S(1)}) custom-call(f32[19,16,16,128]{3,2,1,0:T(8,128)S(1)} %copy-done, s32[16,16,128]{2,1,0:T(8,128)S(1)} %copy-done.2), custom_call_target="tpu_custom_call" | custom-call | flops 3000000 | bytes 4000000 | tf_op jit(solution)/shard_map/moments/pallas_call | solution.py:279
  18.4 0.0 copy-start.4
  18.4 0.7 %copy-done.4 = f32[3,256,128]{2,1,0:T(8,128)} copy-done((f32[3,256,128]{2,1,0:T(8,128)}, f32[3,256,128]{2,1,0:T(8,128)S(1)}, u32[]{:S(2)}) %copy-start.4) | copy-done | bytes 393240
  19.1 0.0 all-to-all-done.beads_ref
  19.1 1.0 %copy-done.5 = f32[3,256,128]{2,1,0:T(8,128)S(1)} copy-done((f32[3,256,128]{2,1,0:T(8,128)S(1)}, f32[3,256,128]{2,1,0:T(8,128)}, u32[]{:S(2)}) %copy-start.5) | copy-done | bytes 393240
  20.1 1.7 %couple.1 = (f32[3,16,16,128]{3,2,1,0:T(8,128)S(1)}, f32[2,16,128]{2,1,0:T(8,128)S(1)}, f32[4,8,128]{2,1,0:T(8,128)S(1)}, f32[8,128]{1,0:T(8,128)S(1)}) custom-call(f32[8,8,128]{2,1,0:T(8,128)S(1)} %all-to-all-done.beads_ref, f32[3,256,128]{2,1,0:T(8,128)S(1)} %copy-done.5, f32[20,16,128]{2,1,0:T(8,128)S(1)} %get-tuple-element.19.column_ref), custom_call_target="tpu_custom_call" | custom-call | tf_op jit(solution)/shard_map/couple/pallas_call | solution.py:390
  21.8 0.1 collective-permute-start
  21.9 1.2 %collective-permute-done.face_ref = f32[2,16,128]{2,1,0:T(8,128)S(1)} collective-permute-done((f32[2,16,128]{2,1,0:T(8,128)S(1)}, f32[2,16,128]{2,1,0:T(8,128)S(1)}, u32[]{:S(2)}, u32[]{:S(2)}) %collective-permute-start) | collective-permute-done | bytes 16416 | tf_op jit(solution)/shard_map/ppermute | solution.py:144
  23.0 0.4 faces.1
  23.4 2.0 %collective-permute-start.1 = (f32[88,128]{1,0:T(8,128)S(1)}, f32[88,128]{1,0:T(8,128)S(1)}, u32[]{:S(2)}, u32[]{:S(2)}) collective-permute-start(f32[88,128]{1,0:T(8,128)S(1)} %get-tuple-element.28), channel_id=1, source_target_pairs={{0,4},{1,5},{2,6},{3,7},{4,8},{5,9},{6,10},{7,11},{8,12},{9,13},{1... | collective-permute-start | bytes 135176 | tf_op jit(solution)/shard_map/ppermute | solution.py:144
  25.4 1.9 %collective-permute-start.2 = (f32[88,128]{1,0:T(8,128)S(1)}, f32[88,128]{1,0:T(8,128)S(1)}, u32[]{:S(2)}, u32[]{:S(2)}) collective-permute-start(f32[88,128]{1,0:T(8,128)S(1)} %get-tuple-element.29), channel_id=1, source_target_pairs={{0,12},{1,13},{2,14},{3,15},{4,0},{5,1},{6,2},{7,3},{8,4},{9,5},{1... | collective-permute-start | bytes 135176 | tf_op jit(solution)/shard_map/ppermute | solution.py:144
  27.3 1.1 %collective-permute-start.3 = (f32[8,128]{1,0:T(8,128)S(1)}, f32[8,128]{1,0:T(8,128)S(1)}, u32[]{:S(2)}, u32[]{:S(2)}) collective-permute-start(f32[8,128]{1,0:T(8,128)S(1)} %get-tuple-element.31), channel_id=1, source_target_pairs={{0,8},{1,9},{2,10},{3,11},{4,12},{5,13},{6,14},{7,15},{8,0},{9,1},... | collective-permute-start | bytes 12296 | tf_op jit(solution)/shard_map/ppermute | solution.py:144
  28.4 3.4 %collective-permute-done.3.refs_1_.refs_2_ = f32[8,128]{1,0:T(8,128)S(1)} collective-permute-done((f32[8,128]{1,0:T(8,128)S(1)}, f32[8,128]{1,0:T(8,128)S(1)}, u32[]{:S(2)}, u32[]{:S(2)}) %collective-permute-start.3) | collective-permute-done | bytes 4128 | tf_op jit(solution)/shard_map/ppermute | solution.py:144
  31.8 2.0 %collective-permute-start.4 = (f32[192,128]{1,0:T(8,128)S(1)}, f32[192,128]{1,0:T(8,128)S(1)}, u32[]{:S(2)}, u32[]{:S(2)}) collective-permute-start(f32[192,128]{1,0:T(8,128)S(1)} %rows.1), channel_id=1, source_target_pairs={{0,2},{1,3},{2,0},{3,1},{4,6},{5,7},{6,4},{7,5},{8,10},{9,11},{10,... | collective-permute-start | bytes 294920 | tf_op jit(solution)/shard_map/ppermute | solution.py:144
  33.9 3.7 %stream.1 = (f32[19,16,16,128]{3,2,1,0:T(8,128)}, f32[10,16,8,128]{3,2,1,0:T(8,128)S(1)}) custom-call(f32[19,16,16,128]{3,2,1,0:T(8,128)S(1)} %copy-done.1, s32[16,16,128]{2,1,0:T(8,128)S(1)} %copy-done.3, f32[3,16,16,128]{3,2,1,0:T(8,128)S(1)} %get-tuple-element.20.force_ref, f32[2,16,128]{2,1,0:T(8,128)S(1)} %collective-permute-done.face_ref), custom_call_target="tpu_custom_call" | custom-call | flops 10000000 | bytes 6000000 | tf_op jit(solution)/shard_map/stream/pallas_call | solution.py:530
  37.6 1.6 %finish.1 = (f32[19,16,16,128]{3,2,1,0:T(8,128)}, f32[3,128]{1,0:T(4,128)}) custom-call(f32[19,16,16,128]{3,2,1,0:T(8,128)} %get-tuple-element.22.whole_ref, s32[1,128]{1,0:T(1,128)S(1)} %get-tuple-element.23.target_ref, f32[10,16,8,128]{3,2,1,0:T(8,128)S(1)} %get-tuple-element.24.tile_ref, ...), custom_call_target="tpu_custom_call", output_to_operand_aliasing={{0}: (0, {})} | custom-call | tf_op jit(solution)/shard_map/finish/pallas_call | solution.py:638
  (15 shorter events, 0.0 us)
Async XLA Ops:
  0.6 0.7 %copy-start.6 = (s32[3,128]{1,0:T(4,128)S(1)}, s32[3,128]{1,0:T(4,128)}, u32[]{:S(2)}) copy-start(s32[3,128]{1,0:T(4,128)} %base_ref.1) | copy-start | bytes 4612
  1.3 0.7 %copy-start.7 = (f32[3,128]{1,0:T(4,128)S(1)}, f32[3,128]{1,0:T(4,128)}, u32[]{:S(2)}) copy-start(f32[3,128]{1,0:T(4,128)} %offset_ref.1) | copy-start | bytes 4612
  2.0 0.7 %copy-start.8 = (f32[3,128]{1,0:T(4,128)S(1)}, f32[3,128]{1,0:T(4,128)}, u32[]{:S(2)}) copy-start(f32[3,128]{1,0:T(4,128)} %velocity_ref.1) | copy-start | bytes 4612
  2.7 0.7 %copy-start.9 = (s32[128]{0:T(128)S(1)}, s32[128]{0:T(128)}, u32[]{:S(2)}) copy-start(s32[128]{0:T(128)} %param.8) | copy-start | bytes 1540
  4.3 14.8 %all-to-all-start = ((f32[8,8,128]{2,1,0:T(8,128)}), f32[8,8,128]{2,1,0:T(8,128)S(1)}, u32[]{:S(2)}, u32[]{:S(2)}) async-start(f32[8,8,128]{2,1,0:T(8,128)} %get-tuple-element.17), calls=%async_computation | async-start | bytes 65536 | tf_op jit(solution)/shard_map/all_to_all | solution.py:667
  11.6 1.7 %copy-start = (f32[19,16,16,128]{3,2,1,0:T(8,128)S(1)}, f32[19,16,16,128]{3,2,1,0:T(8,128)}, u32[]{:S(2)}) copy-start(f32[19,16,16,128]{3,2,1,0:T(8,128)} %pops_ref.3) | copy-start | bytes 7471108
  13.3 0.9 %copy-start.2 = (s32[16,16,128]{2,1,0:T(8,128)S(1)}, s32[16,16,128]{2,1,0:T(8,128)}, u32[]{:S(2)}) copy-start(s32[16,16,128]{2,1,0:T(8,128)} %solid_ref.3) | copy-start | bytes 393220
  14.2 19.6 %copy-start.1 = (f32[19,16,16,128]{3,2,1,0:T(8,128)S(1)}, f32[19,16,16,128]{3,2,1,0:T(8,128)}, u32[]{:S(2)}) copy-start(f32[19,16,16,128]{3,2,1,0:T(8,128)} %pops_ref.3) | copy-start | bytes 7471108
  14.2 19.7 %copy-start.3 = (s32[16,16,128]{2,1,0:T(8,128)S(1)}, s32[16,16,128]{2,1,0:T(8,128)}, u32[]{:S(2)}) copy-start(s32[16,16,128]{2,1,0:T(8,128)} %solid_ref.3) | copy-start | bytes 393220
  18.4 0.7 %copy-start.4 = (f32[3,256,128]{2,1,0:T(8,128)}, f32[3,256,128]{2,1,0:T(8,128)S(1)}, u32[]{:S(2)}) copy-start(f32[3,256,128]{2,1,0:T(8,128)S(1)} %get-tuple-element.18.flow_ref) | copy-start | bytes 1179652
  19.1 1.0 %copy-start.5 = (f32[3,256,128]{2,1,0:T(8,128)S(1)}, f32[3,256,128]{2,1,0:T(8,128)}, u32[]{:S(2)}) copy-start(f32[3,256,128]{2,1,0:T(8,128)} %copy-done.4) | copy-start | bytes 1179652
  21.8 1.2 %collective-permute-start = (f32[2,16,128]{2,1,0:T(8,128)S(1)}, f32[2,16,128]{2,1,0:T(8,128)S(1)}, u32[]{:S(2)}, u32[]{:S(2)}) collective-permute-start(f32[2,16,128]{2,1,0:T(8,128)S(1)} %get-tuple-element.21), channel_id=1, source_target_pairs={{0,1},{1,0},{2,3},{3,2},{4,5},{5,4},{6,7},{7,6},{8,9},{9,8},{10,11... | collective-permute-start | bytes 49160 | tf_op jit(solution)/shard_map/ppermute | solution.py:144
  23.4 8.4 %collective-permute-start.1 = (f32[88,128]{1,0:T(8,128)S(1)}, f32[88,128]{1,0:T(8,128)S(1)}, u32[]{:S(2)}, u32[]{:S(2)}) collective-permute-start(f32[88,128]{1,0:T(8,128)S(1)} %get-tuple-element.28), channel_id=1, source_target_pairs={{0,4},{1,5},{2,6},{3,7},{4,8},{5,9},{6,10},{7,11},{8,12},{9,13},{1... | collective-permute-start | bytes 135176 | tf_op jit(solution)/shard_map/ppermute | solution.py:144
  25.4 6.4 %collective-permute-start.2 = (f32[88,128]{1,0:T(8,128)S(1)}, f32[88,128]{1,0:T(8,128)S(1)}, u32[]{:S(2)}, u32[]{:S(2)}) collective-permute-start(f32[88,128]{1,0:T(8,128)S(1)} %get-tuple-element.29), channel_id=1, source_target_pairs={{0,12},{1,13},{2,14},{3,15},{4,0},{5,1},{6,2},{7,3},{8,4},{9,5},{1... | collective-permute-start | bytes 135176 | tf_op jit(solution)/shard_map/ppermute | solution.py:144
  27.3 4.5 %collective-permute-start.3 = (f32[8,128]{1,0:T(8,128)S(1)}, f32[8,128]{1,0:T(8,128)S(1)}, u32[]{:S(2)}, u32[]{:S(2)}) collective-permute-start(f32[8,128]{1,0:T(8,128)S(1)} %get-tuple-element.31), channel_id=1, source_target_pairs={{0,8},{1,9},{2,10},{3,11},{4,12},{5,13},{6,14},{7,15},{8,0},{9,1},... | collective-permute-start | bytes 12296 | tf_op jit(solution)/shard_map/ppermute | solution.py:144
  31.8 5.7 %collective-permute-start.4 = (f32[192,128]{1,0:T(8,128)S(1)}, f32[192,128]{1,0:T(8,128)S(1)}, u32[]{:S(2)}, u32[]{:S(2)}) collective-permute-start(f32[192,128]{1,0:T(8,128)S(1)} %rows.1), channel_id=1, source_target_pairs={{0,2},{1,3},{2,0},{3,1},{4,6},{5,7},{6,4},{7,5},{8,10},{9,11},{10,... | collective-permute-start | bytes 294920 | tf_op jit(solution)/shard_map/ppermute | solution.py:144

commit v4 on v3

--- a/solution.py
+++ b/solution.py
@@ -164,7 +164,16 @@
 
 def x_place(i):
     group = 0 if STEP[i, 0] == 1 else 1
-    return group, ENTER[0][group].index(i)
+    place = ENTER[0][group].index(i)
+    return place // 4, (place % 4) * 32 + group
+
+
+def x_ends(planes):
+    lane = lax.shift_right_logical(iota(planes[0].shape, 1), 1)
+    tile = jnp.ones(planes[0].shape, F32)
+    for z, value in enumerate(planes):
+        tile = jnp.where(lane == z, pltpu.roll(value, 2 * z + 1, 1), tile)
+    return tile
 
 
 def pack_kernel(owner_ref, base_ref, offset_ref, velocity_ref, target_ref, out_ref, table):
@@ -215,7 +224,7 @@
         ],
         scratch_shapes=[pltpu.VMEM((24, count), F32)],
         compiler_params=pltpu.CompilerParams(
-            vmem_limit_bytes=(4 << 20) if owners == GROUP else (48 << 20)
+            vmem_limit_bytes=None if owners == GROUP else (48 << 20)
         ),
         name="pack",
     )(*args)
@@ -252,25 +261,17 @@
     edge_solid_ref[1] = held_solid[depth - 1]
     edge_solid_ref[2] = held_solid[:, 0, :]
     edge_solid_ref[3] = held_solid[:, rows - 1, :]
-    lane = iota((rows, 128), 1)
-
-    def ends(planes):
-        tile = jnp.ones((rows, 128), F32)
-        for z, value in enumerate(planes):
-            tile = jnp.where(lane == z, spread_column(value, 0), tile)
-            tile = jnp.where(lane == depth + z, spread_column(value, width - 1), tile)
-        return tile
 
     def population(i, carry):
         edge_ref[i, 0] = held[i, 0]
         edge_ref[i, 1] = held[i, depth - 1]
         edge_ref[i, 2] = held[i, :, 0, :]
         edge_ref[i, 3] = held[i, :, rows - 1, :]
-        column_ref[i] = ends([held[i, z] for z in range(depth)])
+        column_ref[i] = x_ends([held[i, z] for z in range(depth)])
         return carry
 
     lax.fori_loop(0, 19, population, 0)
-    column_ref[19] = ends([held_solid[z].astype(F32) for z in range(depth)])
+    column_ref[19] = x_ends([held_solid[z].astype(F32) for z in range(depth)])
 
 
 def moments(pops, solid):
@@ -290,7 +291,7 @@
             pltpu.VMEM(solid.shape, jnp.int32),
             pltpu.SemaphoreType.DMA((5,)),
         ],
-        compiler_params=pltpu.CompilerParams(vmem_limit_bytes=12 << 20),
+        compiler_params=pltpu.CompilerParams(vmem_limit_bytes=64650000),
         cost_estimate=pl.CostEstimate(flops=3000000, bytes_accessed=4000000, transcendentals=0),
         name="moments",
     )(pops, solid)
@@ -364,22 +365,12 @@
 
         lax.fori_loop(0, beads_ref.shape[0] // GROUP, group, 0)
 
-    lane = iota((rows, 128), 1)
-    force = []
-    for d in range(3):
-        tile = jnp.zeros((rows, 128), F32)
-        for z in range(depth):
-            plane = force_ref[d, z]
-            tile = jnp.where(lane == z, spread_column(plane, 0), tile)
-            tile = jnp.where(lane == depth + z, spread_column(plane, width - 1), tile)
-        force.append(tile)
+    force = [x_ends([force_ref[d, z] for z in range(depth)]) for d in range(3)]
     out = collide([column_ref[i] for i in range(19)], column_ref[19] == 1.0, force)
-    blank = jnp.zeros((rows, 128 - 5 * depth), F32)
-    for group in range(2):
-        side = slice(depth, 2 * depth) if group == 0 else slice(0, depth)
-        face_ref[group] = jnp.concatenate(
-            [out[i][:, side] for i in ENTER[0][group]] + [blank], axis=1
-        )
+    high = lax.rem(iota((rows, 128), 1), 2) == 0
+    ends = [jnp.where(high, out[i], out[j])[:, 0:32] for i, j in zip(*ENTER[0])]
+    face_ref[0] = jnp.concatenate(ends[0:4], axis=1)
+    face_ref[1] = jnp.concatenate([ends[4], jnp.zeros((rows, 96), F32)], axis=1)
 
 
 def couple(shape, beads, flow, columns, depth, rows):
@@ -394,45 +385,52 @@
             jax.ShapeDtypeStruct((2, rows, 128), F32),
         ]
         + [jax.ShapeDtypeStruct(d.shape, F32) for d in drags],
-        compiler_params=pltpu.CompilerParams(vmem_limit_bytes=24 << 20),
+        compiler_params=pltpu.CompilerParams(vmem_limit_bytes=ROOM),
         name="couple",
     )(beads, flow, columns)
 
 
-def faces_kernel(force_ref, edge_ref, edge_solid_ref, face_ref, drag_ref, up_ref, down_ref, draft_ref):
+def faces_kernel(
+    force_ref, edge_ref, edge_solid_ref, face_ref, drag_ref, up_ref, down_ref, draft_ref, token_ref, turned
+):
     depth, rows, width = force_ref.shape[1:]
-    faces = [face_ref[0], face_ref[1]]
-    turned = [f.T for f in faces]
+    token_ref[...] = jnp.zeros_like(token_ref)
+    tiles = [face_ref[0], face_ref[1]]
+    for n in range(2):
+        turned[n] = tiles[n].T
     for side in range(4):
-        pops = [edge_ref[i, side] for i in range(19)]
         first = side % 2 == 0
         if side < 2:
-            force = [force_ref[d, 0 if first else depth - 1] for d in range(3)]
+            at = (0 if first else depth - 1, slice(None))
         else:
-            force = [force_ref[d, :, 0 if first else rows - 1, :] for d in range(3)]
+            at = (slice(None), 0 if first else rows - 1)
+        pops = [edge_ref[i, side] for i in range(19)]
+        force = [force_ref[(d,) + at] for d in range(3)]
         out = collide(pops, edge_solid_ref[side] == 1, force)
         axis = 2 if side < 2 else 1
         group = 1 if first else 0
         for k, i in enumerate(ENTER[axis][group]):
             value = out[i]
             if STEP[i, 0] != 0:
-                which, place = x_place(i)
+                tile, lane = x_place(i)
                 if axis == 2:
-                    z = 0 if first else depth - 1
-                    column = spread_column(faces[which], place * depth + z)
+                    column = spread_column(tiles[tile], lane + 2 * at[0])
                 else:
-                    y = 0 if first else rows - 1
-                    block = turned[which][place * depth : (place + 1) * depth]
-                    column = jnp.broadcast_to(block[:, y : y + 1], (depth, width))
+                    block = turned[tile, pl.ds(lane, depth, stride=2), :]
+                    column = jnp.broadcast_to(block[:, at[1] : at[1] + 1], (depth, width))
                 value = enter_x(value, i, column)
             if axis == 2:
                 (down_ref if first else up_ref)[k * rows : (k + 1) * rows] = value
             else:
-                at = (group * 5 + k) * depth
-                draft_ref[at : at + depth] = turn(value, STEP[i, 2], 0)
+                row = (group * 5 + k) * depth
+                draft_ref[row : row + depth] = turn(value, STEP[i, 2], 0)
     if up_ref.shape[0] > 5 * rows:
         up_ref[5 * rows : 5 * rows + 8] = drag_ref[drag_ref.shape[0] - 1]
         down_ref[5 * rows : 5 * rows + 8] = drag_ref[1]
+
+
+TOKEN = jax.ShapeDtypeStruct((8, 128), F32)
+ROOM = 56 << 20
 
 
 def faces(single, force, edge, edge_solid, face, drag):
@@ -440,13 +438,16 @@
     message = jax.ShapeDtypeStruct((5 * rows + (8 if single else 0), width), F32)
     return pl.pallas_call(
         faces_kernel,
-        out_shape=[message, message, jax.ShapeDtypeStruct((10 * depth, width), F32)],
-        compiler_params=pltpu.CompilerParams(vmem_limit_bytes=8 << 20),
+        out_shape=[message, message, jax.ShapeDtypeStruct((10 * depth, width), F32), TOKEN],
+        scratch_shapes=[pltpu.VMEM((2, 128, rows), F32)],
+        compiler_params=pltpu.CompilerParams(vmem_limit_bytes=ROOM),
         name="faces",
     )(force, edge, edge_solid, face, drag)
 
 
-def rows_kernel(depth, rows, draft_ref, up_ref, down_ref, *refs):
+def rows_kernel(depth, rows, before_ref, draft_ref, up_ref, down_ref, *refs):
+    refs, token_ref = refs[:-1], refs[-1]
+    token_ref[...] = jnp.zeros_like(token_ref)
     outs = refs[-1:] if len(refs) == 3 else refs
     for group in range(2):
         out_ref = outs[0] if len(outs) == 1 else outs[group]
@@ -469,24 +470,31 @@
         out_ref[at + 24 : at + 32] = up_ref[tail : tail + 8]
 
 
-def leaving_rows(shape, depth, rows, draft, up, down, drags):
+def leaving_rows(shape, depth, rows, before, draft, up, down, drags):
     width = draft.shape[1]
     if drags:
         sizes = [10 * depth + 8 * shape[0]]
     else:
         sizes = [5 * depth] * 2
+    args = (draft, up, down, *drags)
     return pl.pallas_call(
         functools.partial(rows_kernel, depth, rows),
-        out_shape=[jax.ShapeDtypeStruct((n, width), F32) for n in sizes],
-        compiler_params=pltpu.CompilerParams(vmem_limit_bytes=4 << 20),
+        out_shape=[jax.ShapeDtypeStruct((n, width), F32) for n in sizes] + [TOKEN],
+        in_specs=[pl.BlockSpec(memory_space=pl.ANY)]
+        + [pl.BlockSpec(memory_space=pltpu.VMEM)] * len(args),
+        compiler_params=pltpu.CompilerParams(vmem_limit_bytes=ROOM),
         name="rows",
-    )(draft, up, down, *drags)
-
-
-def stream_kernel(pops_ref, solid_ref, force_ref, face_ref, out_ref, tile_ref, held, sem):
+    )(before, *args)
+
+
+def stream_kernel(low, high, before_ref, *refs):
+    if low > 0:
+        refs = refs[1:]
+    pops_ref, solid_ref, force_ref, face_ref, out_ref, tile_ref, token_ref, held, sem = refs
     depth, rows, width = pops_ref.shape[1:]
-    chunks = 4
-    span = depth // chunks
+    token_ref[...] = jnp.zeros_like(token_ref)
+    chunks = 2
+    span = (high - low) // chunks
 
     def plane(z, faces):
         out = collide(
@@ -497,55 +505,65 @@
         for i in range(19):
             value = out[i]
             if STEP[i, 0] != 0:
-                which, place = x_place(i)
-                value = enter_x(value, i, spread_column(faces[which], place * depth))
-            held[i, z + 1 + int(STEP[i, 2])] = turn(value, STEP[i, 1], 0)
-        return tuple(pltpu.roll(f, 127, 1) for f in faces)
+                tile, lane = x_place(i)
+                value = enter_x(value, i, spread_column(faces[tile], lane))
+            held[i, z - low] = turn(value, STEP[i, 1], 0)
+        return tuple(pltpu.roll(f, 126, 1) for f in faces)
 
     runs = [(0, 5), (5, 6), (6, 7), (7, 11)] + [(i, i + 1) for i in range(11, 19)]
     copies = []
     carry = (face_ref[0], face_ref[1])
+    if low > 0:
+        carry = tuple(pltpu.roll(f, 128 - 2 * low, 1) for f in carry)
     for k in range(chunks):
-        carry = lax.fori_loop(k * span, (k + 1) * span, plane, carry)
+        first = low + k * span
+        carry = lax.fori_loop(first, first + span, plane, carry)
         for n, (a, b) in enumerate(runs):
             step = int(STEP[a, 2])
-            low = max(k * span + step, 0)
-            high = min((k + 1) * span + step, depth)
+            start, stop = max(first + step, 0), min(first + span + step, depth)
             copy = pltpu.make_async_copy(
-                held.at[a:b, low + 1 : high + 1], out_ref.at[a:b, low:high], sem.at[k, n]
+                held.at[a:b, start - step - low : stop - step - low],
+                out_ref.at[a:b, start:stop],
+                sem.at[k, n],
             )
             copy.start()
             copies.append(copy)
     for group in range(2):
         first = 0 if group == 0 else rows - 8
         for k, i in enumerate(ENTER[1][group]):
-            tile_ref[group * 5 + k] = held[i, 1 : depth + 1, first : first + 8, :]
+            tile_ref[group * 5 + k] = held[i, :, first : first + 8, :]
     for copy in copies:
         copy.wait()
 
 
-def stream(pops, solid, force, face):
+def stream(low, high, before, whole, pops, solid, force, face):
     _, depth, rows, width = pops.shape
     vmem = pl.BlockSpec(memory_space=pltpu.VMEM)
+    hbm = pl.BlockSpec(memory_space=pltpu.HBM)
+    whole = [] if whole is None else [whole]
     return pl.pallas_call(
-        stream_kernel,
+        functools.partial(stream_kernel, low, high),
         out_shape=[
             jax.ShapeDtypeStruct(pops.shape, F32),
-            jax.ShapeDtypeStruct((10, depth, 8, width), F32),
+            jax.ShapeDtypeStruct((10, high - low, 8, width), F32),
+            TOKEN,
         ],
-        in_specs=[vmem] * 4,
-        out_specs=[pl.BlockSpec(memory_space=pltpu.HBM), vmem],
+        in_specs=[pl.BlockSpec(memory_space=pl.ANY)] + [hbm] * len(whole) + [vmem] * 4,
+        out_specs=[hbm, vmem, vmem],
         scratch_shapes=[
-            pltpu.VMEM((19, depth + 2, rows, width), F32),
-            pltpu.SemaphoreType.DMA((4, 12)),
+            pltpu.VMEM((19, high - low, rows, width), F32),
+            pltpu.SemaphoreType.DMA((2, 12)),
         ],
-        compiler_params=pltpu.CompilerParams(vmem_limit_bytes=16 << 20),
-        cost_estimate=pl.CostEstimate(flops=10000000, bytes_accessed=6000000, transcendentals=0),
+        input_output_aliases={1: 0} if whole else {},
+        compiler_params=pltpu.CompilerParams(vmem_limit_bytes=ROOM),
+        cost_estimate=pl.CostEstimate(flops=5000000, bytes_accessed=3000000, transcendentals=0),
         name="stream",
-    )(pops, solid, force, face)
-
-
-def finish_kernel(shape, n_rows, whole_ref, target_ref, tile_ref, up_ref, down_ref, *refs):
+    )(before, *whole, pops, solid, force, face)
+
+
+def finish_kernel(
+    shape, n_rows, whole_ref, target_ref, lower_ref, upper_ref, up_ref, down_ref, *refs
+):
     row_refs, refs = refs[:n_rows], refs[n_rows:]
     drag_refs, (out_ref, bead_ref, planes, tiles, sem) = refs[:-5], refs[-5:]
     depth, rows, width = whole_ref.shape[1:]
@@ -583,10 +601,13 @@
         first = 0 if group == 0 else rows - 8
         for k, i in enumerate(ENTER[1][group]):
             n = group * 5 + k
-            tiles[n] = tile_ref[n]
-            tiles[n, :, 0 if group == 0 else 7, :] = entering(group, k)
-            low, high = (1 if STEP[i, 2] == 1 else 0), (depth - 1 if STEP[i, 2] == -1 else depth)
-            leave(tiles.at[n, low:high], out_ref.at[i, low:high, first : first + 8])
+            step = int(STEP[i, 2])
+            half = lower_ref.shape[1]
+            tiles[n, 1 + step : 1 + step + half] = lower_ref[n]
+            tiles[n, 1 + step + half : 1 + step + depth] = upper_ref[n]
+            tiles[n, 1 : 1 + depth, 0 if group == 0 else 7, :] = entering(group, k)
+            low, high = max(step, 0), min(depth + step, depth)
+            leave(tiles.at[n, 1 + low : 1 + high], out_ref.at[i, low:high, first : first + 8])
 
     count = target_ref.shape[1]
     target = target_ref[...]
@@ -630,11 +651,11 @@
         copy.wait()
 
 
-def finish(shape, whole, target, tiles, up, down, entered, drags):
+def finish(shape, whole, target, lower, upper, up, down, entered, drags):
     _, depth, rows, width = whole.shape
     vmem = pl.BlockSpec(memory_space=pltpu.VMEM)
     hbm = pl.BlockSpec(memory_space=pltpu.HBM)
-    args = [whole, target, tiles, up, down, *entered, *drags]
+    args = [whole, target, lower, upper, up, down, *entered, *drags]
     return pl.pallas_call(
         functools.partial(finish_kernel, shape, len(entered)),
         out_shape=[
@@ -645,11 +666,11 @@
         out_specs=[hbm, vmem],
         scratch_shapes=[
             pltpu.VMEM((10, rows, width), F32),
-            pltpu.VMEM((10, depth, 8, width), F32),
+            pltpu.VMEM((10, depth + 2, 8, width), F32),
             pltpu.SemaphoreType.DMA((20,)),
         ],
         input_output_aliases={0: 0},
-        compiler_params=pltpu.CompilerParams(vmem_limit_bytes=24 << 20),
+        compiler_params=pltpu.CompilerParams(vmem_limit_bytes=ROOM),
         name="finish",
     )(*args)
 
@@ -672,14 +693,16 @@
         far = send(far[0], shape, (2, 0, 0))
     else:
         drag = swap(drag)
-    up, down, draft = faces(single, force, edge, edge_solid, face, drag)
+    up, down, draft, token = faces(single, force, edge, edge_solid, face, drag)
     up = send(up, shape, (1, 0, 0))
     down = send(down, shape, (-1, 0, 0))
-    whole, tiles = stream(populations, solid_mask, force, face)
+    fields = (populations, solid_mask, force, face)
+    whole, lower, token = stream(0, depth // 2, token, None, *fields)
     drags = [drag, far] if single else []
-    leaving = leaving_rows(shape, depth, rows, draft, up, down, drags)
+    *leaving, token = leaving_rows(shape, depth, rows, token, draft, up, down, drags)
     entered = [send(value, shape, (0, sign, 0)) for value, sign in zip(leaving, (1, -1))]
-    return tuple(finish(shape, whole, target, tiles, up, down, entered, drags or [drag]))
+    whole, upper, _ = stream(depth // 2, depth, token, whole, *fields)
+    return tuple(finish(shape, whole, target, lower, upper, up, down, entered, drags or [drag]))
 
 
 def solution(mesh):

time: 39.5 us -> 45 us (1.14)
  Pallas kernels: 12.5 us -> 26.3 us
  local copies, waits for them, and re-layouts: 7.04 us -> 2.43 us
  starting transfers between devices: 14.3 us -> 11.8 us
  waiting for transfers between devices: 4.62 us -> 3.24 us
    pallas_call x1 -> x2, Pallas kernels: 3.7 us -> 9.79 us  [stream(): pl.pallas_call(functools.partial(stream_kernel, low, high), out_shape=[ja...]
    unnamed x20 -> x12, local copies, waits for them, and re-layouts: 7.04 us -> 2.43 us
    ppermute x5, waiting for transfers between devices: 4.62 us -> 1.4 us  [send(): return lax.ppermute(value, ('slab', 'col', 'pair'), perm)]
    ppermute x5, starting transfers between devices: 7.05 us -> 4.59 us  [send(): return lax.ppermute(value, ('slab', 'col', 'pair'), perm)]
    pallas_call x1, Pallas kernels: 0.35 us -> 2.23 us  [faces(): pl.pallas_call(faces_kernel, out_shape=[message, message, jax.ShapeDtypeS...]
    all_to_all x1, waiting for transfers between devices: 0.01 us -> 1.84 us  [shards(): beads = swap(beads)]
    pallas_call x1, Pallas kernels: 1.68 us -> 3.34 us  [couple(): pl.pallas_call(functools.partial(couple_kernel, shape, depth, rows), out_...]
    pallas_call x1, Pallas kernels: 0.01 us -> 1.58 us  [leaving_rows(): pl.pallas_call(functools.partial(rows_kernel, depth, rows), out_shape=[ja...]
  transfers between devices with their start and end apart: 6 -> 6, of which waited for: 2 -> 2; matrix products, arithmetic and copies ran while one was open for 0% -> 0% of each run, Pallas kernels for 20% -> 33%
where the time goes in v4:
time: 45 us; the launch traced here: 44.5 us
  Pallas kernels  26.3 us (58%)
  starting transfers between devices  11.8 us (26%)
  waiting for transfers between devices  3.24 us (7%)
  local copies, waits for them, and re-layouts  2.43 us (5%)
  between operations  0.73 us (2%)
    pallas_call x2, Pallas kernels, stream(): pl.pallas_call(functools.partial(stream_kernel, low, high), out_shape=[ja...  9.79 us
    all_to_all x1, starting transfers between devices, shards(): beads = swap(beads)  7.25 us
    pallas_call x1, Pallas kernels, moments(): pl.pallas_call(moments_kernel, out_shape=[jax.ShapeDtypeStruct((3, depth...  4.84 us
    ppermute x5, starting transfers between devices, send(): return lax.ppermute(value, ('slab', 'col', 'pair'), perm)  4.59 us
    pallas_call x1, Pallas kernels, couple(): pl.pallas_call(functools.partial(couple_kernel, shape, depth, rows), out_...  3.34 us
    pallas_call x1, Pallas kernels, finish(): pl.pallas_call(functools.partial(finish_kernel, shape, len(entered)), out...  2.76 us
    unnamed x12, local copies, waits for them, and re-layouts  2.43 us
    pallas_call x1, Pallas kernels, faces(): pl.pallas_call(faces_kernel, out_shape=[message, message, jax.ShapeDtypeS...  2.23 us
  transfers between devices with their start and end apart: 6, of which 2 were waited for; matrix products, arithmetic and copies ran while one was open for 0% of the time, Pallas kernels for 33%

profile of v4, /device:TPU:0, one launch (start us, length us, event | category | flops | bytes accessed | tf_op | source)
XLA Modules:
  0.0 44.5 jit_solution(593902794724897804)
XLA Ops:
  0.6 1.7 %pack.1 = (s32[1,128]{1,0:T(1,128)}, f32[8,8,128]{2,1,0:T(8,128)}) custom-call(s32[1,128]{1,0:T(1,128)} %bitcast.1, s32[3,128]{1,0:T(4,128)} %base_ref.1, f32[3,128]{1,0:T(4,128)} %offset_ref.1, f32[3,128]{1,0:T(4,128)} %velocity_ref.1), custom_call_target="tpu_custom_call" | custom-call | tf_op jit(solution)/shard_map/pack/pallas_call | solution.py:213
  2.4 7.3 %all-to-all-start = ((f32[8,8,128]{2,1,0:T(8,128)}), f32[8,8,128]{2,1,0:T(8,128)S(1)}, u32[]{:S(2)}, u32[]{:S(2)}) async-start(f32[8,8,128]{2,1,0:T(8,128)} %get-tuple-element.23), calls=%async_computation | async-start | bytes 65536 | tf_op jit(solution)/shard_map/all_to_all | solution.py:688
  9.6 4.8 %moments.1 = (f32[3,256,128]{2,1,0:T(8,128)}, f32[19,4,16,128]{3,2,1,0:T(8,128)}, s32[4,16,128]{2,1,0:T(8,128)}, f32[20,16,128]{2,1,0:T(8,128)}) custom-call(f32[19,16,16,128]{3,2,1,0:T(8,128)} %refs_1_.3, s32[16,16,128]{2,1,0:T(8,128)} %refs_2_.1), custom_call_target="tpu_custom_call" | custom-call | flops 3000000 | bytes 4000000 | tf_op jit(solution)/shard_map/moments/pallas_call | solution.py:280
  14.5 1.8 %all-to-all-done.beads_ref = f32[8,8,128]{2,1,0:T(8,128)S(1)} async-done(((f32[8,8,128]{2,1,0:T(8,128)}), f32[8,8,128]{2,1,0:T(8,128)S(1)}, u32[]{:S(2)}, u32[]{:S(2)}) %all-to-all-start) | async-done | bytes 32800 | tf_op jit(solution)/shard_map/all_to_all | solution.py:688
  16.3 0.6 %copy-done.3 = f32[8,8,128]{2,1,0:T(8,128)} copy-done((f32[8,8,128]{2,1,0:T(8,128)}, f32[8,8,128]{2,1,0:T(8,128)S(1)}, u32[]{:S(2)}) %copy-start.3) | copy-done | bytes 32792
  16.9 3.3 %couple.1 = (f32[3,16,16,128]{3,2,1,0:T(8,128)}, f32[2,16,128]{2,1,0:T(8,128)}, f32[4,8,128]{2,1,0:T(8,128)}, f32[8,128]{1,0:T(8,128)}) custom-call(f32[8,8,128]{2,1,0:T(8,128)} %copy-done.3, f32[3,256,128]{2,1,0:T(8,128)} %get-tuple-element.24.flow_ref, f32[20,16,128]{2,1,0:T(8,128)} %get-tuple-element.25.column_ref), custom_call_target="tpu_custom_call" | custom-call | tf_op jit(solution)/shard_map/couple/pallas_call | solution.py:381
  20.3 0.0 collective-permute-start
  20.3 1.4 %collective-permute-done.face_ref.refs_3_.refs_4_ = f32[2,16,128]{2,1,0:T(8,128)S(1)} collective-permute-done((f32[2,16,128]{2,1,0:T(8,128)}, f32[2,16,128]{2,1,0:T(8,128)S(1)}, u32[]{:S(2)}, u32[]{:S(2)}) %collective-permute-start) | collective-permute-done | bytes 16416 | tf_op jit(solution)/shard_map/ppermute | solution.py:144
  21.6 0.6 %copy-done.2 = f32[2,16,128]{2,1,0:T(8,128)} copy-done((f32[2,16,128]{2,1,0:T(8,128)}, f32[2,16,128]{2,1,0:T(8,128)S(1)}, u32[]{:S(2)}) %copy-start.2) | copy-done | bytes 16408
  22.2 2.2 %faces.1 = (f32[88,128]{1,0:T(8,128)}, f32[88,128]{1,0:T(8,128)}, f32[160,128]{1,0:T(8,128)}, f32[8,128]{1,0:T(8,128)}) custom-call(f32[3,16,16,128]{3,2,1,0:T(8,128)} %get-tuple-element.26.force_ref.refs_2_.refs_3_, f32[19,4,16,128]{3,2,1,0:T(8,128)} %get-tuple-element.27.edge_ref, s32[4,16,128]{2,1,0:T(8,128)} %get-tuple-element.28.edge_solid_ref, ...), custom_call_target="tpu_custom_call" | custom-call | tf_op jit(solution)/shard_map/faces/pallas_call | solution.py:439
  24.5 0.4 collective-permute-start.1
  24.9 3.4 %collective-permute-start.2 = (f32[88,128]{1,0:T(8,128)}, f32[88,128]{1,0:T(8,128)S(1)}, u32[]{:S(2)}, u32[]{:S(2)}) collective-permute-start(f32[88,128]{1,0:T(8,128)} %get-tuple-element.35), channel_id=1, source_target_pairs={{0,12},{1,13},{2,14},{3,15},{4,0},{5,1},{6,2},{7,3},{8,4},{9,5},{1... | collective-permute-start | bytes 135176 | tf_op jit(solution)/shard_map/ppermute | solution.py:144
  28.3 0.0 collective-permute-start.3
  28.3 4.9 %stream.2 = (f32[19,16,16,128]{3,2,1,0:T(8,128)}, f32[10,8,8,128]{3,2,1,0:T(8,128)}, f32[8,128]{1,0:T(8,128)}) custom-call(f32[8,128]{1,0:T(8,128)} %get-tuple-element.31.before_ref, f32[19,16,16,128]{3,2,1,0:T(8,128)} %refs_1_.3, s32[16,16,128]{2,1,0:T(8,128)} %refs_2_.1, f32[3,16,16,128]{3,2,1,0:T(8,128)} %get-tuple-element.26.force_ref.refs_2_.refs_3_, ...), custom_call_target="tpu_custom_call" | custom-call | flops 5000000 | bytes 3000000 | tf_op jit(solution)/shard_map/stream/pallas_call | solution.py:544
  33.2 0.0 collective-permute-done.1.up_ref
  33.2 0.0 collective-permute-done.2.down_ref
  33.2 0.5 %copy-done.5 = f32[8,128]{1,0:T(8,128)} copy-done((f32[8,128]{1,0:T(8,128)}, f32[8,128]{1,0:T(8,128)S(1)}, u32[]{:S(2)}) %copy-start.5) | copy-done | bytes 4120
  33.8 0.1 copy-done
  33.8 0.0 copy-done.1
  33.9 1.6 %rows.1 = (f32[192,128]{1,0:T(8,128)}, f32[8,128]{1,0:T(8,128)}) custom-call(f32[8,128]{1,0:T(8,128)} %get-tuple-element.32.before_ref, f32[160,128]{1,0:T(8,128)} %get-tuple-element.33.draft_ref, f32[88,128]{1,0:T(8,128)} %copy-done, f32[88,128]{1,0:T(8,128)} %copy-done.1, f32[4,8,128]{2,1,0:T(8,128)} %get-tuple-element.30.drag_ref.refs_0_.refs_1_, ...), custom_call_target="tpu_custom_call" | custom-call | tf_op jit(solution)/shard_map/rows/pallas_call | solution.py:480
  35.4 0.8 %collective-permute-start.4 = (f32[192,128]{1,0:T(8,128)}, f32[192,128]{1,0:T(8,128)S(1)}, u32[]{:S(2)}, u32[]{:S(2)}) collective-permute-start(f32[192,128]{1,0:T(8,128)} %get-tuple-element.43), channel_id=1, source_target_pairs={{0,2},{1,3},{2,0},{3,1},{4,6},{5,7},{6,4},{7,5},{8,10},{9,11},{10,... | collective-permute-start | bytes 294920 | tf_op jit(solution)/shard_map/ppermute | solution.py:144
  36.2 4.9 %stream.3 = (f32[19,16,16,128]{3,2,1,0:T(8,128)}, f32[10,8,8,128]{3,2,1,0:T(8,128)}, f32[8,128]{1,0:T(8,128)}) custom-call(f32[8,128]{1,0:T(8,128)} %get-tuple-element.37.before_ref, f32[19,16,16,128]{3,2,1,0:T(8,128)} %get-tuple-element.38.refs_0_, f32[19,16,16,128]{3,2,1,0:T(8,128)} %refs_1_.3, ...), custom_call_target="tpu_custom_call", output_to_operand_aliasing={{0}: (1, {})} | custom-call | flops 5000000 | bytes 3000000 | tf_op jit(solution)/shard_map/stream/pallas_call | solution.py:544
  41.1 0.6 %copy-done.4 = f32[192,128]{1,0:T(8,128)} copy-done((f32[192,128]{1,0:T(8,128)}, f32[192,128]{1,0:T(8,128)S(1)}, u32[]{:S(2)}) %copy-start.4) | copy-done | bytes 98328
  41.8 2.8 %finish.1 = (f32[19,16,16,128]{3,2,1,0:T(8,128)}, f32[3,128]{1,0:T(4,128)}) custom-call(f32[19,16,16,128]{3,2,1,0:T(8,128)} %get-tuple-element.39.whole_ref, s32[1,128]{1,0:T(1,128)} %get-tuple-element.40.target_ref, f32[10,8,8,128]{3,2,1,0:T(8,128)} %get-tuple-element.41.lower_ref, ...), custom_call_target="tpu_custom_call", output_to_operand_aliasing={{0}: (0, {})} | custom-call | tf_op jit(solution)/shard_map/finish/pallas_call | solution.py:659
  (8 shorter events, 0.0 us)
Async XLA Ops:
  2.4 13.9 %all-to-all-start = ((f32[8,8,128]{2,1,0:T(8,128)}), f32[8,8,128]{2,1,0:T(8,128)S(1)}, u32[]{:S(2)}, u32[]{:S(2)}) async-start(f32[8,8,128]{2,1,0:T(8,128)} %get-tuple-element.23), calls=%async_computation | async-start | bytes 65536 | tf_op jit(solution)/shard_map/all_to_all | solution.py:688
  16.3 0.6 %copy-start.3 = (f32[8,8,128]{2,1,0:T(8,128)}, f32[8,8,128]{2,1,0:T(8,128)S(1)}, u32[]{:S(2)}) copy-start(f32[8,8,128]{2,1,0:T(8,128)S(1)} %all-to-all-done.beads_ref) | copy-start | bytes 98308
  20.3 1.4 %collective-permute-start = (f32[2,16,128]{2,1,0:T(8,128)}, f32[2,16,128]{2,1,0:T(8,128)S(1)}, u32[]{:S(2)}, u32[]{:S(2)}) collective-permute-start(f32[2,16,128]{2,1,0:T(8,128)} %get-tuple-element.29), channel_id=1, source_target_pairs={{0,1},{1,0},{2,3},{3,2},{4,5},{5,4},{6,7},{7,6},{8,9},{9,8},{10,11... | collective-permute-start | bytes 49160 | tf_op jit(solution)/shard_map/ppermute | solution.py:144
  21.6 0.6 %copy-start.2 = (f32[2,16,128]{2,1,0:T(8,128)}, f32[2,16,128]{2,1,0:T(8,128)S(1)}, u32[]{:S(2)}) copy-start(f32[2,16,128]{2,1,0:T(8,128)S(1)} %collective-permute-done.face_ref.refs_3_.refs_4_) | copy-start | bytes 49156
  24.5 8.7 %collective-permute-start.1 = (f32[88,128]{1,0:T(8,128)}, f32[88,128]{1,0:T(8,128)S(1)}, u32[]{:S(2)}, u32[]{:S(2)}) collective-permute-start(f32[88,128]{1,0:T(8,128)} %get-tuple-element.34), channel_id=1, source_target_pairs={{0,4},{1,5},{2,6},{3,7},{4,8},{5,9},{6,10},{7,11},{8,12},{9,13},{1... | collective-permute-start | bytes 135176 | tf_op jit(solution)/shard_map/ppermute | solution.py:144
  24.9 8.4 %collective-permute-start.2 = (f32[88,128]{1,0:T(8,128)}, f32[88,128]{1,0:T(8,128)S(1)}, u32[]{:S(2)}, u32[]{:S(2)}) collective-permute-start(f32[88,128]{1,0:T(8,128)} %get-tuple-element.35), channel_id=1, source_target_pairs={{0,12},{1,13},{2,14},{3,15},{4,0},{5,1},{6,2},{7,3},{8,4},{9,5},{1... | collective-permute-start | bytes 135176 | tf_op jit(solution)/shard_map/ppermute | solution.py:144
  28.3 4.9 %collective-permute-start.3 = (f32[8,128]{1,0:T(8,128)}, f32[8,128]{1,0:T(8,128)S(1)}, u32[]{:S(2)}, u32[]{:S(2)}) collective-permute-start(f32[8,128]{1,0:T(8,128)} %get-tuple-element.36), channel_id=1, source_target_pairs={{0,8},{1,9},{2,10},{3,11},{4,12},{5,13},{6,14},{7,15},{8,0},{9,1},... | collective-permute-start | bytes 12296 | tf_op jit(solution)/shard_map/ppermute | solution.py:144
  33.2 0.6 %copy-start.5 = (f32[8,128]{1,0:T(8,128)}, f32[8,128]{1,0:T(8,128)S(1)}, u32[]{:S(2)}) copy-start(f32[8,128]{1,0:T(8,128)S(1)} %collective-permute-done.3.refs_1_.refs_2_) | copy-start | bytes 12292
  33.2 0.6 %copy-start = (f32[88,128]{1,0:T(8,128)}, f32[88,128]{1,0:T(8,128)S(1)}, u32[]{:S(2)}) copy-start(f32[88,128]{1,0:T(8,128)S(1)} %collective-permute-done.1.up_ref) | copy-start | bytes 135172
  33.2 0.6 %copy-start.1 = (f32[88,128]{1,0:T(8,128)}, f32[88,128]{1,0:T(8,128)S(1)}, u32[]{:S(2)}) copy-start(f32[88,128]{1,0:T(8,128)S(1)} %collective-permute-done.2.down_ref) | copy-start | bytes 135172
  35.4 5.7 %collective-permute-start.4 = (f32[192,128]{1,0:T(8,128)}, f32[192,128]{1,0:T(8,128)S(1)}, u32[]{:S(2)}, u32[]{:S(2)}) collective-permute-start(f32[192,128]{1,0:T(8,128)} %get-tuple-element.43), channel_id=1, source_target_pairs={{0,2},{1,3},{2,0},{3,1},{4,6},{5,7},{6,4},{7,5},{8,10},{9,11},{10,... | collective-permute-start | bytes 294920 | tf_op jit(solution)/shard_map/ppermute | solution.py:144
  41.1 0.6 %copy-start.4 = (f32[192,128]{1,0:T(8,128)}, f32[192,128]{1,0:T(8,128)S(1)}, u32[]{:S(2)}) copy-start(f32[192,128]{1,0:T(8,128)S(1)} %collective-permute-done.4.refs_0_) | copy-start | bytes 294916

commit v5 on v4

--- a/solution.py
+++ b/solution.py
@@ -291,7 +291,7 @@
             pltpu.VMEM(solid.shape, jnp.int32),
             pltpu.SemaphoreType.DMA((5,)),
         ],
-        compiler_params=pltpu.CompilerParams(vmem_limit_bytes=64650000),
+        compiler_params=pltpu.CompilerParams(vmem_limit_bytes=54000000),
         cost_estimate=pl.CostEstimate(flops=3000000, bytes_accessed=4000000, transcendentals=0),
         name="moments",
     )(pops, solid)
@@ -430,7 +430,7 @@
 
 
 TOKEN = jax.ShapeDtypeStruct((8, 128), F32)
-ROOM = 56 << 20
+ROOM = 16 << 20
 
 
 def faces(single, force, edge, edge_solid, face, drag):

time: 45 us -> 35.6 us (0.79)
  Pallas kernels: 26.3 us -> 14.8 us
  waiting for transfers between devices: 3.24 us -> 4.76 us
  starting transfers between devices: 11.8 us -> 12.4 us
    pallas_call x2, Pallas kernels: 9.79 us -> 5.26 us  [stream(): pl.pallas_call(functools.partial(stream_kernel, low, high), out_shape=[ja...]
    ppermute x5, waiting for transfers between devices: 1.4 us -> 3.79 us  [send(): return lax.ppermute(value, ('slab', 'col', 'pair'), perm)]
    pallas_call x1, Pallas kernels: 2.23 us -> 0.38 us  [faces(): pl.pallas_call(faces_kernel, out_shape=[message, message, jax.ShapeDtypeS...]
    pallas_call x1, Pallas kernels: 3.34 us -> 1.6 us  [couple(): pl.pallas_call(functools.partial(couple_kernel, shape, depth, rows), out_...]
    pallas_call x1, Pallas kernels: 1.58 us -> 0.01 us  [leaving_rows(): pl.pallas_call(functools.partial(rows_kernel, depth, rows), out_shape=[ja...]
    pallas_call x1, Pallas kernels: 2.76 us -> 1.61 us  [finish(): pl.pallas_call(functools.partial(finish_kernel, shape, len(entered)), out...]
    all_to_all x1, waiting for transfers between devices: 1.84 us -> 0.96 us  [shards(): beads = swap(beads)]
    pallas_call x1, Pallas kernels: 4.84 us -> 4.06 us  [moments(): pl.pallas_call(moments_kernel, out_shape=[jax.ShapeDtypeStruct((3, depth...]
  transfers between devices with their start and end apart: 6 -> 6, of which waited for: 2 -> 4; matrix products, arithmetic and copies ran while one was open for 0% -> 0% of each run, Pallas kernels for 33% -> 26%
where the time goes in v5:
time: 35.6 us; the launch traced here: 35.3 us
  Pallas kernels  14.8 us (42%)
  starting transfers between devices  12.4 us (35%)
  waiting for transfers between devices  4.76 us (13%)
  local copies, waits for them, and re-layouts  2.65 us (7%)
  between operations  0.7 us (2%)
    all_to_all x1, starting transfers between devices, shards(): beads = swap(beads)  7.25 us
    pallas_call x2, Pallas kernels, stream(): pl.pallas_call(functools.partial(stream_kernel, low, high), out_shape=[ja...  5.26 us
    ppermute x5, starting transfers between devices, send(): return lax.ppermute(value, ('slab', 'col', 'pair'), perm)  5.13 us
    pallas_call x1, Pallas kernels, moments(): pl.pallas_call(moments_kernel, out_shape=[jax.ShapeDtypeStruct((3, depth...  4.06 us
    ppermute x5, waiting for transfers between devices, send(): return lax.ppermute(value, ('slab', 'col', 'pair'), perm)  3.79 us
    unnamed x12, local copies, waits for them, and re-layouts  2.65 us
    pallas_call x1, Pallas kernels, pack(): pl.pallas_call(pack_kernel, out_shape=[jax.ShapeDtypeStruct((1, count), j...  1.89 us
    pallas_call x1, Pallas kernels, finish(): pl.pallas_call(functools.partial(finish_kernel, shape, len(entered)), out...  1.61 us
  transfers between devices with their start and end apart: 6, of which 4 were waited for; matrix products, arithmetic and copies ran while one was open for 0% of the time, Pallas kernels for 26%

profile of v5, /device:TPU:0, one launch (start us, length us, event | category | flops | bytes accessed | tf_op | source)
XLA Modules:
  0.0 35.3 jit_solution(1525705013991739064)
XLA Ops:
  0.6 0.0 copy-start
  0.6 1.9 %pack.1 = (s32[1,128]{1,0:T(1,128)}, f32[8,8,128]{2,1,0:T(8,128)}) custom-call(s32[1,128]{1,0:T(1,128)} %bitcast.1, s32[3,128]{1,0:T(4,128)} %base_ref.1, f32[3,128]{1,0:T(4,128)} %offset_ref.1, f32[3,128]{1,0:T(4,128)} %velocity_ref.1), custom_call_target="tpu_custom_call" | custom-call | tf_op jit(solution)/shard_map/pack/pallas_call | solution.py:213
  2.5 7.3 %all-to-all-start = ((f32[8,8,128]{2,1,0:T(8,128)}), f32[8,8,128]{2,1,0:T(8,128)S(1)}, u32[]{:S(2)}, u32[]{:S(2)}) async-start(f32[8,8,128]{2,1,0:T(8,128)} %get-tuple-element.23), calls=%async_computation | async-start | bytes 65536 | tf_op jit(solution)/shard_map/all_to_all | solution.py:688
  9.8 0.9 %copy-done.1 = s32[16,16,128]{2,1,0:T(8,128)S(1)} copy-done((s32[16,16,128]{2,1,0:T(8,128)S(1)}, s32[16,16,128]{2,1,0:T(8,128)}, u32[]{:S(2)}) %copy-start.1) | copy-done | bytes 131096
  10.7 4.1 %moments.1 = (f32[3,256,128]{2,1,0:T(8,128)S(1)}, f32[19,4,16,128]{3,2,1,0:T(8,128)S(1)}, s32[4,16,128]{2,1,0:T(8,128)S(1)}, f32[20,16,128]{2,1,0:T(8,128)S(1)}) custom-call(f32[19,16,16,128]{3,2,1,0:T(8,128)} %refs_1_.3, s32[16,16,128]{2,1,0:T(8,128)S(1)} %copy-done.1), custom_call_target="tpu_custom_call" | custom-call | flops 3000000 | bytes 4000000 | tf_op jit(solution)/shard_map/moments/pallas_call | solution.py:280
  14.8 0.0 copy-start.3
  14.8 0.7 %copy-done.3 = f32[3,256,128]{2,1,0:T(8,128)} copy-done((f32[3,256,128]{2,1,0:T(8,128)}, f32[3,256,128]{2,1,0:T(8,128)S(1)}, u32[]{:S(2)}) %copy-start.3) | copy-done | bytes 393240
  15.5 1.0 %all-to-all-done.beads_ref = f32[8,8,128]{2,1,0:T(8,128)S(1)} async-done(((f32[8,8,128]{2,1,0:T(8,128)}), f32[8,8,128]{2,1,0:T(8,128)S(1)}, u32[]{:S(2)}, u32[]{:S(2)}) %all-to-all-start) | async-done | bytes 32800 | tf_op jit(solution)/shard_map/all_to_all | solution.py:688
  16.5 1.0 %copy-done.4 = f32[3,256,128]{2,1,0:T(8,128)S(1)} copy-done((f32[3,256,128]{2,1,0:T(8,128)S(1)}, f32[3,256,128]{2,1,0:T(8,128)}, u32[]{:S(2)}) %copy-start.4) | copy-done | bytes 393240
  17.5 1.6 %couple.1 = (f32[3,16,16,128]{3,2,1,0:T(8,128)S(1)}, f32[2,16,128]{2,1,0:T(8,128)S(1)}, f32[4,8,128]{2,1,0:T(8,128)S(1)}, f32[8,128]{1,0:T(8,128)S(1)}) custom-call(f32[8,8,128]{2,1,0:T(8,128)S(1)} %all-to-all-done.beads_ref, f32[3,256,128]{2,1,0:T(8,128)S(1)} %copy-done.4, f32[20,16,128]{2,1,0:T(8,128)S(1)} %get-tuple-element.25.column_ref), custom_call_target="tpu_custom_call" | custom-call | tf_op jit(solution)/shard_map/couple/pallas_call | solution.py:381
  19.1 0.0 collective-permute-start
  19.1 1.2 %collective-permute-done.face_ref.refs_3_.refs_4_ = f32[2,16,128]{2,1,0:T(8,128)S(1)} collective-permute-done((f32[2,16,128]{2,1,0:T(8,128)S(1)}, f32[2,16,128]{2,1,0:T(8,128)S(1)}, u32[]{:S(2)}, u32[]{:S(2)}) %collective-permute-start) | collective-permute-done | bytes 16416 | tf_op jit(solution)/shard_map/ppermute | solution.py:144
  20.3 0.4 %faces.1 = (f32[88,128]{1,0:T(8,128)S(1)}, f32[88,128]{1,0:T(8,128)S(1)}, f32[160,128]{1,0:T(8,128)S(1)}, f32[8,128]{1,0:T(8,128)S(1)}) custom-call(f32[3,16,16,128]{3,2,1,0:T(8,128)S(1)} %get-tuple-element.26.force_ref.refs_2_.refs_3_, f32[19,4,16,128]{3,2,1,0:T(8,128)S(1)} %get-tuple-element.27.edge_ref, ...), custom_call_target="tpu_custom_call" | custom-call | tf_op jit(solution)/shard_map/faces/pallas_call | solution.py:439
  20.6 1.1 %collective-permute-start.1 = (f32[88,128]{1,0:T(8,128)S(1)}, f32[88,128]{1,0:T(8,128)S(1)}, u32[]{:S(2)}, u32[]{:S(2)}) collective-permute-start(f32[88,128]{1,0:T(8,128)S(1)} %get-tuple-element.34), channel_id=1, source_target_pairs={{0,4},{1,5},{2,6},{3,7},{4,8},{5,9},{6,10},{7,11},{8,12},{9,13},{1... | collective-permute-start | bytes 135176 | tf_op jit(solution)/shard_map/ppermute | solution.py:144
  21.7 2.8 %collective-permute-start.2 = (f32[88,128]{1,0:T(8,128)S(1)}, f32[88,128]{1,0:T(8,128)S(1)}, u32[]{:S(2)}, u32[]{:S(2)}) collective-permute-start(f32[88,128]{1,0:T(8,128)S(1)} %get-tuple-element.35), channel_id=1, source_target_pairs={{0,12},{1,13},{2,14},{3,15},{4,0},{5,1},{6,2},{7,3},{8,4},{9,5},{1... | collective-permute-start | bytes 135176 | tf_op jit(solution)/shard_map/ppermute | solution.py:144
  24.5 0.2 collective-permute-start.3
  24.6 2.3 %stream.2 = (f32[19,16,16,128]{3,2,1,0:T(8,128)}, f32[10,8,8,128]{3,2,1,0:T(8,128)S(1)}, f32[8,128]{1,0:T(8,128)S(1)}) custom-call(f32[8,128]{1,0:T(8,128)S(1)} %get-tuple-element.31.before_ref, f32[19,16,16,128]{3,2,1,0:T(8,128)S(1)} %copy-done, s32[16,16,128]{2,1,0:T(8,128)S(1)} %copy-done.2, ...), custom_call_target="tpu_custom_call" | custom-call | flops 5000000 | bytes 3000000 | tf_op jit(solution)/shard_map/stream/pallas_call | solution.py:544
  27.0 2.0 %collective-permute-done.3.refs_1_.refs_2_ = f32[8,128]{1,0:T(8,128)S(1)} collective-permute-done((f32[8,128]{1,0:T(8,128)S(1)}, f32[8,128]{1,0:T(8,128)S(1)}, u32[]{:S(2)}, u32[]{:S(2)}) %collective-permute-start.3) | collective-permute-done | bytes 4128 | tf_op jit(solution)/shard_map/ppermute | solution.py:144
  29.0 0.0 collective-permute-done.1.up_ref
  29.0 0.0 collective-permute-done.2.down_ref
  29.0 1.1 %collective-permute-start.4 = (f32[192,128]{1,0:T(8,128)S(1)}, f32[192,128]{1,0:T(8,128)S(1)}, u32[]{:S(2)}, u32[]{:S(2)}) collective-permute-start(f32[192,128]{1,0:T(8,128)S(1)} %get-tuple-element.43), channel_id=1, source_target_pairs={{0,2},{1,3},{2,0},{3,1},{4,6},{5,7},{6,4},{7,5},{8,10},{9,11},{10,... | collective-permute-start | bytes 294920 | tf_op jit(solution)/shard_map/ppermute | solution.py:144
  30.1 3.0 %stream.3 = (f32[19,16,16,128]{3,2,1,0:T(8,128)}, f32[10,8,8,128]{3,2,1,0:T(8,128)S(1)}, f32[8,128]{1,0:T(8,128)}) custom-call(f32[8,128]{1,0:T(8,128)S(1)} %get-tuple-element.37.before_ref, f32[19,16,16,128]{3,2,1,0:T(8,128)} %get-tuple-element.38.refs_0_, f32[19,16,16,128]{3,2,1,0:T(8,128)S(1)} %copy-done, ...), custom_call_target="tpu_custom_call", output_to_operand_aliasing={{0}: (1, {})} | custom-call | flops 5000000 | bytes 3000000 | tf_op jit(solution)/shard_map/stream/pallas_call | solution.py:544
  33.1 0.6 %collective-permute-done.4.refs_0_ = f32[192,128]{1,0:T(8,128)S(1)} collective-permute-done((f32[192,128]{1,0:T(8,128)S(1)}, f32[192,128]{1,0:T(8,128)S(1)}, u32[]{:S(2)}, u32[]{:S(2)}) %collective-permute-start.4) | collective-permute-done | bytes 98336 | tf_op jit(solution)/shard_map/ppermute | solution.py:144
  33.7 1.6 %finish.1 = (f32[19,16,16,128]{3,2,1,0:T(8,128)}, f32[3,128]{1,0:T(4,128)}) custom-call(f32[19,16,16,128]{3,2,1,0:T(8,128)} %get-tuple-element.39.whole_ref, s32[1,128]{1,0:T(1,128)S(1)} %copy-done.5, f32[10,8,8,128]{3,2,1,0:T(8,128)S(1)} %get-tuple-element.41.lower_ref, ...), custom_call_target="tpu_custom_call", output_to_operand_aliasing={{0}: (0, {})} | custom-call | tf_op jit(solution)/shard_map/finish/pallas_call | solution.py:659
  (8 shorter events, 0.0 us)
Async XLA Ops:
  0.6 24.0 %copy-start = (f32[19,16,16,128]{3,2,1,0:T(8,128)S(1)}, f32[19,16,16,128]{3,2,1,0:T(8,128)}, u32[]{:S(2)}) copy-start(f32[19,16,16,128]{3,2,1,0:T(8,128)} %refs_1_.3) | copy-start | bytes 7471108
  2.5 13.9 %all-to-all-start = ((f32[8,8,128]{2,1,0:T(8,128)}), f32[8,8,128]{2,1,0:T(8,128)S(1)}, u32[]{:S(2)}, u32[]{:S(2)}) async-start(f32[8,8,128]{2,1,0:T(8,128)} %get-tuple-element.23), calls=%async_computation | async-start | bytes 65536 | tf_op jit(solution)/shard_map/all_to_all | solution.py:688
  9.8 0.9 %copy-start.1 = (s32[16,16,128]{2,1,0:T(8,128)S(1)}, s32[16,16,128]{2,1,0:T(8,128)}, u32[]{:S(2)}) copy-start(s32[16,16,128]{2,1,0:T(8,128)} %refs_2_.1) | copy-start | bytes 393220
  10.7 13.9 %copy-start.2 = (s32[16,16,128]{2,1,0:T(8,128)S(1)}, s32[16,16,128]{2,1,0:T(8,128)}, u32[]{:S(2)}) copy-start(s32[16,16,128]{2,1,0:T(8,128)} %refs_2_.1) | copy-start | bytes 393220
  14.8 0.7 %copy-start.3 = (f32[3,256,128]{2,1,0:T(8,128)}, f32[3,256,128]{2,1,0:T(8,128)S(1)}, u32[]{:S(2)}) copy-start(f32[3,256,128]{2,1,0:T(8,128)S(1)} %get-tuple-element.24.flow_ref) | copy-start | bytes 1179652
  16.5 1.0 %copy-start.4 = (f32[3,256,128]{2,1,0:T(8,128)S(1)}, f32[3,256,128]{2,1,0:T(8,128)}, u32[]{:S(2)}) copy-start(f32[3,256,128]{2,1,0:T(8,128)} %copy-done.3) | copy-start | bytes 1179652
  19.1 1.2 %collective-permute-start = (f32[2,16,128]{2,1,0:T(8,128)S(1)}, f32[2,16,128]{2,1,0:T(8,128)S(1)}, u32[]{:S(2)}, u32[]{:S(2)}) collective-permute-start(f32[2,16,128]{2,1,0:T(8,128)S(1)} %get-tuple-element.29), channel_id=1, source_target_pairs={{0,1},{1,0},{2,3},{3,2},{4,5},{5,4},{6,7},{7,6},{8,9},{9,8},{10,11... | collective-permute-start | bytes 49160 | tf_op jit(solution)/shard_map/ppermute | solution.py:144
  20.6 8.3 %collective-permute-start.1 = (f32[88,128]{1,0:T(8,128)S(1)}, f32[88,128]{1,0:T(8,128)S(1)}, u32[]{:S(2)}, u32[]{:S(2)}) collective-permute-start(f32[88,128]{1,0:T(8,128)S(1)} %get-tuple-element.34), channel_id=1, source_target_pairs={{0,4},{1,5},{2,6},{3,7},{4,8},{5,9},{6,10},{7,11},{8,12},{9,13},{1... | collective-permute-start | bytes 135176 | tf_op jit(solution)/shard_map/ppermute | solution.py:144
  21.7 7.3 %collective-permute-start.2 = (f32[88,128]{1,0:T(8,128)S(1)}, f32[88,128]{1,0:T(8,128)S(1)}, u32[]{:S(2)}, u32[]{:S(2)}) collective-permute-start(f32[88,128]{1,0:T(8,128)S(1)} %get-tuple-element.35), channel_id=1, source_target_pairs={{0,12},{1,13},{2,14},{3,15},{4,0},{5,1},{6,2},{7,3},{8,4},{9,5},{1... | collective-permute-start | bytes 135176 | tf_op jit(solution)/shard_map/ppermute | solution.py:144
  24.5 4.5 %collective-permute-start.3 = (f32[8,128]{1,0:T(8,128)S(1)}, f32[8,128]{1,0:T(8,128)S(1)}, u32[]{:S(2)}, u32[]{:S(2)}) collective-permute-start(f32[8,128]{1,0:T(8,128)S(1)} %get-tuple-element.36), channel_id=1, source_target_pairs={{0,8},{1,9},{2,10},{3,11},{4,12},{5,13},{6,14},{7,15},{8,0},{9,1},... | collective-permute-start | bytes 12296 | tf_op jit(solution)/shard_map/ppermute | solution.py:144
  29.0 4.7 %collective-permute-start.4 = (f32[192,128]{1,0:T(8,128)S(1)}, f32[192,128]{1,0:T(8,128)S(1)}, u32[]{:S(2)}, u32[]{:S(2)}) collective-permute-start(f32[192,128]{1,0:T(8,128)S(1)} %get-tuple-element.43), channel_id=1, source_target_pairs={{0,2},{1,3},{2,0},{3,1},{4,6},{5,7},{6,4},{7,5},{8,10},{9,11},{10,... | collective-permute-start | bytes 294920 | tf_op jit(solution)/shard_map/ppermute | solution.py:144
  30.1 3.6 %copy-start.5 = (s32[1,128]{1,0:T(1,128)S(1)}, s32[1,128]{1,0:T(1,128)}, u32[]{:S(2)}) copy-start(s32[1,128]{1,0:T(1,128)} %get-tuple-element.40.target_ref) | copy-start | bytes 1540

commit v6 on v5

--- a/solution.py
+++ b/solution.py
@@ -231,7 +231,7 @@
 
 
 def moments_kernel(
-    pops_ref, solid_ref, flow_ref, edge_ref, edge_solid_ref, column_ref, held, held_solid, sem
+    pops_ref, solid_ref, flow_ref, column_ref, held, held_solid, sem
 ):
     depth, rows, width = pops_ref.shape[1:]
     chunks = 4
@@ -255,22 +255,10 @@
 
     for k in range(chunks):
         copies[1 + k].wait()
-        lax.fori_loop(k * span, (k + 1) * span, plane, 0)
+        lax.fori_loop(k * span, (k + 1) * span, plane, 0, unroll=2)
     copies[0].wait()
-    edge_solid_ref[0] = held_solid[0]
-    edge_solid_ref[1] = held_solid[depth - 1]
-    edge_solid_ref[2] = held_solid[:, 0, :]
-    edge_solid_ref[3] = held_solid[:, rows - 1, :]
-
-    def population(i, carry):
-        edge_ref[i, 0] = held[i, 0]
-        edge_ref[i, 1] = held[i, depth - 1]
-        edge_ref[i, 2] = held[i, :, 0, :]
-        edge_ref[i, 3] = held[i, :, rows - 1, :]
+    for i in range(19):
         column_ref[i] = x_ends([held[i, z] for z in range(depth)])
-        return carry
-
-    lax.fori_loop(0, 19, population, 0)
     column_ref[19] = x_ends([held_solid[z].astype(F32) for z in range(depth)])
 
 
@@ -281,8 +269,6 @@
         moments_kernel,
         out_shape=[
             jax.ShapeDtypeStruct((3, depth * rows, width), F32),
-            jax.ShapeDtypeStruct((19, 4, rows, width), F32),
-            jax.ShapeDtypeStruct((4, rows, width), jnp.int32),
             jax.ShapeDtypeStruct((20, rows, 128), F32),
         ],
         in_specs=[hbm, hbm],
@@ -391,7 +377,7 @@
 
 
 def faces_kernel(
-    force_ref, edge_ref, edge_solid_ref, face_ref, drag_ref, up_ref, down_ref, draft_ref, token_ref, turned
+    force_ref, pops_ref, solid_ref, face_ref, drag_ref, up_ref, down_ref, draft_ref, token_ref, turned
 ):
     depth, rows, width = force_ref.shape[1:]
     token_ref[...] = jnp.zeros_like(token_ref)
@@ -404,9 +390,9 @@
             at = (0 if first else depth - 1, slice(None))
         else:
             at = (slice(None), 0 if first else rows - 1)
-        pops = [edge_ref[i, side] for i in range(19)]
+        pops = [pops_ref[(i,) + at] for i in range(19)]
         force = [force_ref[(d,) + at] for d in range(3)]
-        out = collide(pops, edge_solid_ref[side] == 1, force)
+        out = collide(pops, solid_ref[at] == 1, force)
         axis = 2 if side < 2 else 1
         group = 1 if first else 0
         for k, i in enumerate(ENTER[axis][group]):
@@ -433,7 +419,7 @@
 ROOM = 16 << 20
 
 
-def faces(single, force, edge, edge_solid, face, drag):
+def faces(single, force, pops, solid, face, drag):
     _, depth, rows, width = force.shape
     message = jax.ShapeDtypeStruct((5 * rows + (8 if single else 0), width), F32)
     return pl.pallas_call(
@@ -442,7 +428,7 @@
         scratch_shapes=[pltpu.VMEM((2, 128, rows), F32)],
         compiler_params=pltpu.CompilerParams(vmem_limit_bytes=ROOM),
         name="faces",
-    )(force, edge, edge_solid, face, drag)
+    )(force, pops, solid, face, drag)
 
 
 def rows_kernel(depth, rows, before_ref, draft_ref, up_ref, down_ref, *refs):
@@ -517,7 +503,7 @@
         carry = tuple(pltpu.roll(f, 128 - 2 * low, 1) for f in carry)
     for k in range(chunks):
         first = low + k * span
-        carry = lax.fori_loop(first, first + span, plane, carry)
+        carry = lax.fori_loop(first, first + span, plane, carry, unroll=2)
         for n, (a, b) in enumerate(runs):
             step = int(STEP[a, 2])
             start, stop = max(first + step, 0), min(first + span + step, depth)
@@ -686,14 +672,14 @@
 
     target, beads = pack(owners, bead_owner, bead_base, bead_offset, bead_velocity)
     beads = swap(beads)
-    flow, edge, edge_solid, columns = moments(populations, solid_mask)
+    flow, columns = moments(populations, solid_mask)
     force, face, drag, *far = couple(shape, beads, flow, columns, depth, rows)
     face = send(face, shape, (0, 0, 1))
     if single:
         far = send(far[0], shape, (2, 0, 0))
     else:
         drag = swap(drag)
-    up, down, draft, token = faces(single, force, edge, edge_solid, face, drag)
+    up, down, draft, token = faces(single, force, populations, solid_mask, face, drag)
     up = send(up, shape, (1, 0, 0))
     down = send(down, shape, (-1, 0, 0))
     fields = (populations, solid_mask, force, face)

time: 35.6 us -> 35.2 us (0.989)
  waiting for transfers between devices: 4.76 us -> 7.91 us
  local copies, waits for them, and re-layouts: 2.65 us -> 0.91 us
  Pallas kernels: 14.8 us -> 13.8 us
  starting transfers between devices: 12.4 us -> 11.6 us
    all_to_all x1, waiting for transfers between devices: 0.96 us -> 3.12 us  [shards(): beads = swap(beads)]
    unnamed x12 -> x8, local copies, waits for them, and re-layouts: 2.65 us -> 0.91 us
    pallas_call x1, Pallas kernels: 4.06 us -> 2.65 us  [moments(): pl.pallas_call(moments_kernel, out_shape=[jax.ShapeDtypeStruct((3, depth...]
    ppermute x5, waiting for transfers between devices: 3.79 us -> 4.78 us  [send(): return lax.ppermute(value, ('slab', 'col', 'pair'), perm)]
    ppermute x5, starting transfers between devices: 5.13 us -> 4.39 us  [send(): return lax.ppermute(value, ('slab', 'col', 'pair'), perm)]
    pallas_call x1, Pallas kernels: 0.38 us -> 1.04 us  [faces(): pl.pallas_call(faces_kernel, out_shape=[message, message, jax.ShapeDtypeS...]
  transfers between devices with their start and end apart: 6 -> 6, of which waited for: 4 -> 4; matrix products, arithmetic and copies ran while one was open for 0% -> 0% of each run, Pallas kernels for 26% -> 22%
where the time goes in v6:
time: 35.2 us; the launch traced here: 35 us
  Pallas kernels  13.8 us (39%)
  starting transfers between devices  11.6 us (33%)
  waiting for transfers between devices  7.91 us (22%)
  local copies, waits for them, and re-layouts  0.91 us (3%)
  between operations  0.69 us (2%)
    all_to_all x1, starting transfers between devices, shards(): beads = swap(beads)  7.25 us
    pallas_call x2, Pallas kernels, stream(): pl.pallas_call(functools.partial(stream_kernel, low, high), out_shape=[ja...  5.02 us
    ppermute x5, waiting for transfers between devices, send(): return lax.ppermute(value, ('slab', 'col', 'pair'), perm)  4.78 us
    ppermute x5, starting transfers between devices, send(): return lax.ppermute(value, ('slab', 'col', 'pair'), perm)  4.39 us
    all_to_all x1, waiting for transfers between devices, shards(): beads = swap(beads)  3.12 us
    pallas_call x1, Pallas kernels, moments(): pl.pallas_call(moments_kernel, out_shape=[jax.ShapeDtypeStruct((3, depth...  2.65 us
    pallas_call x1, Pallas kernels, pack(): pl.pallas_call(pack_kernel, out_shape=[jax.ShapeDtypeStruct((1, count), j...  1.89 us
    pallas_call x1, Pallas kernels, finish(): pl.pallas_call(functools.partial(finish_kernel, shape, len(entered)), out...  1.61 us
  transfers between devices with their start and end apart: 6, of which 4 were waited for; matrix products, arithmetic and copies ran while one was open for 0% of the time, Pallas kernels for 22%

profile of v6, /device:TPU:0, one launch (start us, length us, event | category | flops | bytes accessed | tf_op | source)
XLA Modules:
  0.0 35.0 jit_solution(5476296381438611442)
XLA Ops:
  0.6 0.0 copy-start
  0.6 1.9 %pack.1 = (s32[1,128]{1,0:T(1,128)}, f32[8,8,128]{2,1,0:T(8,128)}) custom-call(s32[1,128]{1,0:T(1,128)} %bitcast.1, s32[3,128]{1,0:T(4,128)} %base_ref.1, f32[3,128]{1,0:T(4,128)} %offset_ref.1, f32[3,128]{1,0:T(4,128)} %velocity_ref.1), custom_call_target="tpu_custom_call" | custom-call | tf_op jit(solution)/shard_map/pack/pallas_call | solution.py:213
  2.5 7.3 %all-to-all-start = ((f32[8,8,128]{2,1,0:T(8,128)}), f32[8,8,128]{2,1,0:T(8,128)S(1)}, u32[]{:S(2)}, u32[]{:S(2)}) async-start(f32[8,8,128]{2,1,0:T(8,128)} %get-tuple-element.21), calls=%async_computation | async-start | bytes 65536 | tf_op jit(solution)/shard_map/all_to_all | solution.py:674
  9.8 0.9 %copy-done.1 = s32[16,16,128]{2,1,0:T(8,128)S(1)} copy-done((s32[16,16,128]{2,1,0:T(8,128)S(1)}, s32[16,16,128]{2,1,0:T(8,128)}, u32[]{:S(2)}) %copy-start.1) | copy-done | bytes 131096
  10.7 2.6 %moments.1 = (f32[3,256,128]{2,1,0:T(8,128)S(1)}, f32[20,16,128]{2,1,0:T(8,128)S(1)}) custom-call(f32[19,16,16,128]{3,2,1,0:T(8,128)} %refs_1_.3, s32[16,16,128]{2,1,0:T(8,128)S(1)} %copy-done.1), custom_call_target="tpu_custom_call" | custom-call | flops 3000000 | bytes 4000000 | tf_op jit(solution)/shard_map/moments/pallas_call | solution.py:268
  13.4 3.1 %all-to-all-done.beads_ref = f32[8,8,128]{2,1,0:T(8,128)S(1)} async-done(((f32[8,8,128]{2,1,0:T(8,128)}), f32[8,8,128]{2,1,0:T(8,128)S(1)}, u32[]{:S(2)}, u32[]{:S(2)}) %all-to-all-start) | async-done | bytes 32800 | tf_op jit(solution)/shard_map/all_to_all | solution.py:674
  16.5 1.6 %couple.1 = (f32[3,16,16,128]{3,2,1,0:T(8,128)S(1)}, f32[2,16,128]{2,1,0:T(8,128)S(1)}, f32[4,8,128]{2,1,0:T(8,128)S(1)}, f32[8,128]{1,0:T(8,128)S(1)}) custom-call(f32[8,8,128]{2,1,0:T(8,128)S(1)} %all-to-all-done.beads_ref, f32[3,256,128]{2,1,0:T(8,128)S(1)} %get-tuple-element.22.flow_ref, f32[20,16,128]{2,1,0:T(8,128)S(1)} %get-tuple-element.23.column_ref), custom_call_target="tpu_custom_call" | custom-call | tf_op jit(solution)/shard_map/couple/pallas_call | solution.py:367
  18.1 0.0 collective-permute-start
  18.1 1.2 %collective-permute-done.face_ref.refs_3_.refs_4_ = f32[2,16,128]{2,1,0:T(8,128)S(1)} collective-permute-done((f32[2,16,128]{2,1,0:T(8,128)S(1)}, f32[2,16,128]{2,1,0:T(8,128)S(1)}, u32[]{:S(2)}, u32[]{:S(2)}) %collective-permute-start) | collective-permute-done | bytes 16416 | tf_op jit(solution)/shard_map/ppermute | solution.py:144
  19.3 0.0 copy-done
  19.3 0.0 copy-done.2
  19.3 1.0 %faces.1 = (f32[88,128]{1,0:T(8,128)S(1)}, f32[88,128]{1,0:T(8,128)S(1)}, f32[160,128]{1,0:T(8,128)S(1)}, f32[8,128]{1,0:T(8,128)S(1)}) custom-call(f32[3,16,16,128]{3,2,1,0:T(8,128)S(1)} %get-tuple-element.24.force_ref.refs_2_.refs_3_, f32[19,16,16,128]{3,2,1,0:T(8,128)S(1)} %copy-done, s32[16,16,128]{2,1,0:T(8,128)S(1)} %copy-done.2, ...), custom_call_target="tpu_custom_call" | custom-call | tf_op jit(solution)/shard_map/faces/pallas_call | solution.py:425
  20.3 0.4 %collective-permute-start.1 = (f32[88,128]{1,0:T(8,128)S(1)}, f32[88,128]{1,0:T(8,128)S(1)}, u32[]{:S(2)}, u32[]{:S(2)}) collective-permute-start(f32[88,128]{1,0:T(8,128)S(1)} %get-tuple-element.30), channel_id=1, source_target_pairs={{0,4},{1,5},{2,6},{3,7},{4,8},{5,9},{6,10},{7,11},{8,12},{9,13},{1... | collective-permute-start | bytes 135176 | tf_op jit(solution)/shard_map/ppermute | solution.py:144
  20.7 3.4 %collective-permute-start.2 = (f32[88,128]{1,0:T(8,128)S(1)}, f32[88,128]{1,0:T(8,128)S(1)}, u32[]{:S(2)}, u32[]{:S(2)}) collective-permute-start(f32[88,128]{1,0:T(8,128)S(1)} %get-tuple-element.31), channel_id=1, source_target_pairs={{0,12},{1,13},{2,14},{3,15},{4,0},{5,1},{6,2},{7,3},{8,4},{9,5},{1... | collective-permute-start | bytes 135176 | tf_op jit(solution)/shard_map/ppermute | solution.py:144
  24.1 0.0 collective-permute-start.3
  24.1 2.2 %stream.2 = (f32[19,16,16,128]{3,2,1,0:T(8,128)}, f32[10,8,8,128]{3,2,1,0:T(8,128)S(1)}, f32[8,128]{1,0:T(8,128)S(1)}) custom-call(f32[8,128]{1,0:T(8,128)S(1)} %get-tuple-element.27.before_ref, f32[19,16,16,128]{3,2,1,0:T(8,128)S(1)} %copy-done, s32[16,16,128]{2,1,0:T(8,128)S(1)} %copy-done.2, ...), custom_call_target="tpu_custom_call" | custom-call | flops 5000000 | bytes 3000000 | tf_op jit(solution)/shard_map/stream/pallas_call | solution.py:530
  26.3 2.3 %collective-permute-done.3.refs_1_.refs_2_ = f32[8,128]{1,0:T(8,128)S(1)} collective-permute-done((f32[8,128]{1,0:T(8,128)S(1)}, f32[8,128]{1,0:T(8,128)S(1)}, u32[]{:S(2)}, u32[]{:S(2)}) %collective-permute-start.3) | collective-permute-done | bytes 4128 | tf_op jit(solution)/shard_map/ppermute | solution.py:144
  28.6 0.0 collective-permute-done.1.up_ref
  28.7 0.0 collective-permute-done.2.down_ref
  28.7 0.5 %collective-permute-start.4 = (f32[192,128]{1,0:T(8,128)S(1)}, f32[192,128]{1,0:T(8,128)S(1)}, u32[]{:S(2)}, u32[]{:S(2)}) collective-permute-start(f32[192,128]{1,0:T(8,128)S(1)} %get-tuple-element.39), channel_id=1, source_target_pairs={{0,2},{1,3},{2,0},{3,1},{4,6},{5,7},{6,4},{7,5},{8,10},{9,11},{10,... | collective-permute-start | bytes 294920 | tf_op jit(solution)/shard_map/ppermute | solution.py:144
  29.2 2.8 %stream.3 = (f32[19,16,16,128]{3,2,1,0:T(8,128)}, f32[10,8,8,128]{3,2,1,0:T(8,128)S(1)}, f32[8,128]{1,0:T(8,128)}) custom-call(f32[8,128]{1,0:T(8,128)S(1)} %get-tuple-element.33.before_ref, f32[19,16,16,128]{3,2,1,0:T(8,128)} %get-tuple-element.34.refs_0_, f32[19,16,16,128]{3,2,1,0:T(8,128)S(1)} %copy-done, ...), custom_call_target="tpu_custom_call", output_to_operand_aliasing={{0}: (1, {})} | custom-call | flops 5000000 | bytes 3000000 | tf_op jit(solution)/shard_map/stream/pallas_call | solution.py:530
  32.1 1.3 %collective-permute-done.4.refs_0_ = f32[192,128]{1,0:T(8,128)S(1)} collective-permute-done((f32[192,128]{1,0:T(8,128)S(1)}, f32[192,128]{1,0:T(8,128)S(1)}, u32[]{:S(2)}, u32[]{:S(2)}) %collective-permute-start.4) | collective-permute-done | bytes 98336 | tf_op jit(solution)/shard_map/ppermute | solution.py:144
  33.4 0.0 copy-done.3
  33.4 1.6 %finish.1 = (f32[19,16,16,128]{3,2,1,0:T(8,128)}, f32[3,128]{1,0:T(4,128)}) custom-call(f32[19,16,16,128]{3,2,1,0:T(8,128)} %get-tuple-element.35.whole_ref, s32[1,128]{1,0:T(1,128)S(1)} %copy-done.3, f32[10,8,8,128]{3,2,1,0:T(8,128)S(1)} %get-tuple-element.37.lower_ref, ...), custom_call_target="tpu_custom_call", output_to_operand_aliasing={{0}: (0, {})} | custom-call | tf_op jit(solution)/shard_map/finish/pallas_call | solution.py:645
  (4 shorter events, 0.0 us)
Async XLA Ops:
  0.6 18.6 %copy-start = (f32[19,16,16,128]{3,2,1,0:T(8,128)S(1)}, f32[19,16,16,128]{3,2,1,0:T(8,128)}, u32[]{:S(2)}) copy-start(f32[19,16,16,128]{3,2,1,0:T(8,128)} %refs_1_.3) | copy-start | bytes 7471108
  2.5 13.9 %all-to-all-start = ((f32[8,8,128]{2,1,0:T(8,128)}), f32[8,8,128]{2,1,0:T(8,128)S(1)}, u32[]{:S(2)}, u32[]{:S(2)}) async-start(f32[8,8,128]{2,1,0:T(8,128)} %get-tuple-element.21), calls=%async_computation | async-start | bytes 65536 | tf_op jit(solution)/shard_map/all_to_all | solution.py:674
  9.8 0.9 %copy-start.1 = (s32[16,16,128]{2,1,0:T(8,128)S(1)}, s32[16,16,128]{2,1,0:T(8,128)}, u32[]{:S(2)}) copy-start(s32[16,16,128]{2,1,0:T(8,128)} %refs_2_.1) | copy-start | bytes 393220
  10.7 8.6 %copy-start.2 = (s32[16,16,128]{2,1,0:T(8,128)S(1)}, s32[16,16,128]{2,1,0:T(8,128)}, u32[]{:S(2)}) copy-start(s32[16,16,128]{2,1,0:T(8,128)} %refs_2_.1) | copy-start | bytes 393220
  18.1 1.2 %collective-permute-start = (f32[2,16,128]{2,1,0:T(8,128)S(1)}, f32[2,16,128]{2,1,0:T(8,128)S(1)}, u32[]{:S(2)}, u32[]{:S(2)}) collective-permute-start(f32[2,16,128]{2,1,0:T(8,128)S(1)} %get-tuple-element.25), channel_id=1, source_target_pairs={{0,1},{1,0},{2,3},{3,2},{4,5},{5,4},{6,7},{7,6},{8,9},{9,8},{10,11... | collective-permute-start | bytes 49160 | tf_op jit(solution)/shard_map/ppermute | solution.py:144
  20.3 8.3 %collective-permute-start.1 = (f32[88,128]{1,0:T(8,128)S(1)}, f32[88,128]{1,0:T(8,128)S(1)}, u32[]{:S(2)}, u32[]{:S(2)}) collective-permute-start(f32[88,128]{1,0:T(8,128)S(1)} %get-tuple-element.30), channel_id=1, source_target_pairs={{0,4},{1,5},{2,6},{3,7},{4,8},{5,9},{6,10},{7,11},{8,12},{9,13},{1... | collective-permute-start | bytes 135176 | tf_op jit(solution)/shard_map/ppermute | solution.py:144
  20.7 7.9 %collective-permute-start.2 = (f32[88,128]{1,0:T(8,128)S(1)}, f32[88,128]{1,0:T(8,128)S(1)}, u32[]{:S(2)}, u32[]{:S(2)}) collective-permute-start(f32[88,128]{1,0:T(8,128)S(1)} %get-tuple-element.31), channel_id=1, source_target_pairs={{0,12},{1,13},{2,14},{3,15},{4,0},{5,1},{6,2},{7,3},{8,4},{9,5},{1... | collective-permute-start | bytes 135176 | tf_op jit(solution)/shard_map/ppermute | solution.py:144
  24.1 4.5 %collective-permute-start.3 = (f32[8,128]{1,0:T(8,128)S(1)}, f32[8,128]{1,0:T(8,128)S(1)}, u32[]{:S(2)}, u32[]{:S(2)}) collective-permute-start(f32[8,128]{1,0:T(8,128)S(1)} %get-tuple-element.32), channel_id=1, source_target_pairs={{0,8},{1,9},{2,10},{3,11},{4,12},{5,13},{6,14},{7,15},{8,0},{9,1},... | collective-permute-start | bytes 12296 | tf_op jit(solution)/shard_map/ppermute | solution.py:144
  28.7 4.7 %collective-permute-start.4 = (f32[192,128]{1,0:T(8,128)S(1)}, f32[192,128]{1,0:T(8,128)S(1)}, u32[]{:S(2)}, u32[]{:S(2)}) collective-permute-start(f32[192,128]{1,0:T(8,128)S(1)} %get-tuple-element.39), channel_id=1, source_target_pairs={{0,2},{1,3},{2,0},{3,1},{4,6},{5,7},{6,4},{7,5},{8,10},{9,11},{10,... | collective-permute-start | bytes 294920 | tf_op jit(solution)/shard_map/ppermute | solution.py:144
  29.2 4.1 %copy-start.3 = (s32[1,128]{1,0:T(1,128)S(1)}, s32[1,128]{1,0:T(1,128)}, u32[]{:S(2)}) copy-start(s32[1,128]{1,0:T(1,128)} %get-tuple-element.36.target_ref) | copy-start | bytes 1540

commit v7 on v6

--- a/solution.py
+++ b/solution.py
@@ -45,6 +45,8 @@
 BF16 = jnp.bfloat16
 
 ENTER = [[[i for i in range(19) if STEP[i, a] == sign] for sign in (1, -1)] for a in range(3)]
+TOKEN = jax.ShapeDtypeStruct((8, 128), F32)
+ROOM = 16 << 20
 NT = (((1,), (1,)), ((), ()))
 NN = (((1,), (0,)), ((), ()))
 
@@ -132,15 +134,18 @@
 
 
 def send(value, shape, offset):
-    slabs, cols, pairs = shape
-    perm = []
-    for s in range(slabs):
-        for c in range(cols):
-            for p in range(pairs):
-                there = (
-                    ((s + offset[0]) % slabs) * cols + (c + offset[1]) % cols
-                ) * pairs + (p + offset[2]) % pairs
-                perm.append(((s * cols + c) * pairs + p, there))
+    return permute(value, shape, lambda at: [(a + b) % n for a, b, n in zip(at, offset, shape)])
+
+
+def exchange(value, shape, bits):
+    return permute(value, shape, lambda at: [a ^ b for a, b in zip(at, bits)])
+
+
+def permute(value, shape, target):
+    def flat(at):
+        return (at[0] * shape[1] + at[1]) * shape[2] + at[2]
+
+    perm = [(flat(at), flat(target(at))) for at in np.ndindex(*shape)]
     return lax.ppermute(value, ("slab", "col", "pair"), perm)
 
 
@@ -230,57 +235,137 @@
     )(*args)
 
 
-def moments_kernel(
-    pops_ref, solid_ref, flow_ref, column_ref, held, held_solid, sem
-):
-    depth, rows, width = pops_ref.shape[1:]
-    chunks = 4
-    span = depth // chunks
-    copies = [pltpu.make_async_copy(solid_ref, held_solid, sem.at[chunks])]
-    for k in range(chunks):
-        part = pl.ds(k * span, span)
-        copies.append(
-            pltpu.make_async_copy(pops_ref.at[:, part], held.at[:, part], sem.at[k])
-        )
-    for copy in copies:
-        copy.start()
+def publish_kernel(owner_ref, base_ref, offset_ref, velocity_ref, out_ref):
+    out_ref[0:1] = owner_ref[...].astype(F32)
+    out_ref[1:4] = base_ref[...].astype(F32) + 1.0
+    out_ref[4:7] = offset_ref[...]
+    out_ref[7:10] = velocity_ref[...]
+    out_ref[10:16] = jnp.zeros((6, out_ref.shape[1]), F32)
+
+
+def publish(owner, base, offset, velocity):
+    count = owner.shape[0]
+    return pl.pallas_call(
+        publish_kernel, out_shape=jax.ShapeDtypeStruct((16, count), F32), name="publish"
+    )(owner.reshape(1, count), base, offset, velocity)
+
+
+def join_kernel(before_ref, *refs):
+    refs, out_ref, token_ref = refs[:-2], refs[-2], refs[-1]
+    row = 0
+    for ref in refs:
+        out_ref[row : row + ref.shape[0]] = ref[...]
+        row += ref.shape[0]
+    token_ref[...] = jnp.zeros_like(token_ref)
+
+
+def join(before, *parts):
+    rows = sum(p.shape[0] for p in parts)
+    return pl.pallas_call(
+        join_kernel,
+        out_shape=[jax.ShapeDtypeStruct((rows, parts[0].shape[1]), F32), TOKEN],
+        in_specs=[pl.BlockSpec(memory_space=pl.ANY)]
+        + [pl.BlockSpec(memory_space=pltpu.VMEM)] * len(parts),
+        compiler_params=pltpu.CompilerParams(vmem_limit_bytes=ROOM),
+        name="join",
+    )(before, *parts)
+
+
+def own_slots(blocks, me):
+    owner = jnp.concatenate([block[0:1] for block in blocks], axis=0)
+    member = (owner == me.astype(F32)).astype(F32)
+    place = jnp.where(member > 0.0, rank_among(member), -1.0).astype(jnp.int32)
+    slots = []
+    for k, block in enumerate(blocks):
+        choose = (iota((CAP, owner.shape[1]), 0) == place[k : k + 1]).astype(F32).astype(BF16)
+        slots.append(dot_select(block, choose, NT))
+    return jnp.concatenate(slots, axis=1)
+
+
+def flow_kernel(low, high, before_ref, pops_ref, flow_ref, token_ref, *own):
+    rows = pops_ref.shape[2]
+    copies = []
+    if own:
+        held, sem = own
+        span = (high - low) // sem.shape[0]
+        for k in range(sem.shape[0]):
+            part = pl.ds(low + k * span, span)
+            copies.append(
+                pltpu.make_async_copy(
+                    pops_ref.at[:, part], held.at[:, pl.ds(k * span, span)], sem.at[k]
+                )
+            )
+            copies[-1].start()
+    else:
+        held, span = pops_ref, high - low
 
     def plane(z, carry):
-        pops = [held[i, z] for i in range(19)]
-        density, momentum = density_momentum(pops)
+        density, momentum = density_momentum([held[i, z] for i in range(19)])
         inverse = 1.0 / density
+        first = 0 if own else low
+        at = pl.ds(pl.multiple_of((z - first) * rows, rows), rows)
         for axis in range(3):
-            flow_ref[axis, pl.ds(pl.multiple_of(z * rows, rows), rows)] = momentum[axis] * inverse
+            flow_ref[axis, at] = momentum[axis] * inverse
         return carry
 
-    for k in range(chunks):
-        copies[1 + k].wait()
-        lax.fori_loop(k * span, (k + 1) * span, plane, 0, unroll=2)
-    copies[0].wait()
+    if own:
+        for k, copy in enumerate(copies):
+            copy.wait()
+            lax.fori_loop(k * span, (k + 1) * span, plane, 0, unroll=2)
+    else:
+        lax.fori_loop(low, high, plane, 0, unroll=2)
+    token_ref[...] = jnp.zeros_like(token_ref)
+
+
+def flow_of(low, high, before, pops, own):
+    _, _, rows, width = pops.shape
+    kind = pltpu.HBM if own else pltpu.VMEM
+    scratch = [
+        pltpu.VMEM((19, high - low, rows, width), F32),
+        pltpu.SemaphoreType.DMA((2,)),
+    ]
+    return pl.pallas_call(
+        functools.partial(flow_kernel, low, high),
+        out_shape=[jax.ShapeDtypeStruct((3, (high - low) * rows, width), F32), TOKEN],
+        in_specs=[pl.BlockSpec(memory_space=pl.ANY), pl.BlockSpec(memory_space=kind)],
+        scratch_shapes=scratch if own else [],
+        compiler_params=pltpu.CompilerParams(vmem_limit_bytes=54000000 if own else ROOM),
+        cost_estimate=pl.CostEstimate(flops=1000000, bytes_accessed=1500000, transcendentals=0),
+        name="flow",
+    )(before, pops)
+
+
+def edges_kernel(before_ref, pops_ref, solid_ref, owner_ref, column_ref, side_ref, wall_ref, target_ref):
+    depth, rows = pops_ref.shape[1:3]
     for i in range(19):
-        column_ref[i] = x_ends([held[i, z] for z in range(depth)])
-    column_ref[19] = x_ends([held_solid[z].astype(F32) for z in range(depth)])
-
-
-def moments(pops, solid):
+        column_ref[i] = x_ends([pops_ref[i, z] for z in range(depth)])
+        side_ref[i, 0] = pops_ref[i, :, 0, :]
+        side_ref[i, 1] = pops_ref[i, :, rows - 1, :]
+    column_ref[19] = x_ends([solid_ref[z].astype(F32) for z in range(depth)])
+    wall_ref[0] = solid_ref[:, 0, :]
+    wall_ref[1] = solid_ref[:, rows - 1, :]
+    owner = owner_ref[...]
+    member = (iota((GROUP, owner.shape[1]), 0) == owner).astype(F32)
+    rank = jnp.sum(member * rank_among(member), axis=0, keepdims=True)
+    target_ref[...] = owner * CAP + rank.astype(jnp.int32)
+
+
+def edges(before, pops, solid, owner):
     _, depth, rows, width = pops.shape
-    hbm = pl.BlockSpec(memory_space=pltpu.HBM)
-    return pl.pallas_call(
-        moments_kernel,
+    count = owner.shape[0]
+    return pl.pallas_call(
+        edges_kernel,
         out_shape=[
-            jax.ShapeDtypeStruct((3, depth * rows, width), F32),
             jax.ShapeDtypeStruct((20, rows, 128), F32),
+            jax.ShapeDtypeStruct((19, 2, depth, width), F32),
+            jax.ShapeDtypeStruct((2, depth, width), jnp.int32),
+            jax.ShapeDtypeStruct((1, count), jnp.int32),
         ],
-        in_specs=[hbm, hbm],
-        scratch_shapes=[
-            pltpu.VMEM(pops.shape, F32),
-            pltpu.VMEM(solid.shape, jnp.int32),
-            pltpu.SemaphoreType.DMA((5,)),
-        ],
-        compiler_params=pltpu.CompilerParams(vmem_limit_bytes=54000000),
-        cost_estimate=pl.CostEstimate(flops=3000000, bytes_accessed=4000000, transcendentals=0),
-        name="moments",
-    )(pops, solid)
+        in_specs=[pl.BlockSpec(memory_space=pl.ANY)] + [pl.BlockSpec(memory_space=pltpu.VMEM)] * 3,
+        compiler_params=pltpu.CompilerParams(vmem_limit_bytes=ROOM),
+        cost_estimate=pl.CostEstimate(flops=1000000, bytes_accessed=3000000, transcendentals=0),
+        name="edges",
+    )(before, pops, solid, owner.reshape(1, count))
 
 
 def unpack(tiles):
@@ -311,35 +396,42 @@
     return drag, dot_split(spread, hat_x, NT)
 
 
-def couple_kernel(shape, depth, rows, beads_ref, flow_ref, column_ref, force_ref, face_ref, *drag_refs):
+def couple_kernel(single, shape, depth, rows, n_beads, *refs):
+    bead_refs, refs = refs[:n_beads], refs[n_beads:]
+    lower_ref, upper_ref, column_ref, force_ref, face_ref, *drag_refs = refs
     slabs, cols, _ = shape
-    width = flow_ref.shape[2]
-    flow = flow_ref[...].reshape(3 * depth * rows, width)
+    width = lower_ref.shape[2]
+    halves = (lower_ref, upper_ref)
+    flow = jnp.concatenate([ref[d] for d in range(3) for ref in halves], axis=0)
     hollow = jnp.zeros((5, GROUP * CAP), F32)
 
-    if len(drag_refs) == 2:
+    if single:
         slab, col = lax.axis_index("slab"), lax.axis_index("col")
-        got = []
-        for r in range(GROUP):
-            there = [a - b for a, b in zip((slab, col), divmod(r, cols))]
-            there = [jnp.where(a < 0, a + n, a) for a, n in zip(there, (slabs, cols))]
-            got.append(beads_ref[there[0] * cols + there[1]])
-        drag, force = couple_group(*unpack(got), flow, depth, rows)
+        blocks = [
+            ref[k : k + 16] for ref in bead_refs for k in range(0, ref.shape[0], 16)
+        ]
+        slots = own_slots(blocks, slab * cols + col)
+        drag, force = couple_group(slots[1:4], slots[4:7], slots[7:10], flow, depth, rows)
         force_ref[...] = force.reshape(3, depth, rows, width)
         stacked = jnp.concatenate(drag + [hollow], axis=0)
         lanes = cols * CAP
         blank = jnp.zeros((8, 128 - lanes), F32)
-        for dz in range(slabs):
-            tile = jnp.concatenate([stacked[:, dz * lanes : (dz + 1) * lanes], blank], axis=1)
-            drag_refs[0][dz] = tile
-            if dz == 2:
-                drag_refs[1][...] = tile
+        tiles = [
+            jnp.concatenate([stacked[:, k * lanes : (k + 1) * lanes], blank], axis=1)
+            for k in range(slabs)
+        ]
+        even = lax.rem(slab, 2) == 0
+        drag_refs[0][0] = tiles[0]
+        drag_refs[0][1] = jnp.where(even, tiles[3], tiles[1])
+        drag_refs[0][2] = tiles[2]
+        drag_refs[0][3] = jnp.where(even, tiles[1], tiles[3])
+        drag_refs[1][...] = tiles[2]
     else:
         force_ref[...] = jnp.zeros_like(force_ref)
         blank = jnp.zeros((8, 128 - CAP), F32)
 
         def group(k, carry):
-            got = [beads_ref[k * GROUP + r] for r in range(GROUP)]
+            got = [bead_refs[0][k * GROUP + r] for r in range(GROUP)]
             drag, force = couple_group(*unpack(got), flow, depth, rows)
             force_ref[...] += force.reshape(3, depth, rows, width)
             stacked = jnp.concatenate(drag + [hollow], axis=0)
@@ -349,7 +441,7 @@
                 )
             return carry
 
-        lax.fori_loop(0, beads_ref.shape[0] // GROUP, group, 0)
+        lax.fori_loop(0, bead_refs[0].shape[0] // GROUP, group, 0)
 
     force = [x_ends([force_ref[d, z] for z in range(depth)]) for d in range(3)]
     out = collide([column_ref[i] for i in range(19)], column_ref[19] == 1.0, force)
@@ -359,13 +451,12 @@
     face_ref[1] = jnp.concatenate([ends[4], jnp.zeros((rows, 96), F32)], axis=1)
 
 
-def couple(shape, beads, flow, columns, depth, rows):
-    width = flow.shape[2]
-    single = beads.shape[0] == GROUP
+def couple(single, shape, beads, flow, columns, depth, rows):
+    width = flow[0].shape[2]
     tile = jax.ShapeDtypeStruct((8, 128), F32)
-    drags = [jax.ShapeDtypeStruct((shape[0], 8, 128), F32), tile] if single else [beads]
-    return pl.pallas_call(
-        functools.partial(couple_kernel, shape, depth, rows),
+    drags = [jax.ShapeDtypeStruct((shape[0], 8, 128), F32), tile] if single else beads
+    return pl.pallas_call(
+        functools.partial(couple_kernel, single, shape, depth, rows, len(beads)),
         out_shape=[
             jax.ShapeDtypeStruct((3, depth, rows, width), F32),
             jax.ShapeDtypeStruct((2, rows, 128), F32),
@@ -373,11 +464,11 @@
         + [jax.ShapeDtypeStruct(d.shape, F32) for d in drags],
         compiler_params=pltpu.CompilerParams(vmem_limit_bytes=ROOM),
         name="couple",
-    )(beads, flow, columns)
+    )(*beads, *flow, columns)
 
 
 def faces_kernel(
-    force_ref, pops_ref, solid_ref, face_ref, drag_ref, up_ref, down_ref, draft_ref, token_ref, turned
+    force_ref, pops_ref, solid_ref, side_ref, wall_ref, face_ref, drag_ref, up_ref, down_ref, draft_ref, token_ref, turned
 ):
     depth, rows, width = force_ref.shape[1:]
     token_ref[...] = jnp.zeros_like(token_ref)
@@ -390,9 +481,12 @@
             at = (0 if first else depth - 1, slice(None))
         else:
             at = (slice(None), 0 if first else rows - 1)
-        pops = [pops_ref[(i,) + at] for i in range(19)]
         force = [force_ref[(d,) + at] for d in range(3)]
-        out = collide(pops, solid_ref[at] == 1, force)
+        if side < 2:
+            pops, wall = [pops_ref[i, at[0]] for i in range(19)], solid_ref[at[0]]
+        else:
+            pops, wall = [side_ref[i, side - 2] for i in range(19)], wall_ref[side - 2]
+        out = collide(pops, wall == 1, force)
         axis = 2 if side < 2 else 1
         group = 1 if first else 0
         for k, i in enumerate(ENTER[axis][group]):
@@ -415,11 +509,7 @@
         down_ref[5 * rows : 5 * rows + 8] = drag_ref[1]
 
 
-TOKEN = jax.ShapeDtypeStruct((8, 128), F32)
-ROOM = 16 << 20
-
-
-def faces(single, force, pops, solid, face, drag):
+def faces(single, force, pops, solid, sides, walls, face, drag):
     _, depth, rows, width = force.shape
     message = jax.ShapeDtypeStruct((5 * rows + (8 if single else 0), width), F32)
     return pl.pallas_call(
@@ -428,7 +518,7 @@
         scratch_shapes=[pltpu.VMEM((2, 128, rows), F32)],
         compiler_params=pltpu.CompilerParams(vmem_limit_bytes=ROOM),
         name="faces",
-    )(force, pops, solid, face, drag)
+    )(force, pops, solid, sides, walls, face, drag)
 
 
 def rows_kernel(depth, rows, before_ref, draft_ref, up_ref, down_ref, *refs):
@@ -670,16 +760,38 @@
         lax.all_to_all, axis_name=("slab", "col"), split_axis=0, concat_axis=0, tiled=True
     )
 
-    target, beads = pack(owners, bead_owner, bead_base, bead_offset, bead_velocity)
-    beads = swap(beads)
-    flow, columns = moments(populations, solid_mask)
-    force, face, drag, *far = couple(shape, beads, flow, columns, depth, rows)
+    beads = (bead_owner, bead_base, bead_offset, bead_velocity)
+    half = depth // 2
+    if single:
+        token = own = publish(*beads)
+        first = exchange(own, shape, (0, 1, 0))
+        lower, token = flow_of(0, half, token, populations, True)
+        pair, token = join(token, own, first)
+        second = exchange(pair, shape, (1, 0, 0))
+        upper, token = flow_of(half, depth, token, populations, False)
+        four, token = join(token, pair, second)
+        third = exchange(four, shape, (2, 0, 0))
+        beads = [four, third]
+    else:
+        token = jnp.zeros(TOKEN.shape, F32)
+        target, messages = pack(owners, *beads)
+        beads = [swap(messages)]
+        lower, _ = flow_of(0, half, token, populations, True)
+        upper, _ = flow_of(half, depth, token, populations, False)
+    columns, sides, walls, slots = edges(token, populations, solid_mask, bead_owner)
+    if single:
+        target = slots
+    force, face, drag, *far = couple(
+        single, shape, beads, (lower, upper), columns, depth, rows
+    )
     face = send(face, shape, (0, 0, 1))
     if single:
         far = send(far[0], shape, (2, 0, 0))
     else:
         drag = swap(drag)
-    up, down, draft, token = faces(single, force, populations, solid_mask, face, drag)
+    up, down, draft, token = faces(
+        single, force, populations, solid_mask, sides, walls, face, drag
+    )
     up = send(up, shape, (1, 0, 0))
     down = send(down, shape, (-1, 0, 0))
     fields = (populations, solid_mask, force, face)

time: 35.2 us -> 35.2 us (level)
  starting transfers between devices: 11.6 us -> 14.1 us
  waiting for transfers between devices: 7.91 us -> 5.9 us
  Pallas kernels: 13.8 us -> 12.8 us
  local copies, waits for them, and re-layouts: 0.91 us -> 1.44 us
    ppermute x5 -> x8, starting transfers between devices: 4.39 us -> 14.1 us  [permute(): return lax.ppermute(value, ('slab', 'col', 'pair'), perm)]
    all_to_all x1 -> x0, starting transfers between devices: 7.25 us -> none  [shards(): beads = swap(beads)]
    all_to_all x1 -> x0, waiting for transfers between devices: 3.12 us -> none  [shards(): beads = swap(beads)]
    ppermute x5 -> x8, waiting for transfers between devices: 4.78 us -> 5.9 us  [permute(): return lax.ppermute(value, ('slab', 'col', 'pair'), perm)]
    pallas_call x1, Pallas kernels: 1.04 us -> 0.38 us  [faces(): pl.pallas_call(faces_kernel, out_shape=[message, message, jax.ShapeDtypeS...]
    unnamed x8 -> x10, local copies, waits for them, and re-layouts: 0.91 us -> 1.44 us
    pallas_call x3 -> x7, Pallas kernels: 6.14 us -> 5.77 us  [the longest x1 1.92 us: couple(): pl.pallas_call(functools.partial(couple_kernel, single, shape, depth, row...]
  transfers between devices with their start and end apart: 6 -> 8, of which waited for: 4 -> 5; matrix products, arithmetic and copies ran while one was open for 0% -> 0% of each run, Pallas kernels for 22% -> 21%
where the time goes in v7:
time: 35.2 us; the launch traced here: 34.9 us
  starting transfers between devices  14.1 us (40%)
  Pallas kernels  12.8 us (36%)
  waiting for transfers between devices  5.9 us (17%)
  local copies, waits for them, and re-layouts  1.44 us (4%)
  between operations  0.71 us (2%)
    ppermute x8, starting transfers between devices, permute(): return lax.ppermute(value, ('slab', 'col', 'pair'), perm)  14.1 us
    ppermute x8, waiting for transfers between devices, permute(): return lax.ppermute(value, ('slab', 'col', 'pair'), perm)  5.9 us
    pallas_call x2, Pallas kernels, stream(): pl.pallas_call(functools.partial(stream_kernel, low, high), out_shape=[ja...  5.01 us
    pallas_call x1, Pallas kernels, couple(): pl.pallas_call(functools.partial(couple_kernel, single, shape, depth, row...  1.92 us
    pallas_call x1, Pallas kernels, finish(): pl.pallas_call(functools.partial(finish_kernel, shape, len(entered)), out...  1.61 us
    pallas_call x2, Pallas kernels, flow_of(): pl.pallas_call(functools.partial(flow_kernel, low, high), out_shape=[jax....  1.51 us
    pallas_call x1, Pallas kernels, publish(): pl.pallas_call(publish_kernel, out_shape=jax.ShapeDtypeStruct((16, count)...  1.48 us
    unnamed x10, local copies, waits for them, and re-layouts  1.44 us
  transfers between devices with their start and end apart: 8, of which 5 were waited for; matrix products, arithmetic and copies ran while one was open for 0% of the time, Pallas kernels for 21%

profile of v7, /device:TPU:0, one launch (start us, length us, event | category | flops | bytes accessed | tf_op | source)
XLA Modules:
  0.0 34.9 jit_solution(8479066844294364402)
XLA Ops:
  0.6 1.5 %publish.1.before_ref.refs_0_ = f32[16,128]{1,0:T(8,128)} custom-call(s32[1,128]{1,0:T(1,128)} %bitcast.1, s32[3,128]{1,0:T(4,128)} %base_ref.1, f32[3,128]{1,0:T(4,128)} %offset_ref.1, f32[3,128]{1,0:T(4,128)} %velocity_ref.1), custom_call_target="tpu_custom_call" | custom-call | tf_op jit(solution)/shard_map/publish/pallas_call | solution.py:248
  2.1 2.9 %collective-permute-start = (f32[16,128]{1,0:T(8,128)}, f32[16,128]{1,0:T(8,128)S(1)}, u32[]{:S(2)}, u32[]{:S(2)}) collective-permute-start(f32[16,128]{1,0:T(8,128)} %publish.1.before_ref.refs_0_), channel_id=1, source_target_pairs={{0,2},{1,3},{2,0},{3,1},{4,6},{5,7},{6,4},{7,5},{8,10},{9,11},{10,... | collective-permute-start | bytes 24584 | tf_op jit(solution)/shard_map/ppermute | solution.py:149
  5.1 0.7 %copy-done.2 = f32[16,128]{1,0:T(8,128)S(1)} copy-done((f32[16,128]{1,0:T(8,128)S(1)}, f32[16,128]{1,0:T(8,128)}, u32[]{:S(2)}) %copy-start.2) | copy-done | bytes 8216
  5.8 1.4 %flow.2 = (f32[3,128,128]{2,1,0:T(8,128)S(1)}, f32[8,128]{1,0:T(8,128)S(1)}) custom-call(f32[16,128]{1,0:T(8,128)S(1)} %copy-done.2, f32[19,16,16,128]{3,2,1,0:T(8,128)} %refs_1_.3), custom_call_target="tpu_custom_call" | custom-call | flops 1000000 | bytes 1500000 | tf_op jit(solution)/shard_map/flow/pallas_call | solution.py:327
  7.2 0.7 %copy-done.3 = f32[16,128]{1,0:T(8,128)S(1)} copy-done((f32[16,128]{1,0:T(8,128)S(1)}, f32[16,128]{1,0:T(8,128)}, u32[]{:S(2)}) %copy-start.3) | copy-done | bytes 8216
  7.9 1.8 %collective-permute-start.1 = (f32[32,128]{1,0:T(8,128)S(1)}, f32[32,128]{1,0:T(8,128)S(1)}, u32[]{:S(2)}, u32[]{:S(2)}) collective-permute-start(f32[32,128]{1,0:T(8,128)S(1)} %get-tuple-element.32.refs_0_), channel_id=1, source_target_pairs={{0,4},{1,5},{2,6},{3,7},{4,0},{5,1},{6,2},{7,3},{8,12},{9,13},{10,... | collective-permute-start | bytes 49160 | tf_op jit(solution)/shard_map/ppermute | solution.py:149
  9.7 0.2 flow.3
  9.9 1.7 %collective-permute-done.1.refs_1_ = f32[32,128]{1,0:T(8,128)S(1)} collective-permute-done((f32[32,128]{1,0:T(8,128)S(1)}, f32[32,128]{1,0:T(8,128)S(1)}, u32[]{:S(2)}, u32[]{:S(2)}) %collective-permute-start.1) | collective-permute-done | bytes 16416 | tf_op jit(solution)/shard_map/ppermute | solution.py:149
  11.6 2.8 %collective-permute-start.2 = (f32[64,128]{1,0:T(8,128)S(1)}, f32[64,128]{1,0:T(8,128)S(1)}, u32[]{:S(2)}, u32[]{:S(2)}) collective-permute-start(f32[64,128]{1,0:T(8,128)S(1)} %get-tuple-element.33.refs_0_), channel_id=1, source_target_pairs={{0,8},{1,9},{2,10},{3,11},{4,12},{5,13},{6,14},{7,15},{8,0},{9,1},... | collective-permute-start | bytes 98312 | tf_op jit(solution)/shard_map/ppermute | solution.py:149
  14.5 0.8 %edges.1 = (f32[20,16,128]{2,1,0:T(8,128)S(1)}, f32[19,2,16,128]{3,2,1,0:T(8,128)S(1)}, s32[2,16,128]{2,1,0:T(8,128)S(1)}, s32[1,128]{1,0:T(1,128)S(1)}) custom-call(f32[8,128]{1,0:T(8,128)S(1)} %get-tuple-element.36.before_ref, f32[19,16,16,128]{3,2,1,0:T(8,128)S(1)} %copy-done, s32[16,16,128]{2,1,0:T(8,128)S(1)} %copy-done.1, s32[1,128]{1,0:T(1,128)S(1)} %bitcast.2), custom_call_target="tpu_custom_call" | custom-call | flops 1000000 | bytes 3000000 | tf_op jit(solution)/shard_map/edges/pallas_call | solution.py:356
  15.3 1.1 %collective-permute-done.2.refs_1_ = f32[64,128]{1,0:T(8,128)S(1)} collective-permute-done((f32[64,128]{1,0:T(8,128)S(1)}, f32[64,128]{1,0:T(8,128)S(1)}, u32[]{:S(2)}, u32[]{:S(2)}) %collective-permute-start.2) | collective-permute-done | bytes 32800 | tf_op jit(solution)/shard_map/ppermute | solution.py:149
  16.4 1.9 %couple.1 = (f32[3,16,16,128]{3,2,1,0:T(8,128)S(1)}, f32[2,16,128]{2,1,0:T(8,128)S(1)}, f32[4,8,128]{2,1,0:T(8,128)S(1)}, f32[8,128]{1,0:T(8,128)S(1)}) custom-call(f32[64,128]{1,0:T(8,128)S(1)} %get-tuple-element.33.refs_0_, f32[64,128]{1,0:T(8,128)S(1)} %collective-permute-done.2.refs_1_, f32[3,128,128]{2,1,0:T(8,128)S(1)} %get-tuple-element.34.refs_2_, ...), custom_call_target="tpu_custom_call" | custom-call | tf_op jit(solution)/shard_map/couple/pallas_call | solution.py:458
  18.4 0.0 collective-permute-start.3
  18.4 1.2 %collective-permute-done.3.face_ref.refs_3_.refs_4_ = f32[2,16,128]{2,1,0:T(8,128)S(1)} collective-permute-done((f32[2,16,128]{2,1,0:T(8,128)S(1)}, f32[2,16,128]{2,1,0:T(8,128)S(1)}, u32[]{:S(2)}, u32[]{:S(2)}) %collective-permute-start.3) | collective-permute-done | bytes 16416 | tf_op jit(solution)/shard_map/ppermute | solution.py:149
  19.6 0.4 %faces.1 = (f32[88,128]{1,0:T(8,128)S(1)}, f32[88,128]{1,0:T(8,128)S(1)}, f32[160,128]{1,0:T(8,128)S(1)}, f32[8,128]{1,0:T(8,128)S(1)}) custom-call(f32[3,16,16,128]{3,2,1,0:T(8,128)S(1)} %get-tuple-element.38.force_ref.refs_2_.refs_3_, f32[19,16,16,128]{3,2,1,0:T(8,128)S(1)} %copy-done, s32[16,16,128]{2,1,0:T(8,128)S(1)} %copy-done.1, ...), custom_call_target="tpu_custom_call" | custom-call | tf_op jit(solution)/shard_map/faces/pallas_call | solution.py:515
  19.9 1.8 %collective-permute-start.4 = (f32[88,128]{1,0:T(8,128)S(1)}, f32[88,128]{1,0:T(8,128)S(1)}, u32[]{:S(2)}, u32[]{:S(2)}) collective-permute-start(f32[88,128]{1,0:T(8,128)S(1)} %get-tuple-element.46), channel_id=1, source_target_pairs={{0,4},{1,5},{2,6},{3,7},{4,8},{5,9},{6,10},{7,11},{8,12},{9,13},{1... | collective-permute-start | bytes 135176 | tf_op jit(solution)/shard_map/ppermute | solution.py:149
  21.8 2.3 %collective-permute-start.5 = (f32[88,128]{1,0:T(8,128)S(1)}, f32[88,128]{1,0:T(8,128)S(1)}, u32[]{:S(2)}, u32[]{:S(2)}) collective-permute-start(f32[88,128]{1,0:T(8,128)S(1)} %get-tuple-element.47), channel_id=1, source_target_pairs={{0,12},{1,13},{2,14},{3,15},{4,0},{5,1},{6,2},{7,3},{8,4},{9,5},{1... | collective-permute-start | bytes 135176 | tf_op jit(solution)/shard_map/ppermute | solution.py:149
  24.1 0.7 %collective-permute-start.6 = (f32[8,128]{1,0:T(8,128)S(1)}, f32[8,128]{1,0:T(8,128)S(1)}, u32[]{:S(2)}, u32[]{:S(2)}) collective-permute-start(f32[8,128]{1,0:T(8,128)S(1)} %get-tuple-element.48), channel_id=1, source_target_pairs={{0,8},{1,9},{2,10},{3,11},{4,12},{5,13},{6,14},{7,15},{8,0},{9,1},... | collective-permute-start | bytes 12296 | tf_op jit(solution)/shard_map/ppermute | solution.py:149
  24.8 2.2 %stream.2 = (f32[19,16,16,128]{3,2,1,0:T(8,128)}, f32[10,8,8,128]{3,2,1,0:T(8,128)S(1)}, f32[8,128]{1,0:T(8,128)S(1)}) custom-call(f32[8,128]{1,0:T(8,128)S(1)} %get-tuple-element.43.before_ref, f32[19,16,16,128]{3,2,1,0:T(8,128)S(1)} %copy-done, s32[16,16,128]{2,1,0:T(8,128)S(1)} %copy-done.1, ...), custom_call_target="tpu_custom_call" | custom-call | flops 5000000 | bytes 3000000 | tf_op jit(solution)/shard_map/stream/pallas_call | solution.py:620
  27.0 1.6 %collective-permute-done.6.refs_1_.refs_2_ = f32[8,128]{1,0:T(8,128)S(1)} collective-permute-done((f32[8,128]{1,0:T(8,128)S(1)}, f32[8,128]{1,0:T(8,128)S(1)}, u32[]{:S(2)}, u32[]{:S(2)}) %collective-permute-start.6) | collective-permute-done | bytes 4128 | tf_op jit(solution)/shard_map/ppermute | solution.py:149
  28.6 1.6 %collective-permute-start.7 = (f32[192,128]{1,0:T(8,128)S(1)}, f32[192,128]{1,0:T(8,128)S(1)}, u32[]{:S(2)}, u32[]{:S(2)}) collective-permute-start(f32[192,128]{1,0:T(8,128)S(1)} %get-tuple-element.55), channel_id=1, source_target_pairs={{0,2},{1,3},{2,0},{3,1},{4,6},{5,7},{6,4},{7,5},{8,10},{9,11},{10,... | collective-permute-start | bytes 294920 | tf_op jit(solution)/shard_map/ppermute | solution.py:149
  30.2 2.8 %stream.3 = (f32[19,16,16,128]{3,2,1,0:T(8,128)}, f32[10,8,8,128]{3,2,1,0:T(8,128)S(1)}, f32[8,128]{1,0:T(8,128)}) custom-call(f32[8,128]{1,0:T(8,128)S(1)} %get-tuple-element.49.before_ref, f32[19,16,16,128]{3,2,1,0:T(8,128)} %get-tuple-element.50.refs_0_, f32[19,16,16,128]{3,2,1,0:T(8,128)S(1)} %copy-done, ...), custom_call_target="tpu_custom_call", output_to_operand_aliasing={{0}: (1, {})} | custom-call | flops 5000000 | bytes 3000000 | tf_op jit(solution)/shard_map/stream/pallas_call | solution.py:620
  33.0 0.3 collective-permute-done.7.refs_0_
  33.3 1.6 %finish.1 = (f32[19,16,16,128]{3,2,1,0:T(8,128)}, f32[3,128]{1,0:T(4,128)}) custom-call(f32[19,16,16,128]{3,2,1,0:T(8,128)} %get-tuple-element.51.whole_ref, s32[1,128]{1,0:T(1,128)S(1)} %get-tuple-element.52.target_ref, f32[10,8,8,128]{3,2,1,0:T(8,128)S(1)} %get-tuple-element.53.lower_ref, ...), custom_call_target="tpu_custom_call", output_to_operand_aliasing={{0}: (0, {})} | custom-call | tf_op jit(solution)/shard_map/finish/pallas_call | solution.py:735
  (14 shorter events, 0.0 us)
Async XLA Ops:
  0.6 9.1 %copy-start = (f32[19,16,16,128]{3,2,1,0:T(8,128)S(1)}, f32[19,16,16,128]{3,2,1,0:T(8,128)}, u32[]{:S(2)}) copy-start(f32[19,16,16,128]{3,2,1,0:T(8,128)} %refs_1_.3) | copy-start | bytes 7471108
  2.1 12.3 %copy-start.1 = (s32[16,16,128]{2,1,0:T(8,128)S(1)}, s32[16,16,128]{2,1,0:T(8,128)}, u32[]{:S(2)}) copy-start(s32[16,16,128]{2,1,0:T(8,128)} %refs_2_.1) | copy-start | bytes 393220
  2.1 5.0 %collective-permute-start = (f32[16,128]{1,0:T(8,128)}, f32[16,128]{1,0:T(8,128)S(1)}, u32[]{:S(2)}, u32[]{:S(2)}) collective-permute-start(f32[16,128]{1,0:T(8,128)} %publish.1.before_ref.refs_0_), channel_id=1, source_target_pairs={{0,2},{1,3},{2,0},{3,1},{4,6},{5,7},{6,4},{7,5},{8,10},{9,11},{10,... | collective-permute-start | bytes 24584 | tf_op jit(solution)/shard_map/ppermute | solution.py:149
  5.1 0.7 %copy-start.2 = (f32[16,128]{1,0:T(8,128)S(1)}, f32[16,128]{1,0:T(8,128)}, u32[]{:S(2)}) copy-start(f32[16,128]{1,0:T(8,128)} %publish.1.before_ref.refs_0_) | copy-start | bytes 24580
  7.2 0.7 %copy-start.3 = (f32[16,128]{1,0:T(8,128)S(1)}, f32[16,128]{1,0:T(8,128)}, u32[]{:S(2)}) copy-start(f32[16,128]{1,0:T(8,128)} %publish.1.before_ref.refs_0_) | copy-start | bytes 24580
  7.9 6.6 %copy-start.4 = (s32[128]{0:T(128)S(1)}, s32[128]{0:T(128)}, u32[]{:S(2)}) copy-start(s32[128]{0:T(128)} %param.8) | copy-start | bytes 1540
  7.9 3.7 %collective-permute-start.1 = (f32[32,128]{1,0:T(8,128)S(1)}, f32[32,128]{1,0:T(8,128)S(1)}, u32[]{:S(2)}, u32[]{:S(2)}) collective-permute-start(f32[32,128]{1,0:T(8,128)S(1)} %get-tuple-element.32.refs_0_), channel_id=1, source_target_pairs={{0,4},{1,5},{2,6},{3,7},{4,0},{5,1},{6,2},{7,3},{8,12},{9,13},{10,... | collective-permute-start | bytes 49160 | tf_op jit(solution)/shard_map/ppermute | solution.py:149
  11.6 4.8 %collective-permute-start.2 = (f32[64,128]{1,0:T(8,128)S(1)}, f32[64,128]{1,0:T(8,128)S(1)}, u32[]{:S(2)}, u32[]{:S(2)}) collective-permute-start(f32[64,128]{1,0:T(8,128)S(1)} %get-tuple-element.33.refs_0_), channel_id=1, source_target_pairs={{0,8},{1,9},{2,10},{3,11},{4,12},{5,13},{6,14},{7,15},{8,0},{9,1},... | collective-permute-start | bytes 98312 | tf_op jit(solution)/shard_map/ppermute | solution.py:149
  18.4 1.2 %collective-permute-start.3 = (f32[2,16,128]{2,1,0:T(8,128)S(1)}, f32[2,16,128]{2,1,0:T(8,128)S(1)}, u32[]{:S(2)}, u32[]{:S(2)}) collective-permute-start(f32[2,16,128]{2,1,0:T(8,128)S(1)} %get-tuple-element.41), channel_id=1, source_target_pairs={{0,1},{1,0},{2,3},{3,2},{4,5},{5,4},{6,7},{7,6},{8,9},{9,8},{10,11... | collective-permute-start | bytes 49160 | tf_op jit(solution)/shard_map/ppermute | solution.py:149
  19.9 8.7 %collective-permute-start.4 = (f32[88,128]{1,0:T(8,128)S(1)}, f32[88,128]{1,0:T(8,128)S(1)}, u32[]{:S(2)}, u32[]{:S(2)}) collective-permute-start(f32[88,128]{1,0:T(8,128)S(1)} %get-tuple-element.46), channel_id=1, source_target_pairs={{0,4},{1,5},{2,6},{3,7},{4,8},{5,9},{6,10},{7,11},{8,12},{9,13},{1... | collective-permute-start | bytes 135176 | tf_op jit(solution)/shard_map/ppermute | solution.py:149
  21.8 6.8 %collective-permute-start.5 = (f32[88,128]{1,0:T(8,128)S(1)}, f32[88,128]{1,0:T(8,128)S(1)}, u32[]{:S(2)}, u32[]{:S(2)}) collective-permute-start(f32[88,128]{1,0:T(8,128)S(1)} %get-tuple-element.47), channel_id=1, source_target_pairs={{0,12},{1,13},{2,14},{3,15},{4,0},{5,1},{6,2},{7,3},{8,4},{9,5},{1... | collective-permute-start | bytes 135176 | tf_op jit(solution)/shard_map/ppermute | solution.py:149
  24.1 4.5 %collective-permute-start.6 = (f32[8,128]{1,0:T(8,128)S(1)}, f32[8,128]{1,0:T(8,128)S(1)}, u32[]{:S(2)}, u32[]{:S(2)}) collective-permute-start(f32[8,128]{1,0:T(8,128)S(1)} %get-tuple-element.48), channel_id=1, source_target_pairs={{0,8},{1,9},{2,10},{3,11},{4,12},{5,13},{6,14},{7,15},{8,0},{9,1},... | collective-permute-start | bytes 12296 | tf_op jit(solution)/shard_map/ppermute | solution.py:149
  28.6 4.7 %collective-permute-start.7 = (f32[192,128]{1,0:T(8,128)S(1)}, f32[192,128]{1,0:T(8,128)S(1)}, u32[]{:S(2)}, u32[]{:S(2)}) collective-permute-start(f32[192,128]{1,0:T(8,128)S(1)} %get-tuple-element.55), channel_id=1, source_target_pairs={{0,2},{1,3},{2,0},{3,1},{4,6},{5,7},{6,4},{7,5},{8,10},{9,11},{10,... | collective-permute-start | bytes 294920 | tf_op jit(solution)/shard_map/ppermute | solution.py:149

commit v8 on v6

--- a/solution.py
+++ b/solution.py
@@ -45,6 +45,8 @@
 BF16 = jnp.bfloat16
 
 ENTER = [[[i for i in range(19) if STEP[i, a] == sign] for sign in (1, -1)] for a in range(3)]
+TOKEN = jax.ShapeDtypeStruct((8, 128), F32)
+ROOM = 16 << 20
 NT = (((1,), (1,)), ((), ()))
 NN = (((1,), (0,)), ((), ()))
 
@@ -131,17 +133,23 @@
     return pltpu.roll(value, int(amount) % value.shape[axis], axis)
 
 
-def send(value, shape, offset):
-    slabs, cols, pairs = shape
-    perm = []
-    for s in range(slabs):
-        for c in range(cols):
-            for p in range(pairs):
-                there = (
-                    ((s + offset[0]) % slabs) * cols + (c + offset[1]) % cols
-                ) * pairs + (p + offset[2]) % pairs
-                perm.append(((s * cols + c) * pairs + p, there))
+def send(value, shape, target):
+    def flat(at):
+        return (at[0] * shape[1] + at[1]) * shape[2] + at[2]
+
+    perm = [(flat(at), flat(target(*at))) for at in np.ndindex(*shape)]
     return lax.ppermute(value, ("slab", "col", "pair"), perm)
+
+
+def send_slab(value, shape, which):
+    def target(s, c, p):
+        return ((s + (1 if s % 2 == which else -1)) % shape[0], c, p)
+
+    return send(value, shape, target)
+
+
+def even_slab():
+    return lax.rem(lax.axis_index("slab"), 2) == 0
 
 
 def rank_among(member):
@@ -176,22 +184,23 @@
     return tile
 
 
-def pack_kernel(owner_ref, base_ref, offset_ref, velocity_ref, target_ref, out_ref, table):
+def pack_kernel(
+    steps, owner_ref, base_ref, offset_ref, velocity_ref, target_ref, out_ref, table
+):
     count = owner_ref.shape[1]
-    local = owner_ref[...] - pl.program_id(0) * GROUP
+    step = 0 if steps == 1 else pl.program_id(0)
+    local = owner_ref[...] - step * GROUP
     member = (iota((GROUP, count), 0) == local).astype(F32)
     rank = jnp.sum(member * rank_among(member), axis=0, keepdims=True).astype(jnp.int32)
     inside = (local >= 0) & (local < GROUP)
     target = jnp.where(inside, local * CAP + rank, -1)
     whole_target = jnp.where(inside, owner_ref[...] * CAP + rank, -1)
 
-    @pl.when(pl.program_id(0) == 0)
-    def _():
+    if steps == 1:
         target_ref[...] = whole_target
-
-    @pl.when(pl.program_id(0) > 0)
-    def _():
-        target_ref[...] = jnp.maximum(target_ref[...], whole_target)
+    else:
+        known = jnp.where(step == 0, -1, target_ref[...])
+        target_ref[...] = jnp.maximum(known, whole_target)
 
     choose = (iota((GROUP * CAP, count), 0) == target).astype(F32).astype(BF16)
     table[...] = jnp.zeros_like(table)
@@ -208,30 +217,33 @@
 
 
 def pack(owners, owner, base, offset, velocity):
-    count = owner.shape[0]
+    count, steps = owner.shape[0], owners // GROUP
     args = (owner.reshape(1, count), base, offset, velocity)
+    blocks = {}
+    if steps > 1:
+        blocks = dict(
+            grid=(steps,),
+            in_specs=[pl.BlockSpec(a.shape, lambda k: (0, 0)) for a in args],
+            out_specs=[
+                pl.BlockSpec((1, count), lambda k: (0, 0)),
+                pl.BlockSpec((GROUP, 8, 128), lambda k: (k, 0, 0)),
+            ],
+            compiler_params=pltpu.CompilerParams(vmem_limit_bytes=48 << 20),
+        )
     return pl.pallas_call(
-        pack_kernel,
+        functools.partial(pack_kernel, steps),
         out_shape=[
             jax.ShapeDtypeStruct((1, count), jnp.int32),
             jax.ShapeDtypeStruct((owners, 8, 128), F32),
         ],
-        grid=(owners // GROUP,),
-        in_specs=[pl.BlockSpec(a.shape, lambda k: (0, 0)) for a in args],
-        out_specs=[
-            pl.BlockSpec((1, count), lambda k: (0, 0)),
-            pl.BlockSpec((GROUP, 8, 128), lambda k: (k, 0, 0)),
-        ],
         scratch_shapes=[pltpu.VMEM((24, count), F32)],
-        compiler_params=pltpu.CompilerParams(
-            vmem_limit_bytes=None if owners == GROUP else (48 << 20)
-        ),
         name="pack",
+        **blocks,
     )(*args)
 
 
 def moments_kernel(
-    pops_ref, solid_ref, flow_ref, column_ref, held, held_solid, sem
+    pops_ref, solid_ref, flow_ref, column_ref, side_ref, wall_ref, held, held_solid, sem
 ):
     depth, rows, width = pops_ref.shape[1:]
     chunks = 4
@@ -259,6 +271,10 @@
     copies[0].wait()
     for i in range(19):
         column_ref[i] = x_ends([held[i, z] for z in range(depth)])
+        side_ref[i, 0] = held[i, :, 0, :]
+        side_ref[i, 1] = held[i, :, rows - 1, :]
+    wall_ref[0] = held_solid[:, 0, :]
+    wall_ref[1] = held_solid[:, rows - 1, :]
     column_ref[19] = x_ends([held_solid[z].astype(F32) for z in range(depth)])
 
 
@@ -270,6 +286,8 @@
         out_shape=[
             jax.ShapeDtypeStruct((3, depth * rows, width), F32),
             jax.ShapeDtypeStruct((20, rows, 128), F32),
+            jax.ShapeDtypeStruct((19, 2, depth, width), F32),
+            jax.ShapeDtypeStruct((2, depth, width), jnp.int32),
         ],
         in_specs=[hbm, hbm],
         scratch_shapes=[
@@ -377,8 +395,9 @@
 
 
 def faces_kernel(
-    force_ref, pops_ref, solid_ref, face_ref, drag_ref, up_ref, down_ref, draft_ref, token_ref, turned
+    force_ref, pops_ref, solid_ref, side_ref, wall_ref, face_ref, drag_ref, *refs
 ):
+    first_ref, second_ref, draft_ref, token_ref, turned, leaving = refs
     depth, rows, width = force_ref.shape[1:]
     token_ref[...] = jnp.zeros_like(token_ref)
     tiles = [face_ref[0], face_ref[1]]
@@ -390,9 +409,12 @@
             at = (0 if first else depth - 1, slice(None))
         else:
             at = (slice(None), 0 if first else rows - 1)
-        pops = [pops_ref[(i,) + at] for i in range(19)]
         force = [force_ref[(d,) + at] for d in range(3)]
-        out = collide(pops, solid_ref[at] == 1, force)
+        if side < 2:
+            pops, wall = [pops_ref[i, at[0]] for i in range(19)], solid_ref[at[0]]
+        else:
+            pops, wall = [side_ref[i, side - 2] for i in range(19)], wall_ref[side - 2]
+        out = collide(pops, wall == 1, force)
         axis = 2 if side < 2 else 1
         group = 1 if first else 0
         for k, i in enumerate(ENTER[axis][group]):
@@ -406,32 +428,36 @@
                     column = jnp.broadcast_to(block[:, at[1] : at[1] + 1], (depth, width))
                 value = enter_x(value, i, column)
             if axis == 2:
-                (down_ref if first else up_ref)[k * rows : (k + 1) * rows] = value
+                leaving[group, k * rows : (k + 1) * rows] = value
             else:
                 row = (group * 5 + k) * depth
                 draft_ref[row : row + depth] = turn(value, STEP[i, 2], 0)
-    if up_ref.shape[0] > 5 * rows:
-        up_ref[5 * rows : 5 * rows + 8] = drag_ref[drag_ref.shape[0] - 1]
-        down_ref[5 * rows : 5 * rows + 8] = drag_ref[1]
-
-
-TOKEN = jax.ShapeDtypeStruct((8, 128), F32)
-ROOM = 16 << 20
-
-
-def faces(single, force, pops, solid, face, drag):
+    if leaving.shape[1] > 5 * rows:
+        leaving[0, 5 * rows : 5 * rows + 8] = drag_ref[drag_ref.shape[0] - 1]
+        leaving[1, 5 * rows : 5 * rows + 8] = drag_ref[1]
+    even = even_slab()
+    first_ref[...] = jnp.where(even, leaving[0], leaving[1])
+    second_ref[...] = jnp.where(even, leaving[1], leaving[0])
+
+
+def faces(single, force, pops, solid, sides, walls, face, drag):
     _, depth, rows, width = force.shape
     message = jax.ShapeDtypeStruct((5 * rows + (8 if single else 0), width), F32)
     return pl.pallas_call(
         faces_kernel,
         out_shape=[message, message, jax.ShapeDtypeStruct((10 * depth, width), F32), TOKEN],
-        scratch_shapes=[pltpu.VMEM((2, 128, rows), F32)],
+        scratch_shapes=[pltpu.VMEM((2, 128, rows), F32), pltpu.VMEM((2, *message.shape), F32)],
         compiler_params=pltpu.CompilerParams(vmem_limit_bytes=ROOM),
         name="faces",
-    )(force, pops, solid, face, drag)
-
-
-def rows_kernel(depth, rows, before_ref, draft_ref, up_ref, down_ref, *refs):
+    )(force, pops, solid, sides, walls, face, drag)
+
+
+def entered_z(first_ref, second_ref, side, rows):
+    even = even_slab() if side == 0 else jnp.logical_not(even_slab())
+    return jnp.where(even, second_ref[rows], first_ref[rows])
+
+
+def rows_kernel(depth, rows, before_ref, draft_ref, first_ref, second_ref, *refs):
     refs, token_ref = refs[:-1], refs[-1]
     token_ref[...] = jnp.zeros_like(token_ref)
     outs = refs[-1:] if len(refs) == 3 else refs
@@ -446,23 +472,25 @@
                 side = 0 if STEP[i, 2] == 1 else 1
                 z = 0 if side == 0 else depth - 1
                 row = ENTER[2][side].index(i) * rows + y
-                out_ref[at + z : at + z + 1] = (up_ref, down_ref)[side][row : row + 1]
+                out_ref[at + z : at + z + 1] = entered_z(
+                    first_ref, second_ref, side, slice(row, row + 1)
+                )
     if len(refs) == 3:
         own_ref, far_ref, out_ref = refs
         at, tail = 10 * depth, 5 * rows
         out_ref[at : at + 8] = own_ref[0]
-        out_ref[at + 8 : at + 16] = down_ref[tail : tail + 8]
+        out_ref[at + 8 : at + 16] = entered_z(first_ref, second_ref, 1, slice(tail, tail + 8))
         out_ref[at + 16 : at + 24] = far_ref[...]
-        out_ref[at + 24 : at + 32] = up_ref[tail : tail + 8]
-
-
-def leaving_rows(shape, depth, rows, before, draft, up, down, drags):
+        out_ref[at + 24 : at + 32] = entered_z(first_ref, second_ref, 0, slice(tail, tail + 8))
+
+
+def leaving_rows(shape, depth, rows, before, draft, first, second, drags):
     width = draft.shape[1]
     if drags:
         sizes = [10 * depth + 8 * shape[0]]
     else:
         sizes = [5 * depth] * 2
-    args = (draft, up, down, *drags)
+    args = (draft, first, second, *drags)
     return pl.pallas_call(
         functools.partial(rows_kernel, depth, rows),
         out_shape=[jax.ShapeDtypeStruct((n, width), F32) for n in sizes] + [TOKEN],
@@ -548,7 +576,7 @@
 
 
 def finish_kernel(
-    shape, n_rows, whole_ref, target_ref, lower_ref, upper_ref, up_ref, down_ref, *refs
+    shape, n_rows, whole_ref, target_ref, lower_ref, upper_ref, first_ref, second_ref, *refs
 ):
     row_refs, refs = refs[:n_rows], refs[n_rows:]
     drag_refs, (out_ref, bead_ref, planes, tiles, sem) = refs[:-5], refs[-5:]
@@ -570,7 +598,7 @@
     for group in range(2):
         z = 0 if group == 0 else depth - 1
         for k, i in enumerate(ENTER[2][group]):
-            value = (up_ref, down_ref)[group][k * rows : (k + 1) * rows]
+            value = entered_z(first_ref, second_ref, group, slice(k * rows, (k + 1) * rows))
             if STEP[i, 1] != 0:
                 side = 0 if STEP[i, 1] == 1 else 1
                 row = entering(side, ENTER[1][side].index(i))[z : z + 1]
@@ -601,9 +629,10 @@
         own_ref, far_ref = drag_refs
         slabs, cols, _ = shape
         at, tail = 10 * depth, 5 * rows
-        direct = jnp.concatenate(
-            [own_ref[0], down_ref[tail : tail + 8], far_ref[...], up_ref[tail : tail + 8]], axis=0
-        )
+        came = [
+            entered_z(first_ref, second_ref, side, slice(tail, tail + 8)) for side in range(2)
+        ]
+        direct = jnp.concatenate([own_ref[0], came[1], far_ref[...], came[0]], axis=0)
         passed = row_refs[0][at : at + 8 * slabs]
         table = jnp.where(iota(direct.shape, 1) < CAP, direct, passed)
         owner = lax.shift_right_logical(target, 5)
@@ -637,11 +666,11 @@
         copy.wait()
 
 
-def finish(shape, whole, target, lower, upper, up, down, entered, drags):
+def finish(shape, whole, target, lower, upper, first, second, entered, drags):
     _, depth, rows, width = whole.shape
     vmem = pl.BlockSpec(memory_space=pltpu.VMEM)
     hbm = pl.BlockSpec(memory_space=pltpu.HBM)
-    args = [whole, target, lower, upper, up, down, *entered, *drags]
+    args = [whole, target, lower, upper, first, second, *entered, *drags]
     return pl.pallas_call(
         functools.partial(finish_kernel, shape, len(entered)),
         out_shape=[
@@ -670,25 +699,31 @@
         lax.all_to_all, axis_name=("slab", "col"), split_axis=0, concat_axis=0, tiled=True
     )
 
-    target, beads = pack(owners, bead_owner, bead_base, bead_offset, bead_velocity)
-    beads = swap(beads)
-    flow, columns = moments(populations, solid_mask)
-    force, face, drag, *far = couple(shape, beads, flow, columns, depth, rows)
-    face = send(face, shape, (0, 0, 1))
+    target, messages = pack(owners, bead_owner, bead_base, bead_offset, bead_velocity)
+    messages = swap(messages)
+    flow, columns, sides, walls = moments(populations, solid_mask)
+    force, face, drag, *far = couple(shape, messages, flow, columns, depth, rows)
+    face = send(face, shape, lambda s, c, p: (s, c, (p + 1) % pairs))
     if single:
-        far = send(far[0], shape, (2, 0, 0))
+        far = send(far[0], shape, lambda s, c, p: ((s + 2) % slabs, c, p))
     else:
         drag = swap(drag)
-    up, down, draft, token = faces(single, force, populations, solid_mask, face, drag)
-    up = send(up, shape, (1, 0, 0))
-    down = send(down, shape, (-1, 0, 0))
+    first, second, draft, token = faces(
+        single, force, populations, solid_mask, sides, walls, face, drag
+    )
+    first, second = send_slab(first, shape, 0), send_slab(second, shape, 1)
     fields = (populations, solid_mask, force, face)
     whole, lower, token = stream(0, depth // 2, token, None, *fields)
     drags = [drag, far] if single else []
-    *leaving, token = leaving_rows(shape, depth, rows, token, draft, up, down, drags)
-    entered = [send(value, shape, (0, sign, 0)) for value, sign in zip(leaving, (1, -1))]
+    *leaving, token = leaving_rows(shape, depth, rows, token, draft, first, second, drags)
+    entered = [
+        send(value, shape, lambda s, c, p, sign=sign: (s, (c + sign) % cols, p))
+        for value, sign in zip(leaving, (1, -1))
+    ]
     whole, upper, _ = stream(depth // 2, depth, token, whole, *fields)
-    return tuple(finish(shape, whole, target, lower, upper, up, down, entered, drags or [drag]))
+    return tuple(
+        finish(shape, whole, target, lower, upper, first, second, entered, drags or [drag])
+    )
 
 
 def solution(mesh):

time: 35.2 us -> 32.7 us (0.929)
  waiting for transfers between devices: 7.91 us -> 5.9 us
  Pallas kernels: 13.8 us -> 13.3 us
    ppermute x5, waiting for transfers between devices: 4.78 us -> 2.88 us  [send(): return lax.ppermute(value, ('slab', 'col', 'pair'), perm)]
    pallas_call x1, Pallas kernels: 1.04 us -> 0.38 us  [faces(): pl.pallas_call(faces_kernel, out_shape=[message, message, jax.ShapeDtypeS...]
  transfers between devices with their start and end apart: 6 -> 6, of which waited for: 4 -> 4; matrix products, arithmetic and copies ran while one was open for 0% -> 0% of each run, Pallas kernels for 22% -> 24%
where the time goes in v8:
time: 32.7 us; the launch traced here: 32.5 us
  Pallas kernels  13.3 us (41%)
  starting transfers between devices  11.7 us (36%)
  waiting for transfers between devices  5.9 us (18%)
  local copies, waits for them, and re-layouts  0.91 us (3%)
  between operations  0.69 us (2%)
    all_to_all x1, starting transfers between devices, shards(): messages = swap(messages)  7.25 us
    pallas_call x2, Pallas kernels, stream(): pl.pallas_call(functools.partial(stream_kernel, low, high), out_shape=[ja...  5.02 us
    ppermute x5, starting transfers between devices, send(): return lax.ppermute(value, ('slab', 'col', 'pair'), perm)  4.46 us
    all_to_all x1, waiting for transfers between devices, shards(): messages = swap(messages)  3.02 us
    ppermute x5, waiting for transfers between devices, send(): return lax.ppermute(value, ('slab', 'col', 'pair'), perm)  2.88 us
    pallas_call x1, Pallas kernels, moments(): pl.pallas_call(moments_kernel, out_shape=[jax.ShapeDtypeStruct((3, depth...  2.75 us
    pallas_call x1, Pallas kernels, pack(): pl.pallas_call(functools.partial(pack_kernel, steps), out_shape=[jax.Shap...  1.89 us
    pallas_call x1, Pallas kernels, finish(): pl.pallas_call(functools.partial(finish_kernel, shape, len(entered)), out...  1.62 us
  transfers between devices with their start and end apart: 6, of which 4 were waited for; matrix products, arithmetic and copies ran while one was open for 0% of the time, Pallas kernels for 24%

profile of v8, /device:TPU:0, one launch (start us, length us, event | category | flops | bytes accessed | tf_op | source)
XLA Modules:
  0.0 32.5 jit_solution(14999606051133434209)
XLA Ops:
  0.6 0.0 copy-start
  0.6 1.9 %pack.1 = (s32[1,128]{1,0:T(1,128)}, f32[8,8,128]{2,1,0:T(8,128)}) custom-call(s32[1,128]{1,0:T(1,128)} %bitcast.1, s32[3,128]{1,0:T(4,128)} %base_ref.1, f32[3,128]{1,0:T(4,128)} %offset_ref.1, f32[3,128]{1,0:T(4,128)} %velocity_ref.1), custom_call_target="tpu_custom_call" | custom-call | tf_op jit(solution)/shard_map/pack/pallas_call | solution.py:233
  2.5 7.3 %all-to-all-start = ((f32[8,8,128]{2,1,0:T(8,128)}), f32[8,8,128]{2,1,0:T(8,128)S(1)}, u32[]{:S(2)}, u32[]{:S(2)}) async-start(f32[8,8,128]{2,1,0:T(8,128)} %get-tuple-element.23), calls=%async_computation | async-start | bytes 65536 | tf_op jit(solution)/shard_map/all_to_all | solution.py:703
  9.8 0.9 %copy-done.1 = s32[16,16,128]{2,1,0:T(8,128)S(1)} copy-done((s32[16,16,128]{2,1,0:T(8,128)S(1)}, s32[16,16,128]{2,1,0:T(8,128)}, u32[]{:S(2)}) %copy-start.1) | copy-done | bytes 131096
  10.7 2.7 %moments.1 = (f32[3,256,128]{2,1,0:T(8,128)S(1)}, f32[20,16,128]{2,1,0:T(8,128)S(1)}, f32[19,2,16,128]{3,2,1,0:T(8,128)S(1)}, s32[2,16,128]{2,1,0:T(8,128)S(1)}) custom-call(f32[19,16,16,128]{3,2,1,0:T(8,128)} %refs_1_.3, s32[16,16,128]{2,1,0:T(8,128)S(1)} %copy-done.1), custom_call_target="tpu_custom_call" | custom-call | flops 3000000 | bytes 4000000 | tf_op jit(solution)/shard_map/moments/pallas_call | solution.py:284
  13.4 3.0 %all-to-all-done.beads_ref = f32[8,8,128]{2,1,0:T(8,128)S(1)} async-done(((f32[8,8,128]{2,1,0:T(8,128)}), f32[8,8,128]{2,1,0:T(8,128)S(1)}, u32[]{:S(2)}, u32[]{:S(2)}) %all-to-all-start) | async-done | bytes 32800 | tf_op jit(solution)/shard_map/all_to_all | solution.py:703
  16.5 1.6 %couple.1 = (f32[3,16,16,128]{3,2,1,0:T(8,128)S(1)}, f32[2,16,128]{2,1,0:T(8,128)S(1)}, f32[4,8,128]{2,1,0:T(8,128)S(1)}, f32[8,128]{1,0:T(8,128)S(1)}) custom-call(f32[8,8,128]{2,1,0:T(8,128)S(1)} %all-to-all-done.beads_ref, f32[3,256,128]{2,1,0:T(8,128)S(1)} %get-tuple-element.24.flow_ref, f32[20,16,128]{2,1,0:T(8,128)S(1)} %get-tuple-element.25.column_ref), custom_call_target="tpu_custom_call" | custom-call | tf_op jit(solution)/shard_map/couple/pallas_call | solution.py:385
  18.1 0.0 collective-permute-start
  18.1 1.2 %collective-permute-done.face_ref.refs_3_.refs_4_ = f32[2,16,128]{2,1,0:T(8,128)S(1)} collective-permute-done((f32[2,16,128]{2,1,0:T(8,128)S(1)}, f32[2,16,128]{2,1,0:T(8,128)S(1)}, u32[]{:S(2)}, u32[]{:S(2)}) %collective-permute-start) | collective-permute-done | bytes 16416 | tf_op jit(solution)/shard_map/ppermute | solution.py:141
  19.3 0.0 copy-done
  19.3 0.0 copy-done.2
  19.3 0.4 %faces.1 = (f32[88,128]{1,0:T(8,128)S(1)}, f32[88,128]{1,0:T(8,128)S(1)}, f32[160,128]{1,0:T(8,128)S(1)}, f32[8,128]{1,0:T(8,128)S(1)}) custom-call(f32[3,16,16,128]{3,2,1,0:T(8,128)S(1)} %get-tuple-element.26.force_ref.refs_2_.refs_3_, f32[19,16,16,128]{3,2,1,0:T(8,128)S(1)} %copy-done, s32[16,16,128]{2,1,0:T(8,128)S(1)} %copy-done.2, ...), custom_call_target="tpu_custom_call" | custom-call | tf_op jit(solution)/shard_map/faces/pallas_call | solution.py:446
  19.7 0.4 %collective-permute-start.1 = (f32[88,128]{1,0:T(8,128)S(1)}, f32[88,128]{1,0:T(8,128)S(1)}, u32[]{:S(2)}, u32[]{:S(2)}) collective-permute-start(f32[88,128]{1,0:T(8,128)S(1)} %get-tuple-element.34), channel_id=1, source_target_pairs={{0,4},{1,5},{2,6},{3,7},{4,0},{5,1},{6,2},{7,3},{8,12},{9,13},{10,... | collective-permute-start | bytes 135176 | tf_op jit(solution)/shard_map/ppermute | solution.py:141
  20.1 1.6 %collective-permute-start.2 = (f32[88,128]{1,0:T(8,128)S(1)}, f32[88,128]{1,0:T(8,128)S(1)}, u32[]{:S(2)}, u32[]{:S(2)}) collective-permute-start(f32[88,128]{1,0:T(8,128)S(1)} %get-tuple-element.35), channel_id=1, source_target_pairs={{0,12},{1,13},{2,14},{3,15},{4,8},{5,9},{6,10},{7,11},{8,4},{9,5},... | collective-permute-start | bytes 135176 | tf_op jit(solution)/shard_map/ppermute | solution.py:141
  21.7 1.5 %collective-permute-start.3 = (f32[8,128]{1,0:T(8,128)S(1)}, f32[8,128]{1,0:T(8,128)S(1)}, u32[]{:S(2)}, u32[]{:S(2)}) collective-permute-start(f32[8,128]{1,0:T(8,128)S(1)} %get-tuple-element.36), channel_id=1, source_target_pairs={{0,8},{1,9},{2,10},{3,11},{4,12},{5,13},{6,14},{7,15},{8,0},{9,1},... | collective-permute-start | bytes 12296 | tf_op jit(solution)/shard_map/ppermute | solution.py:141
  23.2 2.2 %stream.2 = (f32[19,16,16,128]{3,2,1,0:T(8,128)}, f32[10,8,8,128]{3,2,1,0:T(8,128)S(1)}, f32[8,128]{1,0:T(8,128)S(1)}) custom-call(f32[8,128]{1,0:T(8,128)S(1)} %get-tuple-element.31.before_ref, f32[19,16,16,128]{3,2,1,0:T(8,128)S(1)} %copy-done, s32[16,16,128]{2,1,0:T(8,128)S(1)} %copy-done.2, ...), custom_call_target="tpu_custom_call" | custom-call | flops 5000000 | bytes 3000000 | tf_op jit(solution)/shard_map/stream/pallas_call | solution.py:558
  25.3 0.8 %collective-permute-done.3.refs_1_.refs_2_ = f32[8,128]{1,0:T(8,128)S(1)} collective-permute-done((f32[8,128]{1,0:T(8,128)S(1)}, f32[8,128]{1,0:T(8,128)S(1)}, u32[]{:S(2)}, u32[]{:S(2)}) %collective-permute-start.3) | collective-permute-done | bytes 4128 | tf_op jit(solution)/shard_map/ppermute | solution.py:141
  26.2 0.0 collective-permute-done.1.first_ref
  26.2 0.0 collective-permute-done.2.second_ref
  26.2 0.9 %collective-permute-start.4 = (f32[192,128]{1,0:T(8,128)S(1)}, f32[192,128]{1,0:T(8,128)S(1)}, u32[]{:S(2)}, u32[]{:S(2)}) collective-permute-start(f32[192,128]{1,0:T(8,128)S(1)} %get-tuple-element.43), channel_id=1, source_target_pairs={{0,2},{1,3},{2,0},{3,1},{4,6},{5,7},{6,4},{7,5},{8,10},{9,11},{10,... | collective-permute-start | bytes 294920 | tf_op jit(solution)/shard_map/ppermute | solution.py:141
  27.1 2.8 %stream.3 = (f32[19,16,16,128]{3,2,1,0:T(8,128)}, f32[10,8,8,128]{3,2,1,0:T(8,128)S(1)}, f32[8,128]{1,0:T(8,128)}) custom-call(f32[8,128]{1,0:T(8,128)S(1)} %get-tuple-element.37.before_ref, f32[19,16,16,128]{3,2,1,0:T(8,128)} %get-tuple-element.38.refs_0_, f32[19,16,16,128]{3,2,1,0:T(8,128)S(1)} %copy-done, ...), custom_call_target="tpu_custom_call", output_to_operand_aliasing={{0}: (1, {})} | custom-call | flops 5000000 | bytes 3000000 | tf_op jit(solution)/shard_map/stream/pallas_call | solution.py:558
  30.0 0.9 %collective-permute-done.4.refs_0_ = f32[192,128]{1,0:T(8,128)S(1)} collective-permute-done((f32[192,128]{1,0:T(8,128)S(1)}, f32[192,128]{1,0:T(8,128)S(1)}, u32[]{:S(2)}, u32[]{:S(2)}) %collective-permute-start.4) | collective-permute-done | bytes 98336 | tf_op jit(solution)/shard_map/ppermute | solution.py:141
  30.9 0.0 copy-done.3
  30.9 1.6 %finish.1 = (f32[19,16,16,128]{3,2,1,0:T(8,128)}, f32[3,128]{1,0:T(4,128)}) custom-call(f32[19,16,16,128]{3,2,1,0:T(8,128)} %get-tuple-element.39.whole_ref, s32[1,128]{1,0:T(1,128)S(1)} %copy-done.3, f32[10,8,8,128]{3,2,1,0:T(8,128)S(1)} %get-tuple-element.41.lower_ref, ...), custom_call_target="tpu_custom_call", output_to_operand_aliasing={{0}: (0, {})} | custom-call | tf_op jit(solution)/shard_map/finish/pallas_call | solution.py:674
  (4 shorter events, 0.0 us)
Async XLA Ops:
  0.6 18.6 %copy-start = (f32[19,16,16,128]{3,2,1,0:T(8,128)S(1)}, f32[19,16,16,128]{3,2,1,0:T(8,128)}, u32[]{:S(2)}) copy-start(f32[19,16,16,128]{3,2,1,0:T(8,128)} %refs_1_.3) | copy-start | bytes 7471108
  2.5 13.9 %all-to-all-start = ((f32[8,8,128]{2,1,0:T(8,128)}), f32[8,8,128]{2,1,0:T(8,128)S(1)}, u32[]{:S(2)}, u32[]{:S(2)}) async-start(f32[8,8,128]{2,1,0:T(8,128)} %get-tuple-element.23), calls=%async_computation | async-start | bytes 65536 | tf_op jit(solution)/shard_map/all_to_all | solution.py:703
  9.8 0.9 %copy-start.1 = (s32[16,16,128]{2,1,0:T(8,128)S(1)}, s32[16,16,128]{2,1,0:T(8,128)}, u32[]{:S(2)}) copy-start(s32[16,16,128]{2,1,0:T(8,128)} %refs_2_.1) | copy-start | bytes 393220
  10.7 8.6 %copy-start.2 = (s32[16,16,128]{2,1,0:T(8,128)S(1)}, s32[16,16,128]{2,1,0:T(8,128)}, u32[]{:S(2)}) copy-start(s32[16,16,128]{2,1,0:T(8,128)} %refs_2_.1) | copy-start | bytes 393220
  18.1 1.2 %collective-permute-start = (f32[2,16,128]{2,1,0:T(8,128)S(1)}, f32[2,16,128]{2,1,0:T(8,128)S(1)}, u32[]{:S(2)}, u32[]{:S(2)}) collective-permute-start(f32[2,16,128]{2,1,0:T(8,128)S(1)} %get-tuple-element.29), channel_id=1, source_target_pairs={{0,1},{1,0},{2,3},{3,2},{4,5},{5,4},{6,7},{7,6},{8,9},{9,8},{10,11... | collective-permute-start | bytes 49160 | tf_op jit(solution)/shard_map/ppermute | solution.py:141
  19.7 6.5 %collective-permute-start.1 = (f32[88,128]{1,0:T(8,128)S(1)}, f32[88,128]{1,0:T(8,128)S(1)}, u32[]{:S(2)}, u32[]{:S(2)}) collective-permute-start(f32[88,128]{1,0:T(8,128)S(1)} %get-tuple-element.34), channel_id=1, source_target_pairs={{0,4},{1,5},{2,6},{3,7},{4,0},{5,1},{6,2},{7,3},{8,12},{9,13},{10,... | collective-permute-start | bytes 135176 | tf_op jit(solution)/shard_map/ppermute | solution.py:141
  20.1 6.1 %collective-permute-start.2 = (f32[88,128]{1,0:T(8,128)S(1)}, f32[88,128]{1,0:T(8,128)S(1)}, u32[]{:S(2)}, u32[]{:S(2)}) collective-permute-start(f32[88,128]{1,0:T(8,128)S(1)} %get-tuple-element.35), channel_id=1, source_target_pairs={{0,12},{1,13},{2,14},{3,15},{4,8},{5,9},{6,10},{7,11},{8,4},{9,5},... | collective-permute-start | bytes 135176 | tf_op jit(solution)/shard_map/ppermute | solution.py:141
  21.7 4.5 %collective-permute-start.3 = (f32[8,128]{1,0:T(8,128)S(1)}, f32[8,128]{1,0:T(8,128)S(1)}, u32[]{:S(2)}, u32[]{:S(2)}) collective-permute-start(f32[8,128]{1,0:T(8,128)S(1)} %get-tuple-element.36), channel_id=1, source_target_pairs={{0,8},{1,9},{2,10},{3,11},{4,12},{5,13},{6,14},{7,15},{8,0},{9,1},... | collective-permute-start | bytes 12296 | tf_op jit(solution)/shard_map/ppermute | solution.py:141
  26.2 4.7 %collective-permute-start.4 = (f32[192,128]{1,0:T(8,128)S(1)}, f32[192,128]{1,0:T(8,128)S(1)}, u32[]{:S(2)}, u32[]{:S(2)}) collective-permute-start(f32[192,128]{1,0:T(8,128)S(1)} %get-tuple-element.43), channel_id=1, source_target_pairs={{0,2},{1,3},{2,0},{3,1},{4,6},{5,7},{6,4},{7,5},{8,10},{9,11},{10,... | collective-permute-start | bytes 294920 | tf_op jit(solution)/shard_map/ppermute | solution.py:141
  27.1 3.7 %copy-start.3 = (s32[1,128]{1,0:T(1,128)S(1)}, s32[1,128]{1,0:T(1,128)}, u32[]{:S(2)}) copy-start(s32[1,128]{1,0:T(1,128)} %get-tuple-element.40.target_ref) | copy-start | bytes 1540

commit v9 on v8

--- a/solution.py
+++ b/solution.py
@@ -61,8 +61,7 @@
 
 
 def dot_split(left, right, dims):
-    a, b = high_low(left)
-    c, d = high_low(right)
+    (a, b), (c, d) = left, right
     mul = functools.partial(lax.dot_general, dimension_numbers=dims, preferred_element_type=F32)
     return mul(a, c) + (mul(a, d) + mul(b, c))
 
@@ -162,12 +161,9 @@
     return jnp.broadcast_to(tile[:, lane : lane + 1], tile.shape)
 
 
-def enter_x(value, i, column):
-    step = STEP[i, 0]
-    if step == 0:
-        return value
-    side = 0 if step == 1 else value.shape[1] - 1
-    return jnp.where(iota(value.shape, 1) == side, column, turn(value, step, 1))
+def patch_x(value, i, column):
+    side = 0 if STEP[i, 0] == 1 else value.shape[1] - 1
+    return jnp.where(iota(value.shape, 1) == side, column, value)
 
 
 def x_place(i):
@@ -243,7 +239,7 @@
 
 
 def moments_kernel(
-    pops_ref, solid_ref, flow_ref, column_ref, side_ref, wall_ref, held, held_solid, sem
+    pops_ref, solid_ref, high_ref, low_ref, column_ref, side_ref, wall_ref, held, held_solid, sem
 ):
     depth, rows, width = pops_ref.shape[1:]
     chunks = 4
@@ -262,7 +258,8 @@
         density, momentum = density_momentum(pops)
         inverse = 1.0 / density
         for axis in range(3):
-            flow_ref[axis, pl.ds(pl.multiple_of(z * rows, rows), rows)] = momentum[axis] * inverse
+            at = pl.ds(pl.multiple_of(axis * depth * rows + z * rows, rows), rows)
+            high_ref[at], low_ref[at] = high_low(momentum[axis] * inverse)
         return carry
 
     for k in range(chunks):
@@ -284,7 +281,8 @@
     return pl.pallas_call(
         moments_kernel,
         out_shape=[
-            jax.ShapeDtypeStruct((3, depth * rows, width), F32),
+            jax.ShapeDtypeStruct((3 * depth * rows, width), BF16),
+            jax.ShapeDtypeStruct((3 * depth * rows, width), BF16),
             jax.ShapeDtypeStruct((20, rows, 128), F32),
             jax.ShapeDtypeStruct((19, 2, depth, width), F32),
             jax.ShapeDtypeStruct((2, depth, width), jnp.int32),
@@ -308,7 +306,7 @@
 
 
 def couple_group(base, part, velocity, flow, depth, rows):
-    width, slots = flow.shape[1], GROUP * CAP
+    width, slots = flow[0].shape[1], GROUP * CAP
     start = base.astype(jnp.int32) - 1
 
     def hat(axis, length):
@@ -316,7 +314,7 @@
         low, share = start[axis : axis + 1], part[axis : axis + 1]
         return jnp.where(cell == low, 1.0 - share, 0.0) + jnp.where(cell == low + 1, share, 0.0)
 
-    hat_x, hat_y, hat_z = hat(0, width), hat(1, rows), hat(2, depth)
+    hat_x, hat_y, hat_z = high_low(hat(0, width)), hat(1, rows), hat(2, depth)
     weight = (hat_z[:, None, :] * hat_y[None, :, :]).reshape(depth * rows, slots)
     across = dot_split(flow, hat_x, NN)
     cells = depth * rows
@@ -326,13 +324,14 @@
     ]
     drag = [DRAG_COEF * (sampled[d] - velocity[d : d + 1]) for d in range(3)]
     spread = jnp.concatenate([weight * (-drag[d]) for d in range(3)], axis=0)
-    return drag, dot_split(spread, hat_x, NT)
-
-
-def couple_kernel(shape, depth, rows, beads_ref, flow_ref, column_ref, force_ref, face_ref, *drag_refs):
+    return drag, dot_split(high_low(spread), hat_x, NT)
+
+
+def couple_kernel(shape, depth, rows, beads_ref, high_ref, low_ref, *refs):
     slabs, cols, _ = shape
-    width = flow_ref.shape[2]
-    flow = flow_ref[...].reshape(3 * depth * rows, width)
+    column_ref, force_ref, face_ref, *drag_refs = refs
+    width = high_ref.shape[1]
+    flow = (high_ref[...], low_ref[...])
     hollow = jnp.zeros((5, GROUP * CAP), F32)
 
     if len(drag_refs) == 2:
@@ -378,7 +377,7 @@
 
 
 def couple(shape, beads, flow, columns, depth, rows):
-    width = flow.shape[2]
+    width = flow[0].shape[1]
     single = beads.shape[0] == GROUP
     tile = jax.ShapeDtypeStruct((8, 128), F32)
     drags = [jax.ShapeDtypeStruct((shape[0], 8, 128), F32), tile] if single else [beads]
@@ -391,65 +390,78 @@
         + [jax.ShapeDtypeStruct(d.shape, F32) for d in drags],
         compiler_params=pltpu.CompilerParams(vmem_limit_bytes=ROOM),
         name="couple",
-    )(beads, flow, columns)
-
-
-def faces_kernel(
-    force_ref, pops_ref, solid_ref, side_ref, wall_ref, face_ref, drag_ref, *refs
-):
-    first_ref, second_ref, draft_ref, token_ref, turned, leaving = refs
+    )(beads, *flow, columns)
+
+
+def faces_kernel(force_ref, pops_ref, solid_ref, side_ref, wall_ref, leaving_ref, draft_ref, token_ref):
     depth, rows, width = force_ref.shape[1:]
     token_ref[...] = jnp.zeros_like(token_ref)
-    tiles = [face_ref[0], face_ref[1]]
-    for n in range(2):
-        turned[n] = tiles[n].T
     for side in range(4):
         first = side % 2 == 0
+        group = 1 if first else 0
         if side < 2:
-            at = (0 if first else depth - 1, slice(None))
+            z = 0 if first else depth - 1
+            force = [force_ref[d, z] for d in range(3)]
+            pops, wall = [pops_ref[i, z] for i in range(19)], solid_ref[z]
         else:
-            at = (slice(None), 0 if first else rows - 1)
-        force = [force_ref[(d,) + at] for d in range(3)]
-        if side < 2:
-            pops, wall = [pops_ref[i, at[0]] for i in range(19)], solid_ref[at[0]]
-        else:
+            force = [force_ref[d, :, 0 if first else rows - 1, :] for d in range(3)]
             pops, wall = [side_ref[i, side - 2] for i in range(19)], wall_ref[side - 2]
         out = collide(pops, wall == 1, force)
-        axis = 2 if side < 2 else 1
-        group = 1 if first else 0
-        for k, i in enumerate(ENTER[axis][group]):
-            value = out[i]
-            if STEP[i, 0] != 0:
-                tile, lane = x_place(i)
-                if axis == 2:
-                    column = spread_column(tiles[tile], lane + 2 * at[0])
-                else:
-                    block = turned[tile, pl.ds(lane, depth, stride=2), :]
-                    column = jnp.broadcast_to(block[:, at[1] : at[1] + 1], (depth, width))
-                value = enter_x(value, i, column)
-            if axis == 2:
-                leaving[group, k * rows : (k + 1) * rows] = value
+        for k, i in enumerate(ENTER[2 if side < 2 else 1][group]):
+            value = turn(out[i], STEP[i, 0], 1)
+            if side < 2:
+                leaving_ref[group, k * rows : (k + 1) * rows] = value
             else:
                 row = (group * 5 + k) * depth
                 draft_ref[row : row + depth] = turn(value, STEP[i, 2], 0)
-    if leaving.shape[1] > 5 * rows:
-        leaving[0, 5 * rows : 5 * rows + 8] = drag_ref[drag_ref.shape[0] - 1]
-        leaving[1, 5 * rows : 5 * rows + 8] = drag_ref[1]
-    even = even_slab()
-    first_ref[...] = jnp.where(even, leaving[0], leaving[1])
-    second_ref[...] = jnp.where(even, leaving[1], leaving[0])
-
-
-def faces(single, force, pops, solid, sides, walls, face, drag):
+
+
+def faces(force, pops, solid, sides, walls):
     _, depth, rows, width = force.shape
-    message = jax.ShapeDtypeStruct((5 * rows + (8 if single else 0), width), F32)
     return pl.pallas_call(
         faces_kernel,
-        out_shape=[message, message, jax.ShapeDtypeStruct((10 * depth, width), F32), TOKEN],
-        scratch_shapes=[pltpu.VMEM((2, 128, rows), F32), pltpu.VMEM((2, *message.shape), F32)],
+        out_shape=[
+            jax.ShapeDtypeStruct((2, 5 * rows, width), F32),
+            jax.ShapeDtypeStruct((10 * depth, width), F32),
+            TOKEN,
+        ],
         compiler_params=pltpu.CompilerParams(vmem_limit_bytes=ROOM),
         name="faces",
-    )(force, pops, solid, sides, walls, face, drag)
+    )(force, pops, solid, sides, walls)
+
+
+def planes_kernel(depth, rows, leaving_ref, face_ref, drag_ref, first_ref, second_ref, token_ref):
+    width = leaving_ref.shape[2]
+    token_ref[...] = jnp.zeros_like(token_ref)
+    tiles = [face_ref[0], face_ref[1]]
+    even = even_slab()
+    for k in range(5):
+        at = slice(k * rows, (k + 1) * rows)
+        both = []
+        for group in range(2):
+            i = ENTER[2][group][k]
+            value = leaving_ref[group, at]
+            if STEP[i, 0] != 0:
+                tile, lane = x_place(i)
+                z = depth - 1 if group == 0 else 0
+                value = patch_x(value, i, spread_column(tiles[tile], lane + 2 * z))
+            both.append(value)
+        first_ref[at] = jnp.where(even, both[0], both[1])
+        second_ref[at] = jnp.where(even, both[1], both[0])
+    if first_ref.shape[0] > 5 * rows:
+        up, down = drag_ref[drag_ref.shape[0] - 1], drag_ref[1]
+        first_ref[5 * rows : 5 * rows + 8] = jnp.where(even, up, down)
+        second_ref[5 * rows : 5 * rows + 8] = jnp.where(even, down, up)
+
+
+def planes(single, rows, depth, leaving, face, drag):
+    message = jax.ShapeDtypeStruct((5 * rows + (8 if single else 0), leaving.shape[2]), F32)
+    return pl.pallas_call(
+        functools.partial(planes_kernel, depth, rows),
+        out_shape=[message, message, TOKEN],
+        compiler_params=pltpu.CompilerParams(vmem_limit_bytes=ROOM),
+        name="planes",
+    )(leaving, face, drag)
 
 
 def entered_z(first_ref, second_ref, side, rows):
@@ -457,17 +469,24 @@
     return jnp.where(even, second_ref[rows], first_ref[rows])
 
 
-def rows_kernel(depth, rows, before_ref, draft_ref, first_ref, second_ref, *refs):
-    refs, token_ref = refs[:-1], refs[-1]
+def rows_kernel(depth, rows, before_ref, draft_ref, face_ref, first_ref, second_ref, *refs):
+    refs, token_ref, turned = refs[:-2], refs[-2], refs[-1]
     token_ref[...] = jnp.zeros_like(token_ref)
     outs = refs[-1:] if len(refs) == 3 else refs
+    for n in range(2):
+        turned[n] = face_ref[n].T
     for group in range(2):
         out_ref = outs[0] if len(outs) == 1 else outs[group]
         base = group * 5 * depth if len(outs) == 1 else 0
         y = rows - 1 if group == 0 else 0
         for k, i in enumerate(ENTER[1][group]):
             at = base + k * depth
-            out_ref[at : at + depth] = draft_ref[(group * 5 + k) * depth : (group * 5 + k + 1) * depth]
+            value = draft_ref[(group * 5 + k) * depth : (group * 5 + k + 1) * depth]
+            if STEP[i, 0] != 0:
+                tile, lane = x_place(i)
+                column = turned[tile, pl.ds(lane, depth, stride=2), :][:, y : y + 1]
+                value = patch_x(value, i, jnp.broadcast_to(column, value.shape))
+            out_ref[at : at + depth] = value
             if STEP[i, 2] != 0:
                 side = 0 if STEP[i, 2] == 1 else 1
                 z = 0 if side == 0 else depth - 1
@@ -477,25 +496,33 @@
                 )
     if len(refs) == 3:
         own_ref, far_ref, out_ref = refs
-        at, tail = 10 * depth, 5 * rows
-        out_ref[at : at + 8] = own_ref[0]
-        out_ref[at + 8 : at + 16] = entered_z(first_ref, second_ref, 1, slice(tail, tail + 8))
-        out_ref[at + 16 : at + 24] = far_ref[...]
-        out_ref[at + 24 : at + 32] = entered_z(first_ref, second_ref, 0, slice(tail, tail + 8))
-
-
-def leaving_rows(shape, depth, rows, before, draft, first, second, drags):
+        came = arrived_drag(own_ref, far_ref, first_ref, second_ref, 5 * rows)
+        out_ref[10 * depth : 10 * depth + 8] = one_tile(came, 1)
+
+
+def arrived_drag(own_ref, far_ref, first_ref, second_ref, tail):
+    at = slice(tail, tail + 8)
+    up, down = [entered_z(first_ref, second_ref, side, at) for side in range(2)]
+    return [own_ref[0], down, far_ref[...], up]
+
+
+def one_tile(tiles, col):
+    return jnp.concatenate([t[:, col * CAP : (col + 1) * CAP] for t in tiles], axis=1)
+
+
+def leaving_rows(depth, rows, before, draft, face, first, second, drags):
     width = draft.shape[1]
     if drags:
-        sizes = [10 * depth + 8 * shape[0]]
+        sizes = [10 * depth + 8]
     else:
         sizes = [5 * depth] * 2
-    args = (draft, first, second, *drags)
+    args = (draft, face, first, second, *drags)
     return pl.pallas_call(
         functools.partial(rows_kernel, depth, rows),
         out_shape=[jax.ShapeDtypeStruct((n, width), F32) for n in sizes] + [TOKEN],
         in_specs=[pl.BlockSpec(memory_space=pl.ANY)]
         + [pl.BlockSpec(memory_space=pltpu.VMEM)] * len(args),
+        scratch_shapes=[pltpu.VMEM((2, 128, rows), F32)],
         compiler_params=pltpu.CompilerParams(vmem_limit_bytes=ROOM),
         name="rows",
     )(before, *args)
@@ -520,7 +547,8 @@
             value = out[i]
             if STEP[i, 0] != 0:
                 tile, lane = x_place(i)
-                value = enter_x(value, i, spread_column(faces[tile], lane))
+                value = turn(value, STEP[i, 0], 1)
+                value = patch_x(value, i, spread_column(faces[tile], lane))
             held[i, z - low] = turn(value, STEP[i, 1], 0)
         return tuple(pltpu.roll(f, 126, 1) for f in faces)
 
@@ -579,7 +607,7 @@
     shape, n_rows, whole_ref, target_ref, lower_ref, upper_ref, first_ref, second_ref, *refs
 ):
     row_refs, refs = refs[:n_rows], refs[n_rows:]
-    drag_refs, (out_ref, bead_ref, planes, tiles, sem) = refs[:-5], refs[-5:]
+    drag_refs, (out_ref, bead_ref, planes, tiles, bead, sem) = refs[:-6], refs[-6:]
     depth, rows, width = whole_ref.shape[1:]
 
     def entering(group, k):
@@ -626,28 +654,19 @@
     count = target_ref.shape[1]
     target = target_ref[...]
     if n_rows == 1:
-        own_ref, far_ref = drag_refs
         slabs, cols, _ = shape
-        at, tail = 10 * depth, 5 * rows
-        came = [
-            entered_z(first_ref, second_ref, side, slice(tail, tail + 8)) for side in range(2)
-        ]
-        direct = jnp.concatenate([own_ref[0], came[1], far_ref[...], came[0]], axis=0)
-        passed = row_refs[0][at : at + 8 * slabs]
-        table = jnp.where(iota(direct.shape, 1) < CAP, direct, passed)
+        came = arrived_drag(*drag_refs, first_ref, second_ref, 5 * rows)
+        passed = row_refs[0][10 * depth : 10 * depth + 8]
+        table = jnp.concatenate([one_tile(came, 0), passed], axis=1)
         owner = lax.shift_right_logical(target, 5)
-        slot = target - owner * CAP
         owner_slab = lax.shift_right_logical(owner, cols.bit_length() - 1)
         away_col = owner - owner_slab * cols - lax.axis_index("col")
         away_col = jnp.where(away_col < 0, away_col + cols, away_col)
         away_slab = owner_slab - lax.axis_index("slab")
         away_slab = jnp.where(away_slab < 0, away_slab + slabs, away_slab)
-        choose = (iota((128, count), 0) == away_col * CAP + slot).astype(F32).astype(BF16)
-        picked = dot_select(table, choose, NN)
-        total = jnp.where(away_slab == 0, picked[0:8], 0.0)
-        for dz in range(1, slabs):
-            total = total + jnp.where(away_slab == dz, picked[8 * dz : 8 * dz + 8], 0.0)
-        bead_ref[...] = total[0:3]
+        place = away_col * 128 + away_slab * CAP + target - owner * CAP
+        choose = (iota((256, count), 0) == place).astype(F32).astype(BF16)
+        total = dot_select(table, choose, NN)
     else:
         back_ref = drag_refs[0]
 
@@ -661,7 +680,8 @@
         total = lax.fori_loop(
             0, back_ref.shape[0] // GROUP, group, jnp.zeros((8, count), F32)
         )
-        bead_ref[...] = total[0:3]
+    bead[...] = total[0:3]
+    leave(bead, bead_ref)
     for copy in copies:
         copy.wait()
 
@@ -678,11 +698,12 @@
             jax.ShapeDtypeStruct((3, target.shape[1]), F32),
         ],
         in_specs=[hbm] + [vmem] * (len(args) - 1),
-        out_specs=[hbm, vmem],
+        out_specs=[hbm, hbm],
         scratch_shapes=[
             pltpu.VMEM((10, rows, width), F32),
             pltpu.VMEM((10, depth + 2, 8, width), F32),
-            pltpu.SemaphoreType.DMA((20,)),
+            pltpu.VMEM((3, target.shape[1]), F32),
+            pltpu.SemaphoreType.DMA((21,)),
         ],
         input_output_aliases={0: 0},
         compiler_params=pltpu.CompilerParams(vmem_limit_bytes=ROOM),
@@ -701,21 +722,20 @@
 
     target, messages = pack(owners, bead_owner, bead_base, bead_offset, bead_velocity)
     messages = swap(messages)
-    flow, columns, sides, walls = moments(populations, solid_mask)
+    *flow, columns, sides, walls = moments(populations, solid_mask)
     force, face, drag, *far = couple(shape, messages, flow, columns, depth, rows)
+    leaving, draft, token = faces(force, populations, solid_mask, sides, walls)
     face = send(face, shape, lambda s, c, p: (s, c, (p + 1) % pairs))
     if single:
         far = send(far[0], shape, lambda s, c, p: ((s + 2) % slabs, c, p))
     else:
         drag = swap(drag)
-    first, second, draft, token = faces(
-        single, force, populations, solid_mask, sides, walls, face, drag
-    )
+    first, second, token = planes(single, rows, depth, leaving, face, drag)
     first, second = send_slab(first, shape, 0), send_slab(second, shape, 1)
     fields = (populations, solid_mask, force, face)
     whole, lower, token = stream(0, depth // 2, token, None, *fields)
     drags = [drag, far] if single else []
-    *leaving, token = leaving_rows(shape, depth, rows, token, draft, first, second, drags)
+    *leaving, token = leaving_rows(depth, rows, token, draft, face, first, second, drags)
     entered = [
         send(value, shape, lambda s, c, p, sign=sign: (s, (c + sign) % cols, p))
         for value, sign in zip(leaving, (1, -1))

time: 32.7 us -> 31.9 us (0.976)
  waiting for transfers between devices: 5.9 us -> 4.92 us
    ppermute x5, waiting for transfers between devices: 2.88 us -> 1.91 us  [send(): return lax.ppermute(value, ('slab', 'col', 'pair'), perm)]
    pallas_call x1, Pallas kernels: 1.62 us -> 1.07 us  [finish(): pl.pallas_call(functools.partial(finish_kernel, shape, len(entered)), out...]
    pallas_call x2 -> x3, Pallas kernels: 3.13 us -> 3.66 us  [the longest x1 2.76 us: moments(): pl.pallas_call(moments_kernel, out_shape=[jax.ShapeDtypeStruct((3 * depth...]
  transfers between devices with their start and end apart: 6 -> 6, of which waited for: 4 -> 4; matrix products, arithmetic and copies ran while one was open for 0% -> 0% of each run, Pallas kernels for 24% -> 27%
where the time goes in v9:
time: 31.9 us; the launch traced here: 31.7 us
  Pallas kernels  13.4 us (42%)
  starting transfers between devices  11.7 us (37%)
  waiting for transfers between devices  4.92 us (15%)
  local copies, waits for them, and re-layouts  0.91 us (3%)
  between operations  0.71 us (2%)
    all_to_all x1, starting transfers between devices, shards(): messages = swap(messages)  7.25 us
    pallas_call x2, Pallas kernels, stream(): pl.pallas_call(functools.partial(stream_kernel, low, high), out_shape=[ja...  5 us
    ppermute x5, starting transfers between devices, send(): return lax.ppermute(value, ('slab', 'col', 'pair'), perm)  4.49 us
    all_to_all x1, waiting for transfers between devices, shards(): messages = swap(messages)  3.01 us
    pallas_call x1, Pallas kernels, moments(): pl.pallas_call(moments_kernel, out_shape=[jax.ShapeDtypeStruct((3 * depth...  2.76 us
    ppermute x5, waiting for transfers between devices, send(): return lax.ppermute(value, ('slab', 'col', 'pair'), perm)  1.91 us
    pallas_call x1, Pallas kernels, pack(): pl.pallas_call(functools.partial(pack_kernel, steps), out_shape=[jax.Shap...  1.89 us
    pallas_call x1, Pallas kernels, couple(): pl.pallas_call(functools.partial(couple_kernel, shape, depth, rows), out_...  1.6 us
  transfers between devices with their start and end apart: 6, of which 4 were waited for; matrix products, arithmetic and copies ran while one was open for 0% of the time, Pallas kernels for 27%

profile of v9, /device:TPU:0, one launch (start us, length us, event | category | flops | bytes accessed | tf_op | source)
XLA Modules:
  0.0 31.7 jit_solution(5626212549481235319)
XLA Ops:
  0.6 0.0 copy-start
  0.6 1.9 %pack.1 = (s32[1,128]{1,0:T(1,128)}, f32[8,8,128]{2,1,0:T(8,128)}) custom-call(s32[1,128]{1,0:T(1,128)} %bitcast.1, s32[3,128]{1,0:T(4,128)} %base_ref.1, f32[3,128]{1,0:T(4,128)} %offset_ref.1, f32[3,128]{1,0:T(4,128)} %velocity_ref.1), custom_call_target="tpu_custom_call" | custom-call | tf_op jit(solution)/shard_map/pack/pallas_call | solution.py:229
  2.5 7.3 %all-to-all-start = ((f32[8,8,128]{2,1,0:T(8,128)}), f32[8,8,128]{2,1,0:T(8,128)S(1)}, u32[]{:S(2)}, u32[]{:S(2)}) async-start(f32[8,8,128]{2,1,0:T(8,128)} %get-tuple-element.25), calls=%async_computation | async-start | bytes 65536 | tf_op jit(solution)/shard_map/all_to_all | solution.py:724
  9.8 0.9 %copy-done.1 = s32[16,16,128]{2,1,0:T(8,128)S(1)} copy-done((s32[16,16,128]{2,1,0:T(8,128)S(1)}, s32[16,16,128]{2,1,0:T(8,128)}, u32[]{:S(2)}) %copy-start.1) | copy-done | bytes 131096
  10.7 2.8 %moments.1 = (bf16[768,128]{1,0:T(8,128)(2,1)S(1)}, bf16[768,128]{1,0:T(8,128)(2,1)S(1)}, f32[20,16,128]{2,1,0:T(8,128)S(1)}, f32[19,2,16,128]{3,2,1,0:T(8,128)S(1)}, s32[2,16,128]{2,1,0:T(8,128)S(1)}) custom-call(f32[19,16,16,128]{3,2,1,0:T(8,128)} %refs_1_.3, s32[16,16,128]{2,1,0:T(8,128)S(1)} %copy-done.1), custom_call_target="tpu_custom_call" | custom-call | flops 3000000 | bytes 4000000 | tf_op jit(solution)/shard_map/moments/pallas_call | solution.py:281
  13.5 3.0 %all-to-all-done.beads_ref = f32[8,8,128]{2,1,0:T(8,128)S(1)} async-done(((f32[8,8,128]{2,1,0:T(8,128)}), f32[8,8,128]{2,1,0:T(8,128)S(1)}, u32[]{:S(2)}, u32[]{:S(2)}) %all-to-all-start) | async-done | bytes 32800 | tf_op jit(solution)/shard_map/all_to_all | solution.py:724
  16.5 1.6 %couple.1 = (f32[3,16,16,128]{3,2,1,0:T(8,128)S(1)}, f32[2,16,128]{2,1,0:T(8,128)S(1)}, f32[4,8,128]{2,1,0:T(8,128)S(1)}, f32[8,128]{1,0:T(8,128)S(1)}) custom-call(f32[8,8,128]{2,1,0:T(8,128)S(1)} %all-to-all-done.beads_ref, bf16[768,128]{1,0:T(8,128)(2,1)S(1)} %get-tuple-element.26.high_ref, bf16[768,128]{1,0:T(8,128)(2,1)S(1)} %get-tuple-element.27.low_ref, ...), custom_call_target="tpu_custom_call" | custom-call | tf_op jit(solution)/shard_map/couple/pallas_call | solution.py:384
  18.1 0.0 collective-permute-start
  18.1 0.0 copy-done
  18.1 0.8 %faces.1 = (f32[2,80,128]{2,1,0:T(8,128)S(1)}, f32[160,128]{1,0:T(8,128)S(1)}, f32[8,128]{1,0:T(8,128)}) custom-call(f32[3,16,16,128]{3,2,1,0:T(8,128)S(1)} %get-tuple-element.29.force_ref.refs_2_.refs_3_, f32[19,16,16,128]{3,2,1,0:T(8,128)S(1)} %copy-done, s32[16,16,128]{2,1,0:T(8,128)S(1)} %copy-done.2, f32[19,2,16,128]{3,2,1,0:T(8,128)S(1)} %get-tuple-element.30.side_ref, ...), custom_call_target="tpu_custom_call" | custom-call | tf_op jit(solution)/shard_map/faces/pallas_call | solution.py:421
  18.9 0.3 %collective-permute-done.face_ref.refs_3_.refs_4_ = f32[2,16,128]{2,1,0:T(8,128)S(1)} collective-permute-done((f32[2,16,128]{2,1,0:T(8,128)S(1)}, f32[2,16,128]{2,1,0:T(8,128)S(1)}, u32[]{:S(2)}, u32[]{:S(2)}) %collective-permute-start) | collective-permute-done | bytes 16416 | tf_op jit(solution)/shard_map/ppermute | solution.py:140
  19.3 0.1 planes.1
  19.4 0.4 %collective-permute-start.1 = (f32[88,128]{1,0:T(8,128)S(1)}, f32[88,128]{1,0:T(8,128)S(1)}, u32[]{:S(2)}, u32[]{:S(2)}) collective-permute-start(f32[88,128]{1,0:T(8,128)S(1)} %get-tuple-element.38), channel_id=1, source_target_pairs={{0,4},{1,5},{2,6},{3,7},{4,0},{5,1},{6,2},{7,3},{8,12},{9,13},{10,... | collective-permute-start | bytes 135176 | tf_op jit(solution)/shard_map/ppermute | solution.py:140
  19.8 1.6 %collective-permute-start.2 = (f32[88,128]{1,0:T(8,128)S(1)}, f32[88,128]{1,0:T(8,128)S(1)}, u32[]{:S(2)}, u32[]{:S(2)}) collective-permute-start(f32[88,128]{1,0:T(8,128)S(1)} %get-tuple-element.39), channel_id=1, source_target_pairs={{0,12},{1,13},{2,14},{3,15},{4,8},{5,9},{6,10},{7,11},{8,4},{9,5},... | collective-permute-start | bytes 135176 | tf_op jit(solution)/shard_map/ppermute | solution.py:140
  21.4 1.5 %collective-permute-start.3 = (f32[8,128]{1,0:T(8,128)S(1)}, f32[8,128]{1,0:T(8,128)S(1)}, u32[]{:S(2)}, u32[]{:S(2)}) collective-permute-start(f32[8,128]{1,0:T(8,128)S(1)} %get-tuple-element.40), channel_id=1, source_target_pairs={{0,8},{1,9},{2,10},{3,11},{4,12},{5,13},{6,14},{7,15},{8,0},{9,1},... | collective-permute-start | bytes 12296 | tf_op jit(solution)/shard_map/ppermute | solution.py:140
  22.9 2.2 %stream.2 = (f32[19,16,16,128]{3,2,1,0:T(8,128)}, f32[10,8,8,128]{3,2,1,0:T(8,128)S(1)}, f32[8,128]{1,0:T(8,128)S(1)}) custom-call(f32[8,128]{1,0:T(8,128)S(1)} %get-tuple-element.35.before_ref, f32[19,16,16,128]{3,2,1,0:T(8,128)S(1)} %copy-done, s32[16,16,128]{2,1,0:T(8,128)S(1)} %copy-done.2, ...), custom_call_target="tpu_custom_call" | custom-call | flops 5000000 | bytes 3000000 | tf_op jit(solution)/shard_map/stream/pallas_call | solution.py:586
  25.1 0.8 %collective-permute-done.3.refs_1_.refs_2_ = f32[8,128]{1,0:T(8,128)S(1)} collective-permute-done((f32[8,128]{1,0:T(8,128)S(1)}, f32[8,128]{1,0:T(8,128)S(1)}, u32[]{:S(2)}, u32[]{:S(2)}) %collective-permute-start.3) | collective-permute-done | bytes 4128 | tf_op jit(solution)/shard_map/ppermute | solution.py:140
  25.9 0.0 collective-permute-done.1.first_ref
  25.9 0.0 collective-permute-done.2.second_ref
  25.9 0.2 rows.1
  26.0 1.0 %collective-permute-start.4 = (f32[168,128]{1,0:T(8,128)S(1)}, f32[168,128]{1,0:T(8,128)S(1)}, u32[]{:S(2)}, u32[]{:S(2)}) collective-permute-start(f32[168,128]{1,0:T(8,128)S(1)} %get-tuple-element.47), channel_id=1, source_target_pairs={{0,2},{1,3},{2,0},{3,1},{4,6},{5,7},{6,4},{7,5},{8,10},{9,11},{10,... | collective-permute-start | bytes 258056 | tf_op jit(solution)/shard_map/ppermute | solution.py:140
  27.0 2.8 %stream.3 = (f32[19,16,16,128]{3,2,1,0:T(8,128)}, f32[10,8,8,128]{3,2,1,0:T(8,128)S(1)}, f32[8,128]{1,0:T(8,128)}) custom-call(f32[8,128]{1,0:T(8,128)S(1)} %get-tuple-element.41.before_ref, f32[19,16,16,128]{3,2,1,0:T(8,128)} %get-tuple-element.42.refs_0_, f32[19,16,16,128]{3,2,1,0:T(8,128)S(1)} %copy-done, ...), custom_call_target="tpu_custom_call", output_to_operand_aliasing={{0}: (1, {})} | custom-call | flops 5000000 | bytes 3000000 | tf_op jit(solution)/shard_map/stream/pallas_call | solution.py:586
  29.8 0.8 %collective-permute-done.4.refs_0_ = f32[168,128]{1,0:T(8,128)S(1)} collective-permute-done((f32[168,128]{1,0:T(8,128)S(1)}, f32[168,128]{1,0:T(8,128)S(1)}, u32[]{:S(2)}, u32[]{:S(2)}) %collective-permute-start.4) | collective-permute-done | bytes 86048 | tf_op jit(solution)/shard_map/ppermute | solution.py:140
  30.6 1.1 %finish.1 = (f32[19,16,16,128]{3,2,1,0:T(8,128)}, f32[3,128]{1,0:T(4,128)}) custom-call(f32[19,16,16,128]{3,2,1,0:T(8,128)} %get-tuple-element.43.whole_ref, s32[1,128]{1,0:T(1,128)S(1)} %copy-done.3, f32[10,8,8,128]{3,2,1,0:T(8,128)S(1)} %get-tuple-element.45.lower_ref, ...), custom_call_target="tpu_custom_call", output_to_operand_aliasing={{0}: (0, {})} | custom-call | tf_op jit(solution)/shard_map/finish/pallas_call | solution.py:694
  (5 shorter events, 0.0 us)
Async XLA Ops:
  0.6 17.5 %copy-start = (f32[19,16,16,128]{3,2,1,0:T(8,128)S(1)}, f32[19,16,16,128]{3,2,1,0:T(8,128)}, u32[]{:S(2)}) copy-start(f32[19,16,16,128]{3,2,1,0:T(8,128)} %refs_1_.3) | copy-start | bytes 7471108
  2.5 13.9 %all-to-all-start = ((f32[8,8,128]{2,1,0:T(8,128)}), f32[8,8,128]{2,1,0:T(8,128)S(1)}, u32[]{:S(2)}, u32[]{:S(2)}) async-start(f32[8,8,128]{2,1,0:T(8,128)} %get-tuple-element.25), calls=%async_computation | async-start | bytes 65536 | tf_op jit(solution)/shard_map/all_to_all | solution.py:724
  9.8 0.9 %copy-start.1 = (s32[16,16,128]{2,1,0:T(8,128)S(1)}, s32[16,16,128]{2,1,0:T(8,128)}, u32[]{:S(2)}) copy-start(s32[16,16,128]{2,1,0:T(8,128)} %refs_2_.1) | copy-start | bytes 393220
  10.7 7.4 %copy-start.2 = (s32[16,16,128]{2,1,0:T(8,128)S(1)}, s32[16,16,128]{2,1,0:T(8,128)}, u32[]{:S(2)}) copy-start(s32[16,16,128]{2,1,0:T(8,128)} %refs_2_.1) | copy-start | bytes 393220
  18.1 1.2 %collective-permute-start = (f32[2,16,128]{2,1,0:T(8,128)S(1)}, f32[2,16,128]{2,1,0:T(8,128)S(1)}, u32[]{:S(2)}, u32[]{:S(2)}) collective-permute-start(f32[2,16,128]{2,1,0:T(8,128)S(1)} %get-tuple-element.33), channel_id=1, source_target_pairs={{0,1},{1,0},{2,3},{3,2},{4,5},{5,4},{6,7},{7,6},{8,9},{9,8},{10,11... | collective-permute-start | bytes 49160 | tf_op jit(solution)/shard_map/ppermute | solution.py:140
  19.4 6.5 %collective-permute-start.1 = (f32[88,128]{1,0:T(8,128)S(1)}, f32[88,128]{1,0:T(8,128)S(1)}, u32[]{:S(2)}, u32[]{:S(2)}) collective-permute-start(f32[88,128]{1,0:T(8,128)S(1)} %get-tuple-element.38), channel_id=1, source_target_pairs={{0,4},{1,5},{2,6},{3,7},{4,0},{5,1},{6,2},{7,3},{8,12},{9,13},{10,... | collective-permute-start | bytes 135176 | tf_op jit(solution)/shard_map/ppermute | solution.py:140
  19.8 6.1 %collective-permute-start.2 = (f32[88,128]{1,0:T(8,128)S(1)}, f32[88,128]{1,0:T(8,128)S(1)}, u32[]{:S(2)}, u32[]{:S(2)}) collective-permute-start(f32[88,128]{1,0:T(8,128)S(1)} %get-tuple-element.39), channel_id=1, source_target_pairs={{0,12},{1,13},{2,14},{3,15},{4,8},{5,9},{6,10},{7,11},{8,4},{9,5},... | collective-permute-start | bytes 135176 | tf_op jit(solution)/shard_map/ppermute | solution.py:140
  21.4 4.5 %collective-permute-start.3 = (f32[8,128]{1,0:T(8,128)S(1)}, f32[8,128]{1,0:T(8,128)S(1)}, u32[]{:S(2)}, u32[]{:S(2)}) collective-permute-start(f32[8,128]{1,0:T(8,128)S(1)} %get-tuple-element.40), channel_id=1, source_target_pairs={{0,8},{1,9},{2,10},{3,11},{4,12},{5,13},{6,14},{7,15},{8,0},{9,1},... | collective-permute-start | bytes 12296 | tf_op jit(solution)/shard_map/ppermute | solution.py:140
  26.0 4.6 %collective-permute-start.4 = (f32[168,128]{1,0:T(8,128)S(1)}, f32[168,128]{1,0:T(8,128)S(1)}, u32[]{:S(2)}, u32[]{:S(2)}) collective-permute-start(f32[168,128]{1,0:T(8,128)S(1)} %get-tuple-element.47), channel_id=1, source_target_pairs={{0,2},{1,3},{2,0},{3,1},{4,6},{5,7},{6,4},{7,5},{8,10},{9,11},{10,... | collective-permute-start | bytes 258056 | tf_op jit(solution)/shard_map/ppermute | solution.py:140
  27.0 3.6 %copy-start.3 = (s32[1,128]{1,0:T(1,128)S(1)}, s32[1,128]{1,0:T(1,128)}, u32[]{:S(2)}) copy-start(s32[1,128]{1,0:T(1,128)} %get-tuple-element.44.target_ref) | copy-start | bytes 1540

commit v10 on v9

--- a/solution.py
+++ b/solution.py
@@ -327,14 +327,16 @@
     return drag, dot_split(high_low(spread), hat_x, NT)
 
 
-def couple_kernel(shape, depth, rows, beads_ref, high_ref, low_ref, *refs):
+def couple_kernel(shape, depth, rows, n_drags, beads_ref, high_ref, low_ref, *refs):
     slabs, cols, _ = shape
-    column_ref, force_ref, face_ref, *drag_refs = refs
+    column_ref, pops_ref, solid_ref, force_ref, face_ref, first_ref, second_ref, *refs = refs
+    drag_refs, token_ref = refs[:-1], refs[-1]
+    token_ref[...] = jnp.zeros_like(token_ref)
     width = high_ref.shape[1]
     flow = (high_ref[...], low_ref[...])
     hollow = jnp.zeros((5, GROUP * CAP), F32)
 
-    if len(drag_refs) == 2:
+    if n_drags == 2:
         slab, col = lax.axis_index("slab"), lax.axis_index("col")
         got = []
         for r in range(GROUP):
@@ -351,6 +353,9 @@
             drag_refs[0][dz] = tile
             if dz == 2:
                 drag_refs[1][...] = tile
+            if dz == 1:
+                down = tile
+        up = tile
     else:
         force_ref[...] = jnp.zeros_like(force_ref)
         blank = jnp.zeros((8, 128 - CAP), F32)
@@ -376,92 +381,45 @@
     face_ref[1] = jnp.concatenate([ends[4], jnp.zeros((rows, 96), F32)], axis=1)
 
 
-def couple(shape, beads, flow, columns, depth, rows):
+    even = even_slab()
+    leaving = []
+    for group, z in ((0, depth - 1), (1, 0)):
+        out = collide(
+            [pops_ref[i, z] for i in range(19)],
+            solid_ref[z] == 1,
+            [force_ref[d, z] for d in range(3)],
+        )
+        leaving.append([turn(out[i], STEP[i, 0], 1) for i in ENTER[2][group]])
+    if n_drags == 2:
+        leaving[0].append(up)
+        leaving[1].append(down)
+    row = 0
+    for a, b in zip(*leaving):
+        at = slice(row, row + a.shape[0])
+        first_ref[at] = jnp.where(even, a, b)
+        second_ref[at] = jnp.where(even, b, a)
+        row += a.shape[0]
+
+
+def couple(shape, beads, flow, columns, pops, solid, depth, rows):
     width = flow[0].shape[1]
     single = beads.shape[0] == GROUP
     tile = jax.ShapeDtypeStruct((8, 128), F32)
     drags = [jax.ShapeDtypeStruct((shape[0], 8, 128), F32), tile] if single else [beads]
+    message = jax.ShapeDtypeStruct((5 * rows + (8 if single else 0), width), F32)
     return pl.pallas_call(
-        functools.partial(couple_kernel, shape, depth, rows),
+        functools.partial(couple_kernel, shape, depth, rows, len(drags)),
         out_shape=[
             jax.ShapeDtypeStruct((3, depth, rows, width), F32),
             jax.ShapeDtypeStruct((2, rows, 128), F32),
+            message,
+            message,
         ]
-        + [jax.ShapeDtypeStruct(d.shape, F32) for d in drags],
+        + [jax.ShapeDtypeStruct(d.shape, F32) for d in drags]
+        + [TOKEN],
         compiler_params=pltpu.CompilerParams(vmem_limit_bytes=ROOM),
         name="couple",
-    )(beads, *flow, columns)
-
-
-def faces_kernel(force_ref, pops_ref, solid_ref, side_ref, wall_ref, leaving_ref, draft_ref, token_ref):
-    depth, rows, width = force_ref.shape[1:]
-    token_ref[...] = jnp.zeros_like(token_ref)
-    for side in range(4):
-        first = side % 2 == 0
-        group = 1 if first else 0
-        if side < 2:
-            z = 0 if first else depth - 1
-            force = [force_ref[d, z] for d in range(3)]
-            pops, wall = [pops_ref[i, z] for i in range(19)], solid_ref[z]
-        else:
-            force = [force_ref[d, :, 0 if first else rows - 1, :] for d in range(3)]
-            pops, wall = [side_ref[i, side - 2] for i in range(19)], wall_ref[side - 2]
-        out = collide(pops, wall == 1, force)
-        for k, i in enumerate(ENTER[2 if side < 2 else 1][group]):
-            value = turn(out[i], STEP[i, 0], 1)
-            if side < 2:
-                leaving_ref[group, k * rows : (k + 1) * rows] = value
-            else:
-                row = (group * 5 + k) * depth
-                draft_ref[row : row + depth] = turn(value, STEP[i, 2], 0)
-
-
-def faces(force, pops, solid, sides, walls):
-    _, depth, rows, width = force.shape
-    return pl.pallas_call(
-        faces_kernel,
-        out_shape=[
-            jax.ShapeDtypeStruct((2, 5 * rows, width), F32),
-            jax.ShapeDtypeStruct((10 * depth, width), F32),
-            TOKEN,
-        ],
-        compiler_params=pltpu.CompilerParams(vmem_limit_bytes=ROOM),
-        name="faces",
-    )(force, pops, solid, sides, walls)
-
-
-def planes_kernel(depth, rows, leaving_ref, face_ref, drag_ref, first_ref, second_ref, token_ref):
-    width = leaving_ref.shape[2]
-    token_ref[...] = jnp.zeros_like(token_ref)
-    tiles = [face_ref[0], face_ref[1]]
-    even = even_slab()
-    for k in range(5):
-        at = slice(k * rows, (k + 1) * rows)
-        both = []
-        for group in range(2):
-            i = ENTER[2][group][k]
-            value = leaving_ref[group, at]
-            if STEP[i, 0] != 0:
-                tile, lane = x_place(i)
-                z = depth - 1 if group == 0 else 0
-                value = patch_x(value, i, spread_column(tiles[tile], lane + 2 * z))
-            both.append(value)
-        first_ref[at] = jnp.where(even, both[0], both[1])
-        second_ref[at] = jnp.where(even, both[1], both[0])
-    if first_ref.shape[0] > 5 * rows:
-        up, down = drag_ref[drag_ref.shape[0] - 1], drag_ref[1]
-        first_ref[5 * rows : 5 * rows + 8] = jnp.where(even, up, down)
-        second_ref[5 * rows : 5 * rows + 8] = jnp.where(even, down, up)
-
-
-def planes(single, rows, depth, leaving, face, drag):
-    message = jax.ShapeDtypeStruct((5 * rows + (8 if single else 0), leaving.shape[2]), F32)
-    return pl.pallas_call(
-        functools.partial(planes_kernel, depth, rows),
-        out_shape=[message, message, TOKEN],
-        compiler_params=pltpu.CompilerParams(vmem_limit_bytes=ROOM),
-        name="planes",
-    )(leaving, face, drag)
+    )(beads, *flow, columns, pops, solid)
 
 
 def entered_z(first_ref, second_ref, side, rows):
@@ -469,8 +427,11 @@
     return jnp.where(even, second_ref[rows], first_ref[rows])
 
 
+X_EDGES = [i for side in range(2) for i in ENTER[2][side] if STEP[i, 0] != 0]
+
+
 def rows_kernel(depth, rows, before_ref, draft_ref, face_ref, first_ref, second_ref, *refs):
-    refs, token_ref, turned = refs[:-2], refs[-2], refs[-1]
+    refs, (cross_ref, token_ref, turned) = refs[:-3], refs[-3:]
     token_ref[...] = jnp.zeros_like(token_ref)
     outs = refs[-1:] if len(refs) == 3 else refs
     for n in range(2):
@@ -498,6 +459,12 @@
         own_ref, far_ref, out_ref = refs
         came = arrived_drag(own_ref, far_ref, first_ref, second_ref, 5 * rows)
         out_ref[10 * depth : 10 * depth + 8] = one_tile(came, 1)
+    for k, i in enumerate(X_EDGES):
+        side = 0 if STEP[i, 2] == 1 else 1
+        at = ENTER[2][side].index(i) * rows
+        cross_ref[k * rows : (k + 1) * rows] = entered_z(
+            first_ref, second_ref, side, slice(at, at + rows)
+        )
 
 
 def arrived_drag(own_ref, far_ref, first_ref, second_ref, tail):
@@ -519,7 +486,7 @@
     args = (draft, face, first, second, *drags)
     return pl.pallas_call(
         functools.partial(rows_kernel, depth, rows),
-        out_shape=[jax.ShapeDtypeStruct((n, width), F32) for n in sizes] + [TOKEN],
+        out_shape=[jax.ShapeDtypeStruct((n, width), F32) for n in sizes + [4 * rows]] + [TOKEN],
         in_specs=[pl.BlockSpec(memory_space=pl.ANY)]
         + [pl.BlockSpec(memory_space=pltpu.VMEM)] * len(args),
         scratch_shapes=[pltpu.VMEM((2, 128, rows), F32)],
@@ -528,15 +495,17 @@
     )(before, *args)
 
 
-def stream_kernel(low, high, before_ref, *refs):
-    if low > 0:
-        refs = refs[1:]
-    pops_ref, solid_ref, force_ref, face_ref, out_ref, tile_ref, token_ref, held, sem = refs
-    depth, rows, width = pops_ref.shape[1:]
-    token_ref[...] = jnp.zeros_like(token_ref)
-    chunks = 2
-    span = (high - low) // chunks
-
+def runs(members):
+    found = []
+    for i in members:
+        if found and found[-1][1] == i and STEP[i, 2] == STEP[i - 1, 2]:
+            found[-1] = (found[-1][0], i + 1)
+        else:
+            found.append((i, i + 1))
+    return found
+
+
+def stream_planes(low, high, faces, pops_ref, solid_ref, force_ref, held):
     def plane(z, faces):
         out = collide(
             [pops_ref[i, z] for i in range(19)],
@@ -544,77 +513,125 @@
             [force_ref[d, z] for d in range(3)],
         )
         for i in range(19):
-            value = out[i]
-            if STEP[i, 0] != 0:
+            value = turn(out[i], STEP[i, 0], 1)
+            if STEP[i, 0] != 0 and faces:
                 tile, lane = x_place(i)
-                value = turn(value, STEP[i, 0], 1)
                 value = patch_x(value, i, spread_column(faces[tile], lane))
-            held[i, z - low] = turn(value, STEP[i, 1], 0)
+            held[i, z] = turn(value, STEP[i, 1], 0)
         return tuple(pltpu.roll(f, 126, 1) for f in faces)
 
-    runs = [(0, 5), (5, 6), (6, 7), (7, 11)] + [(i, i + 1) for i in range(11, 19)]
+    return lax.fori_loop(low, high, plane, faces, unroll=2)
+
+
+def lower_kernel(
+    before_ref, pops_ref, solid_ref, force_ref, side_ref, wall_ref, held, draft_ref, token_ref
+):
+    depth, rows, _ = pops_ref.shape[1:]
+    token_ref[...] = jnp.zeros_like(token_ref)
+    for group in range(2):
+        force = [force_ref[d, :, 0 if group else rows - 1, :] for d in range(3)]
+        out = collide([side_ref[i, 1 - group] for i in range(19)], wall_ref[1 - group] == 1, force)
+        for k, i in enumerate(ENTER[1][group]):
+            row = (group * 5 + k) * depth
+            value = turn(out[i], STEP[i, 0], 1)
+            draft_ref[row : row + depth] = turn(value, STEP[i, 2], 0)
+    stream_planes(0, held.shape[1], (), pops_ref, solid_ref, force_ref, held)
+
+
+def upper_kernel(
+    before_ref, lower_ref, pops_ref, solid_ref, force_ref, face_ref, out_ref, tile_ref, held, sem
+):
+    depth, rows, width = pops_ref.shape[1:]
+    half = lower_ref.shape[1]
     copies = []
-    carry = (face_ref[0], face_ref[1])
-    if low > 0:
-        carry = tuple(pltpu.roll(f, 128 - 2 * low, 1) for f in carry)
-    for k in range(chunks):
-        first = low + k * span
-        carry = lax.fori_loop(first, first + span, plane, carry, unroll=2)
-        for n, (a, b) in enumerate(runs):
+
+    def leave(source, members, low, high):
+        for a, b in runs(members):
             step = int(STEP[a, 2])
-            start, stop = max(first + step, 0), min(first + span + step, depth)
+            start, stop = max(low + step, 0), min(high + step, depth)
             copy = pltpu.make_async_copy(
-                held.at[a:b, start - step - low : stop - step - low],
+                source.at[a:b, start - step : stop - step],
                 out_ref.at[a:b, start:stop],
-                sem.at[k, n],
+                sem.at[len(copies)],
             )
             copy.start()
             copies.append(copy)
+
+    straight = [i for i in range(19) if STEP[i, 0] == 0]
+    across = [i for i in range(19) if STEP[i, 0] != 0]
+    leave(lower_ref, straight, 0, half)
+    faces = (face_ref[0], face_ref[1])
+    for i in across:
+        tile, lane = x_place(i)
+        for z in range(half):
+            column = turn(spread_column(faces[tile], lane + 2 * z), STEP[i, 1], 0)
+            held[i, z] = patch_x(lower_ref[i, z], i, column)
+    leave(held, across, 0, half)
+    faces = tuple(pltpu.roll(f, 128 - 2 * half, 1) for f in faces)
+    marks = upper_marks(half, depth)
+    for low, high in zip(marks, marks[1:]):
+        faces = stream_planes(low, high, faces, pops_ref, solid_ref, force_ref, held)
+        leave(held, range(19), low, high)
     for group in range(2):
-        first = 0 if group == 0 else rows - 8
+        first = slice(0, 8) if group == 0 else slice(rows - 8, rows)
         for k, i in enumerate(ENTER[1][group]):
-            tile_ref[group * 5 + k] = held[i, :, first : first + 8, :]
+            source = lower_ref if i in straight else held
+            tile_ref[group * 5 + k, 0:half] = source[i, 0:half, first, :]
+            tile_ref[group * 5 + k, half:depth] = held[i, half:depth, first, :]
     for copy in copies:
         copy.wait()
 
 
-def stream(low, high, before, whole, pops, solid, force, face):
+def upper_marks(half, depth):
+    return list(range(half, depth - 2, 4)) + ([depth - 2] if (depth - half) % 4 else []) + [depth]
+
+
+def stream_lower(half, before, pops, solid, force, sides, walls):
     _, depth, rows, width = pops.shape
     vmem = pl.BlockSpec(memory_space=pltpu.VMEM)
-    hbm = pl.BlockSpec(memory_space=pltpu.HBM)
-    whole = [] if whole is None else [whole]
     return pl.pallas_call(
-        functools.partial(stream_kernel, low, high),
+        lower_kernel,
+        out_shape=[
+            jax.ShapeDtypeStruct((19, half, rows, width), F32),
+            jax.ShapeDtypeStruct((10 * depth, width), F32),
+            TOKEN,
+        ],
+        in_specs=[pl.BlockSpec(memory_space=pl.ANY)] + [vmem] * 5,
+        compiler_params=pltpu.CompilerParams(vmem_limit_bytes=ROOM),
+        cost_estimate=pl.CostEstimate(flops=3000000, bytes_accessed=2000000, transcendentals=0),
+        name="lower",
+    )(before, pops, solid, force, sides, walls)
+
+
+def stream_upper(before, lower, pops, solid, force, face):
+    _, depth, rows, width = pops.shape
+    vmem = pl.BlockSpec(memory_space=pltpu.VMEM)
+    return pl.pallas_call(
+        upper_kernel,
         out_shape=[
             jax.ShapeDtypeStruct(pops.shape, F32),
-            jax.ShapeDtypeStruct((10, high - low, 8, width), F32),
-            TOKEN,
+            jax.ShapeDtypeStruct((10, depth, 8, width), F32),
         ],
-        in_specs=[pl.BlockSpec(memory_space=pl.ANY)] + [hbm] * len(whole) + [vmem] * 4,
-        out_specs=[hbm, vmem, vmem],
+        in_specs=[pl.BlockSpec(memory_space=pl.ANY)] + [vmem] * 5,
+        out_specs=[pl.BlockSpec(memory_space=pltpu.HBM), vmem],
         scratch_shapes=[
-            pltpu.VMEM((19, high - low, rows, width), F32),
-            pltpu.SemaphoreType.DMA((2, 12)),
+            pltpu.VMEM(pops.shape, F32),
+            pltpu.SemaphoreType.DMA((20 * len(upper_marks(lower.shape[1], depth)),)),
         ],
-        input_output_aliases={1: 0} if whole else {},
         compiler_params=pltpu.CompilerParams(vmem_limit_bytes=ROOM),
         cost_estimate=pl.CostEstimate(flops=5000000, bytes_accessed=3000000, transcendentals=0),
-        name="stream",
-    )(before, *whole, pops, solid, force, face)
-
-
-def finish_kernel(
-    shape, n_rows, whole_ref, target_ref, lower_ref, upper_ref, first_ref, second_ref, *refs
-):
-    row_refs, refs = refs[:n_rows], refs[n_rows:]
+        name="upper",
+    )(before, lower, pops, solid, force, face)
+
+
+def finish_kernel(shape, n_rows, whole_ref, target_ref, tile_ref, first_ref, second_ref, *refs):
+    row_refs, cross_ref, refs = refs[:n_rows], refs[n_rows], refs[n_rows + 1 :]
     drag_refs, (out_ref, bead_ref, planes, tiles, bead, sem) = refs[:-6], refs[-6:]
     depth, rows, width = whole_ref.shape[1:]
 
     def entering(group, k):
-        if n_rows == 1:
-            at = (group * 5 + k) * depth
-            return row_refs[0][at : at + depth]
-        return row_refs[group][k * depth : (k + 1) * depth]
+        at = (group * 5 + k) * depth if n_rows == 1 else k * depth
+        return row_refs[group % n_rows][at : at + depth]
 
     copies = []
 
@@ -629,13 +646,16 @@
             value = entered_z(first_ref, second_ref, group, slice(k * rows, (k + 1) * rows))
             if STEP[i, 1] != 0:
                 side = 0 if STEP[i, 1] == 1 else 1
+                y = 0 if side == 0 else rows - 1
                 row = entering(side, ENTER[1][side].index(i))[z : z + 1]
-                y = 0 if side == 0 else rows - 1
                 value = jnp.where(
                     iota((rows, width), 0) == y,
                     jnp.broadcast_to(row, (rows, width)),
                     turn(value, STEP[i, 1], 0),
                 )
+            if STEP[i, 0] != 0:
+                at = X_EDGES.index(i) * rows
+                value = patch_x(value, i, cross_ref[at : at + rows])
             n = group * 5 + k
             planes[n] = value
             leave(planes.at[n], out_ref.at[i, z])
@@ -644,16 +664,14 @@
         for k, i in enumerate(ENTER[1][group]):
             n = group * 5 + k
             step = int(STEP[i, 2])
-            half = lower_ref.shape[1]
-            tiles[n, 1 + step : 1 + step + half] = lower_ref[n]
-            tiles[n, 1 + step + half : 1 + step + depth] = upper_ref[n]
+            tiles[n, 1 + step : 1 + step + depth] = tile_ref[n]
             tiles[n, 1 : 1 + depth, 0 if group == 0 else 7, :] = entering(group, k)
             low, high = max(step, 0), min(depth + step, depth)
             leave(tiles.at[n, 1 + low : 1 + high], out_ref.at[i, low:high, first : first + 8])
 
     count = target_ref.shape[1]
     target = target_ref[...]
-    if n_rows == 1:
+    if len(drag_refs) == 2:
         slabs, cols, _ = shape
         came = arrived_drag(*drag_refs, first_ref, second_ref, 5 * rows)
         passed = row_refs[0][10 * depth : 10 * depth + 8]
@@ -686,11 +704,11 @@
         copy.wait()
 
 
-def finish(shape, whole, target, lower, upper, first, second, entered, drags):
+def finish(shape, whole, target, tiles, first, second, entered, cross, drags):
     _, depth, rows, width = whole.shape
     vmem = pl.BlockSpec(memory_space=pltpu.VMEM)
     hbm = pl.BlockSpec(memory_space=pltpu.HBM)
-    args = [whole, target, lower, upper, first, second, *entered, *drags]
+    args = [whole, target, tiles, first, second, *entered, cross, *drags]
     return pl.pallas_call(
         functools.partial(finish_kernel, shape, len(entered)),
         out_shape=[
@@ -723,26 +741,33 @@
     target, messages = pack(owners, bead_owner, bead_base, bead_offset, bead_velocity)
     messages = swap(messages)
     *flow, columns, sides, walls = moments(populations, solid_mask)
-    force, face, drag, *far = couple(shape, messages, flow, columns, depth, rows)
-    leaving, draft, token = faces(force, populations, solid_mask, sides, walls)
-    face = send(face, shape, lambda s, c, p: (s, c, (p + 1) % pairs))
+    force, face, first, second, drag, *far, token = couple(
+        shape, messages, flow, columns, populations, solid_mask, depth, rows
+    )
+
+    def send_pair(value):
+        return send(value, shape, lambda s, c, p: (s, c, (p + 1) % pairs))
+
+    def send_col(values):
+        return [
+            send(value, shape, lambda s, c, p, sign=sign: (s, (c + sign) % cols, p))
+            for value, sign in zip(values, (1, -1))
+        ]
+
+    face = send_pair(face)
+    first, second = send_slab(first, shape, 0), send_slab(second, shape, 1)
     if single:
-        far = send(far[0], shape, lambda s, c, p: ((s + 2) % slabs, c, p))
+        drags = [drag, send(far[0], shape, lambda s, c, p: ((s + 2) % slabs, c, p))]
     else:
+        drags = []
         drag = swap(drag)
-    first, second, token = planes(single, rows, depth, leaving, face, drag)
-    first, second = send_slab(first, shape, 0), send_slab(second, shape, 1)
-    fields = (populations, solid_mask, force, face)
-    whole, lower, token = stream(0, depth // 2, token, None, *fields)
-    drags = [drag, far] if single else []
-    *leaving, token = leaving_rows(depth, rows, token, draft, face, first, second, drags)
-    entered = [
-        send(value, shape, lambda s, c, p, sign=sign: (s, (c + sign) % cols, p))
-        for value, sign in zip(leaving, (1, -1))
-    ]
-    whole, upper, _ = stream(depth // 2, depth, token, whole, *fields)
+    fields = (populations, solid_mask, force)
+    lower, draft, token = stream_lower(depth // 2, token, *fields, sides, walls)
+    *leaving, cross, token = leaving_rows(depth, rows, token, draft, face, first, second, drags)
+    entered, cross = send_col(leaving), send_pair(cross)
+    whole, tiles = stream_upper(token, lower, *fields, face)
     return tuple(
-        finish(shape, whole, target, lower, upper, first, second, entered, drags or [drag])
+        finish(shape, whole, target, tiles, first, second, entered, cross, drags or [drag])
     )
 
 

time: 31.9 us -> 30.7 us (0.962)
  Pallas kernels: 13.4 us -> 11.4 us
  waiting for transfers between devices: 4.92 us -> 5.66 us
    pallas_call x5 -> x3, Pallas kernels: 7.5 us -> 5.49 us  [the longest x1 2.81 us: stream_upper(): pl.pallas_call(upper_kernel, out_shape=[jax.ShapeDtypeStruct(pops.shape,...]
    ppermute x5 -> x6, waiting for transfers between devices: 1.91 us -> 2.65 us  [send(): return lax.ppermute(value, ('slab', 'col', 'pair'), perm)]
    ppermute x5 -> x6, starting transfers between devices: 4.49 us -> 4.51 us  [send(): return lax.ppermute(value, ('slab', 'col', 'pair'), perm)]
  transfers between devices with their start and end apart: 6 -> 7, of which waited for: 4 -> 3; matrix products, arithmetic and copies ran while one was open for 0% -> 0% of each run, Pallas kernels for 27% -> 22%
where the time goes in v10:
time: 30.7 us; the launch traced here: 30.4 us
  starting transfers between devices  11.8 us (38%)
  Pallas kernels  11.4 us (37%)
  waiting for transfers between devices  5.66 us (18%)
  local copies, waits for them, and re-layouts  0.92 us (3%)
  between operations  0.7 us (2%)
    all_to_all x1, starting transfers between devices, shards(): messages = swap(messages)  7.25 us
    ppermute x6, starting transfers between devices, send(): return lax.ppermute(value, ('slab', 'col', 'pair'), perm)  4.51 us
    all_to_all x1, waiting for transfers between devices, shards(): messages = swap(messages)  3.01 us
    pallas_call x1, Pallas kernels, stream_upper(): pl.pallas_call(upper_kernel, out_shape=[jax.ShapeDtypeStruct(pops.shape,...  2.81 us
    pallas_call x1, Pallas kernels, moments(): pl.pallas_call(moments_kernel, out_shape=[jax.ShapeDtypeStruct((3 * depth...  2.76 us
    ppermute x6, waiting for transfers between devices, send(): return lax.ppermute(value, ('slab', 'col', 'pair'), perm)  2.65 us
    pallas_call x1, Pallas kernels, pack(): pl.pallas_call(functools.partial(pack_kernel, steps), out_shape=[jax.Shap...  1.89 us
    pallas_call x1, Pallas kernels, couple(): pl.pallas_call(functools.partial(couple_kernel, shape, depth, rows, len(d...  1.61 us
  transfers between devices with their start and end apart: 7, of which 3 were waited for; matrix products, arithmetic and copies ran while one was open for 0% of the time, Pallas kernels for 22%

profile of v10, /device:TPU:0, one launch (start us, length us, event | category | flops | bytes accessed | tf_op | source)
XLA Modules:
  0.0 30.4 jit_solution(5729164211514891291)
XLA Ops:
  0.6 0.0 copy-start
  0.6 1.9 %pack.1 = (s32[1,128]{1,0:T(1,128)}, f32[8,8,128]{2,1,0:T(8,128)}) custom-call(s32[1,128]{1,0:T(1,128)} %bitcast.1, s32[3,128]{1,0:T(4,128)} %base_ref.1, f32[3,128]{1,0:T(4,128)} %offset_ref.1, f32[3,128]{1,0:T(4,128)} %velocity_ref.1), custom_call_target="tpu_custom_call" | custom-call | tf_op jit(solution)/shard_map/pack/pallas_call | solution.py:229
  2.5 7.3 %all-to-all-start = ((f32[8,8,128]{2,1,0:T(8,128)}), f32[8,8,128]{2,1,0:T(8,128)S(1)}, u32[]{:S(2)}, u32[]{:S(2)}) async-start(f32[8,8,128]{2,1,0:T(8,128)} %get-tuple-element.24), calls=%async_computation | async-start | bytes 65536 | tf_op jit(solution)/shard_map/all_to_all | solution.py:742
  9.8 0.9 %copy-done.1 = s32[16,16,128]{2,1,0:T(8,128)S(1)} copy-done((s32[16,16,128]{2,1,0:T(8,128)S(1)}, s32[16,16,128]{2,1,0:T(8,128)}, u32[]{:S(2)}) %copy-start.1) | copy-done | bytes 131096
  10.7 2.8 %moments.1 = (bf16[768,128]{1,0:T(8,128)(2,1)S(1)}, bf16[768,128]{1,0:T(8,128)(2,1)S(1)}, f32[20,16,128]{2,1,0:T(8,128)S(1)}, f32[19,2,16,128]{3,2,1,0:T(8,128)S(1)}, s32[2,16,128]{2,1,0:T(8,128)S(1)}) custom-call(f32[19,16,16,128]{3,2,1,0:T(8,128)} %pops_ref.5, s32[16,16,128]{2,1,0:T(8,128)S(1)} %copy-done.1), custom_call_target="tpu_custom_call" | custom-call | flops 3000000 | bytes 4000000 | tf_op jit(solution)/shard_map/moments/pallas_call | solution.py:281
  13.5 3.0 %all-to-all-done.beads_ref = f32[8,8,128]{2,1,0:T(8,128)S(1)} async-done(((f32[8,8,128]{2,1,0:T(8,128)}), f32[8,8,128]{2,1,0:T(8,128)S(1)}, u32[]{:S(2)}, u32[]{:S(2)}) %all-to-all-start) | async-done | bytes 32800 | tf_op jit(solution)/shard_map/all_to_all | solution.py:742
  16.5 1.6 %couple.1 = (f32[3,16,16,128]{3,2,1,0:T(8,128)S(1)}, f32[2,16,128]{2,1,0:T(8,128)S(1)}, f32[88,128]{1,0:T(8,128)S(1)}, f32[88,128]{1,0:T(8,128)S(1)}, f32[4,8,12...) custom-call(f32[8,8,128]{2,1,0:T(8,128)S(1)} %all-to-all-done.beads_ref, ...), custom_call_target="tpu_custom_call" | custom-call | tf_op jit(solution)/shard_map/couple/pallas_call | solution.py:410
  18.1 0.4 %collective-permute-start.1 = (f32[88,128]{1,0:T(8,128)S(1)}, f32[88,128]{1,0:T(8,128)S(1)}, u32[]{:S(2)}, u32[]{:S(2)}) collective-permute-start(f32[88,128]{1,0:T(8,128)S(1)} %get-tuple-element.35), channel_id=1, source_target_pairs={{0,4},{1,5},{2,6},{3,7},{4,0},{5,1},{6,2},{7,3},{8,12},{9,13},{10,... | collective-permute-start | bytes 135176 | tf_op jit(solution)/shard_map/ppermute | solution.py:140
  18.5 1.6 %collective-permute-start.2 = (f32[88,128]{1,0:T(8,128)S(1)}, f32[88,128]{1,0:T(8,128)S(1)}, u32[]{:S(2)}, u32[]{:S(2)}) collective-permute-start(f32[88,128]{1,0:T(8,128)S(1)} %get-tuple-element.36), channel_id=1, source_target_pairs={{0,12},{1,13},{2,14},{3,15},{4,8},{5,9},{6,10},{7,11},{8,4},{9,5},... | collective-permute-start | bytes 135176 | tf_op jit(solution)/shard_map/ppermute | solution.py:140
  20.1 0.0 collective-permute-start
  20.1 1.5 %collective-permute-start.3 = (f32[8,128]{1,0:T(8,128)S(1)}, f32[8,128]{1,0:T(8,128)S(1)}, u32[]{:S(2)}, u32[]{:S(2)}) collective-permute-start(f32[8,128]{1,0:T(8,128)S(1)} %get-tuple-element.38), channel_id=1, source_target_pairs={{0,8},{1,9},{2,10},{3,11},{4,12},{5,13},{6,14},{7,15},{8,0},{9,1},... | collective-permute-start | bytes 12296 | tf_op jit(solution)/shard_map/ppermute | solution.py:140
  21.6 1.1 %lower.1 = (f32[19,8,16,128]{3,2,1,0:T(8,128)S(1)}, f32[160,128]{1,0:T(8,128)S(1)}, f32[8,128]{1,0:T(8,128)S(1)}) custom-call(f32[8,128]{1,0:T(8,128)S(1)} %get-tuple-element.28.before_ref, f32[19,16,16,128]{3,2,1,0:T(8,128)S(1)} %copy-done, s32[16,16,128]{2,1,0:T(8,128)S(1)} %copy-done.2, f32[3,16,16,128]{3,2,1,0:T(8,128)S(1)} %get-tuple-element.29.force_ref, ...), custom_call_target="tpu_custom_call" | custom-call | flops 3000000 | bytes 2000000 | tf_op jit(solution)/shard_map/lower/pallas_call | solution.py:592
  22.7 0.0 copy-start.3
  22.7 1.9 %collective-permute-done.3.refs_1_.refs_3_ = f32[8,128]{1,0:T(8,128)S(1)} collective-permute-done((f32[8,128]{1,0:T(8,128)S(1)}, f32[8,128]{1,0:T(8,128)S(1)}, u32[]{:S(2)}, u32[]{:S(2)}) %collective-permute-start.3) | collective-permute-done | bytes 4128 | tf_op jit(solution)/shard_map/ppermute | solution.py:140
  24.6 0.0 collective-permute-done.face_ref
  24.6 0.0 collective-permute-done.1.first_ref
  24.6 0.0 collective-permute-done.2.second_ref
  24.6 0.2 rows.1
  24.8 1.0 %collective-permute-start.4 = (f32[168,128]{1,0:T(8,128)S(1)}, f32[168,128]{1,0:T(8,128)S(1)}, u32[]{:S(2)}, u32[]{:S(2)}) collective-permute-start(f32[168,128]{1,0:T(8,128)S(1)} %get-tuple-element.44), channel_id=1, source_target_pairs={{0,2},{1,3},{2,0},{3,1},{4,6},{5,7},{6,4},{7,5},{8,10},{9,11},{10,... | collective-permute-start | bytes 258056 | tf_op jit(solution)/shard_map/ppermute | solution.py:140
  25.8 0.0 collective-permute-start.5
  25.8 2.8 %upper.1 = (f32[19,16,16,128]{3,2,1,0:T(8,128)}, f32[10,16,8,128]{3,2,1,0:T(8,128)S(1)}) custom-call(f32[8,128]{1,0:T(8,128)S(1)} %get-tuple-element.39.before_ref, f32[19,8,16,128]{3,2,1,0:T(8,128)S(1)} %get-tuple-element.40.lower_ref, f32[19,16,16,128]{3,2,1,0:T(8,128)S(1)} %copy-done, s32[16,16,128]{2,1,0:T(8,128)S(1)} %copy-done.2, ...), custom_call_target="tpu_custom_call" | custom-call | flops 5000000 | bytes 3000000 | tf_op jit(solution)/shard_map/upper/pallas_call | solution.py:609
  28.6 0.0 collective-permute-done.5.refs_1_
  28.6 0.7 %collective-permute-done.4.refs_0_ = f32[168,128]{1,0:T(8,128)S(1)} collective-permute-done((f32[168,128]{1,0:T(8,128)S(1)}, f32[168,128]{1,0:T(8,128)S(1)}, u32[]{:S(2)}, u32[]{:S(2)}) %collective-permute-start.4) | collective-permute-done | bytes 86048 | tf_op jit(solution)/shard_map/ppermute | solution.py:140
  29.3 1.1 %finish.1 = (f32[19,16,16,128]{3,2,1,0:T(8,128)}, f32[3,128]{1,0:T(4,128)}) custom-call(f32[19,16,16,128]{3,2,1,0:T(8,128)} %get-tuple-element.41.whole_ref, s32[1,128]{1,0:T(1,128)S(1)} %copy-done.3, f32[10,16,8,128]{3,2,1,0:T(8,128)S(1)} %get-tuple-element.43.tile_ref, ...), custom_call_target="tpu_custom_call", output_to_operand_aliasing={{0}: (0, {})} | custom-call | tf_op jit(solution)/shard_map/finish/pallas_call | solution.py:712
  (5 shorter events, 0.0 us)
Async XLA Ops:
  0.6 15.8 %copy-start = (f32[19,16,16,128]{3,2,1,0:T(8,128)S(1)}, f32[19,16,16,128]{3,2,1,0:T(8,128)}, u32[]{:S(2)}) copy-start(f32[19,16,16,128]{3,2,1,0:T(8,128)} %pops_ref.5) | copy-start | bytes 7471108
  2.5 13.9 %all-to-all-start = ((f32[8,8,128]{2,1,0:T(8,128)}), f32[8,8,128]{2,1,0:T(8,128)S(1)}, u32[]{:S(2)}, u32[]{:S(2)}) async-start(f32[8,8,128]{2,1,0:T(8,128)} %get-tuple-element.24), calls=%async_computation | async-start | bytes 65536 | tf_op jit(solution)/shard_map/all_to_all | solution.py:742
  9.8 0.9 %copy-start.1 = (s32[16,16,128]{2,1,0:T(8,128)S(1)}, s32[16,16,128]{2,1,0:T(8,128)}, u32[]{:S(2)}) copy-start(s32[16,16,128]{2,1,0:T(8,128)} %solid_ref.5) | copy-start | bytes 393220
  10.7 5.8 %copy-start.2 = (s32[16,16,128]{2,1,0:T(8,128)S(1)}, s32[16,16,128]{2,1,0:T(8,128)}, u32[]{:S(2)}) copy-start(s32[16,16,128]{2,1,0:T(8,128)} %solid_ref.5) | copy-start | bytes 393220
  18.1 6.5 %collective-permute-start.1 = (f32[88,128]{1,0:T(8,128)S(1)}, f32[88,128]{1,0:T(8,128)S(1)}, u32[]{:S(2)}, u32[]{:S(2)}) collective-permute-start(f32[88,128]{1,0:T(8,128)S(1)} %get-tuple-element.35), channel_id=1, source_target_pairs={{0,4},{1,5},{2,6},{3,7},{4,0},{5,1},{6,2},{7,3},{8,12},{9,13},{10,... | collective-permute-start | bytes 135176 | tf_op jit(solution)/shard_map/ppermute | solution.py:140
  18.5 6.1 %collective-permute-start.2 = (f32[88,128]{1,0:T(8,128)S(1)}, f32[88,128]{1,0:T(8,128)S(1)}, u32[]{:S(2)}, u32[]{:S(2)}) collective-permute-start(f32[88,128]{1,0:T(8,128)S(1)} %get-tuple-element.36), channel_id=1, source_target_pairs={{0,12},{1,13},{2,14},{3,15},{4,8},{5,9},{6,10},{7,11},{8,4},{9,5},... | collective-permute-start | bytes 135176 | tf_op jit(solution)/shard_map/ppermute | solution.py:140
  20.1 4.5 %collective-permute-start = (f32[2,16,128]{2,1,0:T(8,128)S(1)}, f32[2,16,128]{2,1,0:T(8,128)S(1)}, u32[]{:S(2)}, u32[]{:S(2)}) collective-permute-start(f32[2,16,128]{2,1,0:T(8,128)S(1)} %get-tuple-element.34), channel_id=1, source_target_pairs={{0,1},{1,0},{2,3},{3,2},{4,5},{5,4},{6,7},{7,6},{8,9},{9,8},{10,11... | collective-permute-start | bytes 49160 | tf_op jit(solution)/shard_map/ppermute | solution.py:140
  20.1 4.5 %collective-permute-start.3 = (f32[8,128]{1,0:T(8,128)S(1)}, f32[8,128]{1,0:T(8,128)S(1)}, u32[]{:S(2)}, u32[]{:S(2)}) collective-permute-start(f32[8,128]{1,0:T(8,128)S(1)} %get-tuple-element.38), channel_id=1, source_target_pairs={{0,8},{1,9},{2,10},{3,11},{4,12},{5,13},{6,14},{7,15},{8,0},{9,1},... | collective-permute-start | bytes 12296 | tf_op jit(solution)/shard_map/ppermute | solution.py:140
  22.7 6.7 %copy-start.3 = (s32[1,128]{1,0:T(1,128)S(1)}, s32[1,128]{1,0:T(1,128)}, u32[]{:S(2)}) copy-start(s32[1,128]{1,0:T(1,128)} %get-tuple-element.42.target_ref) | copy-start | bytes 1540
  24.8 4.6 %collective-permute-start.4 = (f32[168,128]{1,0:T(8,128)S(1)}, f32[168,128]{1,0:T(8,128)S(1)}, u32[]{:S(2)}, u32[]{:S(2)}) collective-permute-start(f32[168,128]{1,0:T(8,128)S(1)} %get-tuple-element.44), channel_id=1, source_target_pairs={{0,2},{1,3},{2,0},{3,1},{4,6},{5,7},{6,4},{7,5},{8,10},{9,11},{10,... | collective-permute-start | bytes 258056 | tf_op jit(solution)/shard_map/ppermute | solution.py:140
  25.8 2.8 %collective-permute-start.5 = (f32[64,128]{1,0:T(8,128)S(1)}, f32[64,128]{1,0:T(8,128)S(1)}, u32[]{:S(2)}, u32[]{:S(2)}) collective-permute-start(f32[64,128]{1,0:T(8,128)S(1)} %get-tuple-element.45), channel_id=1, source_target_pairs={{0,1},{1,0},{2,3},{3,2},{4,5},{5,4},{6,7},{7,6},{8,9},{9,8},{10,11... | collective-permute-start | bytes 98312 | tf_op jit(solution)/shard_map/ppermute | solution.py:140

commit v11 on v10

--- a/solution.py
+++ b/solution.py
@@ -147,8 +147,8 @@
     return send(value, shape, target)
 
 
-def even_slab():
-    return lax.rem(lax.axis_index("slab"), 2) == 0
+def odd_slab():
+    return lax.rem(lax.axis_index("slab"), 2) == 1
 
 
 def rank_among(member):
@@ -329,7 +329,7 @@
 
 def couple_kernel(shape, depth, rows, n_drags, beads_ref, high_ref, low_ref, *refs):
     slabs, cols, _ = shape
-    column_ref, pops_ref, solid_ref, force_ref, face_ref, first_ref, second_ref, *refs = refs
+    pops_ref, solid_ref, force_ref, first_ref, second_ref, *refs = refs
     drag_refs, token_ref = refs[:-1], refs[-1]
     token_ref[...] = jnp.zeros_like(token_ref)
     width = high_ref.shape[1]
@@ -373,15 +373,7 @@
 
         lax.fori_loop(0, beads_ref.shape[0] // GROUP, group, 0)
 
-    force = [x_ends([force_ref[d, z] for z in range(depth)]) for d in range(3)]
-    out = collide([column_ref[i] for i in range(19)], column_ref[19] == 1.0, force)
-    high = lax.rem(iota((rows, 128), 1), 2) == 0
-    ends = [jnp.where(high, out[i], out[j])[:, 0:32] for i, j in zip(*ENTER[0])]
-    face_ref[0] = jnp.concatenate(ends[0:4], axis=1)
-    face_ref[1] = jnp.concatenate([ends[4], jnp.zeros((rows, 96), F32)], axis=1)
-
-
-    even = even_slab()
+    odd = odd_slab()
     leaving = []
     for group, z in ((0, depth - 1), (1, 0)):
         out = collide(
@@ -396,12 +388,12 @@
     row = 0
     for a, b in zip(*leaving):
         at = slice(row, row + a.shape[0])
-        first_ref[at] = jnp.where(even, a, b)
-        second_ref[at] = jnp.where(even, b, a)
+        first_ref[at] = jnp.where(odd, a, b)
+        second_ref[at] = jnp.where(odd, b, a)
         row += a.shape[0]
 
 
-def couple(shape, beads, flow, columns, pops, solid, depth, rows):
+def couple(shape, beads, flow, pops, solid, depth, rows):
     width = flow[0].shape[1]
     single = beads.shape[0] == GROUP
     tile = jax.ShapeDtypeStruct((8, 128), F32)
@@ -411,7 +403,6 @@
         functools.partial(couple_kernel, shape, depth, rows, len(drags)),
         out_shape=[
             jax.ShapeDtypeStruct((3, depth, rows, width), F32),
-            jax.ShapeDtypeStruct((2, rows, 128), F32),
             message,
             message,
         ]
@@ -419,12 +410,31 @@
         + [TOKEN],
         compiler_params=pltpu.CompilerParams(vmem_limit_bytes=ROOM),
         name="couple",
-    )(beads, *flow, columns, pops, solid)
+    )(beads, *flow, pops, solid)
+
+
+def x_faces_kernel(force_ref, column_ref, face_ref):
+    _, depth, rows, _ = force_ref.shape
+    force = [x_ends([force_ref[d, z] for z in range(depth)]) for d in range(3)]
+    out = collide([column_ref[i] for i in range(19)], column_ref[19] == 1.0, force)
+    high = lax.rem(iota((rows, 128), 1), 2) == 0
+    ends = [jnp.where(high, out[i], out[j])[:, 0:32] for i, j in zip(*ENTER[0])]
+    face_ref[0] = jnp.concatenate(ends[0:4], axis=1)
+    face_ref[1] = jnp.concatenate([ends[4], jnp.zeros((rows, 96), F32)], axis=1)
+
+
+def x_faces(force, columns):
+    return pl.pallas_call(
+        x_faces_kernel,
+        out_shape=jax.ShapeDtypeStruct((2, *columns.shape[1:]), F32),
+        compiler_params=pltpu.CompilerParams(vmem_limit_bytes=ROOM),
+        name="x_faces",
+    )(force, columns)
 
 
 def entered_z(first_ref, second_ref, side, rows):
-    even = even_slab() if side == 0 else jnp.logical_not(even_slab())
-    return jnp.where(even, second_ref[rows], first_ref[rows])
+    odd = odd_slab() if side == 0 else jnp.logical_not(odd_slab())
+    return jnp.where(odd, second_ref[rows], first_ref[rows])
 
 
 X_EDGES = [i for side in range(2) for i in ENTER[2][side] if STEP[i, 0] != 0]
@@ -741,8 +751,8 @@
     target, messages = pack(owners, bead_owner, bead_base, bead_offset, bead_velocity)
     messages = swap(messages)
     *flow, columns, sides, walls = moments(populations, solid_mask)
-    force, face, first, second, drag, *far, token = couple(
-        shape, messages, flow, columns, populations, solid_mask, depth, rows
+    force, first, second, drag, *far, token = couple(
+        shape, messages, flow, populations, solid_mask, depth, rows
     )
 
     def send_pair(value):
@@ -754,15 +764,15 @@
             for value, sign in zip(values, (1, -1))
         ]
 
-    face = send_pair(face)
-    first, second = send_slab(first, shape, 0), send_slab(second, shape, 1)
+    face = send_pair(x_faces(force, columns))
+    first, second = send_slab(first, shape, 1), send_slab(second, shape, 0)
     if single:
         drags = [drag, send(far[0], shape, lambda s, c, p: ((s + 2) % slabs, c, p))]
     else:
         drags = []
         drag = swap(drag)
     fields = (populations, solid_mask, force)
-    lower, draft, token = stream_lower(depth // 2, token, *fields, sides, walls)
+    lower, draft, token = stream_lower(10, token, *fields, sides, walls)
     *leaving, cross, token = leaving_rows(depth, rows, token, draft, face, first, second, drags)
     entered, cross = send_col(leaving), send_pair(cross)
     whole, tiles = stream_upper(token, lower, *fields, face)

time: 30.7 us -> 30.4 us (level)
  waiting for transfers between devices: 5.66 us -> 4.46 us
  starting transfers between devices: 11.8 us -> 12.6 us
    ppermute x6, waiting for transfers between devices: 2.65 us -> 1.45 us  [send(): return lax.ppermute(value, ('slab', 'col', 'pair'), perm)]
    ppermute x6, starting transfers between devices: 4.51 us -> 5.4 us  [send(): return lax.ppermute(value, ('slab', 'col', 'pair'), perm)]
    pallas_call x1, Pallas kernels: 2.81 us -> 2.48 us  [stream_upper(): pl.pallas_call(upper_kernel, out_shape=[jax.ShapeDtypeStruct(pops.shape,...]
where the time goes in v11:
time: 30.4 us; the launch traced here: 30.2 us
  starting transfers between devices  12.6 us (41%)
  Pallas kernels  11.4 us (38%)
  waiting for transfers between devices  4.46 us (15%)
  local copies, waits for them, and re-layouts  0.92 us (3%)
  between operations  0.7 us (2%)
    all_to_all x1, starting transfers between devices, shards(): messages = swap(messages)  7.25 us
    ppermute x6, starting transfers between devices, send(): return lax.ppermute(value, ('slab', 'col', 'pair'), perm)  5.4 us
    all_to_all x1, waiting for transfers between devices, shards(): messages = swap(messages)  3.01 us
    pallas_call x1, Pallas kernels, moments(): pl.pallas_call(moments_kernel, out_shape=[jax.ShapeDtypeStruct((3 * depth...  2.76 us
    pallas_call x1, Pallas kernels, stream_upper(): pl.pallas_call(upper_kernel, out_shape=[jax.ShapeDtypeStruct(pops.shape,...  2.48 us
    pallas_call x1, Pallas kernels, pack(): pl.pallas_call(functools.partial(pack_kernel, steps), out_shape=[jax.Shap...  1.89 us
    pallas_call x1, Pallas kernels, couple(): pl.pallas_call(functools.partial(couple_kernel, shape, depth, rows, len(d...  1.55 us
    ppermute x6, waiting for transfers between devices, send(): return lax.ppermute(value, ('slab', 'col', 'pair'), perm)  1.45 us
  transfers between devices with their start and end apart: 7, of which 3 were waited for; matrix products, arithmetic and copies ran while one was open for 0% of the time, Pallas kernels for 22%

profile of v11, /device:TPU:0, one launch (start us, length us, event | category | flops | bytes accessed | tf_op | source)
XLA Modules:
  0.0 30.2 jit_solution(6930316853649549119)
XLA Ops:
  0.6 0.0 copy-start
  0.6 1.9 %pack.1 = (s32[1,128]{1,0:T(1,128)}, f32[8,8,128]{2,1,0:T(8,128)}) custom-call(s32[1,128]{1,0:T(1,128)} %bitcast.1, s32[3,128]{1,0:T(4,128)} %base_ref.1, f32[3,128]{1,0:T(4,128)} %offset_ref.1, f32[3,128]{1,0:T(4,128)} %velocity_ref.1), custom_call_target="tpu_custom_call" | custom-call | tf_op jit(solution)/shard_map/pack/pallas_call | solution.py:229
  2.5 7.3 %all-to-all-start = ((f32[8,8,128]{2,1,0:T(8,128)}), f32[8,8,128]{2,1,0:T(8,128)S(1)}, u32[]{:S(2)}, u32[]{:S(2)}) async-start(f32[8,8,128]{2,1,0:T(8,128)} %get-tuple-element.23), calls=%async_computation | async-start | bytes 65536 | tf_op jit(solution)/shard_map/all_to_all | solution.py:752
  9.8 0.9 %copy-done.1 = s32[16,16,128]{2,1,0:T(8,128)S(1)} copy-done((s32[16,16,128]{2,1,0:T(8,128)S(1)}, s32[16,16,128]{2,1,0:T(8,128)}, u32[]{:S(2)}) %copy-start.1) | copy-done | bytes 131096
  10.7 2.8 %moments.1 = (bf16[768,128]{1,0:T(8,128)(2,1)S(1)}, bf16[768,128]{1,0:T(8,128)(2,1)S(1)}, f32[20,16,128]{2,1,0:T(8,128)S(1)}, f32[19,2,16,128]{3,2,1,0:T(8,128)S(1)}, s32[2,16,128]{2,1,0:T(8,128)S(1)}) custom-call(f32[19,16,16,128]{3,2,1,0:T(8,128)} %pops_ref.5, s32[16,16,128]{2,1,0:T(8,128)S(1)} %copy-done.1), custom_call_target="tpu_custom_call" | custom-call | flops 3000000 | bytes 4000000 | tf_op jit(solution)/shard_map/moments/pallas_call | solution.py:281
  13.5 3.0 %all-to-all-done.beads_ref = f32[8,8,128]{2,1,0:T(8,128)S(1)} async-done(((f32[8,8,128]{2,1,0:T(8,128)}), f32[8,8,128]{2,1,0:T(8,128)S(1)}, u32[]{:S(2)}, u32[]{:S(2)}) %all-to-all-start) | async-done | bytes 32800 | tf_op jit(solution)/shard_map/all_to_all | solution.py:752
  16.5 1.5 %couple.1 = (f32[3,16,16,128]{3,2,1,0:T(8,128)S(1)}, f32[88,128]{1,0:T(8,128)S(1)}, f32[88,128]{1,0:T(8,128)S(1)}, f32[4,8,128]{2,1,0:T(8,128)S(1)}, f32[8,128]{1,0:T(8,128)S(1)}, /*index=5*/f32[8,128]{1,0:T(8,128)S(1)}) custom-call(f32[8,8,128]{2,1,0:T(8,128)S(1)} %all-to-all-done.beads_ref, bf16[768,128]{1,0:T(8,128)(2,1)S(1)} %get-tuple-element.24.high_ref, ...), custom_call_target="tpu_custom_call" | custom-call | tf_op jit(solution)/shard_map/couple/pallas_call | solution.py:402
  18.0 0.9 %collective-permute-start.1 = (f32[88,128]{1,0:T(8,128)S(1)}, f32[88,128]{1,0:T(8,128)S(1)}, u32[]{:S(2)}, u32[]{:S(2)}) collective-permute-start(f32[88,128]{1,0:T(8,128)S(1)} %get-tuple-element.33), channel_id=1, source_target_pairs={{0,12},{1,13},{2,14},{3,15},{4,8},{5,9},{6,10},{7,11},{8,4},{9,5},... | collective-permute-start | bytes 135176 | tf_op jit(solution)/shard_map/ppermute | solution.py:140
  18.9 0.2 collective-permute-start.2
  19.1 0.3 x_faces.1
  19.4 0.0 collective-permute-start
  19.4 3.4 %collective-permute-start.3 = (f32[8,128]{1,0:T(8,128)S(1)}, f32[8,128]{1,0:T(8,128)S(1)}, u32[]{:S(2)}, u32[]{:S(2)}) collective-permute-start(f32[8,128]{1,0:T(8,128)S(1)} %get-tuple-element.36), channel_id=1, source_target_pairs={{0,8},{1,9},{2,10},{3,11},{4,12},{5,13},{6,14},{7,15},{8,0},{9,1},... | collective-permute-start | bytes 12296 | tf_op jit(solution)/shard_map/ppermute | solution.py:140
  22.8 1.3 %lower.1 = (f32[19,10,16,128]{3,2,1,0:T(8,128)S(1)}, f32[160,128]{1,0:T(8,128)S(1)}, f32[8,128]{1,0:T(8,128)S(1)}) custom-call(f32[8,128]{1,0:T(8,128)S(1)} %get-tuple-element.26.before_ref, f32[19,16,16,128]{3,2,1,0:T(8,128)S(1)} %copy-done, s32[16,16,128]{2,1,0:T(8,128)S(1)} %copy-done.2, f32[3,16,16,128]{3,2,1,0:T(8,128)S(1)} %get-tuple-element.27.force_ref, ...), custom_call_target="tpu_custom_call" | custom-call | flops 3000000 | bytes 2000000 | tf_op jit(solution)/shard_map/lower/pallas_call | solution.py:602
  24.1 0.0 copy-start.3
  24.1 0.3 collective-permute-done.3.refs_1_.refs_3_
  24.4 0.0 collective-permute-done.face_ref
  24.4 0.0 collective-permute-done.1.first_ref
  24.4 0.0 collective-permute-done.2.second_ref
  24.4 0.2 rows.1
  24.5 0.9 %collective-permute-start.4 = (f32[168,128]{1,0:T(8,128)S(1)}, f32[168,128]{1,0:T(8,128)S(1)}, u32[]{:S(2)}, u32[]{:S(2)}) collective-permute-start(f32[168,128]{1,0:T(8,128)S(1)} %get-tuple-element.42), channel_id=1, source_target_pairs={{0,2},{1,3},{2,0},{3,1},{4,6},{5,7},{6,4},{7,5},{8,10},{9,11},{10,... | collective-permute-start | bytes 258056 | tf_op jit(solution)/shard_map/ppermute | solution.py:140
  25.5 0.0 collective-permute-start.5
  25.5 2.5 %upper.1 = (f32[19,16,16,128]{3,2,1,0:T(8,128)}, f32[10,16,8,128]{3,2,1,0:T(8,128)S(1)}) custom-call(f32[8,128]{1,0:T(8,128)S(1)} %get-tuple-element.37.before_ref, f32[19,10,16,128]{3,2,1,0:T(8,128)S(1)} %get-tuple-element.38.lower_ref, f32[19,16,16,128]{3,2,1,0:T(8,128)S(1)} %copy-done, s32[16,16,128]{2,1,0:T(8,128)S(1)} %copy-done.2, ...), custom_call_target="tpu_custom_call" | custom-call | flops 5000000 | bytes 3000000 | tf_op jit(solution)/shard_map/upper/pallas_call | solution.py:619
  28.0 1.1 %collective-permute-done.4.refs_0_ = f32[168,128]{1,0:T(8,128)S(1)} collective-permute-done((f32[168,128]{1,0:T(8,128)S(1)}, f32[168,128]{1,0:T(8,128)S(1)}, u32[]{:S(2)}, u32[]{:S(2)}) %collective-permute-start.4) | collective-permute-done | bytes 86048 | tf_op jit(solution)/shard_map/ppermute | solution.py:140
  29.1 1.1 %finish.1 = (f32[19,16,16,128]{3,2,1,0:T(8,128)}, f32[3,128]{1,0:T(4,128)}) custom-call(f32[19,16,16,128]{3,2,1,0:T(8,128)} %get-tuple-element.39.whole_ref, s32[1,128]{1,0:T(1,128)S(1)} %copy-done.3, f32[10,16,8,128]{3,2,1,0:T(8,128)S(1)} %get-tuple-element.41.tile_ref, ...), custom_call_target="tpu_custom_call", output_to_operand_aliasing={{0}: (0, {})} | custom-call | tf_op jit(solution)/shard_map/finish/pallas_call | solution.py:722
  (6 shorter events, 0.0 us)
Async XLA Ops:
  0.6 15.8 %copy-start = (f32[19,16,16,128]{3,2,1,0:T(8,128)S(1)}, f32[19,16,16,128]{3,2,1,0:T(8,128)}, u32[]{:S(2)}) copy-start(f32[19,16,16,128]{3,2,1,0:T(8,128)} %pops_ref.5) | copy-start | bytes 7471108
  2.5 13.9 %all-to-all-start = ((f32[8,8,128]{2,1,0:T(8,128)}), f32[8,8,128]{2,1,0:T(8,128)S(1)}, u32[]{:S(2)}, u32[]{:S(2)}) async-start(f32[8,8,128]{2,1,0:T(8,128)} %get-tuple-element.23), calls=%async_computation | async-start | bytes 65536 | tf_op jit(solution)/shard_map/all_to_all | solution.py:752
  9.8 0.9 %copy-start.1 = (s32[16,16,128]{2,1,0:T(8,128)S(1)}, s32[16,16,128]{2,1,0:T(8,128)}, u32[]{:S(2)}) copy-start(s32[16,16,128]{2,1,0:T(8,128)} %solid_ref.5) | copy-start | bytes 393220
  10.7 5.8 %copy-start.2 = (s32[16,16,128]{2,1,0:T(8,128)S(1)}, s32[16,16,128]{2,1,0:T(8,128)}, u32[]{:S(2)}) copy-start(s32[16,16,128]{2,1,0:T(8,128)} %solid_ref.5) | copy-start | bytes 393220
  18.0 6.3 %collective-permute-start.1 = (f32[88,128]{1,0:T(8,128)S(1)}, f32[88,128]{1,0:T(8,128)S(1)}, u32[]{:S(2)}, u32[]{:S(2)}) collective-permute-start(f32[88,128]{1,0:T(8,128)S(1)} %get-tuple-element.33), channel_id=1, source_target_pairs={{0,12},{1,13},{2,14},{3,15},{4,8},{5,9},{6,10},{7,11},{8,4},{9,5},... | collective-permute-start | bytes 135176 | tf_op jit(solution)/shard_map/ppermute | solution.py:140
  18.9 5.5 %collective-permute-start.2 = (f32[88,128]{1,0:T(8,128)S(1)}, f32[88,128]{1,0:T(8,128)S(1)}, u32[]{:S(2)}, u32[]{:S(2)}) collective-permute-start(f32[88,128]{1,0:T(8,128)S(1)} %get-tuple-element.34), channel_id=1, source_target_pairs={{0,4},{1,5},{2,6},{3,7},{4,0},{5,1},{6,2},{7,3},{8,12},{9,13},{10,... | collective-permute-start | bytes 135176 | tf_op jit(solution)/shard_map/ppermute | solution.py:140
  19.4 5.0 %collective-permute-start = (f32[2,16,128]{2,1,0:T(8,128)S(1)}, f32[2,16,128]{2,1,0:T(8,128)S(1)}, u32[]{:S(2)}, u32[]{:S(2)}) collective-permute-start(f32[2,16,128]{2,1,0:T(8,128)S(1)} %x_faces.1), channel_id=1, source_target_pairs={{0,1},{1,0},{2,3},{3,2},{4,5},{5,4},{6,7},{7,6},{8,9},{9,8},{10,11... | collective-permute-start | bytes 49160 | tf_op jit(solution)/shard_map/ppermute | solution.py:140
  19.4 5.0 %collective-permute-start.3 = (f32[8,128]{1,0:T(8,128)S(1)}, f32[8,128]{1,0:T(8,128)S(1)}, u32[]{:S(2)}, u32[]{:S(2)}) collective-permute-start(f32[8,128]{1,0:T(8,128)S(1)} %get-tuple-element.36), channel_id=1, source_target_pairs={{0,8},{1,9},{2,10},{3,11},{4,12},{5,13},{6,14},{7,15},{8,0},{9,1},... | collective-permute-start | bytes 12296 | tf_op jit(solution)/shard_map/ppermute | solution.py:140
  24.1 5.0 %copy-start.3 = (s32[1,128]{1,0:T(1,128)S(1)}, s32[1,128]{1,0:T(1,128)}, u32[]{:S(2)}) copy-start(s32[1,128]{1,0:T(1,128)} %get-tuple-element.40.target_ref) | copy-start | bytes 1540
  24.5 4.6 %collective-permute-start.4 = (f32[168,128]{1,0:T(8,128)S(1)}, f32[168,128]{1,0:T(8,128)S(1)}, u32[]{:S(2)}, u32[]{:S(2)}) collective-permute-start(f32[168,128]{1,0:T(8,128)S(1)} %get-tuple-element.42), channel_id=1, source_target_pairs={{0,2},{1,3},{2,0},{3,1},{4,6},{5,7},{6,4},{7,5},{8,10},{9,11},{10,... | collective-permute-start | bytes 258056 | tf_op jit(solution)/shard_map/ppermute | solution.py:140
  25.5 2.5 %collective-permute-start.5 = (f32[64,128]{1,0:T(8,128)S(1)}, f32[64,128]{1,0:T(8,128)S(1)}, u32[]{:S(2)}, u32[]{:S(2)}) collective-permute-start(f32[64,128]{1,0:T(8,128)S(1)} %get-tuple-element.43), channel_id=1, source_target_pairs={{0,1},{1,0},{2,3},{3,2},{4,5},{5,4},{6,7},{7,6},{8,9},{9,8},{10,11... | collective-permute-start | bytes 98312 | tf_op jit(solution)/shard_map/ppermute | solution.py:140

commit v12 on v10

--- a/solution.py
+++ b/solution.py
@@ -147,8 +147,8 @@
     return send(value, shape, target)
 
 
-def even_slab():
-    return lax.rem(lax.axis_index("slab"), 2) == 0
+def odd_slab():
+    return lax.rem(lax.axis_index("slab"), 2) == 1
 
 
 def rank_among(member):
@@ -239,7 +239,7 @@
 
 
 def moments_kernel(
-    pops_ref, solid_ref, high_ref, low_ref, column_ref, side_ref, wall_ref, held, held_solid, sem
+    pops_ref, solid_ref, high_ref, low_ref, column_ref, side_ref, wall_ref, held, held_solid, flow, sem
 ):
     depth, rows, width = pops_ref.shape[1:]
     chunks = 4
@@ -258,14 +258,16 @@
         density, momentum = density_momentum(pops)
         inverse = 1.0 / density
         for axis in range(3):
-            at = pl.ds(pl.multiple_of(axis * depth * rows + z * rows, rows), rows)
-            high_ref[at], low_ref[at] = high_low(momentum[axis] * inverse)
+            flow[axis, pl.ds(pl.multiple_of(z * rows, rows), rows)] = momentum[axis] * inverse
         return carry
 
     for k in range(chunks):
         copies[1 + k].wait()
         lax.fori_loop(k * span, (k + 1) * span, plane, 0, unroll=2)
     copies[0].wait()
+    for axis in range(3):
+        at = slice(axis * width, (axis + 1) * width)
+        high_ref[at], low_ref[at] = high_low(flow[axis].T)
     for i in range(19):
         column_ref[i] = x_ends([held[i, z] for z in range(depth)])
         side_ref[i, 0] = held[i, :, 0, :]
@@ -281,8 +283,8 @@
     return pl.pallas_call(
         moments_kernel,
         out_shape=[
-            jax.ShapeDtypeStruct((3 * depth * rows, width), BF16),
-            jax.ShapeDtypeStruct((3 * depth * rows, width), BF16),
+            jax.ShapeDtypeStruct((3 * width, depth * rows), BF16),
+            jax.ShapeDtypeStruct((3 * width, depth * rows), BF16),
             jax.ShapeDtypeStruct((20, rows, 128), F32),
             jax.ShapeDtypeStruct((19, 2, depth, width), F32),
             jax.ShapeDtypeStruct((2, depth, width), jnp.int32),
@@ -291,6 +293,7 @@
         scratch_shapes=[
             pltpu.VMEM(pops.shape, F32),
             pltpu.VMEM(solid.shape, jnp.int32),
+            pltpu.VMEM((3, depth * rows, width), F32),
             pltpu.SemaphoreType.DMA((5,)),
         ],
         compiler_params=pltpu.CompilerParams(vmem_limit_bytes=54000000),
@@ -305,8 +308,8 @@
     ]
 
 
-def couple_group(base, part, velocity, flow, depth, rows):
-    width, slots = flow[0].shape[1], GROUP * CAP
+def couple_group(base, part, velocity, flow, depth, rows, width):
+    slots = GROUP * CAP
     start = base.astype(jnp.int32) - 1
 
     def hat(axis, length):
@@ -314,26 +317,30 @@
         low, share = start[axis : axis + 1], part[axis : axis + 1]
         return jnp.where(cell == low, 1.0 - share, 0.0) + jnp.where(cell == low + 1, share, 0.0)
 
-    hat_x, hat_y, hat_z = high_low(hat(0, width)), hat(1, rows), hat(2, depth)
-    weight = (hat_z[:, None, :] * hat_y[None, :, :]).reshape(depth * rows, slots)
-    across = dot_split(flow, hat_x, NN)
-    cells = depth * rows
-    sampled = [
-        jnp.sum(across[d * cells : (d + 1) * cells] * weight, axis=0, keepdims=True)
-        for d in range(3)
-    ]
-    drag = [DRAG_COEF * (sampled[d] - velocity[d : d + 1]) for d in range(3)]
-    spread = jnp.concatenate([weight * (-drag[d]) for d in range(3)], axis=0)
-    return drag, dot_split(high_low(spread), hat_x, NT)
-
-
-def couple_kernel(shape, depth, rows, n_drags, beads_ref, high_ref, low_ref, *refs):
+    hat_x, hat_y, hat_z = hat(0, width), hat(1, rows), hat(2, depth)
+    weight = high_low((hat_z[:, None, :] * hat_y[None, :, :]).reshape(depth * rows, slots))
+    across = dot_split(flow, weight, NN)
+    drag = []
+    for d in range(3):
+        sampled = jnp.sum(across[d * width : (d + 1) * width] * hat_x, axis=0, keepdims=True)
+        drag.append(DRAG_COEF * (sampled - velocity[d : d + 1]))
+    spread = jnp.concatenate([hat_x * (-drag[d]) for d in range(3)], axis=0)
+    return drag, dot_split(weight, high_low(spread), NT)
+
+
+def couple_kernel(shape, n_drags, beads_ref, high_ref, low_ref, *refs):
     slabs, cols, _ = shape
     column_ref, pops_ref, solid_ref, force_ref, face_ref, first_ref, second_ref, *refs = refs
     drag_refs, token_ref = refs[:-1], refs[-1]
     token_ref[...] = jnp.zeros_like(token_ref)
-    width = high_ref.shape[1]
+    depth, rows, width = pops_ref.shape[1:]
     flow = (high_ref[...], low_ref[...])
+
+    def grid(force):
+        return [
+            force[:, d * width : (d + 1) * width].reshape(depth, rows, width) for d in range(3)
+        ]
+
     hollow = jnp.zeros((5, GROUP * CAP), F32)
 
     if n_drags == 2:
@@ -343,8 +350,9 @@
             there = [a - b for a, b in zip((slab, col), divmod(r, cols))]
             there = [jnp.where(a < 0, a + n, a) for a, n in zip(there, (slabs, cols))]
             got.append(beads_ref[there[0] * cols + there[1]])
-        drag, force = couple_group(*unpack(got), flow, depth, rows)
-        force_ref[...] = force.reshape(3, depth, rows, width)
+        drag, force = couple_group(*unpack(got), flow, depth, rows, width)
+        for d, value in enumerate(grid(force)):
+            force_ref[d] = value
         stacked = jnp.concatenate(drag + [hollow], axis=0)
         lanes = cols * CAP
         blank = jnp.zeros((8, 128 - lanes), F32)
@@ -362,8 +370,9 @@
 
         def group(k, carry):
             got = [beads_ref[k * GROUP + r] for r in range(GROUP)]
-            drag, force = couple_group(*unpack(got), flow, depth, rows)
-            force_ref[...] += force.reshape(3, depth, rows, width)
+            drag, force = couple_group(*unpack(got), flow, depth, rows, width)
+            for d, value in enumerate(grid(force)):
+                force_ref[d] += value
             stacked = jnp.concatenate(drag + [hollow], axis=0)
             for r in range(GROUP):
                 drag_refs[0][k * GROUP + r] = jnp.concatenate(
@@ -379,9 +388,7 @@
     ends = [jnp.where(high, out[i], out[j])[:, 0:32] for i, j in zip(*ENTER[0])]
     face_ref[0] = jnp.concatenate(ends[0:4], axis=1)
     face_ref[1] = jnp.concatenate([ends[4], jnp.zeros((rows, 96), F32)], axis=1)
-
-
-    even = even_slab()
+    odd = odd_slab()
     leaving = []
     for group, z in ((0, depth - 1), (1, 0)):
         out = collide(
@@ -396,19 +403,19 @@
     row = 0
     for a, b in zip(*leaving):
         at = slice(row, row + a.shape[0])
-        first_ref[at] = jnp.where(even, a, b)
-        second_ref[at] = jnp.where(even, b, a)
+        first_ref[at] = jnp.where(odd, a, b)
+        second_ref[at] = jnp.where(odd, b, a)
         row += a.shape[0]
 
 
-def couple(shape, beads, flow, columns, pops, solid, depth, rows):
-    width = flow[0].shape[1]
+def couple(shape, beads, flow, columns, pops, solid):
+    _, depth, rows, width = pops.shape
     single = beads.shape[0] == GROUP
     tile = jax.ShapeDtypeStruct((8, 128), F32)
     drags = [jax.ShapeDtypeStruct((shape[0], 8, 128), F32), tile] if single else [beads]
     message = jax.ShapeDtypeStruct((5 * rows + (8 if single else 0), width), F32)
     return pl.pallas_call(
-        functools.partial(couple_kernel, shape, depth, rows, len(drags)),
+        functools.partial(couple_kernel, shape, len(drags)),
         out_shape=[
             jax.ShapeDtypeStruct((3, depth, rows, width), F32),
             jax.ShapeDtypeStruct((2, rows, 128), F32),
@@ -423,8 +430,8 @@
 
 
 def entered_z(first_ref, second_ref, side, rows):
-    even = even_slab() if side == 0 else jnp.logical_not(even_slab())
-    return jnp.where(even, second_ref[rows], first_ref[rows])
+    odd = odd_slab() if side == 0 else jnp.logical_not(odd_slab())
+    return jnp.where(odd, second_ref[rows], first_ref[rows])
 
 
 X_EDGES = [i for side in range(2) for i in ENTER[2][side] if STEP[i, 0] != 0]
@@ -742,7 +749,7 @@
     messages = swap(messages)
     *flow, columns, sides, walls = moments(populations, solid_mask)
     force, face, first, second, drag, *far, token = couple(
-        shape, messages, flow, columns, populations, solid_mask, depth, rows
+        shape, messages, flow, columns, populations, solid_mask
     )
 
     def send_pair(value):
@@ -755,14 +762,14 @@
         ]
 
     face = send_pair(face)
-    first, second = send_slab(first, shape, 0), send_slab(second, shape, 1)
+    first, second = send_slab(first, shape, 1), send_slab(second, shape, 0)
     if single:
         drags = [drag, send(far[0], shape, lambda s, c, p: ((s + 2) % slabs, c, p))]
     else:
         drags = []
         drag = swap(drag)
     fields = (populations, solid_mask, force)
-    lower, draft, token = stream_lower(depth // 2, token, *fields, sides, walls)
+    lower, draft, token = stream_lower(10, token, *fields, sides, walls)
     *leaving, cross, token = leaving_rows(depth, rows, token, draft, face, first, second, drags)
     entered, cross = send_col(leaving), send_pair(cross)
     whole, tiles = stream_upper(token, lower, *fields, face)

time: 30.7 us -> 29.8 us (0.971)
  waiting for transfers between devices: 5.66 us -> 4.24 us
  starting transfers between devices: 11.8 us -> 12.7 us
  Pallas kernels: 11.4 us -> 11 us
    ppermute x6, waiting for transfers between devices: 2.65 us -> 1.33 us  [send(): return lax.ppermute(value, ('slab', 'col', 'pair'), perm)]
    ppermute x6, starting transfers between devices: 4.51 us -> 5.43 us  [send(): return lax.ppermute(value, ('slab', 'col', 'pair'), perm)]
    pallas_call x1, Pallas kernels: 2.81 us -> 2.49 us  [stream_upper(): pl.pallas_call(upper_kernel, out_shape=[jax.ShapeDtypeStruct(pops.shape,...]
where the time goes in v12:
time: 29.8 us; the launch traced here: 29.5 us
  starting transfers between devices  12.7 us (43%)
  Pallas kernels  11 us (37%)
  waiting for transfers between devices  4.24 us (14%)
  local copies, waits for them, and re-layouts  0.92 us (3%)
  between operations  0.7 us (2%)
    all_to_all x1, starting transfers between devices, shards(): messages = swap(messages)  7.25 us
    ppermute x6, starting transfers between devices, send(): return lax.ppermute(value, ('slab', 'col', 'pair'), perm)  5.43 us
    all_to_all x1, waiting for transfers between devices, shards(): messages = swap(messages)  2.91 us
    pallas_call x1, Pallas kernels, moments(): pl.pallas_call(moments_kernel, out_shape=[jax.ShapeDtypeStruct((3 * width...  2.86 us
    pallas_call x1, Pallas kernels, stream_upper(): pl.pallas_call(upper_kernel, out_shape=[jax.ShapeDtypeStruct(pops.shape,...  2.49 us
    pallas_call x1, Pallas kernels, pack(): pl.pallas_call(functools.partial(pack_kernel, steps), out_shape=[jax.Shap...  1.89 us
    ppermute x6, waiting for transfers between devices, send(): return lax.ppermute(value, ('slab', 'col', 'pair'), perm)  1.33 us
    pallas_call x1, Pallas kernels, stream_lower(): pl.pallas_call(lower_kernel, out_shape=[jax.ShapeDtypeStruct((19, half, r...  1.28 us
  transfers between devices with their start and end apart: 7, of which 3 were waited for; matrix products, arithmetic and copies ran while one was open for 0% of the time, Pallas kernels for 22%

profile of v12, /device:TPU:0, one launch (start us, length us, event | category | flops | bytes accessed | tf_op | source)
XLA Modules:
  0.0 29.5 jit_solution(8905026475866224075)
XLA Ops:
  0.6 0.0 copy-start
  0.6 1.9 %pack.1 = (s32[1,128]{1,0:T(1,128)}, f32[8,8,128]{2,1,0:T(8,128)}) custom-call(s32[1,128]{1,0:T(1,128)} %bitcast.1, s32[3,128]{1,0:T(4,128)} %base_ref.1, f32[3,128]{1,0:T(4,128)} %offset_ref.1, f32[3,128]{1,0:T(4,128)} %velocity_ref.1), custom_call_target="tpu_custom_call" | custom-call | tf_op jit(solution)/shard_map/pack/pallas_call | solution.py:229
  2.5 7.3 %all-to-all-start = ((f32[8,8,128]{2,1,0:T(8,128)}), f32[8,8,128]{2,1,0:T(8,128)S(1)}, u32[]{:S(2)}, u32[]{:S(2)}) async-start(f32[8,8,128]{2,1,0:T(8,128)} %get-tuple-element.24), calls=%async_computation | async-start | bytes 65536 | tf_op jit(solution)/shard_map/all_to_all | solution.py:749
  9.8 0.9 %copy-done.1 = s32[16,16,128]{2,1,0:T(8,128)S(1)} copy-done((s32[16,16,128]{2,1,0:T(8,128)S(1)}, s32[16,16,128]{2,1,0:T(8,128)}, u32[]{:S(2)}) %copy-start.1) | copy-done | bytes 131096
  10.7 2.9 %moments.1 = (bf16[384,256]{1,0:T(8,128)(2,1)S(1)}, bf16[384,256]{1,0:T(8,128)(2,1)S(1)}, f32[20,16,128]{2,1,0:T(8,128)S(1)}, f32[19,2,16,128]{3,2,1,0:T(8,128)S(1)}, s32[2,16,128]{2,1,0:T(8,128)S(1)}) custom-call(f32[19,16,16,128]{3,2,1,0:T(8,128)} %pops_ref.5, s32[16,16,128]{2,1,0:T(8,128)S(1)} %copy-done.1), custom_call_target="tpu_custom_call" | custom-call | flops 3000000 | bytes 4000000 | tf_op jit(solution)/shard_map/moments/pallas_call | solution.py:283
  13.6 2.9 %all-to-all-done.beads_ref = f32[8,8,128]{2,1,0:T(8,128)S(1)} async-done(((f32[8,8,128]{2,1,0:T(8,128)}), f32[8,8,128]{2,1,0:T(8,128)S(1)}, u32[]{:S(2)}, u32[]{:S(2)}) %all-to-all-start) | async-done | bytes 32800 | tf_op jit(solution)/shard_map/all_to_all | solution.py:749
  16.5 1.2 %couple.1 = (f32[3,16,16,128]{3,2,1,0:T(8,128)S(1)}, f32[2,16,128]{2,1,0:T(8,128)S(1)}, f32[88,128]{1,0:T(8,128)S(1)}, f32[88,128]{1,0:T(8,128)S(1)}, f32[4,8,12...) custom-call(f32[8,8,128]{2,1,0:T(8,128)S(1)} %all-to-all-done.beads_ref, ...), custom_call_target="tpu_custom_call" | custom-call | tf_op jit(solution)/shard_map/couple/pallas_call | solution.py:417
  17.7 1.0 %collective-permute-start.1 = (f32[88,128]{1,0:T(8,128)S(1)}, f32[88,128]{1,0:T(8,128)S(1)}, u32[]{:S(2)}, u32[]{:S(2)}) collective-permute-start(f32[88,128]{1,0:T(8,128)S(1)} %get-tuple-element.35), channel_id=1, source_target_pairs={{0,12},{1,13},{2,14},{3,15},{4,8},{5,9},{6,10},{7,11},{8,4},{9,5},... | collective-permute-start | bytes 135176 | tf_op jit(solution)/shard_map/ppermute | solution.py:140
  18.7 0.1 collective-permute-start.2
  18.8 0.0 collective-permute-start
  18.8 3.3 %collective-permute-start.3 = (f32[8,128]{1,0:T(8,128)S(1)}, f32[8,128]{1,0:T(8,128)S(1)}, u32[]{:S(2)}, u32[]{:S(2)}) collective-permute-start(f32[8,128]{1,0:T(8,128)S(1)} %get-tuple-element.38), channel_id=1, source_target_pairs={{0,8},{1,9},{2,10},{3,11},{4,12},{5,13},{6,14},{7,15},{8,0},{9,1},... | collective-permute-start | bytes 12296 | tf_op jit(solution)/shard_map/ppermute | solution.py:140
  22.1 1.3 %lower.1 = (f32[19,10,16,128]{3,2,1,0:T(8,128)S(1)}, f32[160,128]{1,0:T(8,128)S(1)}, f32[8,128]{1,0:T(8,128)S(1)}) custom-call(f32[8,128]{1,0:T(8,128)S(1)} %get-tuple-element.28.before_ref, f32[19,16,16,128]{3,2,1,0:T(8,128)S(1)} %copy-done, s32[16,16,128]{2,1,0:T(8,128)S(1)} %copy-done.2, f32[3,16,16,128]{3,2,1,0:T(8,128)S(1)} %get-tuple-element.29.force_ref, ...), custom_call_target="tpu_custom_call" | custom-call | flops 3000000 | bytes 2000000 | tf_op jit(solution)/shard_map/lower/pallas_call | solution.py:599
  23.4 0.0 copy-start.3
  23.4 0.3 collective-permute-done.3.refs_1_.refs_3_
  23.7 0.0 collective-permute-done.face_ref
  23.7 0.0 collective-permute-done.1.first_ref
  23.7 0.0 collective-permute-done.2.second_ref
  23.7 0.2 rows.1
  23.9 1.0 %collective-permute-start.4 = (f32[168,128]{1,0:T(8,128)S(1)}, f32[168,128]{1,0:T(8,128)S(1)}, u32[]{:S(2)}, u32[]{:S(2)}) collective-permute-start(f32[168,128]{1,0:T(8,128)S(1)} %get-tuple-element.44), channel_id=1, source_target_pairs={{0,2},{1,3},{2,0},{3,1},{4,6},{5,7},{6,4},{7,5},{8,10},{9,11},{10,... | collective-permute-start | bytes 258056 | tf_op jit(solution)/shard_map/ppermute | solution.py:140
  24.9 0.0 collective-permute-start.5
  24.9 2.5 %upper.1 = (f32[19,16,16,128]{3,2,1,0:T(8,128)}, f32[10,16,8,128]{3,2,1,0:T(8,128)S(1)}) custom-call(f32[8,128]{1,0:T(8,128)S(1)} %get-tuple-element.39.before_ref, f32[19,10,16,128]{3,2,1,0:T(8,128)S(1)} %get-tuple-element.40.lower_ref, f32[19,16,16,128]{3,2,1,0:T(8,128)S(1)} %copy-done, s32[16,16,128]{2,1,0:T(8,128)S(1)} %copy-done.2, ...), custom_call_target="tpu_custom_call" | custom-call | flops 5000000 | bytes 3000000 | tf_op jit(solution)/shard_map/upper/pallas_call | solution.py:616
  27.4 0.0 collective-permute-done.5.refs_1_
  27.4 1.0 %collective-permute-done.4.refs_0_ = f32[168,128]{1,0:T(8,128)S(1)} collective-permute-done((f32[168,128]{1,0:T(8,128)S(1)}, f32[168,128]{1,0:T(8,128)S(1)}, u32[]{:S(2)}, u32[]{:S(2)}) %collective-permute-start.4) | collective-permute-done | bytes 86048 | tf_op jit(solution)/shard_map/ppermute | solution.py:140
  28.4 1.1 %finish.1 = (f32[19,16,16,128]{3,2,1,0:T(8,128)}, f32[3,128]{1,0:T(4,128)}) custom-call(f32[19,16,16,128]{3,2,1,0:T(8,128)} %get-tuple-element.41.whole_ref, s32[1,128]{1,0:T(1,128)S(1)} %copy-done.3, f32[10,16,8,128]{3,2,1,0:T(8,128)S(1)} %get-tuple-element.43.tile_ref, ...), custom_call_target="tpu_custom_call", output_to_operand_aliasing={{0}: (0, {})} | custom-call | tf_op jit(solution)/shard_map/finish/pallas_call | solution.py:719
  (5 shorter events, 0.0 us)
Async XLA Ops:
  0.6 15.8 %copy-start = (f32[19,16,16,128]{3,2,1,0:T(8,128)S(1)}, f32[19,16,16,128]{3,2,1,0:T(8,128)}, u32[]{:S(2)}) copy-start(f32[19,16,16,128]{3,2,1,0:T(8,128)} %pops_ref.5) | copy-start | bytes 7471108
  2.5 13.9 %all-to-all-start = ((f32[8,8,128]{2,1,0:T(8,128)}), f32[8,8,128]{2,1,0:T(8,128)S(1)}, u32[]{:S(2)}, u32[]{:S(2)}) async-start(f32[8,8,128]{2,1,0:T(8,128)} %get-tuple-element.24), calls=%async_computation | async-start | bytes 65536 | tf_op jit(solution)/shard_map/all_to_all | solution.py:749
  9.8 0.9 %copy-start.1 = (s32[16,16,128]{2,1,0:T(8,128)S(1)}, s32[16,16,128]{2,1,0:T(8,128)}, u32[]{:S(2)}) copy-start(s32[16,16,128]{2,1,0:T(8,128)} %solid_ref.5) | copy-start | bytes 393220
  10.7 5.8 %copy-start.2 = (s32[16,16,128]{2,1,0:T(8,128)S(1)}, s32[16,16,128]{2,1,0:T(8,128)}, u32[]{:S(2)}) copy-start(s32[16,16,128]{2,1,0:T(8,128)} %solid_ref.5) | copy-start | bytes 393220
  17.7 6.0 %collective-permute-start.1 = (f32[88,128]{1,0:T(8,128)S(1)}, f32[88,128]{1,0:T(8,128)S(1)}, u32[]{:S(2)}, u32[]{:S(2)}) collective-permute-start(f32[88,128]{1,0:T(8,128)S(1)} %get-tuple-element.35), channel_id=1, source_target_pairs={{0,12},{1,13},{2,14},{3,15},{4,8},{5,9},{6,10},{7,11},{8,4},{9,5},... | collective-permute-start | bytes 135176 | tf_op jit(solution)/shard_map/ppermute | solution.py:140
  18.7 5.0 %collective-permute-start.2 = (f32[88,128]{1,0:T(8,128)S(1)}, f32[88,128]{1,0:T(8,128)S(1)}, u32[]{:S(2)}, u32[]{:S(2)}) collective-permute-start(f32[88,128]{1,0:T(8,128)S(1)} %get-tuple-element.36), channel_id=1, source_target_pairs={{0,4},{1,5},{2,6},{3,7},{4,0},{5,1},{6,2},{7,3},{8,12},{9,13},{10,... | collective-permute-start | bytes 135176 | tf_op jit(solution)/shard_map/ppermute | solution.py:140
  18.8 4.9 %collective-permute-start = (f32[2,16,128]{2,1,0:T(8,128)S(1)}, f32[2,16,128]{2,1,0:T(8,128)S(1)}, u32[]{:S(2)}, u32[]{:S(2)}) collective-permute-start(f32[2,16,128]{2,1,0:T(8,128)S(1)} %get-tuple-element.34), channel_id=1, source_target_pairs={{0,1},{1,0},{2,3},{3,2},{4,5},{5,4},{6,7},{7,6},{8,9},{9,8},{10,11... | collective-permute-start | bytes 49160 | tf_op jit(solution)/shard_map/ppermute | solution.py:140
  18.8 4.9 %collective-permute-start.3 = (f32[8,128]{1,0:T(8,128)S(1)}, f32[8,128]{1,0:T(8,128)S(1)}, u32[]{:S(2)}, u32[]{:S(2)}) collective-permute-start(f32[8,128]{1,0:T(8,128)S(1)} %get-tuple-element.38), channel_id=1, source_target_pairs={{0,8},{1,9},{2,10},{3,11},{4,12},{5,13},{6,14},{7,15},{8,0},{9,1},... | collective-permute-start | bytes 12296 | tf_op jit(solution)/shard_map/ppermute | solution.py:140
  23.4 5.0 %copy-start.3 = (s32[1,128]{1,0:T(1,128)S(1)}, s32[1,128]{1,0:T(1,128)}, u32[]{:S(2)}) copy-start(s32[1,128]{1,0:T(1,128)} %get-tuple-element.42.target_ref) | copy-start | bytes 1540
  23.9 4.6 %collective-permute-start.4 = (f32[168,128]{1,0:T(8,128)S(1)}, f32[168,128]{1,0:T(8,128)S(1)}, u32[]{:S(2)}, u32[]{:S(2)}) collective-permute-start(f32[168,128]{1,0:T(8,128)S(1)} %get-tuple-element.44), channel_id=1, source_target_pairs={{0,2},{1,3},{2,0},{3,1},{4,6},{5,7},{6,4},{7,5},{8,10},{9,11},{10,... | collective-permute-start | bytes 258056 | tf_op jit(solution)/shard_map/ppermute | solution.py:140
  24.9 2.5 %collective-permute-start.5 = (f32[64,128]{1,0:T(8,128)S(1)}, f32[64,128]{1,0:T(8,128)S(1)}, u32[]{:S(2)}, u32[]{:S(2)}) collective-permute-start(f32[64,128]{1,0:T(8,128)S(1)} %get-tuple-element.45), channel_id=1, source_target_pairs={{0,1},{1,0},{2,3},{3,2},{4,5},{5,4},{6,7},{7,6},{8,9},{9,8},{10,11... | collective-permute-start | bytes 98312 | tf_op jit(solution)/shard_map/ppermute | solution.py:140

commit v13 on v12

--- a/solution.py
+++ b/solution.py
@@ -46,6 +46,7 @@
 
 ENTER = [[[i for i in range(19) if STEP[i, a] == sign] for sign in (1, -1)] for a in range(3)]
 TOKEN = jax.ShapeDtypeStruct((8, 128), F32)
+LONG = pl.CostEstimate(flops=5000000000, bytes_accessed=1000000000, transcendentals=0)
 ROOM = 16 << 20
 NT = (((1,), (1,)), ((), ()))
 NN = (((1,), (0,)), ((), ()))
@@ -429,48 +430,73 @@
     )(beads, *flow, columns, pops, solid)
 
 
-def entered_z(first_ref, second_ref, side, rows):
-    odd = odd_slab() if side == 0 else jnp.logical_not(odd_slab())
-    return jnp.where(odd, second_ref[rows], first_ref[rows])
-
-
-X_EDGES = [i for side in range(2) for i in ENTER[2][side] if STEP[i, 0] != 0]
-
-
-def rows_kernel(depth, rows, before_ref, draft_ref, face_ref, first_ref, second_ref, *refs):
-    refs, (cross_ref, token_ref, turned) = refs[:-3], refs[-3:]
+def sides_kernel(before_ref, force_ref, side_ref, wall_ref, face_ref, *refs):
+    outs, token_ref, turned = refs[:-2], refs[-2], refs[-1]
+    depth, rows = force_ref.shape[1:3]
     token_ref[...] = jnp.zeros_like(token_ref)
-    outs = refs[-1:] if len(refs) == 3 else refs
     for n in range(2):
         turned[n] = face_ref[n].T
     for group in range(2):
-        out_ref = outs[0] if len(outs) == 1 else outs[group]
-        base = group * 5 * depth if len(outs) == 1 else 0
         y = rows - 1 if group == 0 else 0
+        force = [force_ref[d, :, y, :] for d in range(3)]
+        out = collide([side_ref[i, 1 - group] for i in range(19)], wall_ref[1 - group] == 1, force)
         for k, i in enumerate(ENTER[1][group]):
-            at = base + k * depth
-            value = draft_ref[(group * 5 + k) * depth : (group * 5 + k + 1) * depth]
+            value = turn(out[i], STEP[i, 0], 1)
             if STEP[i, 0] != 0:
                 tile, lane = x_place(i)
                 column = turned[tile, pl.ds(lane, depth, stride=2), :][:, y : y + 1]
                 value = patch_x(value, i, jnp.broadcast_to(column, value.shape))
-            out_ref[at : at + depth] = value
-            if STEP[i, 2] != 0:
-                side = 0 if STEP[i, 2] == 1 else 1
-                z = 0 if side == 0 else depth - 1
-                row = ENTER[2][side].index(i) * rows + y
-                out_ref[at + z : at + z + 1] = entered_z(
-                    first_ref, second_ref, side, slice(row, row + 1)
-                )
-    if len(refs) == 3:
-        own_ref, far_ref, out_ref = refs
+            out_ref, base = (outs[0], 5 * depth * group) if len(outs) == 1 else (outs[group], 0)
+            at = base + k * depth
+            out_ref[at : at + depth] = turn(value, STEP[i, 2], 0)
+
+
+def side_rows(cols, before, force, sides, walls, face):
+    _, depth, rows, width = force.shape
+    sizes = [10 * depth] if cols == 2 else [5 * depth] * 2
+    return pl.pallas_call(
+        sides_kernel,
+        out_shape=[jax.ShapeDtypeStruct((n, width), F32) for n in sizes] + [TOKEN],
+        in_specs=[pl.BlockSpec(memory_space=pl.ANY)] + [pl.BlockSpec(memory_space=pltpu.VMEM)] * 4,
+        scratch_shapes=[pltpu.VMEM((2, 128, rows), F32)],
+        compiler_params=pltpu.CompilerParams(vmem_limit_bytes=ROOM),
+        name="sides",
+    )(before, force, sides, walls, face)
+
+
+def entered_z(first_ref, second_ref, side, rows):
+    odd = odd_slab() if side == 0 else jnp.logical_not(odd_slab())
+    return jnp.where(odd, second_ref[rows], first_ref[rows])
+
+
+X_EDGES = [i for side in range(2) for i in ENTER[2][side] if STEP[i, 0] != 0]
+Y_EDGES = [[i for i in ENTER[1][side] if STEP[i, 2] != 0] for side in range(2)]
+
+
+def z_side(i):
+    return 0 if STEP[i, 2] == 1 else 1
+
+
+def edges_kernel(rows, before_ref, first_ref, second_ref, *refs):
+    cross_ref, token_ref = refs[-2:]
+    token_ref[...] = jnp.zeros_like(token_ref)
+    own_ref, far_ref = refs[:2] if len(refs) == 5 else (None, None)
+    outs = refs[:-2] if own_ref is None else refs[2:-2]
+    for group in range(2):
+        y = rows - 1 if group == 0 else 0
+        out_ref, row = (outs[0], 2 * group) if len(outs) == 1 else (outs[group], 0)
+        for k, i in enumerate(Y_EDGES[group]):
+            at = ENTER[2][z_side(i)].index(i) * rows + y
+            out_ref[row + k : row + k + 1] = entered_z(
+                first_ref, second_ref, z_side(i), slice(at, at + 1)
+            )
+    if own_ref is not None:
         came = arrived_drag(own_ref, far_ref, first_ref, second_ref, 5 * rows)
-        out_ref[10 * depth : 10 * depth + 8] = one_tile(came, 1)
+        outs[0][8:16] = one_tile(came, 1)
     for k, i in enumerate(X_EDGES):
-        side = 0 if STEP[i, 2] == 1 else 1
-        at = ENTER[2][side].index(i) * rows
+        at = ENTER[2][z_side(i)].index(i) * rows
         cross_ref[k * rows : (k + 1) * rows] = entered_z(
-            first_ref, second_ref, side, slice(at, at + rows)
+            first_ref, second_ref, z_side(i), slice(at, at + rows)
         )
 
 
@@ -484,21 +510,17 @@
     return jnp.concatenate([t[:, col * CAP : (col + 1) * CAP] for t in tiles], axis=1)
 
 
-def leaving_rows(depth, rows, before, draft, face, first, second, drags):
-    width = draft.shape[1]
-    if drags:
-        sizes = [10 * depth + 8]
-    else:
-        sizes = [5 * depth] * 2
-    args = (draft, face, first, second, *drags)
+def edges(cols, rows, before, first, second, drags):
+    width = first.shape[1]
+    sizes = ([16] if drags else [8]) if cols == 2 else [8, 8]
+    args = (first, second, *drags)
     return pl.pallas_call(
-        functools.partial(rows_kernel, depth, rows),
+        functools.partial(edges_kernel, rows),
         out_shape=[jax.ShapeDtypeStruct((n, width), F32) for n in sizes + [4 * rows]] + [TOKEN],
         in_specs=[pl.BlockSpec(memory_space=pl.ANY)]
         + [pl.BlockSpec(memory_space=pltpu.VMEM)] * len(args),
-        scratch_shapes=[pltpu.VMEM((2, 128, rows), F32)],
         compiler_params=pltpu.CompilerParams(vmem_limit_bytes=ROOM),
-        name="rows",
+        name="edges",
     )(before, *args)
 
 
@@ -530,18 +552,8 @@
     return lax.fori_loop(low, high, plane, faces, unroll=2)
 
 
-def lower_kernel(
-    before_ref, pops_ref, solid_ref, force_ref, side_ref, wall_ref, held, draft_ref, token_ref
-):
-    depth, rows, _ = pops_ref.shape[1:]
+def lower_kernel(before_ref, pops_ref, solid_ref, force_ref, held, token_ref):
     token_ref[...] = jnp.zeros_like(token_ref)
-    for group in range(2):
-        force = [force_ref[d, :, 0 if group else rows - 1, :] for d in range(3)]
-        out = collide([side_ref[i, 1 - group] for i in range(19)], wall_ref[1 - group] == 1, force)
-        for k, i in enumerate(ENTER[1][group]):
-            row = (group * 5 + k) * depth
-            value = turn(out[i], STEP[i, 0], 1)
-            draft_ref[row : row + depth] = turn(value, STEP[i, 2], 0)
     stream_planes(0, held.shape[1], (), pops_ref, solid_ref, force_ref, held)
 
 
@@ -593,21 +605,17 @@
     return list(range(half, depth - 2, 4)) + ([depth - 2] if (depth - half) % 4 else []) + [depth]
 
 
-def stream_lower(half, before, pops, solid, force, sides, walls):
-    _, depth, rows, width = pops.shape
+def stream_lower(half, before, pops, solid, force):
+    _, _, rows, width = pops.shape
     vmem = pl.BlockSpec(memory_space=pltpu.VMEM)
     return pl.pallas_call(
         lower_kernel,
-        out_shape=[
-            jax.ShapeDtypeStruct((19, half, rows, width), F32),
-            jax.ShapeDtypeStruct((10 * depth, width), F32),
-            TOKEN,
-        ],
-        in_specs=[pl.BlockSpec(memory_space=pl.ANY)] + [vmem] * 5,
+        out_shape=[jax.ShapeDtypeStruct((19, half, rows, width), F32), TOKEN],
+        in_specs=[pl.BlockSpec(memory_space=pl.ANY)] + [vmem] * 3,
         compiler_params=pltpu.CompilerParams(vmem_limit_bytes=ROOM),
-        cost_estimate=pl.CostEstimate(flops=3000000, bytes_accessed=2000000, transcendentals=0),
+        cost_estimate=pl.CostEstimate(flops=300000000, bytes_accessed=100000000, transcendentals=0),
         name="lower",
-    )(before, pops, solid, force, sides, walls)
+    )(before, pops, solid, force)
 
 
 def stream_upper(before, lower, pops, solid, force, face):
@@ -626,19 +634,30 @@
             pltpu.SemaphoreType.DMA((20 * len(upper_marks(lower.shape[1], depth)),)),
         ],
         compiler_params=pltpu.CompilerParams(vmem_limit_bytes=ROOM),
-        cost_estimate=pl.CostEstimate(flops=5000000, bytes_accessed=3000000, transcendentals=0),
+        cost_estimate=LONG,
         name="upper",
     )(before, lower, pops, solid, force, face)
 
 
 def finish_kernel(shape, n_rows, whole_ref, target_ref, tile_ref, first_ref, second_ref, *refs):
-    row_refs, cross_ref, refs = refs[:n_rows], refs[n_rows], refs[n_rows + 1 :]
+    row_refs, edge_refs, refs = refs[:n_rows], refs[n_rows : 2 * n_rows], refs[2 * n_rows :]
+    cross_ref, refs = refs[0], refs[1:]
     drag_refs, (out_ref, bead_ref, planes, tiles, bead, sem) = refs[:-6], refs[-6:]
     depth, rows, width = whole_ref.shape[1:]
 
     def entering(group, k):
         at = (group * 5 + k) * depth if n_rows == 1 else k * depth
-        return row_refs[group % n_rows][at : at + depth]
+        value = row_refs[group % n_rows][at : at + depth]
+        i = ENTER[1][group][k]
+        if STEP[i, 2] == 0:
+            return value
+        z = 0 if STEP[i, 2] == 1 else depth - 1
+        edge = jnp.broadcast_to(edge_row(group, i), value.shape)
+        return jnp.where(iota(value.shape, 0) == z, edge, value)
+
+    def edge_row(group, i):
+        row = Y_EDGES[group].index(i) + (2 * group if n_rows == 1 else 0)
+        return edge_refs[group % n_rows][row : row + 1]
 
     copies = []
 
@@ -654,10 +673,9 @@
             if STEP[i, 1] != 0:
                 side = 0 if STEP[i, 1] == 1 else 1
                 y = 0 if side == 0 else rows - 1
-                row = entering(side, ENTER[1][side].index(i))[z : z + 1]
                 value = jnp.where(
                     iota((rows, width), 0) == y,
-                    jnp.broadcast_to(row, (rows, width)),
+                    jnp.broadcast_to(edge_row(side, i), (rows, width)),
                     turn(value, STEP[i, 1], 0),
                 )
             if STEP[i, 0] != 0:
@@ -681,7 +699,7 @@
     if len(drag_refs) == 2:
         slabs, cols, _ = shape
         came = arrived_drag(*drag_refs, first_ref, second_ref, 5 * rows)
-        passed = row_refs[0][10 * depth : 10 * depth + 8]
+        passed = edge_refs[0][8:16]
         table = jnp.concatenate([one_tile(came, 0), passed], axis=1)
         owner = lax.shift_right_logical(target, 5)
         owner_slab = lax.shift_right_logical(owner, cols.bit_length() - 1)
@@ -711,11 +729,11 @@
         copy.wait()
 
 
-def finish(shape, whole, target, tiles, first, second, entered, cross, drags):
+def finish(shape, whole, target, tiles, first, second, entered, late, cross, drags):
     _, depth, rows, width = whole.shape
     vmem = pl.BlockSpec(memory_space=pltpu.VMEM)
     hbm = pl.BlockSpec(memory_space=pltpu.HBM)
-    args = [whole, target, tiles, first, second, *entered, cross, *drags]
+    args = [whole, target, tiles, first, second, *entered, *late, cross, *drags]
     return pl.pallas_call(
         functools.partial(finish_kernel, shape, len(entered)),
         out_shape=[
@@ -769,12 +787,16 @@
         drags = []
         drag = swap(drag)
     fields = (populations, solid_mask, force)
-    lower, draft, token = stream_lower(10, token, *fields, sides, walls)
-    *leaving, cross, token = leaving_rows(depth, rows, token, draft, face, first, second, drags)
-    entered, cross = send_col(leaving), send_pair(cross)
+    lower, token = stream_lower(4, token, *fields)
+    *entered, token = side_rows(cols, token, force, sides, walls, face)
+    entered = send_col(entered)
+    *late, cross, token = edges(cols, rows, token, first, second, drags)
+    late, cross = send_col(late), send_pair(cross)
     whole, tiles = stream_upper(token, lower, *fields, face)
     return tuple(
-        finish(shape, whole, target, tiles, first, second, entered, cross, drags or [drag])
+        finish(
+            shape, whole, target, tiles, first, second, entered, late, cross, drags or [drag]
+        )
     )
 
 

time: 29.8 us -> 30.7 us (1.030)
  starting transfers between devices: 12.7 us -> 13.8 us
  waiting for transfers between devices: 4.24 us -> 3.68 us
    ppermute x6 -> x7, starting transfers between devices: 5.43 us -> 6.52 us  [send(): return lax.ppermute(value, ('slab', 'col', 'pair'), perm)]
    pallas_call x1, Pallas kernels: 2.49 us -> 3.43 us  [stream_upper(): pl.pallas_call(upper_kernel, out_shape=[jax.ShapeDtypeStruct(pops.shape,...]
    pallas_call x1, Pallas kernels: 1.28 us -> 0.42 us  [stream_lower(): pl.pallas_call(lower_kernel, out_shape=[jax.ShapeDtypeStruct((19, half, r...]
    ppermute x6 -> x7, waiting for transfers between devices: 1.33 us -> 0.77 us  [send(): return lax.ppermute(value, ('slab', 'col', 'pair'), perm)]
  transfers between devices with their start and end apart: 7 -> 8, of which waited for: 3 -> 2; matrix products, arithmetic and copies ran while one was open for 0% -> 0% of each run, Pallas kernels for 22% -> 23%
where the time goes in v13:
time: 30.7 us; the launch traced here: 30.3 us
  starting transfers between devices  13.8 us (45%)
  Pallas kernels  11.3 us (37%)
  waiting for transfers between devices  3.68 us (12%)
  local copies, waits for them, and re-layouts  0.91 us (3%)
  between operations  0.71 us (2%)
    all_to_all x1, starting transfers between devices, shards(): messages = swap(messages)  7.25 us
    ppermute x7, starting transfers between devices, send(): return lax.ppermute(value, ('slab', 'col', 'pair'), perm)  6.52 us
    pallas_call x1, Pallas kernels, stream_upper(): pl.pallas_call(upper_kernel, out_shape=[jax.ShapeDtypeStruct(pops.shape,...  3.43 us
    all_to_all x1, waiting for transfers between devices, shards(): messages = swap(messages)  2.91 us
    pallas_call x1, Pallas kernels, moments(): pl.pallas_call(moments_kernel, out_shape=[jax.ShapeDtypeStruct((3 * width...  2.86 us
    pallas_call x1, Pallas kernels, pack(): pl.pallas_call(functools.partial(pack_kernel, steps), out_shape=[jax.Shap...  1.89 us
    pallas_call x1, Pallas kernels, couple(): pl.pallas_call(functools.partial(couple_kernel, shape, len(drags)), out_s...  1.23 us
    pallas_call x1, Pallas kernels, finish(): pl.pallas_call(functools.partial(finish_kernel, shape, len(entered)), out...  1.08 us
  transfers between devices with their start and end apart: 8, of which 2 were waited for; matrix products, arithmetic and copies ran while one was open for 0% of the time, Pallas kernels for 23%

profile of v13, /device:TPU:0, one launch (start us, length us, event | category | flops | bytes accessed | tf_op | source)
XLA Modules:
  0.0 30.3 jit_solution(8772147929194492031)
XLA Ops:
  0.6 0.0 copy-start
  0.6 1.9 %pack.1 = (s32[1,128]{1,0:T(1,128)}, f32[8,8,128]{2,1,0:T(8,128)}) custom-call(s32[1,128]{1,0:T(1,128)} %bitcast.1, s32[3,128]{1,0:T(4,128)} %base_ref.1, f32[3,128]{1,0:T(4,128)} %offset_ref.1, f32[3,128]{1,0:T(4,128)} %velocity_ref.1), custom_call_target="tpu_custom_call" | custom-call | tf_op jit(solution)/shard_map/pack/pallas_call | solution.py:230
  2.5 7.3 %all-to-all-start = ((f32[8,8,128]{2,1,0:T(8,128)}), f32[8,8,128]{2,1,0:T(8,128)S(1)}, u32[]{:S(2)}, u32[]{:S(2)}) async-start(f32[8,8,128]{2,1,0:T(8,128)} %get-tuple-element.25), calls=%async_computation | async-start | bytes 65536 | tf_op jit(solution)/shard_map/all_to_all | solution.py:767
  9.8 0.9 %copy-done.1 = s32[16,16,128]{2,1,0:T(8,128)S(1)} copy-done((s32[16,16,128]{2,1,0:T(8,128)S(1)}, s32[16,16,128]{2,1,0:T(8,128)}, u32[]{:S(2)}) %copy-start.1) | copy-done | bytes 131096
  10.7 2.9 %moments.1 = (bf16[384,256]{1,0:T(8,128)(2,1)S(1)}, bf16[384,256]{1,0:T(8,128)(2,1)S(1)}, f32[20,16,128]{2,1,0:T(8,128)S(1)}, f32[19,2,16,128]{3,2,1,0:T(8,128)S(1)}, s32[2,16,128]{2,1,0:T(8,128)S(1)}) custom-call(f32[19,16,16,128]{3,2,1,0:T(8,128)} %pops_ref.5, s32[16,16,128]{2,1,0:T(8,128)S(1)} %copy-done.1), custom_call_target="tpu_custom_call" | custom-call | flops 3000000 | bytes 4000000 | tf_op jit(solution)/shard_map/moments/pallas_call | solution.py:284
  13.6 2.9 %all-to-all-done.beads_ref = f32[8,8,128]{2,1,0:T(8,128)S(1)} async-done(((f32[8,8,128]{2,1,0:T(8,128)}), f32[8,8,128]{2,1,0:T(8,128)S(1)}, u32[]{:S(2)}, u32[]{:S(2)}) %all-to-all-start) | async-done | bytes 32800 | tf_op jit(solution)/shard_map/all_to_all | solution.py:767
  16.5 1.2 %couple.1 = (f32[3,16,16,128]{3,2,1,0:T(8,128)S(1)}, f32[2,16,128]{2,1,0:T(8,128)S(1)}, f32[88,128]{1,0:T(8,128)S(1)}, f32[88,128]{1,0:T(8,128)S(1)}, f32[4,8,12...) custom-call(f32[8,8,128]{2,1,0:T(8,128)S(1)} %all-to-all-done.beads_ref, ...), custom_call_target="tpu_custom_call" | custom-call | tf_op jit(solution)/shard_map/couple/pallas_call | solution.py:418
  17.7 1.0 %collective-permute-start.1 = (f32[88,128]{1,0:T(8,128)S(1)}, f32[88,128]{1,0:T(8,128)S(1)}, u32[]{:S(2)}, u32[]{:S(2)}) collective-permute-start(f32[88,128]{1,0:T(8,128)S(1)} %get-tuple-element.36), channel_id=1, source_target_pairs={{0,12},{1,13},{2,14},{3,15},{4,8},{5,9},{6,10},{7,11},{8,4},{9,5},... | collective-permute-start | bytes 135176 | tf_op jit(solution)/shard_map/ppermute | solution.py:141
  18.7 0.1 collective-permute-start.2
  18.8 3.3 %collective-permute-start.3 = (f32[8,128]{1,0:T(8,128)S(1)}, f32[8,128]{1,0:T(8,128)S(1)}, u32[]{:S(2)}, u32[]{:S(2)}) collective-permute-start(f32[8,128]{1,0:T(8,128)S(1)} %get-tuple-element.39), channel_id=1, source_target_pairs={{0,8},{1,9},{2,10},{3,11},{4,12},{5,13},{6,14},{7,15},{8,0},{9,1},... | collective-permute-start | bytes 12296 | tf_op jit(solution)/shard_map/ppermute | solution.py:141
  22.1 0.0 collective-permute-start
  22.1 0.4 %lower.1 = (f32[19,4,16,128]{3,2,1,0:T(8,128)S(1)}, f32[8,128]{1,0:T(8,128)S(1)}) custom-call(f32[8,128]{1,0:T(8,128)S(1)} %get-tuple-element.29.before_ref, f32[19,16,16,128]{3,2,1,0:T(8,128)S(1)} %copy-done, s32[16,16,128]{2,1,0:T(8,128)S(1)} %copy-done.2, f32[3,16,16,128]{3,2,1,0:T(8,128)S(1)} %get-tuple-element.30.force_ref), custom_call_target="tpu_custom_call" | custom-call | flops 300000000 | bytes 100000000 | tf_op jit(solution)/shard_map/lower/pallas_call | solution.py:611
  22.5 0.8 %collective-permute-done.face_ref = f32[2,16,128]{2,1,0:T(8,128)S(1)} collective-permute-done((f32[2,16,128]{2,1,0:T(8,128)S(1)}, f32[2,16,128]{2,1,0:T(8,128)S(1)}, u32[]{:S(2)}, u32[]{:S(2)}) %collective-permute-start) | collective-permute-done | bytes 16416 | tf_op jit(solution)/shard_map/ppermute | solution.py:141
  23.3 0.3 sides.1
  23.6 0.5 %collective-permute-start.4 = (f32[160,128]{1,0:T(8,128)S(1)}, f32[160,128]{1,0:T(8,128)S(1)}, u32[]{:S(2)}, u32[]{:S(2)}) collective-permute-start(f32[160,128]{1,0:T(8,128)S(1)} %get-tuple-element.45), channel_id=1, source_target_pairs={{0,2},{1,3},{2,0},{3,1},{4,6},{5,7},{6,4},{7,5},{8,10},{9,11},{10,... | collective-permute-start | bytes 245768 | tf_op jit(solution)/shard_map/ppermute | solution.py:141
  24.1 0.0 collective-permute-done.3.refs_1_.refs_4_
  24.1 0.0 collective-permute-done.1.first_ref
  24.1 0.0 collective-permute-done.2.second_ref
  24.1 0.1 edges.1
  24.2 1.6 %collective-permute-start.5 = (f32[16,128]{1,0:T(8,128)S(1)}, f32[16,128]{1,0:T(8,128)S(1)}, u32[]{:S(2)}, u32[]{:S(2)}) collective-permute-start(f32[16,128]{1,0:T(8,128)S(1)} %get-tuple-element.46), channel_id=1, source_target_pairs={{0,2},{1,3},{2,0},{3,1},{4,6},{5,7},{6,4},{7,5},{8,10},{9,11},{10,... | collective-permute-start | bytes 24584 | tf_op jit(solution)/shard_map/ppermute | solution.py:141
  25.8 0.0 collective-permute-start.6
  25.8 3.4 %upper.1 = (f32[19,16,16,128]{3,2,1,0:T(8,128)}, f32[10,16,8,128]{3,2,1,0:T(8,128)S(1)}) custom-call(f32[8,128]{1,0:T(8,128)S(1)} %get-tuple-element.40.before_ref, f32[19,4,16,128]{3,2,1,0:T(8,128)S(1)} %get-tuple-element.41.lower_ref, f32[19,16,16,128]{3,2,1,0:T(8,128)S(1)} %copy-done, s32[16,16,128]{2,1,0:T(8,128)S(1)} %copy-done.2, ...), custom_call_target="tpu_custom_call" | custom-call | flops 5000000000 | bytes 1000000000 | tf_op jit(solution)/shard_map/upper/pallas_call | solution.py:624
  29.2 0.0 collective-permute-done.5.refs_1_
  29.3 1.1 %finish.1 = (f32[19,16,16,128]{3,2,1,0:T(8,128)}, f32[3,128]{1,0:T(4,128)}) custom-call(f32[19,16,16,128]{3,2,1,0:T(8,128)} %get-tuple-element.42.whole_ref, s32[1,128]{1,0:T(1,128)S(1)} %copy-done.3, f32[10,16,8,128]{3,2,1,0:T(8,128)S(1)} %get-tuple-element.44.tile_ref, ...), custom_call_target="tpu_custom_call", output_to_operand_aliasing={{0}: (0, {})} | custom-call | tf_op jit(solution)/shard_map/finish/pallas_call | solution.py:737
  (8 shorter events, 0.0 us)
Async XLA Ops:
  0.6 15.8 %copy-start = (f32[19,16,16,128]{3,2,1,0:T(8,128)S(1)}, f32[19,16,16,128]{3,2,1,0:T(8,128)}, u32[]{:S(2)}) copy-start(f32[19,16,16,128]{3,2,1,0:T(8,128)} %pops_ref.5) | copy-start | bytes 7471108
  2.5 13.9 %all-to-all-start = ((f32[8,8,128]{2,1,0:T(8,128)}), f32[8,8,128]{2,1,0:T(8,128)S(1)}, u32[]{:S(2)}, u32[]{:S(2)}) async-start(f32[8,8,128]{2,1,0:T(8,128)} %get-tuple-element.25), calls=%async_computation | async-start | bytes 65536 | tf_op jit(solution)/shard_map/all_to_all | solution.py:767
  9.8 0.9 %copy-start.1 = (s32[16,16,128]{2,1,0:T(8,128)S(1)}, s32[16,16,128]{2,1,0:T(8,128)}, u32[]{:S(2)}) copy-start(s32[16,16,128]{2,1,0:T(8,128)} %solid_ref.5) | copy-start | bytes 393220
  10.7 5.8 %copy-start.2 = (s32[16,16,128]{2,1,0:T(8,128)S(1)}, s32[16,16,128]{2,1,0:T(8,128)}, u32[]{:S(2)}) copy-start(s32[16,16,128]{2,1,0:T(8,128)} %solid_ref.5) | copy-start | bytes 393220
  17.7 6.4 %collective-permute-start.1 = (f32[88,128]{1,0:T(8,128)S(1)}, f32[88,128]{1,0:T(8,128)S(1)}, u32[]{:S(2)}, u32[]{:S(2)}) collective-permute-start(f32[88,128]{1,0:T(8,128)S(1)} %get-tuple-element.36), channel_id=1, source_target_pairs={{0,12},{1,13},{2,14},{3,15},{4,8},{5,9},{6,10},{7,11},{8,4},{9,5},... | collective-permute-start | bytes 135176 | tf_op jit(solution)/shard_map/ppermute | solution.py:141
  18.7 5.5 %collective-permute-start.2 = (f32[88,128]{1,0:T(8,128)S(1)}, f32[88,128]{1,0:T(8,128)S(1)}, u32[]{:S(2)}, u32[]{:S(2)}) collective-permute-start(f32[88,128]{1,0:T(8,128)S(1)} %get-tuple-element.37), channel_id=1, source_target_pairs={{0,4},{1,5},{2,6},{3,7},{4,0},{5,1},{6,2},{7,3},{8,12},{9,13},{10,... | collective-permute-start | bytes 135176 | tf_op jit(solution)/shard_map/ppermute | solution.py:141
  18.8 5.3 %collective-permute-start.3 = (f32[8,128]{1,0:T(8,128)S(1)}, f32[8,128]{1,0:T(8,128)S(1)}, u32[]{:S(2)}, u32[]{:S(2)}) collective-permute-start(f32[8,128]{1,0:T(8,128)S(1)} %get-tuple-element.39), channel_id=1, source_target_pairs={{0,8},{1,9},{2,10},{3,11},{4,12},{5,13},{6,14},{7,15},{8,0},{9,1},... | collective-permute-start | bytes 12296 | tf_op jit(solution)/shard_map/ppermute | solution.py:141
  22.1 1.2 %collective-permute-start = (f32[2,16,128]{2,1,0:T(8,128)S(1)}, f32[2,16,128]{2,1,0:T(8,128)S(1)}, u32[]{:S(2)}, u32[]{:S(2)}) collective-permute-start(f32[2,16,128]{2,1,0:T(8,128)S(1)} %get-tuple-element.34), channel_id=1, source_target_pairs={{0,1},{1,0},{2,3},{3,2},{4,5},{5,4},{6,7},{7,6},{8,9},{9,8},{10,11... | collective-permute-start | bytes 49160 | tf_op jit(solution)/shard_map/ppermute | solution.py:141
  23.6 5.7 %collective-permute-start.4 = (f32[160,128]{1,0:T(8,128)S(1)}, f32[160,128]{1,0:T(8,128)S(1)}, u32[]{:S(2)}, u32[]{:S(2)}) collective-permute-start(f32[160,128]{1,0:T(8,128)S(1)} %get-tuple-element.45), channel_id=1, source_target_pairs={{0,2},{1,3},{2,0},{3,1},{4,6},{5,7},{6,4},{7,5},{8,10},{9,11},{10,... | collective-permute-start | bytes 245768 | tf_op jit(solution)/shard_map/ppermute | solution.py:141
  24.2 5.0 %collective-permute-start.5 = (f32[16,128]{1,0:T(8,128)S(1)}, f32[16,128]{1,0:T(8,128)S(1)}, u32[]{:S(2)}, u32[]{:S(2)}) collective-permute-start(f32[16,128]{1,0:T(8,128)S(1)} %get-tuple-element.46), channel_id=1, source_target_pairs={{0,2},{1,3},{2,0},{3,1},{4,6},{5,7},{6,4},{7,5},{8,10},{9,11},{10,... | collective-permute-start | bytes 24584 | tf_op jit(solution)/shard_map/ppermute | solution.py:141
  25.8 3.5 %collective-permute-start.6 = (f32[64,128]{1,0:T(8,128)S(1)}, f32[64,128]{1,0:T(8,128)S(1)}, u32[]{:S(2)}, u32[]{:S(2)}) collective-permute-start(f32[64,128]{1,0:T(8,128)S(1)} %get-tuple-element.47), channel_id=1, source_target_pairs={{0,1},{1,0},{2,3},{3,2},{4,5},{5,4},{6,7},{7,6},{8,9},{9,8},{10,11... | collective-permute-start | bytes 98312 | tf_op jit(solution)/shard_map/ppermute | solution.py:141
  25.8 3.5 %copy-start.3 = (s32[1,128]{1,0:T(1,128)S(1)}, s32[1,128]{1,0:T(1,128)}, u32[]{:S(2)}) copy-start(s32[1,128]{1,0:T(1,128)} %get-tuple-element.43.target_ref) | copy-start | bytes 1540

commit v14 on v12

--- a/solution.py
+++ b/solution.py
@@ -46,6 +46,7 @@
 
 ENTER = [[[i for i in range(19) if STEP[i, a] == sign] for sign in (1, -1)] for a in range(3)]
 TOKEN = jax.ShapeDtypeStruct((8, 128), F32)
+LONG = pl.CostEstimate(flops=5000000000, bytes_accessed=1000000000, transcendentals=0)
 ROOM = 16 << 20
 NT = (((1,), (1,)), ((), ()))
 NN = (((1,), (0,)), ((), ()))
@@ -157,8 +158,8 @@
     return lax.dot_general(member.astype(BF16), earlier, NN, preferred_element_type=F32)
 
 
-def spread_column(tile, lane):
-    return jnp.broadcast_to(tile[:, lane : lane + 1], tile.shape)
+def x_pair(i):
+    return ENTER[0][0 if STEP[i, 0] == 1 else 1].index(i)
 
 
 def patch_x(value, i, column):
@@ -169,7 +170,12 @@
 def x_place(i):
     group = 0 if STEP[i, 0] == 1 else 1
     place = ENTER[0][group].index(i)
-    return place // 4, (place % 4) * 32 + group
+    return place // 4, (place % 4) * 32 + 1 - group
+
+
+def x_entering(face, k, z):
+    tile = face[k // 4]
+    return pltpu.roll(tile, tile.shape[1] - ((k % 4) * 32 + 2 * z + 1), 1)
 
 
 def x_ends(planes):
@@ -330,7 +336,8 @@
 
 def couple_kernel(shape, n_drags, beads_ref, high_ref, low_ref, *refs):
     slabs, cols, _ = shape
-    column_ref, pops_ref, solid_ref, force_ref, face_ref, first_ref, second_ref, *refs = refs
+    column_ref, side_ref, wall_ref, pops_ref, solid_ref, *refs = refs
+    force_ref, face_ref, first_ref, second_ref, draft_ref, *refs = refs
     drag_refs, token_ref = refs[:-1], refs[-1]
     token_ref[...] = jnp.zeros_like(token_ref)
     depth, rows, width = pops_ref.shape[1:]
@@ -385,7 +392,10 @@
     force = [x_ends([force_ref[d, z] for z in range(depth)]) for d in range(3)]
     out = collide([column_ref[i] for i in range(19)], column_ref[19] == 1.0, force)
     high = lax.rem(iota((rows, 128), 1), 2) == 0
-    ends = [jnp.where(high, out[i], out[j])[:, 0:32] for i, j in zip(*ENTER[0])]
+    ends = [
+        jnp.where(high, turn(out[j], -1, 1), turn(out[i], 1, 1))[:, 0:32]
+        for i, j in zip(*ENTER[0])
+    ]
     face_ref[0] = jnp.concatenate(ends[0:4], axis=1)
     face_ref[1] = jnp.concatenate([ends[4], jnp.zeros((rows, 96), F32)], axis=1)
     odd = odd_slab()
@@ -406,9 +416,16 @@
         first_ref[at] = jnp.where(odd, a, b)
         second_ref[at] = jnp.where(odd, b, a)
         row += a.shape[0]
-
-
-def couple(shape, beads, flow, columns, pops, solid):
+    for group in range(2):
+        force = [force_ref[d, :, 0 if group else rows - 1, :] for d in range(3)]
+        out = collide([side_ref[i, 1 - group] for i in range(19)], wall_ref[1 - group] == 1, force)
+        for k, i in enumerate(ENTER[1][group]):
+            row = (group * 5 + k) * depth
+            value = turn(out[i], STEP[i, 0], 1)
+            draft_ref[row : row + depth] = turn(value, STEP[i, 2], 0)
+
+
+def couple(shape, beads, flow, columns, sides, walls, pops, solid):
     _, depth, rows, width = pops.shape
     single = beads.shape[0] == GROUP
     tile = jax.ShapeDtypeStruct((8, 128), F32)
@@ -421,12 +438,13 @@
             jax.ShapeDtypeStruct((2, rows, 128), F32),
             message,
             message,
+            jax.ShapeDtypeStruct((10 * depth, width), F32),
         ]
         + [jax.ShapeDtypeStruct(d.shape, F32) for d in drags]
         + [TOKEN],
         compiler_params=pltpu.CompilerParams(vmem_limit_bytes=ROOM),
         name="couple",
-    )(beads, *flow, columns, pops, solid)
+    )(beads, *flow, columns, sides, walls, pops, solid)
 
 
 def entered_z(first_ref, second_ref, side, rows):
@@ -437,10 +455,10 @@
 X_EDGES = [i for side in range(2) for i in ENTER[2][side] if STEP[i, 0] != 0]
 
 
-def rows_kernel(depth, rows, before_ref, draft_ref, face_ref, first_ref, second_ref, *refs):
+def rows_kernel(depth, rows, draft_ref, face_ref, first_ref, second_ref, *refs):
     refs, (cross_ref, token_ref, turned) = refs[:-3], refs[-3:]
     token_ref[...] = jnp.zeros_like(token_ref)
-    outs = refs[-1:] if len(refs) == 3 else refs
+    own_ref, outs = (refs[0], refs[1:]) if len(refs) == 2 and refs[0].shape[-2] == 8 else (None, refs)
     for n in range(2):
         turned[n] = face_ref[n].T
     for group in range(2):
@@ -462,10 +480,9 @@
                 out_ref[at + z : at + z + 1] = entered_z(
                     first_ref, second_ref, side, slice(row, row + 1)
                 )
-    if len(refs) == 3:
-        own_ref, far_ref, out_ref = refs
-        came = arrived_drag(own_ref, far_ref, first_ref, second_ref, 5 * rows)
-        out_ref[10 * depth : 10 * depth + 8] = one_tile(came, 1)
+    if own_ref is not None:
+        came = arrived_drag(own_ref, None, first_ref, second_ref, 5 * rows)
+        outs[0][10 * depth : 10 * depth + 8] = one_tile(came, 1)
     for k, i in enumerate(X_EDGES):
         side = 0 if STEP[i, 2] == 1 else 1
         at = ENTER[2][side].index(i) * rows
@@ -477,29 +494,38 @@
 def arrived_drag(own_ref, far_ref, first_ref, second_ref, tail):
     at = slice(tail, tail + 8)
     up, down = [entered_z(first_ref, second_ref, side, at) for side in range(2)]
-    return [own_ref[0], down, far_ref[...], up]
+    return [own_ref[0], down, jnp.zeros_like(up) if far_ref is None else far_ref[...], up]
 
 
 def one_tile(tiles, col):
     return jnp.concatenate([t[:, col * CAP : (col + 1) * CAP] for t in tiles], axis=1)
 
 
-def leaving_rows(depth, rows, before, draft, face, first, second, drags):
+def leaving_rows(depth, rows, draft, face, first, second, drags):
     width = draft.shape[1]
-    if drags:
-        sizes = [10 * depth + 8]
-    else:
-        sizes = [5 * depth] * 2
-    args = (draft, face, first, second, *drags)
+    sizes = [10 * depth + 8] if drags else [5 * depth] * 2
     return pl.pallas_call(
         functools.partial(rows_kernel, depth, rows),
         out_shape=[jax.ShapeDtypeStruct((n, width), F32) for n in sizes + [4 * rows]] + [TOKEN],
-        in_specs=[pl.BlockSpec(memory_space=pl.ANY)]
-        + [pl.BlockSpec(memory_space=pltpu.VMEM)] * len(args),
         scratch_shapes=[pltpu.VMEM((2, 128, rows), F32)],
         compiler_params=pltpu.CompilerParams(vmem_limit_bytes=ROOM),
         name="rows",
-    )(before, *args)
+    )(draft, face, first, second, *drags)
+
+
+def pass_kernel(before_ref, value_ref, out_ref, token_ref):
+    out_ref[...] = value_ref[...]
+    token_ref[...] = jnp.zeros_like(token_ref)
+
+
+def pass_on(before, value):
+    return pl.pallas_call(
+        pass_kernel,
+        out_shape=[jax.ShapeDtypeStruct(value.shape, F32), TOKEN],
+        in_specs=[pl.BlockSpec(memory_space=pl.ANY), pl.BlockSpec(memory_space=pltpu.VMEM)],
+        compiler_params=pltpu.CompilerParams(vmem_limit_bytes=ROOM),
+        name="pass_on",
+    )(before, value)
 
 
 def runs(members):
@@ -522,26 +548,15 @@
         for i in range(19):
             value = turn(out[i], STEP[i, 0], 1)
             if STEP[i, 0] != 0 and faces:
-                tile, lane = x_place(i)
-                value = patch_x(value, i, spread_column(faces[tile], lane))
+                value = patch_x(value, i, faces[x_pair(i)])
             held[i, z] = turn(value, STEP[i, 1], 0)
         return tuple(pltpu.roll(f, 126, 1) for f in faces)
 
     return lax.fori_loop(low, high, plane, faces, unroll=2)
 
 
-def lower_kernel(
-    before_ref, pops_ref, solid_ref, force_ref, side_ref, wall_ref, held, draft_ref, token_ref
-):
-    depth, rows, _ = pops_ref.shape[1:]
+def lower_kernel(before_ref, pops_ref, solid_ref, force_ref, held, token_ref):
     token_ref[...] = jnp.zeros_like(token_ref)
-    for group in range(2):
-        force = [force_ref[d, :, 0 if group else rows - 1, :] for d in range(3)]
-        out = collide([side_ref[i, 1 - group] for i in range(19)], wall_ref[1 - group] == 1, force)
-        for k, i in enumerate(ENTER[1][group]):
-            row = (group * 5 + k) * depth
-            value = turn(out[i], STEP[i, 0], 1)
-            draft_ref[row : row + depth] = turn(value, STEP[i, 2], 0)
     stream_planes(0, held.shape[1], (), pops_ref, solid_ref, force_ref, held)
 
 
@@ -567,14 +582,14 @@
     straight = [i for i in range(19) if STEP[i, 0] == 0]
     across = [i for i in range(19) if STEP[i, 0] != 0]
     leave(lower_ref, straight, 0, half)
-    faces = (face_ref[0], face_ref[1])
-    for i in across:
-        tile, lane = x_place(i)
+    face = (face_ref[0], face_ref[1])
+    for k, pair in enumerate(zip(*ENTER[0])):
         for z in range(half):
-            column = turn(spread_column(faces[tile], lane + 2 * z), STEP[i, 1], 0)
-            held[i, z] = patch_x(lower_ref[i, z], i, column)
+            column = x_entering(face, k, z)
+            for i in pair:
+                held[i, z] = patch_x(lower_ref[i, z], i, turn(column, STEP[i, 1], 0))
     leave(held, across, 0, half)
-    faces = tuple(pltpu.roll(f, 128 - 2 * half, 1) for f in faces)
+    faces = tuple(x_entering(face, k, half) for k in range(5))
     marks = upper_marks(half, depth)
     for low, high in zip(marks, marks[1:]):
         faces = stream_planes(low, high, faces, pops_ref, solid_ref, force_ref, held)
@@ -593,21 +608,17 @@
     return list(range(half, depth - 2, 4)) + ([depth - 2] if (depth - half) % 4 else []) + [depth]
 
 
-def stream_lower(half, before, pops, solid, force, sides, walls):
-    _, depth, rows, width = pops.shape
+def stream_lower(half, before, pops, solid, force):
+    _, _, rows, width = pops.shape
     vmem = pl.BlockSpec(memory_space=pltpu.VMEM)
     return pl.pallas_call(
         lower_kernel,
-        out_shape=[
-            jax.ShapeDtypeStruct((19, half, rows, width), F32),
-            jax.ShapeDtypeStruct((10 * depth, width), F32),
-            TOKEN,
-        ],
-        in_specs=[pl.BlockSpec(memory_space=pl.ANY)] + [vmem] * 5,
+        out_shape=[jax.ShapeDtypeStruct((19, half, rows, width), F32), TOKEN],
+        in_specs=[pl.BlockSpec(memory_space=pl.ANY)] + [vmem] * 3,
         compiler_params=pltpu.CompilerParams(vmem_limit_bytes=ROOM),
-        cost_estimate=pl.CostEstimate(flops=3000000, bytes_accessed=2000000, transcendentals=0),
+        cost_estimate=LONG,
         name="lower",
-    )(before, pops, solid, force, sides, walls)
+    )(before, pops, solid, force)
 
 
 def stream_upper(before, lower, pops, solid, force, face):
@@ -626,7 +637,7 @@
             pltpu.SemaphoreType.DMA((20 * len(upper_marks(lower.shape[1], depth)),)),
         ],
         compiler_params=pltpu.CompilerParams(vmem_limit_bytes=ROOM),
-        cost_estimate=pl.CostEstimate(flops=5000000, bytes_accessed=3000000, transcendentals=0),
+        cost_estimate=LONG,
         name="upper",
     )(before, lower, pops, solid, force, face)
 
@@ -678,10 +689,15 @@
 
     count = target_ref.shape[1]
     target = target_ref[...]
-    if len(drag_refs) == 2:
+    if len(drag_refs) == 3:
         slabs, cols, _ = shape
-        came = arrived_drag(*drag_refs, first_ref, second_ref, 5 * rows)
+        own_ref, far_ref, passed_ref = drag_refs
+        came = arrived_drag(own_ref, far_ref, first_ref, second_ref, 5 * rows)
         passed = row_refs[0][10 * depth : 10 * depth + 8]
+        passed = jnp.concatenate(
+            [passed[:, 0 : 2 * CAP], passed_ref[:, CAP : 2 * CAP], passed[:, 3 * CAP : 4 * CAP]],
+            axis=1,
+        )
         table = jnp.concatenate([one_tile(came, 0), passed], axis=1)
         owner = lax.shift_right_logical(target, 5)
         owner_slab = lax.shift_right_logical(owner, cols.bit_length() - 1)
@@ -748,8 +764,8 @@
     target, messages = pack(owners, bead_owner, bead_base, bead_offset, bead_velocity)
     messages = swap(messages)
     *flow, columns, sides, walls = moments(populations, solid_mask)
-    force, face, first, second, drag, *far, token = couple(
-        shape, messages, flow, columns, populations, solid_mask
+    force, face, first, second, draft, drag, *far, token = couple(
+        shape, messages, flow, columns, sides, walls, populations, solid_mask
     )
 
     def send_pair(value):
@@ -769,9 +785,12 @@
         drags = []
         drag = swap(drag)
     fields = (populations, solid_mask, force)
-    lower, draft, token = stream_lower(10, token, *fields, sides, walls)
-    *leaving, cross, token = leaving_rows(depth, rows, token, draft, face, first, second, drags)
+    *leaving, cross, token = leaving_rows(depth, rows, draft, face, first, second, drags[:1])
     entered, cross = send_col(leaving), send_pair(cross)
+    lower, token = stream_lower(6, token, *fields)
+    if single:
+        passed, token = pass_on(token, drags[1])
+        drags += send_col([passed])
     whole, tiles = stream_upper(token, lower, *fields, face)
     return tuple(
         finish(shape, whole, target, tiles, first, second, entered, cross, drags or [drag])

time: 29.8 us -> 31.3 us (1.050)
  starting transfers between devices: 12.7 us -> 13.9 us
    ppermute x6 -> x7, starting transfers between devices: 5.43 us -> 6.62 us  [send(): return lax.ppermute(value, ('slab', 'col', 'pair'), perm)]
    pallas_call x1, Pallas kernels: 1.23 us -> 1.91 us  [couple(): pl.pallas_call(functools.partial(couple_kernel, shape, len(drags)), out_s...]
    pallas_call x1, Pallas kernels: 1.28 us -> 0.63 us  [stream_lower(): pl.pallas_call(lower_kernel, out_shape=[jax.ShapeDtypeStruct((19, half, r...]
    ppermute x6 -> x7, waiting for transfers between devices: 1.33 us -> 1.47 us  [send(): return lax.ppermute(value, ('slab', 'col', 'pair'), perm)]
  transfers between devices with their start and end apart: 7 -> 8, of which waited for: 3 -> 2; matrix products, arithmetic and copies ran while one was open for 0% -> 0% of each run, Pallas kernels for 22% -> 20%
where the time goes in v14:
time: 31.3 us; the launch traced here: 31.1 us
  starting transfers between devices  13.9 us (44%)
  Pallas kernels  11.2 us (36%)
  waiting for transfers between devices  4.38 us (14%)
  local copies, waits for them, and re-layouts  0.91 us (3%)
  between operations  0.73 us (2%)
    all_to_all x1, starting transfers between devices, shards(): messages = swap(messages)  7.25 us
    ppermute x7, starting transfers between devices, send(): return lax.ppermute(value, ('slab', 'col', 'pair'), perm)  6.62 us
    all_to_all x1, waiting for transfers between devices, shards(): messages = swap(messages)  2.91 us
    pallas_call x1, Pallas kernels, moments(): pl.pallas_call(moments_kernel, out_shape=[jax.ShapeDtypeStruct((3 * width...  2.86 us
    pallas_call x1, Pallas kernels, stream_upper(): pl.pallas_call(upper_kernel, out_shape=[jax.ShapeDtypeStruct(pops.shape,...  2.64 us
    pallas_call x1, Pallas kernels, couple(): pl.pallas_call(functools.partial(couple_kernel, shape, len(drags)), out_s...  1.91 us
    pallas_call x1, Pallas kernels, pack(): pl.pallas_call(functools.partial(pack_kernel, steps), out_shape=[jax.Shap...  1.89 us
    ppermute x7, waiting for transfers between devices, send(): return lax.ppermute(value, ('slab', 'col', 'pair'), perm)  1.47 us
  transfers between devices with their start and end apart: 8, of which 2 were waited for; matrix products, arithmetic and copies ran while one was open for 0% of the time, Pallas kernels for 20%

profile of v14, /device:TPU:0, one launch (start us, length us, event | category | flops | bytes accessed | tf_op | source)
XLA Modules:
  0.0 31.1 jit_solution(15006507864908715140)
XLA Ops:
  0.6 0.0 copy-start
  0.6 1.9 %pack.1 = (s32[1,128]{1,0:T(1,128)}, f32[8,8,128]{2,1,0:T(8,128)}) custom-call(s32[1,128]{1,0:T(1,128)} %bitcast.1, s32[3,128]{1,0:T(4,128)} %base_ref.1, f32[3,128]{1,0:T(4,128)} %offset_ref.1, f32[3,128]{1,0:T(4,128)} %velocity_ref.1), custom_call_target="tpu_custom_call" | custom-call | tf_op jit(solution)/shard_map/pack/pallas_call | solution.py:235
  2.5 7.3 %all-to-all-start = ((f32[8,8,128]{2,1,0:T(8,128)}), f32[8,8,128]{2,1,0:T(8,128)S(1)}, u32[]{:S(2)}, u32[]{:S(2)}) async-start(f32[8,8,128]{2,1,0:T(8,128)} %get-tuple-element.25), calls=%async_computation | async-start | bytes 65536 | tf_op jit(solution)/shard_map/all_to_all | solution.py:765
  9.8 0.9 %copy-done.1 = s32[16,16,128]{2,1,0:T(8,128)S(1)} copy-done((s32[16,16,128]{2,1,0:T(8,128)S(1)}, s32[16,16,128]{2,1,0:T(8,128)}, u32[]{:S(2)}) %copy-start.1) | copy-done | bytes 131096
  10.7 2.9 %moments.1 = (bf16[384,256]{1,0:T(8,128)(2,1)S(1)}, bf16[384,256]{1,0:T(8,128)(2,1)S(1)}, f32[20,16,128]{2,1,0:T(8,128)S(1)}, f32[19,2,16,128]{3,2,1,0:T(8,128)S(1)}, s32[2,16,128]{2,1,0:T(8,128)S(1)}) custom-call(f32[19,16,16,128]{3,2,1,0:T(8,128)} %pops_ref.5, s32[16,16,128]{2,1,0:T(8,128)S(1)} %copy-done.1), custom_call_target="tpu_custom_call" | custom-call | flops 3000000 | bytes 4000000 | tf_op jit(solution)/shard_map/moments/pallas_call | solution.py:289
  13.6 2.9 %all-to-all-done.beads_ref = f32[8,8,128]{2,1,0:T(8,128)S(1)} async-done(((f32[8,8,128]{2,1,0:T(8,128)}), f32[8,8,128]{2,1,0:T(8,128)S(1)}, u32[]{:S(2)}, u32[]{:S(2)}) %all-to-all-start) | async-done | bytes 32800 | tf_op jit(solution)/shard_map/all_to_all | solution.py:765
  16.5 1.9 %couple.1 = (f32[3,16,16,128]{3,2,1,0:T(8,128)S(1)}, f32[2,16,128]{2,1,0:T(8,128)S(1)}, f32[88,128]{1,0:T(8,128)S(1)}, f32[88,128]{1,0:T(8,128)S(1)}, f32[160,12...) custom-call(f32[8,8,128]{2,1,0:T(8,128)S(1)} %all-to-all-done.beads_ref, ...), custom_call_target="tpu_custom_call" | custom-call | tf_op jit(solution)/shard_map/couple/pallas_call | solution.py:434
  18.4 1.0 %collective-permute-start.1 = (f32[88,128]{1,0:T(8,128)S(1)}, f32[88,128]{1,0:T(8,128)S(1)}, u32[]{:S(2)}, u32[]{:S(2)}) collective-permute-start(f32[88,128]{1,0:T(8,128)S(1)} %get-tuple-element.33), channel_id=1, source_target_pairs={{0,12},{1,13},{2,14},{3,15},{4,8},{5,9},{6,10},{7,11},{8,4},{9,5},... | collective-permute-start | bytes 135176 | tf_op jit(solution)/shard_map/ppermute | solution.py:141
  19.3 0.1 collective-permute-start.2
  19.5 0.0 collective-permute-start
  19.5 3.3 %collective-permute-start.3 = (f32[8,128]{1,0:T(8,128)S(1)}, f32[8,128]{1,0:T(8,128)S(1)}, u32[]{:S(2)}, u32[]{:S(2)}) collective-permute-start(f32[8,128]{1,0:T(8,128)S(1)} %get-tuple-element.39), channel_id=1, source_target_pairs={{0,8},{1,9},{2,10},{3,11},{4,12},{5,13},{6,14},{7,15},{8,0},{9,1},... | collective-permute-start | bytes 12296 | tf_op jit(solution)/shard_map/ppermute | solution.py:141
  22.8 0.0 collective-permute-done.face_ref
  22.8 1.5 %collective-permute-done.1.first_ref = f32[88,128]{1,0:T(8,128)S(1)} collective-permute-done((f32[88,128]{1,0:T(8,128)S(1)}, f32[88,128]{1,0:T(8,128)S(1)}, u32[]{:S(2)}, u32[]{:S(2)}) %collective-permute-start.1) | collective-permute-done | bytes 45088 | tf_op jit(solution)/shard_map/ppermute | solution.py:141
  24.2 0.0 collective-permute-done.2.second_ref
  24.2 0.2 rows.1
  24.4 0.1 collective-permute-start.5
  24.5 1.1 %collective-permute-start.4 = (f32[168,128]{1,0:T(8,128)S(1)}, f32[168,128]{1,0:T(8,128)S(1)}, u32[]{:S(2)}, u32[]{:S(2)}) collective-permute-start(f32[168,128]{1,0:T(8,128)S(1)} %get-tuple-element.45), channel_id=1, source_target_pairs={{0,2},{1,3},{2,0},{3,1},{4,6},{5,7},{6,4},{7,5},{8,10},{9,11},{10,... | collective-permute-start | bytes 258056 | tf_op jit(solution)/shard_map/ppermute | solution.py:141
  25.6 0.6 %lower.1 = (f32[19,6,16,128]{3,2,1,0:T(8,128)S(1)}, f32[8,128]{1,0:T(8,128)S(1)}) custom-call(f32[8,128]{1,0:T(8,128)S(1)} %get-tuple-element.36.before_ref, f32[19,16,16,128]{3,2,1,0:T(8,128)S(1)} %copy-done, s32[16,16,128]{2,1,0:T(8,128)S(1)} %copy-done.2, f32[3,16,16,128]{3,2,1,0:T(8,128)S(1)} %get-tuple-element.37.force_ref), custom_call_target="tpu_custom_call" | custom-call | flops 5000000000 | bytes 1000000000 | tf_op jit(solution)/shard_map/lower/pallas_call | solution.py:614
  26.2 0.0 collective-permute-done.3.value_ref.refs_3_
  26.2 1.1 %collective-permute-start.6 = (f32[8,128]{1,0:T(8,128)S(1)}, f32[8,128]{1,0:T(8,128)S(1)}, u32[]{:S(2)}, u32[]{:S(2)}) collective-permute-start(f32[8,128]{1,0:T(8,128)S(1)} %get-tuple-element.47), channel_id=1, source_target_pairs={{0,2},{1,3},{2,0},{3,1},{4,6},{5,7},{6,4},{7,5},{8,10},{9,11},{10,... | collective-permute-start | bytes 12296 | tf_op jit(solution)/shard_map/ppermute | solution.py:141
  27.3 2.6 %upper.1 = (f32[19,16,16,128]{3,2,1,0:T(8,128)}, f32[10,16,8,128]{3,2,1,0:T(8,128)S(1)}) custom-call(f32[8,128]{1,0:T(8,128)S(1)} %get-tuple-element.40.before_ref, f32[19,6,16,128]{3,2,1,0:T(8,128)S(1)} %get-tuple-element.41.lower_ref, f32[19,16,16,128]{3,2,1,0:T(8,128)S(1)} %copy-done, s32[16,16,128]{2,1,0:T(8,128)S(1)} %copy-done.2, ...), custom_call_target="tpu_custom_call" | custom-call | flops 5000000000 | bytes 1000000000 | tf_op jit(solution)/shard_map/upper/pallas_call | solution.py:627
  29.9 0.0 collective-permute-done.6.refs_4_
  30.0 0.0 collective-permute-done.5.refs_1_
  30.0 1.1 %finish.1 = (f32[19,16,16,128]{3,2,1,0:T(8,128)}, f32[3,128]{1,0:T(4,128)}) custom-call(f32[19,16,16,128]{3,2,1,0:T(8,128)} %get-tuple-element.42.whole_ref, s32[1,128]{1,0:T(1,128)S(1)} %copy-done.3, f32[10,16,8,128]{3,2,1,0:T(8,128)S(1)} %get-tuple-element.44.tile_ref, ...), custom_call_target="tpu_custom_call", output_to_operand_aliasing={{0}: (0, {})} | custom-call | tf_op jit(solution)/shard_map/finish/pallas_call | solution.py:735
  (8 shorter events, 0.0 us)
Async XLA Ops:
  0.6 15.8 %copy-start = (f32[19,16,16,128]{3,2,1,0:T(8,128)S(1)}, f32[19,16,16,128]{3,2,1,0:T(8,128)}, u32[]{:S(2)}) copy-start(f32[19,16,16,128]{3,2,1,0:T(8,128)} %pops_ref.5) | copy-start | bytes 7471108
  2.5 13.9 %all-to-all-start = ((f32[8,8,128]{2,1,0:T(8,128)}), f32[8,8,128]{2,1,0:T(8,128)S(1)}, u32[]{:S(2)}, u32[]{:S(2)}) async-start(f32[8,8,128]{2,1,0:T(8,128)} %get-tuple-element.25), calls=%async_computation | async-start | bytes 65536 | tf_op jit(solution)/shard_map/all_to_all | solution.py:765
  9.8 0.9 %copy-start.1 = (s32[16,16,128]{2,1,0:T(8,128)S(1)}, s32[16,16,128]{2,1,0:T(8,128)}, u32[]{:S(2)}) copy-start(s32[16,16,128]{2,1,0:T(8,128)} %solid_ref.5) | copy-start | bytes 393220
  10.7 5.8 %copy-start.2 = (s32[16,16,128]{2,1,0:T(8,128)S(1)}, s32[16,16,128]{2,1,0:T(8,128)}, u32[]{:S(2)}) copy-start(s32[16,16,128]{2,1,0:T(8,128)} %solid_ref.5) | copy-start | bytes 393220
  18.4 5.8 %collective-permute-start.1 = (f32[88,128]{1,0:T(8,128)S(1)}, f32[88,128]{1,0:T(8,128)S(1)}, u32[]{:S(2)}, u32[]{:S(2)}) collective-permute-start(f32[88,128]{1,0:T(8,128)S(1)} %get-tuple-element.33), channel_id=1, source_target_pairs={{0,12},{1,13},{2,14},{3,15},{4,8},{5,9},{6,10},{7,11},{8,4},{9,5},... | collective-permute-start | bytes 135176 | tf_op jit(solution)/shard_map/ppermute | solution.py:141
  19.3 4.9 %collective-permute-start.2 = (f32[88,128]{1,0:T(8,128)S(1)}, f32[88,128]{1,0:T(8,128)S(1)}, u32[]{:S(2)}, u32[]{:S(2)}) collective-permute-start(f32[88,128]{1,0:T(8,128)S(1)} %get-tuple-element.34), channel_id=1, source_target_pairs={{0,4},{1,5},{2,6},{3,7},{4,0},{5,1},{6,2},{7,3},{8,12},{9,13},{10,... | collective-permute-start | bytes 135176 | tf_op jit(solution)/shard_map/ppermute | solution.py:141
  19.5 3.3 %collective-permute-start = (f32[2,16,128]{2,1,0:T(8,128)S(1)}, f32[2,16,128]{2,1,0:T(8,128)S(1)}, u32[]{:S(2)}, u32[]{:S(2)}) collective-permute-start(f32[2,16,128]{2,1,0:T(8,128)S(1)} %get-tuple-element.32), channel_id=1, source_target_pairs={{0,1},{1,0},{2,3},{3,2},{4,5},{5,4},{6,7},{7,6},{8,9},{9,8},{10,11... | collective-permute-start | bytes 49160 | tf_op jit(solution)/shard_map/ppermute | solution.py:141
  19.5 6.7 %collective-permute-start.3 = (f32[8,128]{1,0:T(8,128)S(1)}, f32[8,128]{1,0:T(8,128)S(1)}, u32[]{:S(2)}, u32[]{:S(2)}) collective-permute-start(f32[8,128]{1,0:T(8,128)S(1)} %get-tuple-element.39), channel_id=1, source_target_pairs={{0,8},{1,9},{2,10},{3,11},{4,12},{5,13},{6,14},{7,15},{8,0},{9,1},... | collective-permute-start | bytes 12296 | tf_op jit(solution)/shard_map/ppermute | solution.py:141
  24.4 5.5 %collective-permute-start.5 = (f32[64,128]{1,0:T(8,128)S(1)}, f32[64,128]{1,0:T(8,128)S(1)}, u32[]{:S(2)}, u32[]{:S(2)}) collective-permute-start(f32[64,128]{1,0:T(8,128)S(1)} %get-tuple-element.46), channel_id=1, source_target_pairs={{0,1},{1,0},{2,3},{3,2},{4,5},{5,4},{6,7},{7,6},{8,9},{9,8},{10,11... | collective-permute-start | bytes 98312 | tf_op jit(solution)/shard_map/ppermute | solution.py:141
  24.5 5.5 %collective-permute-start.4 = (f32[168,128]{1,0:T(8,128)S(1)}, f32[168,128]{1,0:T(8,128)S(1)}, u32[]{:S(2)}, u32[]{:S(2)}) collective-permute-start(f32[168,128]{1,0:T(8,128)S(1)} %get-tuple-element.45), channel_id=1, source_target_pairs={{0,2},{1,3},{2,0},{3,1},{4,6},{5,7},{6,4},{7,5},{8,10},{9,11},{10,... | collective-permute-start | bytes 258056 | tf_op jit(solution)/shard_map/ppermute | solution.py:141
  26.2 3.7 %collective-permute-start.6 = (f32[8,128]{1,0:T(8,128)S(1)}, f32[8,128]{1,0:T(8,128)S(1)}, u32[]{:S(2)}, u32[]{:S(2)}) collective-permute-start(f32[8,128]{1,0:T(8,128)S(1)} %get-tuple-element.47), channel_id=1, source_target_pairs={{0,2},{1,3},{2,0},{3,1},{4,6},{5,7},{6,4},{7,5},{8,10},{9,11},{10,... | collective-permute-start | bytes 12296 | tf_op jit(solution)/shard_map/ppermute | solution.py:141
  27.3 2.7 %copy-start.3 = (s32[1,128]{1,0:T(1,128)S(1)}, s32[1,128]{1,0:T(1,128)}, u32[]{:S(2)}) copy-start(s32[1,128]{1,0:T(1,128)} %get-tuple-element.43.target_ref) | copy-start | bytes 1540

commit v15 on v12

--- a/solution.py
+++ b/solution.py
@@ -46,6 +46,7 @@
 
 ENTER = [[[i for i in range(19) if STEP[i, a] == sign] for sign in (1, -1)] for a in range(3)]
 TOKEN = jax.ShapeDtypeStruct((8, 128), F32)
+LONG = pl.CostEstimate(flops=5000000000, bytes_accessed=1000000000, transcendentals=0)
 ROOM = 16 << 20
 NT = (((1,), (1,)), ((), ()))
 NN = (((1,), (0,)), ((), ()))
@@ -180,24 +181,32 @@
     return tile
 
 
-def pack_kernel(
-    steps, owner_ref, base_ref, offset_ref, velocity_ref, target_ref, out_ref, table
-):
+def pack_kernel(shape, steps, owner_ref, base_ref, offset_ref, velocity_ref, target_ref, *refs):
+    outs, table = refs[:-1], refs[-1]
     count = owner_ref.shape[1]
-    step = 0 if steps == 1 else pl.program_id(0)
-    local = owner_ref[...] - step * GROUP
+    owner = owner_ref[...]
+    if len(outs) == 2:
+        cols = shape[1]
+        slab, col = lax.axis_index("slab"), lax.axis_index("col")
+        to_slab = lax.shift_right_logical(owner, cols.bit_length() - 1)
+        to_col = owner - to_slab * cols
+        away = to_slab - slab
+        away = jnp.where(away < 0, away + shape[0], away)
+        up = jnp.where(odd_slab(), 1, 2)
+        place = jnp.where(away == 1, up, jnp.where(away == 3, 3 - up, jnp.where(away == 2, 3, 0)))
+        local = jnp.where(to_col == col, 0, 4) + place
+    else:
+        local = owner - (0 if steps == 1 else pl.program_id(0)) * GROUP
     member = (iota((GROUP, count), 0) == local).astype(F32)
     rank = jnp.sum(member * rank_among(member), axis=0, keepdims=True).astype(jnp.int32)
     inside = (local >= 0) & (local < GROUP)
     target = jnp.where(inside, local * CAP + rank, -1)
-    whole_target = jnp.where(inside, owner_ref[...] * CAP + rank, -1)
-
+    whole_target = jnp.where(inside, owner * CAP + rank, -1)
     if steps == 1:
         target_ref[...] = whole_target
     else:
-        known = jnp.where(step == 0, -1, target_ref[...])
+        known = jnp.where(pl.program_id(0) == 0, -1, target_ref[...])
         target_ref[...] = jnp.maximum(known, whole_target)
-
     choose = (iota((GROUP * CAP, count), 0) == target).astype(F32).astype(BF16)
     table[...] = jnp.zeros_like(table)
     table[0:3] = base_ref[...].astype(F32) + 1.0
@@ -207,16 +216,24 @@
     blank = jnp.zeros((8, CAP), F32)
     for r in range(GROUP):
         lanes = slice(r * CAP, (r + 1) * CAP)
-        out_ref[r] = jnp.concatenate(
+        tile = jnp.concatenate(
             [packed[0:8, lanes], packed[8:16, lanes], packed[16:24, lanes], blank], axis=1
         )
-
-
-def pack(owners, owner, base, offset, velocity):
+        if len(outs) == 2:
+            outs[r // 4][(r % 4) * 8 : (r % 4) * 8 + 8] = tile
+        else:
+            outs[0][r] = tile
+
+
+def pack(shape, single, owner, base, offset, velocity):
+    owners = shape[0] * shape[1]
     count, steps = owner.shape[0], owners // GROUP
     args = (owner.reshape(1, count), base, offset, velocity)
     blocks = {}
-    if steps > 1:
+    if single:
+        tiles = [jax.ShapeDtypeStruct((32, 128), F32)] * 2
+    else:
+        tiles = [jax.ShapeDtypeStruct((owners, 8, 128), F32)]
         blocks = dict(
             grid=(steps,),
             in_specs=[pl.BlockSpec(a.shape, lambda k: (0, 0)) for a in args],
@@ -227,24 +244,41 @@
             compiler_params=pltpu.CompilerParams(vmem_limit_bytes=48 << 20),
         )
     return pl.pallas_call(
-        functools.partial(pack_kernel, steps),
-        out_shape=[
-            jax.ShapeDtypeStruct((1, count), jnp.int32),
-            jax.ShapeDtypeStruct((owners, 8, 128), F32),
-        ],
+        functools.partial(pack_kernel, shape, steps),
+        out_shape=[jax.ShapeDtypeStruct((1, count), jnp.int32), *tiles],
         scratch_shapes=[pltpu.VMEM((24, count), F32)],
         name="pack",
         **blocks,
     )(*args)
 
 
+def join_kernel(before_ref, own_ref, came_ref, *refs):
+    outs, token_ref = refs[:-1], refs[-1]
+    token_ref[...] = jnp.zeros_like(token_ref)
+    for k, out_ref in enumerate(outs):
+        out_ref[0:8] = own_ref[8 * k : 8 * k + 8]
+        out_ref[8:16] = came_ref[8 * k : 8 * k + 8]
+
+
+def join(before, own, came):
+    vmem = pl.BlockSpec(memory_space=pltpu.VMEM)
+    return pl.pallas_call(
+        join_kernel,
+        out_shape=[jax.ShapeDtypeStruct((16, 128), F32)] * 4 + [TOKEN],
+        in_specs=[pl.BlockSpec(memory_space=pl.ANY), vmem, vmem],
+        compiler_params=pltpu.CompilerParams(vmem_limit_bytes=ROOM),
+        name="join",
+    )(before, own, came)
+
+
 def moments_kernel(
-    pops_ref, solid_ref, high_ref, low_ref, column_ref, side_ref, wall_ref, held, held_solid, flow, sem
+    before_ref, pops_ref, high_ref, low_ref, column_ref, side_ref, token_ref, held, flow, sem
 ):
     depth, rows, width = pops_ref.shape[1:]
     chunks = 4
     span = depth // chunks
-    copies = [pltpu.make_async_copy(solid_ref, held_solid, sem.at[chunks])]
+    copies = []
+    token_ref[...] = jnp.zeros_like(token_ref)
     for k in range(chunks):
         part = pl.ds(k * span, span)
         copies.append(
@@ -262,9 +296,8 @@
         return carry
 
     for k in range(chunks):
-        copies[1 + k].wait()
+        copies[k].wait()
         lax.fori_loop(k * span, (k + 1) * span, plane, 0, unroll=2)
-    copies[0].wait()
     for axis in range(3):
         at = slice(axis * width, (axis + 1) * width)
         high_ref[at], low_ref[at] = high_low(flow[axis].T)
@@ -272,34 +305,51 @@
         column_ref[i] = x_ends([held[i, z] for z in range(depth)])
         side_ref[i, 0] = held[i, :, 0, :]
         side_ref[i, 1] = held[i, :, rows - 1, :]
-    wall_ref[0] = held_solid[:, 0, :]
-    wall_ref[1] = held_solid[:, rows - 1, :]
-    column_ref[19] = x_ends([held_solid[z].astype(F32) for z in range(depth)])
-
-
-def moments(pops, solid):
+
+
+def moments(before, pops):
     _, depth, rows, width = pops.shape
-    hbm = pl.BlockSpec(memory_space=pltpu.HBM)
     return pl.pallas_call(
         moments_kernel,
         out_shape=[
             jax.ShapeDtypeStruct((3 * width, depth * rows), BF16),
             jax.ShapeDtypeStruct((3 * width, depth * rows), BF16),
-            jax.ShapeDtypeStruct((20, rows, 128), F32),
+            jax.ShapeDtypeStruct((19, rows, 128), F32),
             jax.ShapeDtypeStruct((19, 2, depth, width), F32),
+            TOKEN,
+        ],
+        in_specs=[pl.BlockSpec(memory_space=pl.ANY), pl.BlockSpec(memory_space=pltpu.HBM)],
+        scratch_shapes=[
+            pltpu.VMEM(pops.shape, F32),
+            pltpu.VMEM((3, depth * rows, width), F32),
+            pltpu.SemaphoreType.DMA((4,)),
+        ],
+        compiler_params=pltpu.CompilerParams(vmem_limit_bytes=54000000),
+        cost_estimate=LONG,
+        name="moments",
+    )(before, pops)
+
+
+def walls_kernel(before_ref, solid_ref, column_ref, wall_ref):
+    depth, rows = solid_ref.shape[0:2]
+    column_ref[...] = x_ends([solid_ref[z].astype(F32) for z in range(depth)])
+    wall_ref[0] = solid_ref[:, 0, :]
+    wall_ref[1] = solid_ref[:, rows - 1, :]
+
+
+def wall_faces(before, solid):
+    depth, rows, width = solid.shape
+    return pl.pallas_call(
+        walls_kernel,
+        out_shape=[
+            jax.ShapeDtypeStruct((rows, 128), F32),
             jax.ShapeDtypeStruct((2, depth, width), jnp.int32),
         ],
-        in_specs=[hbm, hbm],
-        scratch_shapes=[
-            pltpu.VMEM(pops.shape, F32),
-            pltpu.VMEM(solid.shape, jnp.int32),
-            pltpu.VMEM((3, depth * rows, width), F32),
-            pltpu.SemaphoreType.DMA((5,)),
-        ],
-        compiler_params=pltpu.CompilerParams(vmem_limit_bytes=54000000),
-        cost_estimate=pl.CostEstimate(flops=3000000, bytes_accessed=4000000, transcendentals=0),
-        name="moments",
-    )(pops, solid)
+        in_specs=[pl.BlockSpec(memory_space=pl.ANY), pl.BlockSpec(memory_space=pltpu.VMEM)],
+        compiler_params=pltpu.CompilerParams(vmem_limit_bytes=ROOM),
+        cost_estimate=LONG,
+        name="walls",
+    )(before, solid)
 
 
 def unpack(tiles):
@@ -328,9 +378,11 @@
     return drag, dot_split(weight, high_low(spread), NT)
 
 
-def couple_kernel(shape, n_drags, beads_ref, high_ref, low_ref, *refs):
+def couple_kernel(shape, n_beads, n_drags, *refs):
     slabs, cols, _ = shape
-    column_ref, pops_ref, solid_ref, force_ref, face_ref, first_ref, second_ref, *refs = refs
+    bead_refs, refs = refs[:n_beads], refs[n_beads:]
+    high_ref, low_ref, column_ref, wall_ref, pops_ref, solid_ref, *refs = refs
+    force_ref, face_ref, first_ref, second_ref, *refs = refs
     drag_refs, token_ref = refs[:-1], refs[-1]
     token_ref[...] = jnp.zeros_like(token_ref)
     depth, rows, width = pops_ref.shape[1:]
@@ -344,32 +396,28 @@
     hollow = jnp.zeros((5, GROUP * CAP), F32)
 
     if n_drags == 2:
-        slab, col = lax.axis_index("slab"), lax.axis_index("col")
-        got = []
-        for r in range(GROUP):
-            there = [a - b for a, b in zip((slab, col), divmod(r, cols))]
-            there = [jnp.where(a < 0, a + n, a) for a, n in zip(there, (slabs, cols))]
-            got.append(beads_ref[there[0] * cols + there[1]])
+        got = [ref[k : k + 8] for ref in bead_refs for k in (0, 8)]
         drag, force = couple_group(*unpack(got), flow, depth, rows, width)
         for d, value in enumerate(grid(force)):
             force_ref[d] = value
         stacked = jnp.concatenate(drag + [hollow], axis=0)
         lanes = cols * CAP
         blank = jnp.zeros((8, 128 - lanes), F32)
-        for dz in range(slabs):
-            tile = jnp.concatenate([stacked[:, dz * lanes : (dz + 1) * lanes], blank], axis=1)
+        own, near, next_, far = [
+            jnp.concatenate([stacked[:, k * lanes : (k + 1) * lanes], blank], axis=1)
+            for k in range(slabs)
+        ]
+        odd = odd_slab()
+        down, up = jnp.where(odd, next_, near), jnp.where(odd, near, next_)
+        for dz, tile in enumerate([own, down, far, up]):
             drag_refs[0][dz] = tile
-            if dz == 2:
-                drag_refs[1][...] = tile
-            if dz == 1:
-                down = tile
-        up = tile
+        drag_refs[1][...] = far
     else:
         force_ref[...] = jnp.zeros_like(force_ref)
         blank = jnp.zeros((8, 128 - CAP), F32)
 
         def group(k, carry):
-            got = [beads_ref[k * GROUP + r] for r in range(GROUP)]
+            got = [bead_refs[0][k * GROUP + r] for r in range(GROUP)]
             drag, force = couple_group(*unpack(got), flow, depth, rows, width)
             for d, value in enumerate(grid(force)):
                 force_ref[d] += value
@@ -380,10 +428,10 @@
                 )
             return carry
 
-        lax.fori_loop(0, beads_ref.shape[0] // GROUP, group, 0)
+        lax.fori_loop(0, bead_refs[0].shape[0] // GROUP, group, 0)
 
     force = [x_ends([force_ref[d, z] for z in range(depth)]) for d in range(3)]
-    out = collide([column_ref[i] for i in range(19)], column_ref[19] == 1.0, force)
+    out = collide([column_ref[i] for i in range(19)], wall_ref[...] == 1.0, force)
     high = lax.rem(iota((rows, 128), 1), 2) == 0
     ends = [jnp.where(high, out[i], out[j])[:, 0:32] for i, j in zip(*ENTER[0])]
     face_ref[0] = jnp.concatenate(ends[0:4], axis=1)
@@ -408,14 +456,13 @@
         row += a.shape[0]
 
 
-def couple(shape, beads, flow, columns, pops, solid):
+def couple(single, shape, beads, flow, columns, wall, pops, solid):
     _, depth, rows, width = pops.shape
-    single = beads.shape[0] == GROUP
     tile = jax.ShapeDtypeStruct((8, 128), F32)
-    drags = [jax.ShapeDtypeStruct((shape[0], 8, 128), F32), tile] if single else [beads]
+    drags = [jax.ShapeDtypeStruct((shape[0], 8, 128), F32), tile] if single else beads
     message = jax.ShapeDtypeStruct((5 * rows + (8 if single else 0), width), F32)
     return pl.pallas_call(
-        functools.partial(couple_kernel, shape, len(drags)),
+        functools.partial(couple_kernel, shape, len(beads), len(drags)),
         out_shape=[
             jax.ShapeDtypeStruct((3, depth, rows, width), F32),
             jax.ShapeDtypeStruct((2, rows, 128), F32),
@@ -426,7 +473,7 @@
         + [TOKEN],
         compiler_params=pltpu.CompilerParams(vmem_limit_bytes=ROOM),
         name="couple",
-    )(beads, *flow, columns, pops, solid)
+    )(*beads, *flow, columns, wall, pops, solid)
 
 
 def entered_z(first_ref, second_ref, side, rows):
@@ -745,11 +792,21 @@
         lax.all_to_all, axis_name=("slab", "col"), split_axis=0, concat_axis=0, tiled=True
     )
 
-    target, messages = pack(owners, bead_owner, bead_base, bead_offset, bead_velocity)
-    messages = swap(messages)
-    *flow, columns, sides, walls = moments(populations, solid_mask)
+    target, *tiles = pack(shape, single, bead_owner, bead_base, bead_offset, bead_velocity)
+
+    def send_far(value):
+        return send(value, shape, lambda s, c, p: ((s + 2) % slabs, c, p))
+
+    *flow, columns, sides, token = moments(tiles[0], populations)
+    if single:
+        came = send(tiles[1], shape, lambda s, c, p: (s, (c + 1) % cols, p))
+        own, near, next_, far, token = join(token, tiles[0], came)
+        beads = [own, send_slab(near, shape, 1), send_slab(next_, shape, 0), send_far(far)]
+    else:
+        beads = [swap(tiles[0])]
+    wall, walls = wall_faces(token, solid_mask)
     force, face, first, second, drag, *far, token = couple(
-        shape, messages, flow, columns, populations, solid_mask
+        single, shape, beads, flow, columns, wall, populations, solid_mask
     )
 
     def send_pair(value):
@@ -764,7 +821,7 @@
     face = send_pair(face)
     first, second = send_slab(first, shape, 1), send_slab(second, shape, 0)
     if single:
-        drags = [drag, send(far[0], shape, lambda s, c, p: ((s + 2) % slabs, c, p))]
+        drags = [drag, send_far(far[0])]
     else:
         drags = []
         drag = swap(drag)

time: 29.8 us -> 30.9 us (1.037)
  waiting for transfers between devices: 4.24 us -> 6.03 us
    all_to_all x1 -> x0, starting transfers between devices: 7.25 us -> none  [shards(): messages = swap(messages)]
    ppermute x6 -> x10, starting transfers between devices: 5.43 us -> 12.4 us  [send(): return lax.ppermute(value, ('slab', 'col', 'pair'), perm)]
    ppermute x6 -> x10, waiting for transfers between devices: 1.33 us -> 6.03 us  [send(): return lax.ppermute(value, ('slab', 'col', 'pair'), perm)]
    all_to_all x1 -> x0, waiting for transfers between devices: 2.91 us -> none  [shards(): messages = swap(messages)]
    pallas_call x2 -> x4, Pallas kernels: 3.12 us -> 3.06 us  [the longest x1 1.74 us: pack(): pl.pallas_call(functools.partial(pack_kernel, shape, steps), out_shape=[j...]
  transfers between devices with their start and end apart: 7 -> 10, of which waited for: 3 -> 5; matrix products, arithmetic and copies ran while one was open for 0% -> 0% of each run, Pallas kernels for 22% -> 21%
where the time goes in v15:
time: 30.9 us; the launch traced here: 30.7 us
  starting transfers between devices  12.4 us (40%)
  Pallas kernels  10.8 us (35%)
  waiting for transfers between devices  6.03 us (20%)
  local copies, waits for them, and re-layouts  0.73 us (2%)
  between operations  0.71 us (2%)
    ppermute x10, starting transfers between devices, send(): return lax.ppermute(value, ('slab', 'col', 'pair'), perm)  12.4 us
    ppermute x10, waiting for transfers between devices, send(): return lax.ppermute(value, ('slab', 'col', 'pair'), perm)  6.03 us
    pallas_call x1, Pallas kernels, moments(): pl.pallas_call(moments_kernel, out_shape=[jax.ShapeDtypeStruct((3 * width...  2.71 us
    pallas_call x1, Pallas kernels, stream_upper(): pl.pallas_call(upper_kernel, out_shape=[jax.ShapeDtypeStruct(pops.shape,...  2.49 us
    pallas_call x1, Pallas kernels, pack(): pl.pallas_call(functools.partial(pack_kernel, shape, steps), out_shape=[j...  1.74 us
    pallas_call x1, Pallas kernels, stream_lower(): pl.pallas_call(lower_kernel, out_shape=[jax.ShapeDtypeStruct((19, half, r...  1.3 us
    pallas_call x1, Pallas kernels, couple(): pl.pallas_call(functools.partial(couple_kernel, shape, len(beads), len(dr...  1.22 us
    pallas_call x1, Pallas kernels, finish(): pl.pallas_call(functools.partial(finish_kernel, shape, len(entered)), out...  1.07 us
  transfers between devices with their start and end apart: 10, of which 5 were waited for; matrix products, arithmetic and copies ran while one was open for 0% of the time, Pallas kernels for 21%

profile of v15, /device:TPU:0, one launch (start us, length us, event | category | flops | bytes accessed | tf_op | source)
XLA Modules:
  0.0 30.7 jit_solution(14610224341777678366)
XLA Ops:
  0.6 1.7 %pack.1 = (s32[1,128]{1,0:T(1,128)}, f32[32,128]{1,0:T(8,128)}, f32[32,128]{1,0:T(8,128)}) custom-call(s32[1,128]{1,0:T(1,128)} %bitcast.1, s32[3,128]{1,0:T(4,128)} %base_ref.1, f32[3,128]{1,0:T(4,128)} %offset_ref.1, f32[3,128]{1,0:T(4,128)} %velocity_ref.1), custom_call_target="tpu_custom_call" | custom-call | tf_op jit(solution)/shard_map/pack/pallas_call | solution.py:246
  2.4 2.9 %collective-permute-start = (f32[32,128]{1,0:T(8,128)}, f32[32,128]{1,0:T(8,128)S(1)}, u32[]{:S(2)}, u32[]{:S(2)}) collective-permute-start(f32[32,128]{1,0:T(8,128)} %get-tuple-element.34), channel_id=1, source_target_pairs={{0,2},{1,3},{2,0},{3,1},{4,6},{5,7},{6,4},{7,5},{8,10},{9,11},{10,... | collective-permute-start | bytes 49160 | tf_op jit(solution)/shard_map/ppermute | solution.py:141
  5.3 0.7 %copy-done.2 = f32[32,128]{1,0:T(8,128)S(1)} copy-done((f32[32,128]{1,0:T(8,128)S(1)}, f32[32,128]{1,0:T(8,128)}, u32[]{:S(2)}) %copy-start.2) | copy-done | bytes 16408
  6.0 2.7 %moments.1 = (bf16[384,256]{1,0:T(8,128)(2,1)S(1)}, bf16[384,256]{1,0:T(8,128)(2,1)S(1)}, f32[19,16,128]{2,1,0:T(8,128)S(1)}, f32[19,2,16,128]{3,2,1,0:T(8,128)S(1)}, f32[8,128]{1,0:T(8,128)S(1)}) custom-call(f32[32,128]{1,0:T(8,128)S(1)} %copy-done.2, f32[19,16,16,128]{3,2,1,0:T(8,128)} %pops_ref.5), custom_call_target="tpu_custom_call" | custom-call | flops 5000000000 | bytes 1000000000 | tf_op jit(solution)/shard_map/moments/pallas_call | solution.py:312
  8.7 0.0 collective-permute-done.came_ref
  8.8 3.7 %collective-permute-start.1 = (f32[16,128]{1,0:T(8,128)S(1)}, f32[16,128]{1,0:T(8,128)S(1)}, u32[]{:S(2)}, u32[]{:S(2)}) collective-permute-start(f32[16,128]{1,0:T(8,128)S(1)} %get-tuple-element.36), channel_id=1, source_target_pairs={{0,12},{1,13},{2,14},{3,15},{4,8},{5,9},{6,10},{7,11},{8,4},{9,5},... | collective-permute-start | bytes 24584 | tf_op jit(solution)/shard_map/ppermute | solution.py:141
  12.4 0.0 collective-permute-start.2
  12.4 0.8 %collective-permute-start.3 = (f32[16,128]{1,0:T(8,128)S(1)}, f32[16,128]{1,0:T(8,128)S(1)}, u32[]{:S(2)}, u32[]{:S(2)}) collective-permute-start(f32[16,128]{1,0:T(8,128)S(1)} %get-tuple-element.38), channel_id=1, source_target_pairs={{0,8},{1,9},{2,10},{3,11},{4,12},{5,13},{6,14},{7,15},{8,0},{9,1},... | collective-permute-start | bytes 24584 | tf_op jit(solution)/shard_map/ppermute | solution.py:141
  13.2 0.1 walls.1
  13.3 1.0 %collective-permute-done.1.refs_1_ = f32[16,128]{1,0:T(8,128)S(1)} collective-permute-done((f32[16,128]{1,0:T(8,128)S(1)}, f32[16,128]{1,0:T(8,128)S(1)}, u32[]{:S(2)}, u32[]{:S(2)}) %collective-permute-start.1) | collective-permute-done | bytes 8224 | tf_op jit(solution)/shard_map/ppermute | solution.py:141
  14.3 1.8 %collective-permute-done.2.refs_2_ = f32[16,128]{1,0:T(8,128)S(1)} collective-permute-done((f32[16,128]{1,0:T(8,128)S(1)}, f32[16,128]{1,0:T(8,128)S(1)}, u32[]{:S(2)}, u32[]{:S(2)}) %collective-permute-start.2) | collective-permute-done | bytes 8224 | tf_op jit(solution)/shard_map/ppermute | solution.py:141
  16.1 0.9 %collective-permute-done.3.refs_3_ = f32[16,128]{1,0:T(8,128)S(1)} collective-permute-done((f32[16,128]{1,0:T(8,128)S(1)}, f32[16,128]{1,0:T(8,128)S(1)}, u32[]{:S(2)}, u32[]{:S(2)}) %collective-permute-start.3) | collective-permute-done | bytes 8224 | tf_op jit(solution)/shard_map/ppermute | solution.py:141
  17.0 1.2 %couple.1 = (f32[3,16,16,128]{3,2,1,0:T(8,128)S(1)}, f32[2,16,128]{2,1,0:T(8,128)S(1)}, f32[88,128]{1,0:T(8,128)S(1)}, f32[88,128]{1,0:T(8,128)S(1)}, f32[4,8,12...) custom-call(f32[16,128]{1,0:T(8,128)S(1)} %get-tuple-element.35.refs_0_, ...), custom_call_target="tpu_custom_call" | custom-call | tf_op jit(solution)/shard_map/couple/pallas_call | solution.py:464
  18.2 1.6 %collective-permute-start.5 = (f32[88,128]{1,0:T(8,128)S(1)}, f32[88,128]{1,0:T(8,128)S(1)}, u32[]{:S(2)}, u32[]{:S(2)}) collective-permute-start(f32[88,128]{1,0:T(8,128)S(1)} %get-tuple-element.51), channel_id=1, source_target_pairs={{0,12},{1,13},{2,14},{3,15},{4,8},{5,9},{6,10},{7,11},{8,4},{9,5},... | collective-permute-start | bytes 135176 | tf_op jit(solution)/shard_map/ppermute | solution.py:141
  19.8 0.6 %collective-permute-start.6 = (f32[88,128]{1,0:T(8,128)S(1)}, f32[88,128]{1,0:T(8,128)S(1)}, u32[]{:S(2)}, u32[]{:S(2)}) collective-permute-start(f32[88,128]{1,0:T(8,128)S(1)} %get-tuple-element.52), channel_id=1, source_target_pairs={{0,4},{1,5},{2,6},{3,7},{4,0},{5,1},{6,2},{7,3},{8,12},{9,13},{10,... | collective-permute-start | bytes 135176 | tf_op jit(solution)/shard_map/ppermute | solution.py:141
  20.3 2.3 %collective-permute-start.7 = (f32[8,128]{1,0:T(8,128)S(1)}, f32[8,128]{1,0:T(8,128)S(1)}, u32[]{:S(2)}, u32[]{:S(2)}) collective-permute-start(f32[8,128]{1,0:T(8,128)S(1)} %get-tuple-element.54), channel_id=1, source_target_pairs={{0,8},{1,9},{2,10},{3,11},{4,12},{5,13},{6,14},{7,15},{8,0},{9,1},... | collective-permute-start | bytes 12296 | tf_op jit(solution)/shard_map/ppermute | solution.py:141
  22.6 1.3 %lower.1 = (f32[19,10,16,128]{3,2,1,0:T(8,128)S(1)}, f32[160,128]{1,0:T(8,128)S(1)}, f32[8,128]{1,0:T(8,128)S(1)}) custom-call(f32[8,128]{1,0:T(8,128)S(1)} %get-tuple-element.44.before_ref, f32[19,16,16,128]{3,2,1,0:T(8,128)S(1)} %copy-done, s32[16,16,128]{2,1,0:T(8,128)S(1)} %copy-done.1, f32[3,16,16,128]{3,2,1,0:T(8,128)S(1)} %get-tuple-element.45.force_ref, ...), custom_call_target="tpu_custom_call" | custom-call | flops 3000000 | bytes 2000000 | tf_op jit(solution)/shard_map/lower/pallas_call | solution.py:646
  23.9 0.0 copy-start.3
  23.9 0.9 %collective-permute-done.7.refs_1_.refs_3_ = f32[8,128]{1,0:T(8,128)S(1)} collective-permute-done((f32[8,128]{1,0:T(8,128)S(1)}, f32[8,128]{1,0:T(8,128)S(1)}, u32[]{:S(2)}, u32[]{:S(2)}) %collective-permute-start.7) | collective-permute-done | bytes 4128 | tf_op jit(solution)/shard_map/ppermute | solution.py:141
  24.9 0.2 rows.1
  25.0 0.6 %collective-permute-start.8 = (f32[168,128]{1,0:T(8,128)S(1)}, f32[168,128]{1,0:T(8,128)S(1)}, u32[]{:S(2)}, u32[]{:S(2)}) collective-permute-start(f32[168,128]{1,0:T(8,128)S(1)} %get-tuple-element.60), channel_id=1, source_target_pairs={{0,2},{1,3},{2,0},{3,1},{4,6},{5,7},{6,4},{7,5},{8,10},{9,11},{10,... | collective-permute-start | bytes 258056 | tf_op jit(solution)/shard_map/ppermute | solution.py:141
  25.6 2.5 %upper.1 = (f32[19,16,16,128]{3,2,1,0:T(8,128)}, f32[10,16,8,128]{3,2,1,0:T(8,128)S(1)}) custom-call(f32[8,128]{1,0:T(8,128)S(1)} %get-tuple-element.55.before_ref, f32[19,10,16,128]{3,2,1,0:T(8,128)S(1)} %get-tuple-element.56.lower_ref, f32[19,16,16,128]{3,2,1,0:T(8,128)S(1)} %copy-done, s32[16,16,128]{2,1,0:T(8,128)S(1)} %copy-done.1, ...), custom_call_target="tpu_custom_call" | custom-call | flops 5000000 | bytes 3000000 | tf_op jit(solution)/shard_map/upper/pallas_call | solution.py:663
  28.1 1.4 %collective-permute-done.8.refs_0_ = f32[168,128]{1,0:T(8,128)S(1)} collective-permute-done((f32[168,128]{1,0:T(8,128)S(1)}, f32[168,128]{1,0:T(8,128)S(1)}, u32[]{:S(2)}, u32[]{:S(2)}) %collective-permute-start.8) | collective-permute-done | bytes 86048 | tf_op jit(solution)/shard_map/ppermute | solution.py:141
  29.6 1.1 %finish.1 = (f32[19,16,16,128]{3,2,1,0:T(8,128)}, f32[3,128]{1,0:T(4,128)}) custom-call(f32[19,16,16,128]{3,2,1,0:T(8,128)} %get-tuple-element.57.whole_ref, s32[1,128]{1,0:T(1,128)S(1)} %copy-done.3, f32[10,16,8,128]{3,2,1,0:T(8,128)S(1)} %get-tuple-element.59.tile_ref, ...), custom_call_target="tpu_custom_call", output_to_operand_aliasing={{0}: (0, {})} | custom-call | tf_op jit(solution)/shard_map/finish/pallas_call | solution.py:766
  (13 shorter events, 0.0 us)
Async XLA Ops:
  2.4 6.4 %collective-permute-start = (f32[32,128]{1,0:T(8,128)}, f32[32,128]{1,0:T(8,128)S(1)}, u32[]{:S(2)}, u32[]{:S(2)}) collective-permute-start(f32[32,128]{1,0:T(8,128)} %get-tuple-element.34), channel_id=1, source_target_pairs={{0,2},{1,3},{2,0},{3,1},{4,6},{5,7},{6,4},{7,5},{8,10},{9,11},{10,... | collective-permute-start | bytes 49160 | tf_op jit(solution)/shard_map/ppermute | solution.py:141
  5.3 0.7 %copy-start.2 = (f32[32,128]{1,0:T(8,128)S(1)}, f32[32,128]{1,0:T(8,128)}, u32[]{:S(2)}) copy-start(f32[32,128]{1,0:T(8,128)} %get-tuple-element.32.before_ref.own_ref) | copy-start | bytes 49156
  6.0 7.2 %copy-start.1 = (s32[16,16,128]{2,1,0:T(8,128)S(1)}, s32[16,16,128]{2,1,0:T(8,128)}, u32[]{:S(2)}) copy-start(s32[16,16,128]{2,1,0:T(8,128)} %solid_ref.5) | copy-start | bytes 393220
  8.8 5.5 %collective-permute-start.1 = (f32[16,128]{1,0:T(8,128)S(1)}, f32[16,128]{1,0:T(8,128)S(1)}, u32[]{:S(2)}, u32[]{:S(2)}) collective-permute-start(f32[16,128]{1,0:T(8,128)S(1)} %get-tuple-element.36), channel_id=1, source_target_pairs={{0,12},{1,13},{2,14},{3,15},{4,8},{5,9},{6,10},{7,11},{8,4},{9,5},... | collective-permute-start | bytes 24584 | tf_op jit(solution)/shard_map/ppermute | solution.py:141
  12.4 3.7 %collective-permute-start.2 = (f32[16,128]{1,0:T(8,128)S(1)}, f32[16,128]{1,0:T(8,128)S(1)}, u32[]{:S(2)}, u32[]{:S(2)}) collective-permute-start(f32[16,128]{1,0:T(8,128)S(1)} %get-tuple-element.37), channel_id=1, source_target_pairs={{0,4},{1,5},{2,6},{3,7},{4,0},{5,1},{6,2},{7,3},{8,12},{9,13},{10,... | collective-permute-start | bytes 24584 | tf_op jit(solution)/shard_map/ppermute | solution.py:141
  12.4 4.5 %collective-permute-start.3 = (f32[16,128]{1,0:T(8,128)S(1)}, f32[16,128]{1,0:T(8,128)S(1)}, u32[]{:S(2)}, u32[]{:S(2)}) collective-permute-start(f32[16,128]{1,0:T(8,128)S(1)} %get-tuple-element.38), channel_id=1, source_target_pairs={{0,8},{1,9},{2,10},{3,11},{4,12},{5,13},{6,14},{7,15},{8,0},{9,1},... | collective-permute-start | bytes 24584 | tf_op jit(solution)/shard_map/ppermute | solution.py:141
  13.2 3.8 %copy-start = (f32[19,16,16,128]{3,2,1,0:T(8,128)S(1)}, f32[19,16,16,128]{3,2,1,0:T(8,128)}, u32[]{:S(2)}) copy-start(f32[19,16,16,128]{3,2,1,0:T(8,128)} %pops_ref.5) | copy-start | bytes 7471108
  18.2 6.6 %collective-permute-start.5 = (f32[88,128]{1,0:T(8,128)S(1)}, f32[88,128]{1,0:T(8,128)S(1)}, u32[]{:S(2)}, u32[]{:S(2)}) collective-permute-start(f32[88,128]{1,0:T(8,128)S(1)} %get-tuple-element.51), channel_id=1, source_target_pairs={{0,12},{1,13},{2,14},{3,15},{4,8},{5,9},{6,10},{7,11},{8,4},{9,5},... | collective-permute-start | bytes 135176 | tf_op jit(solution)/shard_map/ppermute | solution.py:141
  19.8 5.1 %collective-permute-start.6 = (f32[88,128]{1,0:T(8,128)S(1)}, f32[88,128]{1,0:T(8,128)S(1)}, u32[]{:S(2)}, u32[]{:S(2)}) collective-permute-start(f32[88,128]{1,0:T(8,128)S(1)} %get-tuple-element.52), channel_id=1, source_target_pairs={{0,4},{1,5},{2,6},{3,7},{4,0},{5,1},{6,2},{7,3},{8,12},{9,13},{10,... | collective-permute-start | bytes 135176 | tf_op jit(solution)/shard_map/ppermute | solution.py:141
  20.3 4.5 %collective-permute-start.4 = (f32[2,16,128]{2,1,0:T(8,128)S(1)}, f32[2,16,128]{2,1,0:T(8,128)S(1)}, u32[]{:S(2)}, u32[]{:S(2)}) collective-permute-start(f32[2,16,128]{2,1,0:T(8,128)S(1)} %get-tuple-element.50), channel_id=1, source_target_pairs={{0,1},{1,0},{2,3},{3,2},{4,5},{5,4},{6,7},{7,6},{8,9},{9,8},{10,11... | collective-permute-start | bytes 49160 | tf_op jit(solution)/shard_map/ppermute | solution.py:141
  20.3 4.5 %collective-permute-start.7 = (f32[8,128]{1,0:T(8,128)S(1)}, f32[8,128]{1,0:T(8,128)S(1)}, u32[]{:S(2)}, u32[]{:S(2)}) collective-permute-start(f32[8,128]{1,0:T(8,128)S(1)} %get-tuple-element.54), channel_id=1, source_target_pairs={{0,8},{1,9},{2,10},{3,11},{4,12},{5,13},{6,14},{7,15},{8,0},{9,1},... | collective-permute-start | bytes 12296 | tf_op jit(solution)/shard_map/ppermute | solution.py:141
  23.9 5.7 %copy-start.3 = (s32[1,128]{1,0:T(1,128)S(1)}, s32[1,128]{1,0:T(1,128)}, u32[]{:S(2)}) copy-start(s32[1,128]{1,0:T(1,128)} %get-tuple-element.58.target_ref) | copy-start | bytes 1540
  25.0 4.6 %collective-permute-start.8 = (f32[168,128]{1,0:T(8,128)S(1)}, f32[168,128]{1,0:T(8,128)S(1)}, u32[]{:S(2)}, u32[]{:S(2)}) collective-permute-start(f32[168,128]{1,0:T(8,128)S(1)} %get-tuple-element.60), channel_id=1, source_target_pairs={{0,2},{1,3},{2,0},{3,1},{4,6},{5,7},{6,4},{7,5},{8,10},{9,11},{10,... | collective-permute-start | bytes 258056 | tf_op jit(solution)/shard_map/ppermute | solution.py:141
  25.6 2.5 %collective-permute-start.9 = (f32[64,128]{1,0:T(8,128)S(1)}, f32[64,128]{1,0:T(8,128)S(1)}, u32[]{:S(2)}, u32[]{:S(2)}) collective-permute-start(f32[64,128]{1,0:T(8,128)S(1)} %get-tuple-element.61), channel_id=1, source_target_pairs={{0,1},{1,0},{2,3},{3,2},{4,5},{5,4},{6,7},{7,6},{8,9},{9,8},{10,11... | collective-permute-start | bytes 98312 | tf_op jit(solution)/shard_map/ppermute | solution.py:141

commit v16 on v12

--- a/solution.py
+++ b/solution.py
@@ -157,19 +157,23 @@
     return lax.dot_general(member.astype(BF16), earlier, NN, preferred_element_type=F32)
 
 
-def spread_column(tile, lane):
-    return jnp.broadcast_to(tile[:, lane : lane + 1], tile.shape)
-
-
 def patch_x(value, i, column):
     side = 0 if STEP[i, 0] == 1 else value.shape[1] - 1
     return jnp.where(iota(value.shape, 1) == side, column, value)
 
 
+def x_pair(i):
+    return ENTER[0][0 if STEP[i, 0] == 1 else 1].index(i)
+
+
 def x_place(i):
-    group = 0 if STEP[i, 0] == 1 else 1
-    place = ENTER[0][group].index(i)
-    return place // 4, (place % 4) * 32 + group
+    k = x_pair(i)
+    return k // 4, (k % 4) * 32 + (1 if STEP[i, 0] == 1 else 0)
+
+
+def x_entering(face, k, z):
+    tile = face[k // 4]
+    return pltpu.roll(tile, tile.shape[1] - ((k % 4) * 32 + 2 * z + 1), 1)
 
 
 def x_ends(planes):
@@ -385,7 +389,10 @@
     force = [x_ends([force_ref[d, z] for z in range(depth)]) for d in range(3)]
     out = collide([column_ref[i] for i in range(19)], column_ref[19] == 1.0, force)
     high = lax.rem(iota((rows, 128), 1), 2) == 0
-    ends = [jnp.where(high, out[i], out[j])[:, 0:32] for i, j in zip(*ENTER[0])]
+    ends = [
+        jnp.where(high, turn(out[j], -1, 1), turn(out[i], 1, 1))[:, 0:32]
+        for i, j in zip(*ENTER[0])
+    ]
     face_ref[0] = jnp.concatenate(ends[0:4], axis=1)
     face_ref[1] = jnp.concatenate([ends[4], jnp.zeros((rows, 96), F32)], axis=1)
     odd = odd_slab()
@@ -437,24 +444,17 @@
 X_EDGES = [i for side in range(2) for i in ENTER[2][side] if STEP[i, 0] != 0]
 
 
-def rows_kernel(depth, rows, before_ref, draft_ref, face_ref, first_ref, second_ref, *refs):
-    refs, (cross_ref, token_ref, turned) = refs[:-3], refs[-3:]
+def rows_kernel(depth, rows, before_ref, draft_ref, first_ref, second_ref, *refs):
+    refs, (cross_ref, token_ref) = refs[:-2], refs[-2:]
     token_ref[...] = jnp.zeros_like(token_ref)
     outs = refs[-1:] if len(refs) == 3 else refs
-    for n in range(2):
-        turned[n] = face_ref[n].T
     for group in range(2):
         out_ref = outs[0] if len(outs) == 1 else outs[group]
         base = group * 5 * depth if len(outs) == 1 else 0
         y = rows - 1 if group == 0 else 0
+        out_ref[base : base + 5 * depth] = draft_ref[group * 5 * depth : (group + 1) * 5 * depth]
         for k, i in enumerate(ENTER[1][group]):
             at = base + k * depth
-            value = draft_ref[(group * 5 + k) * depth : (group * 5 + k + 1) * depth]
-            if STEP[i, 0] != 0:
-                tile, lane = x_place(i)
-                column = turned[tile, pl.ds(lane, depth, stride=2), :][:, y : y + 1]
-                value = patch_x(value, i, jnp.broadcast_to(column, value.shape))
-            out_ref[at : at + depth] = value
             if STEP[i, 2] != 0:
                 side = 0 if STEP[i, 2] == 1 else 1
                 z = 0 if side == 0 else depth - 1
@@ -484,19 +484,18 @@
     return jnp.concatenate([t[:, col * CAP : (col + 1) * CAP] for t in tiles], axis=1)
 
 
-def leaving_rows(depth, rows, before, draft, face, first, second, drags):
+def leaving_rows(depth, rows, before, draft, first, second, drags):
     width = draft.shape[1]
     if drags:
         sizes = [10 * depth + 8]
     else:
         sizes = [5 * depth] * 2
-    args = (draft, face, first, second, *drags)
+    args = (draft, first, second, *drags)
     return pl.pallas_call(
         functools.partial(rows_kernel, depth, rows),
         out_shape=[jax.ShapeDtypeStruct((n, width), F32) for n in sizes + [4 * rows]] + [TOKEN],
         in_specs=[pl.BlockSpec(memory_space=pl.ANY)]
         + [pl.BlockSpec(memory_space=pltpu.VMEM)] * len(args),
-        scratch_shapes=[pltpu.VMEM((2, 128, rows), F32)],
         compiler_params=pltpu.CompilerParams(vmem_limit_bytes=ROOM),
         name="rows",
     )(before, *args)
@@ -521,9 +520,8 @@
         )
         for i in range(19):
             value = turn(out[i], STEP[i, 0], 1)
-            if STEP[i, 0] != 0 and faces:
-                tile, lane = x_place(i)
-                value = patch_x(value, i, spread_column(faces[tile], lane))
+            if STEP[i, 0] != 0:
+                value = patch_x(value, i, faces[x_pair(i)])
             held[i, z] = turn(value, STEP[i, 1], 0)
         return tuple(pltpu.roll(f, 126, 1) for f in faces)
 
@@ -531,18 +529,28 @@
 
 
 def lower_kernel(
-    before_ref, pops_ref, solid_ref, force_ref, side_ref, wall_ref, held, draft_ref, token_ref
+    before_ref, pops_ref, solid_ref, force_ref, side_ref, wall_ref, face_ref, *refs
 ):
+    held, draft_ref, token_ref, turned = refs
     depth, rows, _ = pops_ref.shape[1:]
     token_ref[...] = jnp.zeros_like(token_ref)
+    for n in range(2):
+        turned[n] = face_ref[n].T
     for group in range(2):
-        force = [force_ref[d, :, 0 if group else rows - 1, :] for d in range(3)]
+        y = 0 if group else rows - 1
+        force = [force_ref[d, :, y, :] for d in range(3)]
         out = collide([side_ref[i, 1 - group] for i in range(19)], wall_ref[1 - group] == 1, force)
         for k, i in enumerate(ENTER[1][group]):
             row = (group * 5 + k) * depth
             value = turn(out[i], STEP[i, 0], 1)
+            if STEP[i, 0] != 0:
+                tile, lane = x_place(i)
+                column = turned[tile, pl.ds(lane, depth, stride=2), :][:, y : y + 1]
+                value = patch_x(value, i, jnp.broadcast_to(column, value.shape))
             draft_ref[row : row + depth] = turn(value, STEP[i, 2], 0)
-    stream_planes(0, held.shape[1], (), pops_ref, solid_ref, force_ref, held)
+    face = (face_ref[0], face_ref[1])
+    faces = tuple(x_entering(face, k, 0) for k in range(5))
+    stream_planes(0, held.shape[1], faces, pops_ref, solid_ref, force_ref, held)
 
 
 def upper_kernel(
@@ -564,17 +572,9 @@
             copy.start()
             copies.append(copy)
 
-    straight = [i for i in range(19) if STEP[i, 0] == 0]
-    across = [i for i in range(19) if STEP[i, 0] != 0]
-    leave(lower_ref, straight, 0, half)
-    faces = (face_ref[0], face_ref[1])
-    for i in across:
-        tile, lane = x_place(i)
-        for z in range(half):
-            column = turn(spread_column(faces[tile], lane + 2 * z), STEP[i, 1], 0)
-            held[i, z] = patch_x(lower_ref[i, z], i, column)
-    leave(held, across, 0, half)
-    faces = tuple(pltpu.roll(f, 128 - 2 * half, 1) for f in faces)
+    leave(lower_ref, range(19), 0, half)
+    face = (face_ref[0], face_ref[1])
+    faces = tuple(x_entering(face, k, half) for k in range(5))
     marks = upper_marks(half, depth)
     for low, high in zip(marks, marks[1:]):
         faces = stream_planes(low, high, faces, pops_ref, solid_ref, force_ref, held)
@@ -582,8 +582,7 @@
     for group in range(2):
         first = slice(0, 8) if group == 0 else slice(rows - 8, rows)
         for k, i in enumerate(ENTER[1][group]):
-            source = lower_ref if i in straight else held
-            tile_ref[group * 5 + k, 0:half] = source[i, 0:half, first, :]
+            tile_ref[group * 5 + k, 0:half] = lower_ref[i, :, first, :]
             tile_ref[group * 5 + k, half:depth] = held[i, half:depth, first, :]
     for copy in copies:
         copy.wait()
@@ -593,7 +592,7 @@
     return list(range(half, depth - 2, 4)) + ([depth - 2] if (depth - half) % 4 else []) + [depth]
 
 
-def stream_lower(half, before, pops, solid, force, sides, walls):
+def stream_lower(half, before, pops, solid, force, sides, walls, face):
     _, depth, rows, width = pops.shape
     vmem = pl.BlockSpec(memory_space=pltpu.VMEM)
     return pl.pallas_call(
@@ -603,11 +602,12 @@
             jax.ShapeDtypeStruct((10 * depth, width), F32),
             TOKEN,
         ],
-        in_specs=[pl.BlockSpec(memory_space=pl.ANY)] + [vmem] * 5,
+        in_specs=[pl.BlockSpec(memory_space=pl.ANY)] + [vmem] * 6,
+        scratch_shapes=[pltpu.VMEM((2, 128, rows), F32)],
         compiler_params=pltpu.CompilerParams(vmem_limit_bytes=ROOM),
         cost_estimate=pl.CostEstimate(flops=3000000, bytes_accessed=2000000, transcendentals=0),
         name="lower",
-    )(before, pops, solid, force, sides, walls)
+    )(before, pops, solid, force, sides, walls, face)
 
 
 def stream_upper(before, lower, pops, solid, force, face):
@@ -631,6 +631,30 @@
     )(before, lower, pops, solid, force, face)
 
 
+def choice_kernel(shape, before_ref, target_ref, choice_ref, token_ref):
+    slabs, cols, _ = shape
+    token_ref[...] = jnp.zeros_like(token_ref)
+    target = target_ref[...]
+    owner = lax.shift_right_logical(target, 5)
+    owner_slab = lax.shift_right_logical(owner, cols.bit_length() - 1)
+    away_col = owner - owner_slab * cols - lax.axis_index("col")
+    away_col = jnp.where(away_col < 0, away_col + cols, away_col)
+    away_slab = owner_slab - lax.axis_index("slab")
+    away_slab = jnp.where(away_slab < 0, away_slab + slabs, away_slab)
+    place = away_col * 128 + away_slab * CAP + target - owner * CAP
+    choice_ref[...] = (iota(choice_ref.shape, 0) == place).astype(F32).astype(BF16)
+
+
+def choice_of(shape, before, target):
+    return pl.pallas_call(
+        functools.partial(choice_kernel, shape),
+        out_shape=[jax.ShapeDtypeStruct((256, target.shape[1]), BF16), TOKEN],
+        in_specs=[pl.BlockSpec(memory_space=pl.ANY), pl.BlockSpec(memory_space=pltpu.VMEM)],
+        compiler_params=pltpu.CompilerParams(vmem_limit_bytes=ROOM),
+        name="choice",
+    )(before, target)
+
+
 def finish_kernel(shape, n_rows, whole_ref, target_ref, tile_ref, first_ref, second_ref, *refs):
     row_refs, cross_ref, refs = refs[:n_rows], refs[n_rows], refs[n_rows + 1 :]
     drag_refs, (out_ref, bead_ref, planes, tiles, bead, sem) = refs[:-6], refs[-6:]
@@ -646,6 +670,27 @@
         copy = pltpu.make_async_copy(source, target, sem.at[len(copies)])
         copy.start()
         copies.append(copy)
+
+    count = target_ref.shape[1]
+    if len(drag_refs) == 2:
+        came = arrived_drag(*drag_refs, first_ref, second_ref, 5 * rows)
+        passed = row_refs[0][10 * depth : 10 * depth + 8]
+        table = jnp.concatenate([one_tile(came, 0), passed], axis=1)
+        total = dot_select(table, target_ref[...], NN)
+    else:
+        back_ref = drag_refs[0]
+
+        def group_share(k, total):
+            got = [back_ref[k * GROUP + r] for r in range(GROUP)]
+            slots = jnp.concatenate([t[:, 0:CAP] for t in got], axis=1)
+            first = k * (GROUP * CAP)
+            choose = (iota((GROUP * CAP, count), 0) + first == target_ref[...]).astype(F32)
+            return total + dot_select(slots, choose.astype(BF16), NN)
+
+        total = lax.fori_loop(
+            0, back_ref.shape[0] // GROUP, group_share, jnp.zeros((8, count), F32)
+        )
+    bead[...] = total[0:3]
 
     for group in range(2):
         z = 0 if group == 0 else depth - 1
@@ -666,6 +711,7 @@
             n = group * 5 + k
             planes[n] = value
             leave(planes.at[n], out_ref.at[i, z])
+    leave(bead, bead_ref)
     for group in range(2):
         first = 0 if group == 0 else rows - 8
         for k, i in enumerate(ENTER[1][group]):
@@ -676,37 +722,6 @@
             low, high = max(step, 0), min(depth + step, depth)
             leave(tiles.at[n, 1 + low : 1 + high], out_ref.at[i, low:high, first : first + 8])
 
-    count = target_ref.shape[1]
-    target = target_ref[...]
-    if len(drag_refs) == 2:
-        slabs, cols, _ = shape
-        came = arrived_drag(*drag_refs, first_ref, second_ref, 5 * rows)
-        passed = row_refs[0][10 * depth : 10 * depth + 8]
-        table = jnp.concatenate([one_tile(came, 0), passed], axis=1)
-        owner = lax.shift_right_logical(target, 5)
-        owner_slab = lax.shift_right_logical(owner, cols.bit_length() - 1)
-        away_col = owner - owner_slab * cols - lax.axis_index("col")
-        away_col = jnp.where(away_col < 0, away_col + cols, away_col)
-        away_slab = owner_slab - lax.axis_index("slab")
-        away_slab = jnp.where(away_slab < 0, away_slab + slabs, away_slab)
-        place = away_col * 128 + away_slab * CAP + target - owner * CAP
-        choose = (iota((256, count), 0) == place).astype(F32).astype(BF16)
-        total = dot_select(table, choose, NN)
-    else:
-        back_ref = drag_refs[0]
-
-        def group(k, total):
-            got = [back_ref[k * GROUP + r] for r in range(GROUP)]
-            slots = jnp.concatenate([t[:, 0:CAP] for t in got], axis=1)
-            first = k * (GROUP * CAP)
-            choose = (iota((GROUP * CAP, count), 0) + first == target).astype(F32)
-            return total + dot_select(slots, choose.astype(BF16), NN)
-
-        total = lax.fori_loop(
-            0, back_ref.shape[0] // GROUP, group, jnp.zeros((8, count), F32)
-        )
-    bead[...] = total[0:3]
-    leave(bead, bead_ref)
     for copy in copies:
         copy.wait()
 
@@ -769,9 +784,11 @@
         drags = []
         drag = swap(drag)
     fields = (populations, solid_mask, force)
-    lower, draft, token = stream_lower(10, token, *fields, sides, walls)
-    *leaving, cross, token = leaving_rows(depth, rows, token, draft, face, first, second, drags)
+    lower, draft, token = stream_lower(depth // 2, token, *fields, sides, walls, face)
+    *leaving, cross, token = leaving_rows(depth, rows, token, draft, first, second, drags)
     entered, cross = send_col(leaving), send_pair(cross)
+    if single:
+        target, token = choice_of(shape, token, target)
     whole, tiles = stream_upper(token, lower, *fields, face)
     return tuple(
         finish(shape, whole, target, tiles, first, second, entered, cross, drags or [drag])

time: 29.8 us -> 29.9 us (level)
  waiting for transfers between devices: 4.24 us -> 4.54 us
  transfers between devices with their start and end apart: 7 -> 7, of which waited for: 3 -> 3; matrix products, arithmetic and copies ran while one was open for 0% -> 0% of each run, Pallas kernels for 22% -> 21%
where the time goes in v16:
time: 29.9 us; the launch traced here: 29.6 us
  starting transfers between devices  12.7 us (42%)
  Pallas kernels  10.8 us (36%)
  waiting for transfers between devices  4.54 us (15%)
  local copies, waits for them, and re-layouts  0.92 us (3%)
  between operations  0.7 us (2%)
    all_to_all x1, starting transfers between devices, shards(): messages = swap(messages)  7.25 us
    ppermute x6, starting transfers between devices, send(): return lax.ppermute(value, ('slab', 'col', 'pair'), perm)  5.41 us
    all_to_all x1, waiting for transfers between devices, shards(): messages = swap(messages)  2.91 us
    pallas_call x1, Pallas kernels, moments(): pl.pallas_call(moments_kernel, out_shape=[jax.ShapeDtypeStruct((3 * width...  2.86 us
    pallas_call x1, Pallas kernels, stream_upper(): pl.pallas_call(upper_kernel, out_shape=[jax.ShapeDtypeStruct(pops.shape,...  2.28 us
    pallas_call x1, Pallas kernels, pack(): pl.pallas_call(functools.partial(pack_kernel, steps), out_shape=[jax.Shap...  1.89 us
    ppermute x6, waiting for transfers between devices, send(): return lax.ppermute(value, ('slab', 'col', 'pair'), perm)  1.63 us
    pallas_call x1, Pallas kernels, couple(): pl.pallas_call(functools.partial(couple_kernel, shape, len(drags)), out_s...  1.3 us
  transfers between devices with their start and end apart: 7, of which 3 were waited for; matrix products, arithmetic and copies ran while one was open for 0% of the time, Pallas kernels for 21%

profile of v16, /device:TPU:0, one launch (start us, length us, event | category | flops | bytes accessed | tf_op | source)
XLA Modules:
  0.0 29.6 jit_solution(14098097377039440152)
XLA Ops:
  0.6 0.0 copy-start
  0.6 1.9 %pack.1 = (s32[1,128]{1,0:T(1,128)}, f32[8,8,128]{2,1,0:T(8,128)}) custom-call(s32[1,128]{1,0:T(1,128)} %bitcast.1, s32[3,128]{1,0:T(4,128)} %base_ref.1, f32[3,128]{1,0:T(4,128)} %offset_ref.1, f32[3,128]{1,0:T(4,128)} %velocity_ref.1), custom_call_target="tpu_custom_call" | custom-call | tf_op jit(solution)/shard_map/pack/pallas_call | solution.py:233
  2.5 7.3 %all-to-all-start = ((f32[8,8,128]{2,1,0:T(8,128)}), f32[8,8,128]{2,1,0:T(8,128)S(1)}, u32[]{:S(2)}, u32[]{:S(2)}) async-start(f32[8,8,128]{2,1,0:T(8,128)} %get-tuple-element.26), calls=%async_computation | async-start | bytes 65536 | tf_op jit(solution)/shard_map/all_to_all | solution.py:764
  9.8 0.9 %copy-done.1 = s32[16,16,128]{2,1,0:T(8,128)S(1)} copy-done((s32[16,16,128]{2,1,0:T(8,128)S(1)}, s32[16,16,128]{2,1,0:T(8,128)}, u32[]{:S(2)}) %copy-start.1) | copy-done | bytes 131096
  10.7 2.9 %moments.1 = (bf16[384,256]{1,0:T(8,128)(2,1)S(1)}, bf16[384,256]{1,0:T(8,128)(2,1)S(1)}, f32[20,16,128]{2,1,0:T(8,128)S(1)}, f32[19,2,16,128]{3,2,1,0:T(8,128)S(1)}, s32[2,16,128]{2,1,0:T(8,128)S(1)}) custom-call(f32[19,16,16,128]{3,2,1,0:T(8,128)} %pops_ref.5, s32[16,16,128]{2,1,0:T(8,128)S(1)} %copy-done.1), custom_call_target="tpu_custom_call" | custom-call | flops 3000000 | bytes 4000000 | tf_op jit(solution)/shard_map/moments/pallas_call | solution.py:287
  13.6 2.9 %all-to-all-done.beads_ref = f32[8,8,128]{2,1,0:T(8,128)S(1)} async-done(((f32[8,8,128]{2,1,0:T(8,128)}), f32[8,8,128]{2,1,0:T(8,128)S(1)}, u32[]{:S(2)}, u32[]{:S(2)}) %all-to-all-start) | async-done | bytes 32800 | tf_op jit(solution)/shard_map/all_to_all | solution.py:764
  16.5 1.3 %couple.1 = (f32[3,16,16,128]{3,2,1,0:T(8,128)S(1)}, f32[2,16,128]{2,1,0:T(8,128)S(1)}, f32[88,128]{1,0:T(8,128)S(1)}, f32[88,128]{1,0:T(8,128)S(1)}, f32[4,8,12...) custom-call(f32[8,8,128]{2,1,0:T(8,128)S(1)} %all-to-all-done.beads_ref, ...), custom_call_target="tpu_custom_call" | custom-call | tf_op jit(solution)/shard_map/couple/pallas_call | solution.py:424
  17.8 0.0 copy-start.3
  17.8 1.0 %collective-permute-start.1 = (f32[88,128]{1,0:T(8,128)S(1)}, f32[88,128]{1,0:T(8,128)S(1)}, u32[]{:S(2)}, u32[]{:S(2)}) collective-permute-start(f32[88,128]{1,0:T(8,128)S(1)} %get-tuple-element.37), channel_id=1, source_target_pairs={{0,12},{1,13},{2,14},{3,15},{4,8},{5,9},{6,10},{7,11},{8,4},{9,5},... | collective-permute-start | bytes 135176 | tf_op jit(solution)/shard_map/ppermute | solution.py:140
  18.8 0.1 collective-permute-start.2
  18.9 0.0 collective-permute-start
  19.0 3.3 %collective-permute-start.3 = (f32[8,128]{1,0:T(8,128)S(1)}, f32[8,128]{1,0:T(8,128)S(1)}, u32[]{:S(2)}, u32[]{:S(2)}) collective-permute-start(f32[8,128]{1,0:T(8,128)S(1)} %get-tuple-element.40), channel_id=1, source_target_pairs={{0,8},{1,9},{2,10},{3,11},{4,12},{5,13},{6,14},{7,15},{8,0},{9,1},... | collective-permute-start | bytes 12296 | tf_op jit(solution)/shard_map/ppermute | solution.py:140
  22.3 0.0 collective-permute-done.face_ref
  22.3 1.2 %lower.1 = (f32[19,8,16,128]{3,2,1,0:T(8,128)S(1)}, f32[160,128]{1,0:T(8,128)S(1)}, f32[8,128]{1,0:T(8,128)S(1)}) custom-call(f32[8,128]{1,0:T(8,128)S(1)} %get-tuple-element.30.before_ref, f32[19,16,16,128]{3,2,1,0:T(8,128)S(1)} %copy-done, s32[16,16,128]{2,1,0:T(8,128)S(1)} %copy-done.2, f32[3,16,16,128]{3,2,1,0:T(8,128)S(1)} %get-tuple-element.31.force_ref, ...), custom_call_target="tpu_custom_call" | custom-call | flops 3000000 | bytes 2000000 | tf_op jit(solution)/shard_map/lower/pallas_call | solution.py:598
  23.4 0.4 %collective-permute-done.3.refs_1_.refs_3_ = f32[8,128]{1,0:T(8,128)S(1)} collective-permute-done((f32[8,128]{1,0:T(8,128)S(1)}, f32[8,128]{1,0:T(8,128)S(1)}, u32[]{:S(2)}, u32[]{:S(2)}) %collective-permute-start.3) | collective-permute-done | bytes 4128 | tf_op jit(solution)/shard_map/ppermute | solution.py:140
  23.8 0.0 collective-permute-done.1.first_ref
  23.8 0.0 collective-permute-done.2.second_ref
  23.8 0.1 rows.1
  23.9 1.0 %collective-permute-start.4 = (f32[168,128]{1,0:T(8,128)S(1)}, f32[168,128]{1,0:T(8,128)S(1)}, u32[]{:S(2)}, u32[]{:S(2)}) collective-permute-start(f32[168,128]{1,0:T(8,128)S(1)} %get-tuple-element.48), channel_id=1, source_target_pairs={{0,2},{1,3},{2,0},{3,1},{4,6},{5,7},{6,4},{7,5},{8,10},{9,11},{10,... | collective-permute-start | bytes 258056 | tf_op jit(solution)/shard_map/ppermute | solution.py:140
  24.9 0.0 collective-permute-start.5
  24.9 2.3 %upper.1 = (f32[19,16,16,128]{3,2,1,0:T(8,128)}, f32[10,16,8,128]{3,2,1,0:T(8,128)S(1)}) custom-call(f32[8,128]{1,0:T(8,128)S(1)} %get-tuple-element.43.before_ref, f32[19,8,16,128]{3,2,1,0:T(8,128)S(1)} %get-tuple-element.44.lower_ref, f32[19,16,16,128]{3,2,1,0:T(8,128)S(1)} %copy-done, s32[16,16,128]{2,1,0:T(8,128)S(1)} %copy-done.2, ...), custom_call_target="tpu_custom_call" | custom-call | flops 5000000 | bytes 3000000 | tf_op jit(solution)/shard_map/upper/pallas_call | solution.py:616
  27.2 0.0 collective-permute-done.5.refs_1_
  27.2 1.2 %collective-permute-done.4.refs_0_ = f32[168,128]{1,0:T(8,128)S(1)} collective-permute-done((f32[168,128]{1,0:T(8,128)S(1)}, f32[168,128]{1,0:T(8,128)S(1)}, u32[]{:S(2)}, u32[]{:S(2)}) %collective-permute-start.4) | collective-permute-done | bytes 86048 | tf_op jit(solution)/shard_map/ppermute | solution.py:140
  28.4 1.2 %finish.1 = (f32[19,16,16,128]{3,2,1,0:T(8,128)}, f32[3,128]{1,0:T(4,128)}) custom-call(f32[19,16,16,128]{3,2,1,0:T(8,128)} %get-tuple-element.45.whole_ref, bf16[256,128]{1,0:T(8,128)(2,1)S(1)} %get-tuple-element.46.target_ref, f32[10,16,8,128]{3,2,1,0:T(8,128)S(1)} %get-tuple-element.47.tile_ref, ...), custom_call_target="tpu_custom_call", output_to_operand_aliasing={{0}: (0, {})} | custom-call | tf_op jit(solution)/shard_map/finish/pallas_call | solution.py:734
  (6 shorter events, 0.0 us)
Async XLA Ops:
  0.6 15.8 %copy-start = (f32[19,16,16,128]{3,2,1,0:T(8,128)S(1)}, f32[19,16,16,128]{3,2,1,0:T(8,128)}, u32[]{:S(2)}) copy-start(f32[19,16,16,128]{3,2,1,0:T(8,128)} %pops_ref.5) | copy-start | bytes 7471108
  2.5 13.9 %all-to-all-start = ((f32[8,8,128]{2,1,0:T(8,128)}), f32[8,8,128]{2,1,0:T(8,128)S(1)}, u32[]{:S(2)}, u32[]{:S(2)}) async-start(f32[8,8,128]{2,1,0:T(8,128)} %get-tuple-element.26), calls=%async_computation | async-start | bytes 65536 | tf_op jit(solution)/shard_map/all_to_all | solution.py:764
  9.8 0.9 %copy-start.1 = (s32[16,16,128]{2,1,0:T(8,128)S(1)}, s32[16,16,128]{2,1,0:T(8,128)}, u32[]{:S(2)}) copy-start(s32[16,16,128]{2,1,0:T(8,128)} %solid_ref.5) | copy-start | bytes 393220
  10.7 5.8 %copy-start.2 = (s32[16,16,128]{2,1,0:T(8,128)S(1)}, s32[16,16,128]{2,1,0:T(8,128)}, u32[]{:S(2)}) copy-start(s32[16,16,128]{2,1,0:T(8,128)} %solid_ref.5) | copy-start | bytes 393220
  17.8 7.1 %copy-start.3 = (s32[1,128]{1,0:T(1,128)S(1)}, s32[1,128]{1,0:T(1,128)}, u32[]{:S(2)}) copy-start(s32[1,128]{1,0:T(1,128)} %get-tuple-element.42.target_ref) | copy-start | bytes 1540
  17.8 6.0 %collective-permute-start.1 = (f32[88,128]{1,0:T(8,128)S(1)}, f32[88,128]{1,0:T(8,128)S(1)}, u32[]{:S(2)}, u32[]{:S(2)}) collective-permute-start(f32[88,128]{1,0:T(8,128)S(1)} %get-tuple-element.37), channel_id=1, source_target_pairs={{0,12},{1,13},{2,14},{3,15},{4,8},{5,9},{6,10},{7,11},{8,4},{9,5},... | collective-permute-start | bytes 135176 | tf_op jit(solution)/shard_map/ppermute | solution.py:140
  18.8 5.0 %collective-permute-start.2 = (f32[88,128]{1,0:T(8,128)S(1)}, f32[88,128]{1,0:T(8,128)S(1)}, u32[]{:S(2)}, u32[]{:S(2)}) collective-permute-start(f32[88,128]{1,0:T(8,128)S(1)} %get-tuple-element.38), channel_id=1, source_target_pairs={{0,4},{1,5},{2,6},{3,7},{4,0},{5,1},{6,2},{7,3},{8,12},{9,13},{10,... | collective-permute-start | bytes 135176 | tf_op jit(solution)/shard_map/ppermute | solution.py:140
  18.9 3.3 %collective-permute-start = (f32[2,16,128]{2,1,0:T(8,128)S(1)}, f32[2,16,128]{2,1,0:T(8,128)S(1)}, u32[]{:S(2)}, u32[]{:S(2)}) collective-permute-start(f32[2,16,128]{2,1,0:T(8,128)S(1)} %get-tuple-element.34), channel_id=1, source_target_pairs={{0,1},{1,0},{2,3},{3,2},{4,5},{5,4},{6,7},{7,6},{8,9},{9,8},{10,11... | collective-permute-start | bytes 49160 | tf_op jit(solution)/shard_map/ppermute | solution.py:140
  19.0 4.9 %collective-permute-start.3 = (f32[8,128]{1,0:T(8,128)S(1)}, f32[8,128]{1,0:T(8,128)S(1)}, u32[]{:S(2)}, u32[]{:S(2)}) collective-permute-start(f32[8,128]{1,0:T(8,128)S(1)} %get-tuple-element.40), channel_id=1, source_target_pairs={{0,8},{1,9},{2,10},{3,11},{4,12},{5,13},{6,14},{7,15},{8,0},{9,1},... | collective-permute-start | bytes 12296 | tf_op jit(solution)/shard_map/ppermute | solution.py:140
  23.9 4.5 %collective-permute-start.4 = (f32[168,128]{1,0:T(8,128)S(1)}, f32[168,128]{1,0:T(8,128)S(1)}, u32[]{:S(2)}, u32[]{:S(2)}) collective-permute-start(f32[168,128]{1,0:T(8,128)S(1)} %get-tuple-element.48), channel_id=1, source_target_pairs={{0,2},{1,3},{2,0},{3,1},{4,6},{5,7},{6,4},{7,5},{8,10},{9,11},{10,... | collective-permute-start | bytes 258056 | tf_op jit(solution)/shard_map/ppermute | solution.py:140
  24.9 2.3 %collective-permute-start.5 = (f32[64,128]{1,0:T(8,128)S(1)}, f32[64,128]{1,0:T(8,128)S(1)}, u32[]{:S(2)}, u32[]{:S(2)}) collective-permute-start(f32[64,128]{1,0:T(8,128)S(1)} %get-tuple-element.49), channel_id=1, source_target_pairs={{0,1},{1,0},{2,3},{3,2},{4,5},{5,4},{6,7},{7,6},{8,9},{9,8},{10,11... | collective-permute-start | bytes 98312 | tf_op jit(solution)/shard_map/ppermute | solution.py:140

commit v17 on v16

--- a/solution.py
+++ b/solution.py
@@ -171,6 +171,11 @@
     return k // 4, (k % 4) * 32 + (1 if STEP[i, 0] == 1 else 0)
 
 
+def x_arrived(face_ref):
+    even = lax.rem(iota(face_ref.shape[1:], 1), 2) == 0
+    return [jnp.where(even, turn(face_ref[n], -1, 1), turn(face_ref[n], 1, 1)) for n in range(2)]
+
+
 def x_entering(face, k, z):
     tile = face[k // 4]
     return pltpu.roll(tile, tile.shape[1] - ((k % 4) * 32 + 2 * z + 1), 1)
@@ -389,10 +394,7 @@
     force = [x_ends([force_ref[d, z] for z in range(depth)]) for d in range(3)]
     out = collide([column_ref[i] for i in range(19)], column_ref[19] == 1.0, force)
     high = lax.rem(iota((rows, 128), 1), 2) == 0
-    ends = [
-        jnp.where(high, turn(out[j], -1, 1), turn(out[i], 1, 1))[:, 0:32]
-        for i, j in zip(*ENTER[0])
-    ]
+    ends = [jnp.where(high, out[i], out[j])[:, 0:32] for i, j in zip(*ENTER[0])]
     face_ref[0] = jnp.concatenate(ends[0:4], axis=1)
     face_ref[1] = jnp.concatenate([ends[4], jnp.zeros((rows, 96), F32)], axis=1)
     odd = odd_slab()
@@ -534,8 +536,9 @@
     held, draft_ref, token_ref, turned = refs
     depth, rows, _ = pops_ref.shape[1:]
     token_ref[...] = jnp.zeros_like(token_ref)
+    face = x_arrived(face_ref)
     for n in range(2):
-        turned[n] = face_ref[n].T
+        turned[n] = face[n].T
     for group in range(2):
         y = 0 if group else rows - 1
         force = [force_ref[d, :, y, :] for d in range(3)]
@@ -548,7 +551,6 @@
                 column = turned[tile, pl.ds(lane, depth, stride=2), :][:, y : y + 1]
                 value = patch_x(value, i, jnp.broadcast_to(column, value.shape))
             draft_ref[row : row + depth] = turn(value, STEP[i, 2], 0)
-    face = (face_ref[0], face_ref[1])
     faces = tuple(x_entering(face, k, 0) for k in range(5))
     stream_planes(0, held.shape[1], faces, pops_ref, solid_ref, force_ref, held)
 
@@ -573,7 +575,7 @@
             copies.append(copy)
 
     leave(lower_ref, range(19), 0, half)
-    face = (face_ref[0], face_ref[1])
+    face = x_arrived(face_ref)
     faces = tuple(x_entering(face, k, half) for k in range(5))
     marks = upper_marks(half, depth)
     for low, high in zip(marks, marks[1:]):
@@ -671,27 +673,6 @@
         copy.start()
         copies.append(copy)
 
-    count = target_ref.shape[1]
-    if len(drag_refs) == 2:
-        came = arrived_drag(*drag_refs, first_ref, second_ref, 5 * rows)
-        passed = row_refs[0][10 * depth : 10 * depth + 8]
-        table = jnp.concatenate([one_tile(came, 0), passed], axis=1)
-        total = dot_select(table, target_ref[...], NN)
-    else:
-        back_ref = drag_refs[0]
-
-        def group_share(k, total):
-            got = [back_ref[k * GROUP + r] for r in range(GROUP)]
-            slots = jnp.concatenate([t[:, 0:CAP] for t in got], axis=1)
-            first = k * (GROUP * CAP)
-            choose = (iota((GROUP * CAP, count), 0) + first == target_ref[...]).astype(F32)
-            return total + dot_select(slots, choose.astype(BF16), NN)
-
-        total = lax.fori_loop(
-            0, back_ref.shape[0] // GROUP, group_share, jnp.zeros((8, count), F32)
-        )
-    bead[...] = total[0:3]
-
     for group in range(2):
         z = 0 if group == 0 else depth - 1
         for k, i in enumerate(ENTER[2][group]):
@@ -711,7 +692,6 @@
             n = group * 5 + k
             planes[n] = value
             leave(planes.at[n], out_ref.at[i, z])
-    leave(bead, bead_ref)
     for group in range(2):
         first = 0 if group == 0 else rows - 8
         for k, i in enumerate(ENTER[1][group]):
@@ -722,6 +702,27 @@
             low, high = max(step, 0), min(depth + step, depth)
             leave(tiles.at[n, 1 + low : 1 + high], out_ref.at[i, low:high, first : first + 8])
 
+    count = target_ref.shape[1]
+    if len(drag_refs) == 2:
+        came = arrived_drag(*drag_refs, first_ref, second_ref, 5 * rows)
+        passed = row_refs[0][10 * depth : 10 * depth + 8]
+        table = jnp.concatenate([one_tile(came, 0), passed], axis=1)
+        total = dot_select(table, target_ref[...], NN)
+    else:
+        back_ref = drag_refs[0]
+
+        def group_share(k, total):
+            got = [back_ref[k * GROUP + r] for r in range(GROUP)]
+            slots = jnp.concatenate([t[:, 0:CAP] for t in got], axis=1)
+            first = k * (GROUP * CAP)
+            choose = (iota((GROUP * CAP, count), 0) + first == target_ref[...]).astype(F32)
+            return total + dot_select(slots, choose.astype(BF16), NN)
+
+        total = lax.fori_loop(
+            0, back_ref.shape[0] // GROUP, group_share, jnp.zeros((8, count), F32)
+        )
+    bead[...] = total[0:3]
+    leave(bead, bead_ref)
     for copy in copies:
         copy.wait()
 

time: 29.9 us -> 29.7 us (level)
  transfers between devices with their start and end apart: 7 -> 7, of which waited for: 3 -> 3; matrix products, arithmetic and copies ran while one was open for 0% -> 0% of each run, Pallas kernels for 21% -> 22%
where the time goes in v17:
time: 29.7 us; the launch traced here: 29.4 us
  starting transfers between devices  12.7 us (43%)
  Pallas kernels  10.7 us (36%)
  waiting for transfers between devices  4.45 us (15%)
  local copies, waits for them, and re-layouts  0.91 us (3%)
  between operations  0.69 us (2%)
    all_to_all x1, starting transfers between devices, shards(): messages = swap(messages)  7.25 us
    ppermute x6, starting transfers between devices, send(): return lax.ppermute(value, ('slab', 'col', 'pair'), perm)  5.41 us
    all_to_all x1, waiting for transfers between devices, shards(): messages = swap(messages)  2.91 us
    pallas_call x1, Pallas kernels, moments(): pl.pallas_call(moments_kernel, out_shape=[jax.ShapeDtypeStruct((3 * width...  2.86 us
    pallas_call x1, Pallas kernels, stream_upper(): pl.pallas_call(upper_kernel, out_shape=[jax.ShapeDtypeStruct(pops.shape,...  2.35 us
    pallas_call x1, Pallas kernels, pack(): pl.pallas_call(functools.partial(pack_kernel, steps), out_shape=[jax.Shap...  1.89 us
    ppermute x6, waiting for transfers between devices, send(): return lax.ppermute(value, ('slab', 'col', 'pair'), perm)  1.54 us
    pallas_call x1, Pallas kernels, couple(): pl.pallas_call(functools.partial(couple_kernel, shape, len(drags)), out_s...  1.23 us
  transfers between devices with their start and end apart: 7, of which 3 were waited for; matrix products, arithmetic and copies ran while one was open for 0% of the time, Pallas kernels for 22%

profile of v17, /device:TPU:0, one launch (start us, length us, event | category | flops | bytes accessed | tf_op | source)
XLA Modules:
  0.0 29.4 jit_solution(7141684222600085568)
XLA Ops:
  0.6 0.0 copy-start
  0.6 1.9 %pack.1 = (s32[1,128]{1,0:T(1,128)}, f32[8,8,128]{2,1,0:T(8,128)}) custom-call(s32[1,128]{1,0:T(1,128)} %bitcast.1, s32[3,128]{1,0:T(4,128)} %base_ref.1, f32[3,128]{1,0:T(4,128)} %offset_ref.1, f32[3,128]{1,0:T(4,128)} %velocity_ref.1), custom_call_target="tpu_custom_call" | custom-call | tf_op jit(solution)/shard_map/pack/pallas_call | solution.py:238
  2.5 7.3 %all-to-all-start = ((f32[8,8,128]{2,1,0:T(8,128)}), f32[8,8,128]{2,1,0:T(8,128)S(1)}, u32[]{:S(2)}, u32[]{:S(2)}) async-start(f32[8,8,128]{2,1,0:T(8,128)} %get-tuple-element.26), calls=%async_computation | async-start | bytes 65536 | tf_op jit(solution)/shard_map/all_to_all | solution.py:765
  9.8 0.9 %copy-done.1 = s32[16,16,128]{2,1,0:T(8,128)S(1)} copy-done((s32[16,16,128]{2,1,0:T(8,128)S(1)}, s32[16,16,128]{2,1,0:T(8,128)}, u32[]{:S(2)}) %copy-start.1) | copy-done | bytes 131096
  10.7 2.9 %moments.1 = (bf16[384,256]{1,0:T(8,128)(2,1)S(1)}, bf16[384,256]{1,0:T(8,128)(2,1)S(1)}, f32[20,16,128]{2,1,0:T(8,128)S(1)}, f32[19,2,16,128]{3,2,1,0:T(8,128)S(1)}, s32[2,16,128]{2,1,0:T(8,128)S(1)}) custom-call(f32[19,16,16,128]{3,2,1,0:T(8,128)} %pops_ref.5, s32[16,16,128]{2,1,0:T(8,128)S(1)} %copy-done.1), custom_call_target="tpu_custom_call" | custom-call | flops 3000000 | bytes 4000000 | tf_op jit(solution)/shard_map/moments/pallas_call | solution.py:292
  13.6 2.9 %all-to-all-done.beads_ref = f32[8,8,128]{2,1,0:T(8,128)S(1)} async-done(((f32[8,8,128]{2,1,0:T(8,128)}), f32[8,8,128]{2,1,0:T(8,128)S(1)}, u32[]{:S(2)}, u32[]{:S(2)}) %all-to-all-start) | async-done | bytes 32800 | tf_op jit(solution)/shard_map/all_to_all | solution.py:765
  16.5 0.0 copy-done
  16.5 1.2 %couple.1 = (f32[3,16,16,128]{3,2,1,0:T(8,128)S(1)}, f32[2,16,128]{2,1,0:T(8,128)S(1)}, f32[88,128]{1,0:T(8,128)S(1)}, f32[88,128]{1,0:T(8,128)S(1)}, f32[4,8,12...) custom-call(f32[8,8,128]{2,1,0:T(8,128)S(1)} %all-to-all-done.beads_ref, ...), custom_call_target="tpu_custom_call" | custom-call | tf_op jit(solution)/shard_map/couple/pallas_call | solution.py:426
  17.7 1.0 %collective-permute-start.1 = (f32[88,128]{1,0:T(8,128)S(1)}, f32[88,128]{1,0:T(8,128)S(1)}, u32[]{:S(2)}, u32[]{:S(2)}) collective-permute-start(f32[88,128]{1,0:T(8,128)S(1)} %get-tuple-element.37), channel_id=1, source_target_pairs={{0,12},{1,13},{2,14},{3,15},{4,8},{5,9},{6,10},{7,11},{8,4},{9,5},... | collective-permute-start | bytes 135176 | tf_op jit(solution)/shard_map/ppermute | solution.py:140
  18.7 0.1 collective-permute-start.2
  18.9 0.0 collective-permute-start
  18.9 3.3 %collective-permute-start.3 = (f32[8,128]{1,0:T(8,128)S(1)}, f32[8,128]{1,0:T(8,128)S(1)}, u32[]{:S(2)}, u32[]{:S(2)}) collective-permute-start(f32[8,128]{1,0:T(8,128)S(1)} %get-tuple-element.40), channel_id=1, source_target_pairs={{0,8},{1,9},{2,10},{3,11},{4,12},{5,13},{6,14},{7,15},{8,0},{9,1},... | collective-permute-start | bytes 12296 | tf_op jit(solution)/shard_map/ppermute | solution.py:140
  22.2 0.0 collective-permute-done.face_ref
  22.2 1.2 %lower.1 = (f32[19,8,16,128]{3,2,1,0:T(8,128)S(1)}, f32[160,128]{1,0:T(8,128)S(1)}, f32[8,128]{1,0:T(8,128)S(1)}) custom-call(f32[8,128]{1,0:T(8,128)S(1)} %get-tuple-element.30.before_ref, f32[19,16,16,128]{3,2,1,0:T(8,128)S(1)} %copy-done, s32[16,16,128]{2,1,0:T(8,128)S(1)} %copy-done.2, f32[3,16,16,128]{3,2,1,0:T(8,128)S(1)} %get-tuple-element.31.force_ref, ...), custom_call_target="tpu_custom_call" | custom-call | flops 3000000 | bytes 2000000 | tf_op jit(solution)/shard_map/lower/pallas_call | solution.py:600
  23.4 0.4 %collective-permute-done.3.refs_1_.refs_3_ = f32[8,128]{1,0:T(8,128)S(1)} collective-permute-done((f32[8,128]{1,0:T(8,128)S(1)}, f32[8,128]{1,0:T(8,128)S(1)}, u32[]{:S(2)}, u32[]{:S(2)}) %collective-permute-start.3) | collective-permute-done | bytes 4128 | tf_op jit(solution)/shard_map/ppermute | solution.py:140
  23.8 0.0 collective-permute-done.1.first_ref
  23.8 0.0 collective-permute-done.2.second_ref
  23.8 0.1 rows.1
  23.8 1.0 %collective-permute-start.4 = (f32[168,128]{1,0:T(8,128)S(1)}, f32[168,128]{1,0:T(8,128)S(1)}, u32[]{:S(2)}, u32[]{:S(2)}) collective-permute-start(f32[168,128]{1,0:T(8,128)S(1)} %get-tuple-element.48), channel_id=1, source_target_pairs={{0,2},{1,3},{2,0},{3,1},{4,6},{5,7},{6,4},{7,5},{8,10},{9,11},{10,... | collective-permute-start | bytes 258056 | tf_op jit(solution)/shard_map/ppermute | solution.py:140
  24.8 0.0 collective-permute-start.5
  24.8 2.4 %upper.1 = (f32[19,16,16,128]{3,2,1,0:T(8,128)}, f32[10,16,8,128]{3,2,1,0:T(8,128)S(1)}) custom-call(f32[8,128]{1,0:T(8,128)S(1)} %get-tuple-element.43.before_ref, f32[19,8,16,128]{3,2,1,0:T(8,128)S(1)} %get-tuple-element.44.lower_ref, f32[19,16,16,128]{3,2,1,0:T(8,128)S(1)} %copy-done, s32[16,16,128]{2,1,0:T(8,128)S(1)} %copy-done.2, ...), custom_call_target="tpu_custom_call" | custom-call | flops 5000000 | bytes 3000000 | tf_op jit(solution)/shard_map/upper/pallas_call | solution.py:618
  27.2 0.0 collective-permute-done.5.refs_1_
  27.2 1.1 %collective-permute-done.4.refs_0_ = f32[168,128]{1,0:T(8,128)S(1)} collective-permute-done((f32[168,128]{1,0:T(8,128)S(1)}, f32[168,128]{1,0:T(8,128)S(1)}, u32[]{:S(2)}, u32[]{:S(2)}) %collective-permute-start.4) | collective-permute-done | bytes 86048 | tf_op jit(solution)/shard_map/ppermute | solution.py:140
  28.3 1.1 %finish.1 = (f32[19,16,16,128]{3,2,1,0:T(8,128)}, f32[3,128]{1,0:T(4,128)}) custom-call(f32[19,16,16,128]{3,2,1,0:T(8,128)} %get-tuple-element.45.whole_ref, bf16[256,128]{1,0:T(8,128)(2,1)S(1)} %get-tuple-element.46.target_ref, f32[10,16,8,128]{3,2,1,0:T(8,128)S(1)} %get-tuple-element.47.tile_ref, ...), custom_call_target="tpu_custom_call", output_to_operand_aliasing={{0}: (0, {})} | custom-call | tf_op jit(solution)/shard_map/finish/pallas_call | solution.py:735
  (6 shorter events, 0.0 us)
Async XLA Ops:
  0.6 15.8 %copy-start = (f32[19,16,16,128]{3,2,1,0:T(8,128)S(1)}, f32[19,16,16,128]{3,2,1,0:T(8,128)}, u32[]{:S(2)}) copy-start(f32[19,16,16,128]{3,2,1,0:T(8,128)} %pops_ref.5) | copy-start | bytes 7471108
  2.5 13.9 %all-to-all-start = ((f32[8,8,128]{2,1,0:T(8,128)}), f32[8,8,128]{2,1,0:T(8,128)S(1)}, u32[]{:S(2)}, u32[]{:S(2)}) async-start(f32[8,8,128]{2,1,0:T(8,128)} %get-tuple-element.26), calls=%async_computation | async-start | bytes 65536 | tf_op jit(solution)/shard_map/all_to_all | solution.py:765
  9.8 0.9 %copy-start.1 = (s32[16,16,128]{2,1,0:T(8,128)S(1)}, s32[16,16,128]{2,1,0:T(8,128)}, u32[]{:S(2)}) copy-start(s32[16,16,128]{2,1,0:T(8,128)} %solid_ref.5) | copy-start | bytes 393220
  10.7 5.8 %copy-start.2 = (s32[16,16,128]{2,1,0:T(8,128)S(1)}, s32[16,16,128]{2,1,0:T(8,128)}, u32[]{:S(2)}) copy-start(s32[16,16,128]{2,1,0:T(8,128)} %solid_ref.5) | copy-start | bytes 393220
  17.7 7.1 %copy-start.3 = (s32[1,128]{1,0:T(1,128)S(1)}, s32[1,128]{1,0:T(1,128)}, u32[]{:S(2)}) copy-start(s32[1,128]{1,0:T(1,128)} %get-tuple-element.42.target_ref) | copy-start | bytes 1540
  17.7 6.0 %collective-permute-start.1 = (f32[88,128]{1,0:T(8,128)S(1)}, f32[88,128]{1,0:T(8,128)S(1)}, u32[]{:S(2)}, u32[]{:S(2)}) collective-permute-start(f32[88,128]{1,0:T(8,128)S(1)} %get-tuple-element.37), channel_id=1, source_target_pairs={{0,12},{1,13},{2,14},{3,15},{4,8},{5,9},{6,10},{7,11},{8,4},{9,5},... | collective-permute-start | bytes 135176 | tf_op jit(solution)/shard_map/ppermute | solution.py:140
  18.7 5.0 %collective-permute-start.2 = (f32[88,128]{1,0:T(8,128)S(1)}, f32[88,128]{1,0:T(8,128)S(1)}, u32[]{:S(2)}, u32[]{:S(2)}) collective-permute-start(f32[88,128]{1,0:T(8,128)S(1)} %get-tuple-element.38), channel_id=1, source_target_pairs={{0,4},{1,5},{2,6},{3,7},{4,0},{5,1},{6,2},{7,3},{8,12},{9,13},{10,... | collective-permute-start | bytes 135176 | tf_op jit(solution)/shard_map/ppermute | solution.py:140
  18.9 3.3 %collective-permute-start = (f32[2,16,128]{2,1,0:T(8,128)S(1)}, f32[2,16,128]{2,1,0:T(8,128)S(1)}, u32[]{:S(2)}, u32[]{:S(2)}) collective-permute-start(f32[2,16,128]{2,1,0:T(8,128)S(1)} %get-tuple-element.34), channel_id=1, source_target_pairs={{0,1},{1,0},{2,3},{3,2},{4,5},{5,4},{6,7},{7,6},{8,9},{9,8},{10,11... | collective-permute-start | bytes 49160 | tf_op jit(solution)/shard_map/ppermute | solution.py:140
  18.9 4.9 %collective-permute-start.3 = (f32[8,128]{1,0:T(8,128)S(1)}, f32[8,128]{1,0:T(8,128)S(1)}, u32[]{:S(2)}, u32[]{:S(2)}) collective-permute-start(f32[8,128]{1,0:T(8,128)S(1)} %get-tuple-element.40), channel_id=1, source_target_pairs={{0,8},{1,9},{2,10},{3,11},{4,12},{5,13},{6,14},{7,15},{8,0},{9,1},... | collective-permute-start | bytes 12296 | tf_op jit(solution)/shard_map/ppermute | solution.py:140
  23.8 4.5 %collective-permute-start.4 = (f32[168,128]{1,0:T(8,128)S(1)}, f32[168,128]{1,0:T(8,128)S(1)}, u32[]{:S(2)}, u32[]{:S(2)}) collective-permute-start(f32[168,128]{1,0:T(8,128)S(1)} %get-tuple-element.48), channel_id=1, source_target_pairs={{0,2},{1,3},{2,0},{3,1},{4,6},{5,7},{6,4},{7,5},{8,10},{9,11},{10,... | collective-permute-start | bytes 258056 | tf_op jit(solution)/shard_map/ppermute | solution.py:140
  24.8 2.4 %collective-permute-start.5 = (f32[64,128]{1,0:T(8,128)S(1)}, f32[64,128]{1,0:T(8,128)S(1)}, u32[]{:S(2)}, u32[]{:S(2)}) collective-permute-start(f32[64,128]{1,0:T(8,128)S(1)} %get-tuple-element.49), channel_id=1, source_target_pairs={{0,1},{1,0},{2,3},{3,2},{4,5},{5,4},{6,7},{7,6},{8,9},{9,8},{10,11... | collective-permute-start | bytes 98312 | tf_op jit(solution)/shard_map/ppermute | solution.py:140

commit v18 on v17

--- a/solution.py
+++ b/solution.py
@@ -216,7 +216,7 @@
     blank = jnp.zeros((8, CAP), F32)
     for r in range(GROUP):
         lanes = slice(r * CAP, (r + 1) * CAP)
-        out_ref[r] = jnp.concatenate(
+        out_ref[r * 8 : r * 8 + 8] = jnp.concatenate(
             [packed[0:8, lanes], packed[8:16, lanes], packed[16:24, lanes], blank], axis=1
         )
 
@@ -231,20 +231,21 @@
             in_specs=[pl.BlockSpec(a.shape, lambda k: (0, 0)) for a in args],
             out_specs=[
                 pl.BlockSpec((1, count), lambda k: (0, 0)),
-                pl.BlockSpec((GROUP, 8, 128), lambda k: (k, 0, 0)),
+                pl.BlockSpec((GROUP * 8, 128), lambda k: (k, 0)),
             ],
             compiler_params=pltpu.CompilerParams(vmem_limit_bytes=48 << 20),
         )
-    return pl.pallas_call(
+    target, tiles = pl.pallas_call(
         functools.partial(pack_kernel, steps),
         out_shape=[
             jax.ShapeDtypeStruct((1, count), jnp.int32),
-            jax.ShapeDtypeStruct((owners, 8, 128), F32),
+            jax.ShapeDtypeStruct((owners * 8, 128), F32),
         ],
         scratch_shapes=[pltpu.VMEM((24, count), F32)],
         name="pack",
         **blocks,
     )(*args)
+    return target, tiles.reshape(owners, 8, 128)
 
 
 def moments_kernel(

time: 29.7 us -> 29.7 us (level)
  no operation moved by 1% of the time
where the time goes in v18:
time: 29.7 us; the launch traced here: 29.4 us
  starting transfers between devices  12.7 us (43%)
  Pallas kernels  10.7 us (36%)
  waiting for transfers between devices  4.45 us (15%)
  local copies, waits for them, and re-layouts  0.91 us (3%)
  between operations  0.69 us (2%)
    all_to_all x1, starting transfers between devices, shards(): messages = swap(messages)  7.25 us
    ppermute x6, starting transfers between devices, send(): return lax.ppermute(value, ('slab', 'col', 'pair'), perm)  5.41 us
    all_to_all x1, waiting for transfers between devices, shards(): messages = swap(messages)  2.91 us
    pallas_call x1, Pallas kernels, moments(): pl.pallas_call(moments_kernel, out_shape=[jax.ShapeDtypeStruct((3 * width...  2.86 us
    pallas_call x1, Pallas kernels, stream_upper(): pl.pallas_call(upper_kernel, out_shape=[jax.ShapeDtypeStruct(pops.shape,...  2.35 us
    pallas_call x1, Pallas kernels, pack(): pl.pallas_call(functools.partial(pack_kernel, steps), out_shape=[jax.Shap...  1.89 us
    ppermute x6, waiting for transfers between devices, send(): return lax.ppermute(value, ('slab', 'col', 'pair'), perm)  1.54 us
    pallas_call x1, Pallas kernels, couple(): pl.pallas_call(functools.partial(couple_kernel, shape, len(drags)), out_s...  1.23 us
  transfers between devices with their start and end apart: 7, of which 3 were waited for; matrix products, arithmetic and copies ran while one was open for 0% of the time, Pallas kernels for 22%

profile of v18, /device:TPU:0, one launch (start us, length us, event | category | flops | bytes accessed | tf_op | source)
XLA Modules:
  0.0 29.4 jit_solution(8720819810938700646)
XLA Ops:
  0.6 0.0 copy-start
  0.6 1.9 %pack.1 = (s32[1,128]{1,0:T(1,128)}, f32[64,128]{1,0:T(8,128)}) custom-call(s32[1,128]{1,0:T(1,128)} %bitcast.3, s32[3,128]{1,0:T(4,128)} %base_ref.1, f32[3,128]{1,0:T(4,128)} %offset_ref.1, f32[3,128]{1,0:T(4,128)} %velocity_ref.1), custom_call_target="tpu_custom_call" | custom-call | tf_op jit(solution)/shard_map/pack/pallas_call | solution.py:238
  2.5 7.3 %all-to-all-start = ((f32[8,8,128]{2,1,0:T(8,128)}), f32[8,8,128]{2,1,0:T(8,128)S(1)}, u32[]{:S(2)}, u32[]{:S(2)}) async-start(f32[8,8,128]{2,1,0:T(8,128)} %bitcast.2), calls=%async_computation | async-start | bytes 65536 | tf_op jit(solution)/shard_map/all_to_all | solution.py:766
  9.8 0.9 %copy-done.1 = s32[16,16,128]{2,1,0:T(8,128)S(1)} copy-done((s32[16,16,128]{2,1,0:T(8,128)S(1)}, s32[16,16,128]{2,1,0:T(8,128)}, u32[]{:S(2)}) %copy-start.1) | copy-done | bytes 131096
  10.7 2.9 %moments.1 = (bf16[384,256]{1,0:T(8,128)(2,1)S(1)}, bf16[384,256]{1,0:T(8,128)(2,1)S(1)}, f32[20,16,128]{2,1,0:T(8,128)S(1)}, f32[19,2,16,128]{3,2,1,0:T(8,128)S(1)}, s32[2,16,128]{2,1,0:T(8,128)S(1)}) custom-call(f32[19,16,16,128]{3,2,1,0:T(8,128)} %pops_ref.5, s32[16,16,128]{2,1,0:T(8,128)S(1)} %copy-done.1), custom_call_target="tpu_custom_call" | custom-call | flops 3000000 | bytes 4000000 | tf_op jit(solution)/shard_map/moments/pallas_call | solution.py:293
  13.6 2.9 %all-to-all-done.beads_ref = f32[8,8,128]{2,1,0:T(8,128)S(1)} async-done(((f32[8,8,128]{2,1,0:T(8,128)}), f32[8,8,128]{2,1,0:T(8,128)S(1)}, u32[]{:S(2)}, u32[]{:S(2)}) %all-to-all-start) | async-done | bytes 32800 | tf_op jit(solution)/shard_map/all_to_all | solution.py:766
  16.5 0.0 copy-done
  16.5 1.2 %couple.1 = (f32[3,16,16,128]{3,2,1,0:T(8,128)S(1)}, f32[2,16,128]{2,1,0:T(8,128)S(1)}, f32[88,128]{1,0:T(8,128)S(1)}, f32[88,128]{1,0:T(8,128)S(1)}, f32[4,8,12...) custom-call(f32[8,8,128]{2,1,0:T(8,128)S(1)} %all-to-all-done.beads_ref, ...), custom_call_target="tpu_custom_call" | custom-call | tf_op jit(solution)/shard_map/couple/pallas_call | solution.py:427
  17.7 1.0 %collective-permute-start.1 = (f32[88,128]{1,0:T(8,128)S(1)}, f32[88,128]{1,0:T(8,128)S(1)}, u32[]{:S(2)}, u32[]{:S(2)}) collective-permute-start(f32[88,128]{1,0:T(8,128)S(1)} %get-tuple-element.37), channel_id=1, source_target_pairs={{0,12},{1,13},{2,14},{3,15},{4,8},{5,9},{6,10},{7,11},{8,4},{9,5},... | collective-permute-start | bytes 135176 | tf_op jit(solution)/shard_map/ppermute | solution.py:140
  18.7 0.1 collective-permute-start.2
  18.9 0.0 collective-permute-start
  18.9 3.3 %collective-permute-start.3 = (f32[8,128]{1,0:T(8,128)S(1)}, f32[8,128]{1,0:T(8,128)S(1)}, u32[]{:S(2)}, u32[]{:S(2)}) collective-permute-start(f32[8,128]{1,0:T(8,128)S(1)} %get-tuple-element.40), channel_id=1, source_target_pairs={{0,8},{1,9},{2,10},{3,11},{4,12},{5,13},{6,14},{7,15},{8,0},{9,1},... | collective-permute-start | bytes 12296 | tf_op jit(solution)/shard_map/ppermute | solution.py:140
  22.2 0.0 collective-permute-done.face_ref
  22.2 1.2 %lower.1 = (f32[19,8,16,128]{3,2,1,0:T(8,128)S(1)}, f32[160,128]{1,0:T(8,128)S(1)}, f32[8,128]{1,0:T(8,128)S(1)}) custom-call(f32[8,128]{1,0:T(8,128)S(1)} %get-tuple-element.30.before_ref, f32[19,16,16,128]{3,2,1,0:T(8,128)S(1)} %copy-done, s32[16,16,128]{2,1,0:T(8,128)S(1)} %copy-done.2, f32[3,16,16,128]{3,2,1,0:T(8,128)S(1)} %get-tuple-element.31.force_ref, ...), custom_call_target="tpu_custom_call" | custom-call | flops 3000000 | bytes 2000000 | tf_op jit(solution)/shard_map/lower/pallas_call | solution.py:601
  23.4 0.4 %collective-permute-done.3.refs_1_.refs_3_ = f32[8,128]{1,0:T(8,128)S(1)} collective-permute-done((f32[8,128]{1,0:T(8,128)S(1)}, f32[8,128]{1,0:T(8,128)S(1)}, u32[]{:S(2)}, u32[]{:S(2)}) %collective-permute-start.3) | collective-permute-done | bytes 4128 | tf_op jit(solution)/shard_map/ppermute | solution.py:140
  23.8 0.0 collective-permute-done.1.first_ref
  23.8 0.0 collective-permute-done.2.second_ref
  23.8 0.1 rows.1
  23.8 1.0 %collective-permute-start.4 = (f32[168,128]{1,0:T(8,128)S(1)}, f32[168,128]{1,0:T(8,128)S(1)}, u32[]{:S(2)}, u32[]{:S(2)}) collective-permute-start(f32[168,128]{1,0:T(8,128)S(1)} %get-tuple-element.48), channel_id=1, source_target_pairs={{0,2},{1,3},{2,0},{3,1},{4,6},{5,7},{6,4},{7,5},{8,10},{9,11},{10,... | collective-permute-start | bytes 258056 | tf_op jit(solution)/shard_map/ppermute | solution.py:140
  24.8 0.0 collective-permute-start.5
  24.8 2.4 %upper.1 = (f32[19,16,16,128]{3,2,1,0:T(8,128)}, f32[10,16,8,128]{3,2,1,0:T(8,128)S(1)}) custom-call(f32[8,128]{1,0:T(8,128)S(1)} %get-tuple-element.43.before_ref, f32[19,8,16,128]{3,2,1,0:T(8,128)S(1)} %get-tuple-element.44.lower_ref, f32[19,16,16,128]{3,2,1,0:T(8,128)S(1)} %copy-done, s32[16,16,128]{2,1,0:T(8,128)S(1)} %copy-done.2, ...), custom_call_target="tpu_custom_call" | custom-call | flops 5000000 | bytes 3000000 | tf_op jit(solution)/shard_map/upper/pallas_call | solution.py:619
  27.2 0.0 collective-permute-done.5.refs_1_
  27.2 1.1 %collective-permute-done.4.refs_0_ = f32[168,128]{1,0:T(8,128)S(1)} collective-permute-done((f32[168,128]{1,0:T(8,128)S(1)}, f32[168,128]{1,0:T(8,128)S(1)}, u32[]{:S(2)}, u32[]{:S(2)}) %collective-permute-start.4) | collective-permute-done | bytes 86048 | tf_op jit(solution)/shard_map/ppermute | solution.py:140
  28.3 1.1 %finish.1 = (f32[19,16,16,128]{3,2,1,0:T(8,128)}, f32[3,128]{1,0:T(4,128)}) custom-call(f32[19,16,16,128]{3,2,1,0:T(8,128)} %get-tuple-element.45.whole_ref, bf16[256,128]{1,0:T(8,128)(2,1)S(1)} %get-tuple-element.46.target_ref, f32[10,16,8,128]{3,2,1,0:T(8,128)S(1)} %get-tuple-element.47.tile_ref, ...), custom_call_target="tpu_custom_call", output_to_operand_aliasing={{0}: (0, {})} | custom-call | tf_op jit(solution)/shard_map/finish/pallas_call | solution.py:736
  (6 shorter events, 0.0 us)
Async XLA Ops:
  0.6 15.8 %copy-start = (f32[19,16,16,128]{3,2,1,0:T(8,128)S(1)}, f32[19,16,16,128]{3,2,1,0:T(8,128)}, u32[]{:S(2)}) copy-start(f32[19,16,16,128]{3,2,1,0:T(8,128)} %pops_ref.5) | copy-start | bytes 7471108
  2.5 13.9 %all-to-all-start = ((f32[8,8,128]{2,1,0:T(8,128)}), f32[8,8,128]{2,1,0:T(8,128)S(1)}, u32[]{:S(2)}, u32[]{:S(2)}) async-start(f32[8,8,128]{2,1,0:T(8,128)} %bitcast.2), calls=%async_computation | async-start | bytes 65536 | tf_op jit(solution)/shard_map/all_to_all | solution.py:766
  9.8 0.9 %copy-start.1 = (s32[16,16,128]{2,1,0:T(8,128)S(1)}, s32[16,16,128]{2,1,0:T(8,128)}, u32[]{:S(2)}) copy-start(s32[16,16,128]{2,1,0:T(8,128)} %solid_ref.5) | copy-start | bytes 393220
  10.7 5.8 %copy-start.2 = (s32[16,16,128]{2,1,0:T(8,128)S(1)}, s32[16,16,128]{2,1,0:T(8,128)}, u32[]{:S(2)}) copy-start(s32[16,16,128]{2,1,0:T(8,128)} %solid_ref.5) | copy-start | bytes 393220
  17.7 7.1 %copy-start.3 = (s32[1,128]{1,0:T(1,128)S(1)}, s32[1,128]{1,0:T(1,128)}, u32[]{:S(2)}) copy-start(s32[1,128]{1,0:T(1,128)} %get-tuple-element.42.target_ref) | copy-start | bytes 1540
  17.7 6.0 %collective-permute-start.1 = (f32[88,128]{1,0:T(8,128)S(1)}, f32[88,128]{1,0:T(8,128)S(1)}, u32[]{:S(2)}, u32[]{:S(2)}) collective-permute-start(f32[88,128]{1,0:T(8,128)S(1)} %get-tuple-element.37), channel_id=1, source_target_pairs={{0,12},{1,13},{2,14},{3,15},{4,8},{5,9},{6,10},{7,11},{8,4},{9,5},... | collective-permute-start | bytes 135176 | tf_op jit(solution)/shard_map/ppermute | solution.py:140
  18.7 5.0 %collective-permute-start.2 = (f32[88,128]{1,0:T(8,128)S(1)}, f32[88,128]{1,0:T(8,128)S(1)}, u32[]{:S(2)}, u32[]{:S(2)}) collective-permute-start(f32[88,128]{1,0:T(8,128)S(1)} %get-tuple-element.38), channel_id=1, source_target_pairs={{0,4},{1,5},{2,6},{3,7},{4,0},{5,1},{6,2},{7,3},{8,12},{9,13},{10,... | collective-permute-start | bytes 135176 | tf_op jit(solution)/shard_map/ppermute | solution.py:140
  18.9 3.3 %collective-permute-start = (f32[2,16,128]{2,1,0:T(8,128)S(1)}, f32[2,16,128]{2,1,0:T(8,128)S(1)}, u32[]{:S(2)}, u32[]{:S(2)}) collective-permute-start(f32[2,16,128]{2,1,0:T(8,128)S(1)} %get-tuple-element.34), channel_id=1, source_target_pairs={{0,1},{1,0},{2,3},{3,2},{4,5},{5,4},{6,7},{7,6},{8,9},{9,8},{10,11... | collective-permute-start | bytes 49160 | tf_op jit(solution)/shard_map/ppermute | solution.py:140
  18.9 4.9 %collective-permute-start.3 = (f32[8,128]{1,0:T(8,128)S(1)}, f32[8,128]{1,0:T(8,128)S(1)}, u32[]{:S(2)}, u32[]{:S(2)}) collective-permute-start(f32[8,128]{1,0:T(8,128)S(1)} %get-tuple-element.40), channel_id=1, source_target_pairs={{0,8},{1,9},{2,10},{3,11},{4,12},{5,13},{6,14},{7,15},{8,0},{9,1},... | collective-permute-start | bytes 12296 | tf_op jit(solution)/shard_map/ppermute | solution.py:140
  23.8 4.5 %collective-permute-start.4 = (f32[168,128]{1,0:T(8,128)S(1)}, f32[168,128]{1,0:T(8,128)S(1)}, u32[]{:S(2)}, u32[]{:S(2)}) collective-permute-start(f32[168,128]{1,0:T(8,128)S(1)} %get-tuple-element.48), channel_id=1, source_target_pairs={{0,2},{1,3},{2,0},{3,1},{4,6},{5,7},{6,4},{7,5},{8,10},{9,11},{10,... | collective-permute-start | bytes 258056 | tf_op jit(solution)/shard_map/ppermute | solution.py:140
  24.8 2.4 %collective-permute-start.5 = (f32[64,128]{1,0:T(8,128)S(1)}, f32[64,128]{1,0:T(8,128)S(1)}, u32[]{:S(2)}, u32[]{:S(2)}) collective-permute-start(f32[64,128]{1,0:T(8,128)S(1)} %get-tuple-element.49), channel_id=1, source_target_pairs={{0,1},{1,0},{2,3},{3,2},{4,5},{5,4},{6,7},{7,6},{8,9},{9,8},{10,11... | collective-permute-start | bytes 98312 | tf_op jit(solution)/shard_map/ppermute | solution.py:140

commit v19 on v18

--- a/solution.py
+++ b/solution.py
@@ -189,9 +189,17 @@
     return tile
 
 
-def pack_kernel(
-    steps, owner_ref, base_ref, offset_ref, velocity_ref, target_ref, out_ref, table
-):
+def pack_kernel(steps, *refs):
+    sources, (target_ref, out_ref, table, *held) = refs[:4], refs[4:]
+    copies = []
+    if steps == 1:
+        *held, sem = held
+        for k, (source, place) in enumerate(zip(sources, held)):
+            copies.append(pltpu.make_async_copy(source, place, sem.at[k]))
+            copies[-1].start()
+        copies[0].wait()
+        sources = held
+    owner_ref, base_ref, offset_ref, velocity_ref = sources
     count = owner_ref.shape[1]
     step = 0 if steps == 1 else pl.program_id(0)
     local = owner_ref[...] - step * GROUP
@@ -209,6 +217,8 @@
 
     choose = (iota((GROUP * CAP, count), 0) == target).astype(F32).astype(BF16)
     table[...] = jnp.zeros_like(table)
+    for copy in copies[1:]:
+        copy.wait()
     table[0:3] = base_ref[...].astype(F32) + 1.0
     table[8:11] = offset_ref[...]
     table[16:19] = velocity_ref[...]
@@ -224,8 +234,11 @@
 def pack(owners, owner, base, offset, velocity):
     count, steps = owner.shape[0], owners // GROUP
     args = (owner.reshape(1, count), base, offset, velocity)
-    blocks = {}
-    if steps > 1:
+    scratch = [pltpu.VMEM((24, count), F32)]
+    if steps == 1:
+        blocks = dict(in_specs=[pl.BlockSpec(memory_space=pl.ANY)] * 4)
+        scratch += [pltpu.VMEM(a.shape, a.dtype) for a in args] + [pltpu.SemaphoreType.DMA((4,))]
+    else:
         blocks = dict(
             grid=(steps,),
             in_specs=[pl.BlockSpec(a.shape, lambda k: (0, 0)) for a in args],
@@ -241,7 +254,7 @@
             jax.ShapeDtypeStruct((1, count), jnp.int32),
             jax.ShapeDtypeStruct((owners * 8, 128), F32),
         ],
-        scratch_shapes=[pltpu.VMEM((24, count), F32)],
+        scratch_shapes=scratch,
         name="pack",
         **blocks,
     )(*args)

time: 29.7 us -> 29.7 us (level)
  no operation moved by 1% of the time
where the time goes in v19:
time: 29.7 us; the launch traced here: 29.4 us
  starting transfers between devices  12.7 us (43%)
  Pallas kernels  10.7 us (36%)
  waiting for transfers between devices  4.46 us (15%)
  local copies, waits for them, and re-layouts  0.91 us (3%)
  between operations  0.7 us (2%)
    all_to_all x1, starting transfers between devices, shards(): messages = swap(messages)  7.26 us
    ppermute x6, starting transfers between devices, send(): return lax.ppermute(value, ('slab', 'col', 'pair'), perm)  5.41 us
    all_to_all x1, waiting for transfers between devices, shards(): messages = swap(messages)  2.91 us
    pallas_call x1, Pallas kernels, moments(): pl.pallas_call(moments_kernel, out_shape=[jax.ShapeDtypeStruct((3 * width...  2.86 us
    pallas_call x1, Pallas kernels, stream_upper(): pl.pallas_call(upper_kernel, out_shape=[jax.ShapeDtypeStruct(pops.shape,...  2.35 us
    pallas_call x1, Pallas kernels, pack(): pl.pallas_call(functools.partial(pack_kernel, steps), out_shape=[jax.Shap...  1.86 us
    ppermute x6, waiting for transfers between devices, send(): return lax.ppermute(value, ('slab', 'col', 'pair'), perm)  1.54 us
    pallas_call x1, Pallas kernels, couple(): pl.pallas_call(functools.partial(couple_kernel, shape, len(drags)), out_s...  1.23 us
  transfers between devices with their start and end apart: 7, of which 3 were waited for; matrix products, arithmetic and copies ran while one was open for 0% of the time, Pallas kernels for 22%

profile of v19, /device:TPU:0, one launch (start us, length us, event | category | flops | bytes accessed | tf_op | source)
XLA Modules:
  0.0 29.4 jit_solution(11136368333037163289)
XLA Ops:
  0.6 0.0 copy-start
  0.6 1.9 %pack.1 = (s32[1,128]{1,0:T(1,128)}, f32[64,128]{1,0:T(8,128)}) custom-call(s32[1,128]{1,0:T(1,128)} %bitcast.3, s32[3,128]{1,0:T(4,128)} %refs_1_.2, f32[3,128]{1,0:T(4,128)} %refs_2_.2, f32[3,128]{1,0:T(4,128)} %refs_3_.1), custom_call_target="tpu_custom_call" | custom-call | tf_op jit(solution)/shard_map/pack/pallas_call | solution.py:251
  2.5 7.3 %all-to-all-start = ((f32[8,8,128]{2,1,0:T(8,128)}), f32[8,8,128]{2,1,0:T(8,128)S(1)}, u32[]{:S(2)}, u32[]{:S(2)}) async-start(f32[8,8,128]{2,1,0:T(8,128)} %bitcast.2), calls=%async_computation | async-start | bytes 65536 | tf_op jit(solution)/shard_map/all_to_all | solution.py:779
  9.8 0.9 %copy-done.1 = s32[16,16,128]{2,1,0:T(8,128)S(1)} copy-done((s32[16,16,128]{2,1,0:T(8,128)S(1)}, s32[16,16,128]{2,1,0:T(8,128)}, u32[]{:S(2)}) %copy-start.1) | copy-done | bytes 131096
  10.7 2.9 %moments.1 = (bf16[384,256]{1,0:T(8,128)(2,1)S(1)}, bf16[384,256]{1,0:T(8,128)(2,1)S(1)}, f32[20,16,128]{2,1,0:T(8,128)S(1)}, f32[19,2,16,128]{3,2,1,0:T(8,128)S(1)}, s32[2,16,128]{2,1,0:T(8,128)S(1)}) custom-call(f32[19,16,16,128]{3,2,1,0:T(8,128)} %pops_ref.5, s32[16,16,128]{2,1,0:T(8,128)S(1)} %copy-done.1), custom_call_target="tpu_custom_call" | custom-call | flops 3000000 | bytes 4000000 | tf_op jit(solution)/shard_map/moments/pallas_call | solution.py:306
  13.6 2.9 %all-to-all-done.beads_ref = f32[8,8,128]{2,1,0:T(8,128)S(1)} async-done(((f32[8,8,128]{2,1,0:T(8,128)}), f32[8,8,128]{2,1,0:T(8,128)S(1)}, u32[]{:S(2)}, u32[]{:S(2)}) %all-to-all-start) | async-done | bytes 32800 | tf_op jit(solution)/shard_map/all_to_all | solution.py:779
  16.5 0.0 copy-done
  16.5 1.2 %couple.1 = (f32[3,16,16,128]{3,2,1,0:T(8,128)S(1)}, f32[2,16,128]{2,1,0:T(8,128)S(1)}, f32[88,128]{1,0:T(8,128)S(1)}, f32[88,128]{1,0:T(8,128)S(1)}, f32[4,8,12...) custom-call(f32[8,8,128]{2,1,0:T(8,128)S(1)} %all-to-all-done.beads_ref, ...), custom_call_target="tpu_custom_call" | custom-call | tf_op jit(solution)/shard_map/couple/pallas_call | solution.py:440
  17.7 1.0 %collective-permute-start.1 = (f32[88,128]{1,0:T(8,128)S(1)}, f32[88,128]{1,0:T(8,128)S(1)}, u32[]{:S(2)}, u32[]{:S(2)}) collective-permute-start(f32[88,128]{1,0:T(8,128)S(1)} %get-tuple-element.37), channel_id=1, source_target_pairs={{0,12},{1,13},{2,14},{3,15},{4,8},{5,9},{6,10},{7,11},{8,4},{9,5},... | collective-permute-start | bytes 135176 | tf_op jit(solution)/shard_map/ppermute | solution.py:140
  18.7 0.1 collective-permute-start.2
  18.8 0.0 collective-permute-start
  18.9 3.3 %collective-permute-start.3 = (f32[8,128]{1,0:T(8,128)S(1)}, f32[8,128]{1,0:T(8,128)S(1)}, u32[]{:S(2)}, u32[]{:S(2)}) collective-permute-start(f32[8,128]{1,0:T(8,128)S(1)} %get-tuple-element.40), channel_id=1, source_target_pairs={{0,8},{1,9},{2,10},{3,11},{4,12},{5,13},{6,14},{7,15},{8,0},{9,1},... | collective-permute-start | bytes 12296 | tf_op jit(solution)/shard_map/ppermute | solution.py:140
  22.2 0.0 collective-permute-done.face_ref
  22.2 1.2 %lower.1 = (f32[19,8,16,128]{3,2,1,0:T(8,128)S(1)}, f32[160,128]{1,0:T(8,128)S(1)}, f32[8,128]{1,0:T(8,128)S(1)}) custom-call(f32[8,128]{1,0:T(8,128)S(1)} %get-tuple-element.30.before_ref, f32[19,16,16,128]{3,2,1,0:T(8,128)S(1)} %copy-done, s32[16,16,128]{2,1,0:T(8,128)S(1)} %copy-done.2, f32[3,16,16,128]{3,2,1,0:T(8,128)S(1)} %get-tuple-element.31.force_ref, ...), custom_call_target="tpu_custom_call" | custom-call | flops 3000000 | bytes 2000000 | tf_op jit(solution)/shard_map/lower/pallas_call | solution.py:614
  23.3 0.4 %collective-permute-done.3.refs_1_.refs_3_ = f32[8,128]{1,0:T(8,128)S(1)} collective-permute-done((f32[8,128]{1,0:T(8,128)S(1)}, f32[8,128]{1,0:T(8,128)S(1)}, u32[]{:S(2)}, u32[]{:S(2)}) %collective-permute-start.3) | collective-permute-done | bytes 4128 | tf_op jit(solution)/shard_map/ppermute | solution.py:140
  23.7 0.0 collective-permute-done.1.first_ref
  23.7 0.0 collective-permute-done.2.second_ref
  23.7 0.1 rows.1
  23.8 1.0 %collective-permute-start.4 = (f32[168,128]{1,0:T(8,128)S(1)}, f32[168,128]{1,0:T(8,128)S(1)}, u32[]{:S(2)}, u32[]{:S(2)}) collective-permute-start(f32[168,128]{1,0:T(8,128)S(1)} %get-tuple-element.48), channel_id=1, source_target_pairs={{0,2},{1,3},{2,0},{3,1},{4,6},{5,7},{6,4},{7,5},{8,10},{9,11},{10,... | collective-permute-start | bytes 258056 | tf_op jit(solution)/shard_map/ppermute | solution.py:140
  24.8 0.0 collective-permute-start.5
  24.8 2.4 %upper.1 = (f32[19,16,16,128]{3,2,1,0:T(8,128)}, f32[10,16,8,128]{3,2,1,0:T(8,128)S(1)}) custom-call(f32[8,128]{1,0:T(8,128)S(1)} %get-tuple-element.43.before_ref, f32[19,8,16,128]{3,2,1,0:T(8,128)S(1)} %get-tuple-element.44.lower_ref, f32[19,16,16,128]{3,2,1,0:T(8,128)S(1)} %copy-done, s32[16,16,128]{2,1,0:T(8,128)S(1)} %copy-done.2, ...), custom_call_target="tpu_custom_call" | custom-call | flops 5000000 | bytes 3000000 | tf_op jit(solution)/shard_map/upper/pallas_call | solution.py:632
  27.2 0.0 collective-permute-done.5.refs_1_
  27.2 1.1 %collective-permute-done.4.refs_0_ = f32[168,128]{1,0:T(8,128)S(1)} collective-permute-done((f32[168,128]{1,0:T(8,128)S(1)}, f32[168,128]{1,0:T(8,128)S(1)}, u32[]{:S(2)}, u32[]{:S(2)}) %collective-permute-start.4) | collective-permute-done | bytes 86048 | tf_op jit(solution)/shard_map/ppermute | solution.py:140
  28.3 1.1 %finish.1 = (f32[19,16,16,128]{3,2,1,0:T(8,128)}, f32[3,128]{1,0:T(4,128)}) custom-call(f32[19,16,16,128]{3,2,1,0:T(8,128)} %get-tuple-element.45.whole_ref, bf16[256,128]{1,0:T(8,128)(2,1)S(1)} %get-tuple-element.46.target_ref, f32[10,16,8,128]{3,2,1,0:T(8,128)S(1)} %get-tuple-element.47.tile_ref, ...), custom_call_target="tpu_custom_call", output_to_operand_aliasing={{0}: (0, {})} | custom-call | tf_op jit(solution)/shard_map/finish/pallas_call | solution.py:749
  (6 shorter events, 0.0 us)
Async XLA Ops:
  0.6 15.8 %copy-start = (f32[19,16,16,128]{3,2,1,0:T(8,128)S(1)}, f32[19,16,16,128]{3,2,1,0:T(8,128)}, u32[]{:S(2)}) copy-start(f32[19,16,16,128]{3,2,1,0:T(8,128)} %pops_ref.5) | copy-start | bytes 7471108
  2.5 14.0 %all-to-all-start = ((f32[8,8,128]{2,1,0:T(8,128)}), f32[8,8,128]{2,1,0:T(8,128)S(1)}, u32[]{:S(2)}, u32[]{:S(2)}) async-start(f32[8,8,128]{2,1,0:T(8,128)} %bitcast.2), calls=%async_computation | async-start | bytes 65536 | tf_op jit(solution)/shard_map/all_to_all | solution.py:779
  9.8 0.9 %copy-start.1 = (s32[16,16,128]{2,1,0:T(8,128)S(1)}, s32[16,16,128]{2,1,0:T(8,128)}, u32[]{:S(2)}) copy-start(s32[16,16,128]{2,1,0:T(8,128)} %solid_ref.5) | copy-start | bytes 393220
  10.7 5.8 %copy-start.2 = (s32[16,16,128]{2,1,0:T(8,128)S(1)}, s32[16,16,128]{2,1,0:T(8,128)}, u32[]{:S(2)}) copy-start(s32[16,16,128]{2,1,0:T(8,128)} %solid_ref.5) | copy-start | bytes 393220
  17.7 7.1 %copy-start.3 = (s32[1,128]{1,0:T(1,128)S(1)}, s32[1,128]{1,0:T(1,128)}, u32[]{:S(2)}) copy-start(s32[1,128]{1,0:T(1,128)} %get-tuple-element.42.target_ref) | copy-start | bytes 1540
  17.7 6.0 %collective-permute-start.1 = (f32[88,128]{1,0:T(8,128)S(1)}, f32[88,128]{1,0:T(8,128)S(1)}, u32[]{:S(2)}, u32[]{:S(2)}) collective-permute-start(f32[88,128]{1,0:T(8,128)S(1)} %get-tuple-element.37), channel_id=1, source_target_pairs={{0,12},{1,13},{2,14},{3,15},{4,8},{5,9},{6,10},{7,11},{8,4},{9,5},... | collective-permute-start | bytes 135176 | tf_op jit(solution)/shard_map/ppermute | solution.py:140
  18.7 5.0 %collective-permute-start.2 = (f32[88,128]{1,0:T(8,128)S(1)}, f32[88,128]{1,0:T(8,128)S(1)}, u32[]{:S(2)}, u32[]{:S(2)}) collective-permute-start(f32[88,128]{1,0:T(8,128)S(1)} %get-tuple-element.38), channel_id=1, source_target_pairs={{0,4},{1,5},{2,6},{3,7},{4,0},{5,1},{6,2},{7,3},{8,12},{9,13},{10,... | collective-permute-start | bytes 135176 | tf_op jit(solution)/shard_map/ppermute | solution.py:140
  18.8 3.3 %collective-permute-start = (f32[2,16,128]{2,1,0:T(8,128)S(1)}, f32[2,16,128]{2,1,0:T(8,128)S(1)}, u32[]{:S(2)}, u32[]{:S(2)}) collective-permute-start(f32[2,16,128]{2,1,0:T(8,128)S(1)} %get-tuple-element.34), channel_id=1, source_target_pairs={{0,1},{1,0},{2,3},{3,2},{4,5},{5,4},{6,7},{7,6},{8,9},{9,8},{10,11... | collective-permute-start | bytes 49160 | tf_op jit(solution)/shard_map/ppermute | solution.py:140
  18.9 4.9 %collective-permute-start.3 = (f32[8,128]{1,0:T(8,128)S(1)}, f32[8,128]{1,0:T(8,128)S(1)}, u32[]{:S(2)}, u32[]{:S(2)}) collective-permute-start(f32[8,128]{1,0:T(8,128)S(1)} %get-tuple-element.40), channel_id=1, source_target_pairs={{0,8},{1,9},{2,10},{3,11},{4,12},{5,13},{6,14},{7,15},{8,0},{9,1},... | collective-permute-start | bytes 12296 | tf_op jit(solution)/shard_map/ppermute | solution.py:140
  23.8 4.5 %collective-permute-start.4 = (f32[168,128]{1,0:T(8,128)S(1)}, f32[168,128]{1,0:T(8,128)S(1)}, u32[]{:S(2)}, u32[]{:S(2)}) collective-permute-start(f32[168,128]{1,0:T(8,128)S(1)} %get-tuple-element.48), channel_id=1, source_target_pairs={{0,2},{1,3},{2,0},{3,1},{4,6},{5,7},{6,4},{7,5},{8,10},{9,11},{10,... | collective-permute-start | bytes 258056 | tf_op jit(solution)/shard_map/ppermute | solution.py:140
  24.8 2.4 %collective-permute-start.5 = (f32[64,128]{1,0:T(8,128)S(1)}, f32[64,128]{1,0:T(8,128)S(1)}, u32[]{:S(2)}, u32[]{:S(2)}) collective-permute-start(f32[64,128]{1,0:T(8,128)S(1)} %get-tuple-element.49), channel_id=1, source_target_pairs={{0,1},{1,0},{2,3},{3,2},{4,5},{5,4},{6,7},{7,6},{8,9},{9,8},{10,11... | collective-permute-start | bytes 98312 | tf_op jit(solution)/shard_map/ppermute | solution.py:140

commit v20 on v19

--- a/solution.py
+++ b/solution.py
@@ -688,6 +688,15 @@
         copies.append(copy)
 
     for group in range(2):
+        first = 0 if group == 0 else rows - 8
+        for k, i in enumerate(ENTER[1][group]):
+            n = group * 5 + k
+            step = int(STEP[i, 2])
+            tiles[n, 1 + step : 1 + step + depth] = tile_ref[n]
+            tiles[n, 1 : 1 + depth, 0 if group == 0 else 7, :] = entering(group, k)
+            low, high = max(step, 0), min(depth + step, depth)
+            leave(tiles.at[n, 1 + low : 1 + high], out_ref.at[i, low:high, first : first + 8])
+    for group in range(2):
         z = 0 if group == 0 else depth - 1
         for k, i in enumerate(ENTER[2][group]):
             value = entered_z(first_ref, second_ref, group, slice(k * rows, (k + 1) * rows))
@@ -706,15 +715,6 @@
             n = group * 5 + k
             planes[n] = value
             leave(planes.at[n], out_ref.at[i, z])
-    for group in range(2):
-        first = 0 if group == 0 else rows - 8
-        for k, i in enumerate(ENTER[1][group]):
-            n = group * 5 + k
-            step = int(STEP[i, 2])
-            tiles[n, 1 + step : 1 + step + depth] = tile_ref[n]
-            tiles[n, 1 : 1 + depth, 0 if group == 0 else 7, :] = entering(group, k)
-            low, high = max(step, 0), min(depth + step, depth)
-            leave(tiles.at[n, 1 + low : 1 + high], out_ref.at[i, low:high, first : first + 8])
 
     count = target_ref.shape[1]
     if len(drag_refs) == 2:

time: 29.7 us -> 29.6 us (level)
  no operation moved by 1% of the time
where the time goes in v20:
time: 29.6 us; the launch traced here: 29.4 us
  starting transfers between devices  12.7 us (43%)
  Pallas kernels  10.6 us (36%)
  waiting for transfers between devices  4.46 us (15%)
  local copies, waits for them, and re-layouts  0.91 us (3%)
  between operations  0.7 us (2%)
    all_to_all x1, starting transfers between devices, shards(): messages = swap(messages)  7.26 us
    ppermute x6, starting transfers between devices, send(): return lax.ppermute(value, ('slab', 'col', 'pair'), perm)  5.41 us
    all_to_all x1, waiting for transfers between devices, shards(): messages = swap(messages)  2.91 us
    pallas_call x1, Pallas kernels, moments(): pl.pallas_call(moments_kernel, out_shape=[jax.ShapeDtypeStruct((3 * width...  2.86 us
    pallas_call x1, Pallas kernels, stream_upper(): pl.pallas_call(upper_kernel, out_shape=[jax.ShapeDtypeStruct(pops.shape,...  2.35 us
    pallas_call x1, Pallas kernels, pack(): pl.pallas_call(functools.partial(pack_kernel, steps), out_shape=[jax.Shap...  1.86 us
    ppermute x6, waiting for transfers between devices, send(): return lax.ppermute(value, ('slab', 'col', 'pair'), perm)  1.54 us
    pallas_call x1, Pallas kernels, couple(): pl.pallas_call(functools.partial(couple_kernel, shape, len(drags)), out_s...  1.23 us
  transfers between devices with their start and end apart: 7, of which 3 were waited for; matrix products, arithmetic and copies ran while one was open for 0% of the time, Pallas kernels for 22%

profile of v20, /device:TPU:0, one launch (start us, length us, event | category | flops | bytes accessed | tf_op | source)
XLA Modules:
  0.0 29.4 jit_solution(4822352583386044911)
XLA Ops:
  0.6 0.0 copy-start
  0.6 1.9 %pack.1 = (s32[1,128]{1,0:T(1,128)}, f32[64,128]{1,0:T(8,128)}) custom-call(s32[1,128]{1,0:T(1,128)} %bitcast.3, s32[3,128]{1,0:T(4,128)} %refs_1_.2, f32[3,128]{1,0:T(4,128)} %refs_2_.2, f32[3,128]{1,0:T(4,128)} %refs_3_.1), custom_call_target="tpu_custom_call" | custom-call | tf_op jit(solution)/shard_map/pack/pallas_call | solution.py:251
  2.5 7.3 %all-to-all-start = ((f32[8,8,128]{2,1,0:T(8,128)}), f32[8,8,128]{2,1,0:T(8,128)S(1)}, u32[]{:S(2)}, u32[]{:S(2)}) async-start(f32[8,8,128]{2,1,0:T(8,128)} %bitcast.2), calls=%async_computation | async-start | bytes 65536 | tf_op jit(solution)/shard_map/all_to_all | solution.py:779
  9.8 0.9 %copy-done.1 = s32[16,16,128]{2,1,0:T(8,128)S(1)} copy-done((s32[16,16,128]{2,1,0:T(8,128)S(1)}, s32[16,16,128]{2,1,0:T(8,128)}, u32[]{:S(2)}) %copy-start.1) | copy-done | bytes 131096
  10.7 2.9 %moments.1 = (bf16[384,256]{1,0:T(8,128)(2,1)S(1)}, bf16[384,256]{1,0:T(8,128)(2,1)S(1)}, f32[20,16,128]{2,1,0:T(8,128)S(1)}, f32[19,2,16,128]{3,2,1,0:T(8,128)S(1)}, s32[2,16,128]{2,1,0:T(8,128)S(1)}) custom-call(f32[19,16,16,128]{3,2,1,0:T(8,128)} %pops_ref.5, s32[16,16,128]{2,1,0:T(8,128)S(1)} %copy-done.1), custom_call_target="tpu_custom_call" | custom-call | flops 3000000 | bytes 4000000 | tf_op jit(solution)/shard_map/moments/pallas_call | solution.py:306
  13.6 2.9 %all-to-all-done.beads_ref = f32[8,8,128]{2,1,0:T(8,128)S(1)} async-done(((f32[8,8,128]{2,1,0:T(8,128)}), f32[8,8,128]{2,1,0:T(8,128)S(1)}, u32[]{:S(2)}, u32[]{:S(2)}) %all-to-all-start) | async-done | bytes 32800 | tf_op jit(solution)/shard_map/all_to_all | solution.py:779
  16.5 0.0 copy-done
  16.5 1.2 %couple.1 = (f32[3,16,16,128]{3,2,1,0:T(8,128)S(1)}, f32[2,16,128]{2,1,0:T(8,128)S(1)}, f32[88,128]{1,0:T(8,128)S(1)}, f32[88,128]{1,0:T(8,128)S(1)}, f32[4,8,12...) custom-call(f32[8,8,128]{2,1,0:T(8,128)S(1)} %all-to-all-done.beads_ref, ...), custom_call_target="tpu_custom_call" | custom-call | tf_op jit(solution)/shard_map/couple/pallas_call | solution.py:440
  17.7 1.0 %collective-permute-start.1 = (f32[88,128]{1,0:T(8,128)S(1)}, f32[88,128]{1,0:T(8,128)S(1)}, u32[]{:S(2)}, u32[]{:S(2)}) collective-permute-start(f32[88,128]{1,0:T(8,128)S(1)} %get-tuple-element.37), channel_id=1, source_target_pairs={{0,12},{1,13},{2,14},{3,15},{4,8},{5,9},{6,10},{7,11},{8,4},{9,5},... | collective-permute-start | bytes 135176 | tf_op jit(solution)/shard_map/ppermute | solution.py:140
  18.7 0.1 collective-permute-start.2
  18.8 0.0 collective-permute-start
  18.9 3.3 %collective-permute-start.3 = (f32[8,128]{1,0:T(8,128)S(1)}, f32[8,128]{1,0:T(8,128)S(1)}, u32[]{:S(2)}, u32[]{:S(2)}) collective-permute-start(f32[8,128]{1,0:T(8,128)S(1)} %get-tuple-element.40), channel_id=1, source_target_pairs={{0,8},{1,9},{2,10},{3,11},{4,12},{5,13},{6,14},{7,15},{8,0},{9,1},... | collective-permute-start | bytes 12296 | tf_op jit(solution)/shard_map/ppermute | solution.py:140
  22.2 0.0 collective-permute-done.face_ref
  22.2 1.2 %lower.1 = (f32[19,8,16,128]{3,2,1,0:T(8,128)S(1)}, f32[160,128]{1,0:T(8,128)S(1)}, f32[8,128]{1,0:T(8,128)S(1)}) custom-call(f32[8,128]{1,0:T(8,128)S(1)} %get-tuple-element.30.before_ref, f32[19,16,16,128]{3,2,1,0:T(8,128)S(1)} %copy-done, s32[16,16,128]{2,1,0:T(8,128)S(1)} %copy-done.2, f32[3,16,16,128]{3,2,1,0:T(8,128)S(1)} %get-tuple-element.31.force_ref, ...), custom_call_target="tpu_custom_call" | custom-call | flops 3000000 | bytes 2000000 | tf_op jit(solution)/shard_map/lower/pallas_call | solution.py:614
  23.3 0.4 %collective-permute-done.3.refs_1_.refs_3_ = f32[8,128]{1,0:T(8,128)S(1)} collective-permute-done((f32[8,128]{1,0:T(8,128)S(1)}, f32[8,128]{1,0:T(8,128)S(1)}, u32[]{:S(2)}, u32[]{:S(2)}) %collective-permute-start.3) | collective-permute-done | bytes 4128 | tf_op jit(solution)/shard_map/ppermute | solution.py:140
  23.7 0.0 collective-permute-done.1.first_ref
  23.7 0.0 collective-permute-done.2.second_ref
  23.7 0.1 rows.1
  23.8 1.0 %collective-permute-start.4 = (f32[168,128]{1,0:T(8,128)S(1)}, f32[168,128]{1,0:T(8,128)S(1)}, u32[]{:S(2)}, u32[]{:S(2)}) collective-permute-start(f32[168,128]{1,0:T(8,128)S(1)} %get-tuple-element.48), channel_id=1, source_target_pairs={{0,2},{1,3},{2,0},{3,1},{4,6},{5,7},{6,4},{7,5},{8,10},{9,11},{10,... | collective-permute-start | bytes 258056 | tf_op jit(solution)/shard_map/ppermute | solution.py:140
  24.8 0.0 collective-permute-start.5
  24.8 2.4 %upper.1 = (f32[19,16,16,128]{3,2,1,0:T(8,128)}, f32[10,16,8,128]{3,2,1,0:T(8,128)S(1)}) custom-call(f32[8,128]{1,0:T(8,128)S(1)} %get-tuple-element.43.before_ref, f32[19,8,16,128]{3,2,1,0:T(8,128)S(1)} %get-tuple-element.44.lower_ref, f32[19,16,16,128]{3,2,1,0:T(8,128)S(1)} %copy-done, s32[16,16,128]{2,1,0:T(8,128)S(1)} %copy-done.2, ...), custom_call_target="tpu_custom_call" | custom-call | flops 5000000 | bytes 3000000 | tf_op jit(solution)/shard_map/upper/pallas_call | solution.py:632
  27.2 0.0 collective-permute-done.5.refs_1_
  27.2 1.1 %collective-permute-done.4.refs_0_ = f32[168,128]{1,0:T(8,128)S(1)} collective-permute-done((f32[168,128]{1,0:T(8,128)S(1)}, f32[168,128]{1,0:T(8,128)S(1)}, u32[]{:S(2)}, u32[]{:S(2)}) %collective-permute-start.4) | collective-permute-done | bytes 86048 | tf_op jit(solution)/shard_map/ppermute | solution.py:140
  28.3 1.1 %finish.1 = (f32[19,16,16,128]{3,2,1,0:T(8,128)}, f32[3,128]{1,0:T(4,128)}) custom-call(f32[19,16,16,128]{3,2,1,0:T(8,128)} %get-tuple-element.45.whole_ref, bf16[256,128]{1,0:T(8,128)(2,1)S(1)} %get-tuple-element.46.target_ref, f32[10,16,8,128]{3,2,1,0:T(8,128)S(1)} %get-tuple-element.47.tile_ref, ...), custom_call_target="tpu_custom_call", output_to_operand_aliasing={{0}: (0, {})} | custom-call | tf_op jit(solution)/shard_map/finish/pallas_call | solution.py:749
  (6 shorter events, 0.0 us)
Async XLA Ops:
  0.6 15.8 %copy-start = (f32[19,16,16,128]{3,2,1,0:T(8,128)S(1)}, f32[19,16,16,128]{3,2,1,0:T(8,128)}, u32[]{:S(2)}) copy-start(f32[19,16,16,128]{3,2,1,0:T(8,128)} %pops_ref.5) | copy-start | bytes 7471108
  2.5 14.0 %all-to-all-start = ((f32[8,8,128]{2,1,0:T(8,128)}), f32[8,8,128]{2,1,0:T(8,128)S(1)}, u32[]{:S(2)}, u32[]{:S(2)}) async-start(f32[8,8,128]{2,1,0:T(8,128)} %bitcast.2), calls=%async_computation | async-start | bytes 65536 | tf_op jit(solution)/shard_map/all_to_all | solution.py:779
  9.8 0.9 %copy-start.1 = (s32[16,16,128]{2,1,0:T(8,128)S(1)}, s32[16,16,128]{2,1,0:T(8,128)}, u32[]{:S(2)}) copy-start(s32[16,16,128]{2,1,0:T(8,128)} %solid_ref.5) | copy-start | bytes 393220
  10.7 5.8 %copy-start.2 = (s32[16,16,128]{2,1,0:T(8,128)S(1)}, s32[16,16,128]{2,1,0:T(8,128)}, u32[]{:S(2)}) copy-start(s32[16,16,128]{2,1,0:T(8,128)} %solid_ref.5) | copy-start | bytes 393220
  17.7 7.1 %copy-start.3 = (s32[1,128]{1,0:T(1,128)S(1)}, s32[1,128]{1,0:T(1,128)}, u32[]{:S(2)}) copy-start(s32[1,128]{1,0:T(1,128)} %get-tuple-element.42.target_ref) | copy-start | bytes 1540
  17.7 6.0 %collective-permute-start.1 = (f32[88,128]{1,0:T(8,128)S(1)}, f32[88,128]{1,0:T(8,128)S(1)}, u32[]{:S(2)}, u32[]{:S(2)}) collective-permute-start(f32[88,128]{1,0:T(8,128)S(1)} %get-tuple-element.37), channel_id=1, source_target_pairs={{0,12},{1,13},{2,14},{3,15},{4,8},{5,9},{6,10},{7,11},{8,4},{9,5},... | collective-permute-start | bytes 135176 | tf_op jit(solution)/shard_map/ppermute | solution.py:140
  18.7 5.0 %collective-permute-start.2 = (f32[88,128]{1,0:T(8,128)S(1)}, f32[88,128]{1,0:T(8,128)S(1)}, u32[]{:S(2)}, u32[]{:S(2)}) collective-permute-start(f32[88,128]{1,0:T(8,128)S(1)} %get-tuple-element.38), channel_id=1, source_target_pairs={{0,4},{1,5},{2,6},{3,7},{4,0},{5,1},{6,2},{7,3},{8,12},{9,13},{10,... | collective-permute-start | bytes 135176 | tf_op jit(solution)/shard_map/ppermute | solution.py:140
  18.8 3.3 %collective-permute-start = (f32[2,16,128]{2,1,0:T(8,128)S(1)}, f32[2,16,128]{2,1,0:T(8,128)S(1)}, u32[]{:S(2)}, u32[]{:S(2)}) collective-permute-start(f32[2,16,128]{2,1,0:T(8,128)S(1)} %get-tuple-element.34), channel_id=1, source_target_pairs={{0,1},{1,0},{2,3},{3,2},{4,5},{5,4},{6,7},{7,6},{8,9},{9,8},{10,11... | collective-permute-start | bytes 49160 | tf_op jit(solution)/shard_map/ppermute | solution.py:140
  18.9 4.9 %collective-permute-start.3 = (f32[8,128]{1,0:T(8,128)S(1)}, f32[8,128]{1,0:T(8,128)S(1)}, u32[]{:S(2)}, u32[]{:S(2)}) collective-permute-start(f32[8,128]{1,0:T(8,128)S(1)} %get-tuple-element.40), channel_id=1, source_target_pairs={{0,8},{1,9},{2,10},{3,11},{4,12},{5,13},{6,14},{7,15},{8,0},{9,1},... | collective-permute-start | bytes 12296 | tf_op jit(solution)/shard_map/ppermute | solution.py:140
  23.8 4.5 %collective-permute-start.4 = (f32[168,128]{1,0:T(8,128)S(1)}, f32[168,128]{1,0:T(8,128)S(1)}, u32[]{:S(2)}, u32[]{:S(2)}) collective-permute-start(f32[168,128]{1,0:T(8,128)S(1)} %get-tuple-element.48), channel_id=1, source_target_pairs={{0,2},{1,3},{2,0},{3,1},{4,6},{5,7},{6,4},{7,5},{8,10},{9,11},{10,... | collective-permute-start | bytes 258056 | tf_op jit(solution)/shard_map/ppermute | solution.py:140
  24.8 2.4 %collective-permute-start.5 = (f32[64,128]{1,0:T(8,128)S(1)}, f32[64,128]{1,0:T(8,128)S(1)}, u32[]{:S(2)}, u32[]{:S(2)}) collective-permute-start(f32[64,128]{1,0:T(8,128)S(1)} %get-tuple-element.49), channel_id=1, source_target_pairs={{0,1},{1,0},{2,3},{3,2},{4,5},{5,4},{6,7},{7,6},{8,9},{9,8},{10,11... | collective-permute-start | bytes 98312 | tf_op jit(solution)/shard_map/ppermute | solution.py:140

commit v21 on v19

--- a/solution.py
+++ b/solution.py
@@ -193,7 +193,9 @@
     sources, (target_ref, out_ref, table, *held) = refs[:4], refs[4:]
     copies = []
     if steps == 1:
-        *held, sem = held
+        *held, slots, tiles, sem = held
+        outputs = (target_ref, out_ref)
+        target_ref, out_ref = slots, tiles
         for k, (source, place) in enumerate(zip(sources, held)):
             copies.append(pltpu.make_async_copy(source, place, sem.at[k]))
             copies[-1].start()
@@ -211,6 +213,8 @@
 
     if steps == 1:
         target_ref[...] = whole_target
+        leaving = [pltpu.make_async_copy(target_ref, outputs[0], sem.at[4])]
+        leaving[0].start()
     else:
         known = jnp.where(step == 0, -1, target_ref[...])
         target_ref[...] = jnp.maximum(known, whole_target)
@@ -229,6 +233,15 @@
         out_ref[r * 8 : r * 8 + 8] = jnp.concatenate(
             [packed[0:8, lanes], packed[8:16, lanes], packed[16:24, lanes], blank], axis=1
         )
+        if steps == 1 and r % 4 == 3:
+            part = slice((r - 3) * 8, (r + 1) * 8)
+            leaving.append(
+                pltpu.make_async_copy(out_ref.at[part], outputs[1].at[part], sem.at[5 + r // 4])
+            )
+            leaving[-1].start()
+    if steps == 1:
+        for copy in leaving:
+            copy.wait()
 
 
 def pack(owners, owner, base, offset, velocity):
@@ -236,8 +249,11 @@
     args = (owner.reshape(1, count), base, offset, velocity)
     scratch = [pltpu.VMEM((24, count), F32)]
     if steps == 1:
-        blocks = dict(in_specs=[pl.BlockSpec(memory_space=pl.ANY)] * 4)
-        scratch += [pltpu.VMEM(a.shape, a.dtype) for a in args] + [pltpu.SemaphoreType.DMA((4,))]
+        far = pl.BlockSpec(memory_space=pl.ANY)
+        blocks = dict(in_specs=[far] * 4, out_specs=[far] * 2)
+        scratch += [pltpu.VMEM(a.shape, a.dtype) for a in args]
+        scratch += [pltpu.VMEM((1, count), jnp.int32), pltpu.VMEM((owners * 8, 128), F32)]
+        scratch += [pltpu.SemaphoreType.DMA((7,))]
     else:
         blocks = dict(
             grid=(steps,),

time: 29.7 us -> 29.7 us (level)
  no operation moved by 1% of the time
where the time goes in v21:
time: 29.7 us; the launch traced here: 29.4 us
  starting transfers between devices  12.7 us (43%)
  Pallas kernels  10.7 us (36%)
  waiting for transfers between devices  4.45 us (15%)
  local copies, waits for them, and re-layouts  0.91 us (3%)
  between operations  0.7 us (2%)
    all_to_all x1, starting transfers between devices, shards(): messages = swap(messages)  7.26 us
    ppermute x6, starting transfers between devices, send(): return lax.ppermute(value, ('slab', 'col', 'pair'), perm)  5.41 us
    all_to_all x1, waiting for transfers between devices, shards(): messages = swap(messages)  2.91 us
    pallas_call x1, Pallas kernels, moments(): pl.pallas_call(moments_kernel, out_shape=[jax.ShapeDtypeStruct((3 * width...  2.86 us
    pallas_call x1, Pallas kernels, stream_upper(): pl.pallas_call(upper_kernel, out_shape=[jax.ShapeDtypeStruct(pops.shape,...  2.35 us
    pallas_call x1, Pallas kernels, pack(): pl.pallas_call(functools.partial(pack_kernel, steps), out_shape=[jax.Shap...  1.88 us
    ppermute x6, waiting for transfers between devices, send(): return lax.ppermute(value, ('slab', 'col', 'pair'), perm)  1.54 us
    pallas_call x1, Pallas kernels, couple(): pl.pallas_call(functools.partial(couple_kernel, shape, len(drags)), out_s...  1.23 us
  transfers between devices with their start and end apart: 7, of which 3 were waited for; matrix products, arithmetic and copies ran while one was open for 0% of the time, Pallas kernels for 22%

profile of v21, /device:TPU:0, one launch (start us, length us, event | category | flops | bytes accessed | tf_op | source)
XLA Modules:
  0.0 29.4 jit_solution(15515993452725532756)
XLA Ops:
  0.6 0.0 copy-start
  0.6 1.9 %pack.1 = (s32[1,128]{1,0:T(1,128)}, f32[64,128]{1,0:T(8,128)}) custom-call(s32[1,128]{1,0:T(1,128)} %bitcast.3, s32[3,128]{1,0:T(4,128)} %refs_1_.2, f32[3,128]{1,0:T(4,128)} %refs_2_.2, f32[3,128]{1,0:T(4,128)} %refs_3_.1), custom_call_target="tpu_custom_call" | custom-call | tf_op jit(solution)/shard_map/pack/pallas_call | solution.py:267
  2.5 7.3 %all-to-all-start = ((f32[8,8,128]{2,1,0:T(8,128)}), f32[8,8,128]{2,1,0:T(8,128)S(1)}, u32[]{:S(2)}, u32[]{:S(2)}) async-start(f32[8,8,128]{2,1,0:T(8,128)} %bitcast.2), calls=%async_computation | async-start | bytes 65536 | tf_op jit(solution)/shard_map/all_to_all | solution.py:795
  9.8 0.9 %copy-done.1 = s32[16,16,128]{2,1,0:T(8,128)S(1)} copy-done((s32[16,16,128]{2,1,0:T(8,128)S(1)}, s32[16,16,128]{2,1,0:T(8,128)}, u32[]{:S(2)}) %copy-start.1) | copy-done | bytes 131096
  10.7 2.9 %moments.1 = (bf16[384,256]{1,0:T(8,128)(2,1)S(1)}, bf16[384,256]{1,0:T(8,128)(2,1)S(1)}, f32[20,16,128]{2,1,0:T(8,128)S(1)}, f32[19,2,16,128]{3,2,1,0:T(8,128)S(1)}, s32[2,16,128]{2,1,0:T(8,128)S(1)}) custom-call(f32[19,16,16,128]{3,2,1,0:T(8,128)} %pops_ref.5, s32[16,16,128]{2,1,0:T(8,128)S(1)} %copy-done.1), custom_call_target="tpu_custom_call" | custom-call | flops 3000000 | bytes 4000000 | tf_op jit(solution)/shard_map/moments/pallas_call | solution.py:322
  13.6 2.9 %all-to-all-done.beads_ref = f32[8,8,128]{2,1,0:T(8,128)S(1)} async-done(((f32[8,8,128]{2,1,0:T(8,128)}), f32[8,8,128]{2,1,0:T(8,128)S(1)}, u32[]{:S(2)}, u32[]{:S(2)}) %all-to-all-start) | async-done | bytes 32800 | tf_op jit(solution)/shard_map/all_to_all | solution.py:795
  16.5 1.2 %couple.1 = (f32[3,16,16,128]{3,2,1,0:T(8,128)S(1)}, f32[2,16,128]{2,1,0:T(8,128)S(1)}, f32[88,128]{1,0:T(8,128)S(1)}, f32[88,128]{1,0:T(8,128)S(1)}, f32[4,8,12...) custom-call(f32[8,8,128]{2,1,0:T(8,128)S(1)} %all-to-all-done.beads_ref, ...), custom_call_target="tpu_custom_call" | custom-call | tf_op jit(solution)/shard_map/couple/pallas_call | solution.py:456
  17.7 1.0 %collective-permute-start.1 = (f32[88,128]{1,0:T(8,128)S(1)}, f32[88,128]{1,0:T(8,128)S(1)}, u32[]{:S(2)}, u32[]{:S(2)}) collective-permute-start(f32[88,128]{1,0:T(8,128)S(1)} %get-tuple-element.37), channel_id=1, source_target_pairs={{0,12},{1,13},{2,14},{3,15},{4,8},{5,9},{6,10},{7,11},{8,4},{9,5},... | collective-permute-start | bytes 135176 | tf_op jit(solution)/shard_map/ppermute | solution.py:140
  18.7 0.1 collective-permute-start.2
  18.9 0.0 collective-permute-start
  18.9 3.3 %collective-permute-start.3 = (f32[8,128]{1,0:T(8,128)S(1)}, f32[8,128]{1,0:T(8,128)S(1)}, u32[]{:S(2)}, u32[]{:S(2)}) collective-permute-start(f32[8,128]{1,0:T(8,128)S(1)} %get-tuple-element.40), channel_id=1, source_target_pairs={{0,8},{1,9},{2,10},{3,11},{4,12},{5,13},{6,14},{7,15},{8,0},{9,1},... | collective-permute-start | bytes 12296 | tf_op jit(solution)/shard_map/ppermute | solution.py:140
  22.2 0.0 collective-permute-done.face_ref
  22.2 1.2 %lower.1 = (f32[19,8,16,128]{3,2,1,0:T(8,128)S(1)}, f32[160,128]{1,0:T(8,128)S(1)}, f32[8,128]{1,0:T(8,128)S(1)}) custom-call(f32[8,128]{1,0:T(8,128)S(1)} %get-tuple-element.30.before_ref, f32[19,16,16,128]{3,2,1,0:T(8,128)S(1)} %copy-done, s32[16,16,128]{2,1,0:T(8,128)S(1)} %copy-done.2, f32[3,16,16,128]{3,2,1,0:T(8,128)S(1)} %get-tuple-element.31.force_ref, ...), custom_call_target="tpu_custom_call" | custom-call | flops 3000000 | bytes 2000000 | tf_op jit(solution)/shard_map/lower/pallas_call | solution.py:630
  23.4 0.4 %collective-permute-done.3.refs_1_.refs_3_ = f32[8,128]{1,0:T(8,128)S(1)} collective-permute-done((f32[8,128]{1,0:T(8,128)S(1)}, f32[8,128]{1,0:T(8,128)S(1)}, u32[]{:S(2)}, u32[]{:S(2)}) %collective-permute-start.3) | collective-permute-done | bytes 4128 | tf_op jit(solution)/shard_map/ppermute | solution.py:140
  23.8 0.0 collective-permute-done.1.first_ref
  23.8 0.0 collective-permute-done.2.second_ref
  23.8 0.1 rows.1
  23.8 1.0 %collective-permute-start.4 = (f32[168,128]{1,0:T(8,128)S(1)}, f32[168,128]{1,0:T(8,128)S(1)}, u32[]{:S(2)}, u32[]{:S(2)}) collective-permute-start(f32[168,128]{1,0:T(8,128)S(1)} %get-tuple-element.48), channel_id=1, source_target_pairs={{0,2},{1,3},{2,0},{3,1},{4,6},{5,7},{6,4},{7,5},{8,10},{9,11},{10,... | collective-permute-start | bytes 258056 | tf_op jit(solution)/shard_map/ppermute | solution.py:140
  24.8 0.0 collective-permute-start.5
  24.8 0.0 copy-done.3
  24.8 2.4 %upper.1 = (f32[19,16,16,128]{3,2,1,0:T(8,128)}, f32[10,16,8,128]{3,2,1,0:T(8,128)S(1)}) custom-call(f32[8,128]{1,0:T(8,128)S(1)} %get-tuple-element.43.before_ref, f32[19,8,16,128]{3,2,1,0:T(8,128)S(1)} %get-tuple-element.44.lower_ref, f32[19,16,16,128]{3,2,1,0:T(8,128)S(1)} %copy-done, s32[16,16,128]{2,1,0:T(8,128)S(1)} %copy-done.2, ...), custom_call_target="tpu_custom_call" | custom-call | flops 5000000 | bytes 3000000 | tf_op jit(solution)/shard_map/upper/pallas_call | solution.py:648
  27.2 0.0 collective-permute-done.5.refs_1_
  27.2 1.1 %collective-permute-done.4.refs_0_ = f32[168,128]{1,0:T(8,128)S(1)} collective-permute-done((f32[168,128]{1,0:T(8,128)S(1)}, f32[168,128]{1,0:T(8,128)S(1)}, u32[]{:S(2)}, u32[]{:S(2)}) %collective-permute-start.4) | collective-permute-done | bytes 86048 | tf_op jit(solution)/shard_map/ppermute | solution.py:140
  28.3 1.1 %finish.1 = (f32[19,16,16,128]{3,2,1,0:T(8,128)}, f32[3,128]{1,0:T(4,128)}) custom-call(f32[19,16,16,128]{3,2,1,0:T(8,128)} %get-tuple-element.45.whole_ref, bf16[256,128]{1,0:T(8,128)(2,1)S(1)} %get-tuple-element.46.target_ref, f32[10,16,8,128]{3,2,1,0:T(8,128)S(1)} %get-tuple-element.47.tile_ref, ...), custom_call_target="tpu_custom_call", output_to_operand_aliasing={{0}: (0, {})} | custom-call | tf_op jit(solution)/shard_map/finish/pallas_call | solution.py:765
  (6 shorter events, 0.0 us)
Async XLA Ops:
  0.6 15.9 %copy-start = (f32[19,16,16,128]{3,2,1,0:T(8,128)S(1)}, f32[19,16,16,128]{3,2,1,0:T(8,128)}, u32[]{:S(2)}) copy-start(f32[19,16,16,128]{3,2,1,0:T(8,128)} %pops_ref.5) | copy-start | bytes 7471108
  2.5 14.0 %all-to-all-start = ((f32[8,8,128]{2,1,0:T(8,128)}), f32[8,8,128]{2,1,0:T(8,128)S(1)}, u32[]{:S(2)}, u32[]{:S(2)}) async-start(f32[8,8,128]{2,1,0:T(8,128)} %bitcast.2), calls=%async_computation | async-start | bytes 65536 | tf_op jit(solution)/shard_map/all_to_all | solution.py:795
  9.8 0.9 %copy-start.1 = (s32[16,16,128]{2,1,0:T(8,128)S(1)}, s32[16,16,128]{2,1,0:T(8,128)}, u32[]{:S(2)}) copy-start(s32[16,16,128]{2,1,0:T(8,128)} %solid_ref.5) | copy-start | bytes 393220
  10.7 5.8 %copy-start.2 = (s32[16,16,128]{2,1,0:T(8,128)S(1)}, s32[16,16,128]{2,1,0:T(8,128)}, u32[]{:S(2)}) copy-start(s32[16,16,128]{2,1,0:T(8,128)} %solid_ref.5) | copy-start | bytes 393220
  17.7 7.1 %copy-start.3 = (s32[1,128]{1,0:T(1,128)S(1)}, s32[1,128]{1,0:T(1,128)}, u32[]{:S(2)}) copy-start(s32[1,128]{1,0:T(1,128)} %get-tuple-element.42.target_ref) | copy-start | bytes 1540
  17.7 6.0 %collective-permute-start.1 = (f32[88,128]{1,0:T(8,128)S(1)}, f32[88,128]{1,0:T(8,128)S(1)}, u32[]{:S(2)}, u32[]{:S(2)}) collective-permute-start(f32[88,128]{1,0:T(8,128)S(1)} %get-tuple-element.37), channel_id=1, source_target_pairs={{0,12},{1,13},{2,14},{3,15},{4,8},{5,9},{6,10},{7,11},{8,4},{9,5},... | collective-permute-start | bytes 135176 | tf_op jit(solution)/shard_map/ppermute | solution.py:140
  18.7 5.0 %collective-permute-start.2 = (f32[88,128]{1,0:T(8,128)S(1)}, f32[88,128]{1,0:T(8,128)S(1)}, u32[]{:S(2)}, u32[]{:S(2)}) collective-permute-start(f32[88,128]{1,0:T(8,128)S(1)} %get-tuple-element.38), channel_id=1, source_target_pairs={{0,4},{1,5},{2,6},{3,7},{4,0},{5,1},{6,2},{7,3},{8,12},{9,13},{10,... | collective-permute-start | bytes 135176 | tf_op jit(solution)/shard_map/ppermute | solution.py:140
  18.9 3.3 %collective-permute-start = (f32[2,16,128]{2,1,0:T(8,128)S(1)}, f32[2,16,128]{2,1,0:T(8,128)S(1)}, u32[]{:S(2)}, u32[]{:S(2)}) collective-permute-start(f32[2,16,128]{2,1,0:T(8,128)S(1)} %get-tuple-element.34), channel_id=1, source_target_pairs={{0,1},{1,0},{2,3},{3,2},{4,5},{5,4},{6,7},{7,6},{8,9},{9,8},{10,11... | collective-permute-start | bytes 49160 | tf_op jit(solution)/shard_map/ppermute | solution.py:140
  18.9 4.9 %collective-permute-start.3 = (f32[8,128]{1,0:T(8,128)S(1)}, f32[8,128]{1,0:T(8,128)S(1)}, u32[]{:S(2)}, u32[]{:S(2)}) collective-permute-start(f32[8,128]{1,0:T(8,128)S(1)} %get-tuple-element.40), channel_id=1, source_target_pairs={{0,8},{1,9},{2,10},{3,11},{4,12},{5,13},{6,14},{7,15},{8,0},{9,1},... | collective-permute-start | bytes 12296 | tf_op jit(solution)/shard_map/ppermute | solution.py:140
  23.8 4.5 %collective-permute-start.4 = (f32[168,128]{1,0:T(8,128)S(1)}, f32[168,128]{1,0:T(8,128)S(1)}, u32[]{:S(2)}, u32[]{:S(2)}) collective-permute-start(f32[168,128]{1,0:T(8,128)S(1)} %get-tuple-element.48), channel_id=1, source_target_pairs={{0,2},{1,3},{2,0},{3,1},{4,6},{5,7},{6,4},{7,5},{8,10},{9,11},{10,... | collective-permute-start | bytes 258056 | tf_op jit(solution)/shard_map/ppermute | solution.py:140
  24.8 2.4 %collective-permute-start.5 = (f32[64,128]{1,0:T(8,128)S(1)}, f32[64,128]{1,0:T(8,128)S(1)}, u32[]{:S(2)}, u32[]{:S(2)}) collective-permute-start(f32[64,128]{1,0:T(8,128)S(1)} %get-tuple-element.49), channel_id=1, source_target_pairs={{0,1},{1,0},{2,3},{3,2},{4,5},{5,4},{6,7},{7,6},{8,9},{9,8},{10,11... | collective-permute-start | bytes 98312 | tf_op jit(solution)/shard_map/ppermute | solution.py:140

commit v22 on v19

--- a/solution.py
+++ b/solution.py
@@ -621,7 +621,7 @@
         in_specs=[pl.BlockSpec(memory_space=pl.ANY)] + [vmem] * 6,
         scratch_shapes=[pltpu.VMEM((2, 128, rows), F32)],
         compiler_params=pltpu.CompilerParams(vmem_limit_bytes=ROOM),
-        cost_estimate=pl.CostEstimate(flops=3000000, bytes_accessed=2000000, transcendentals=0),
+        cost_estimate=pl.CostEstimate(flops=5000000000, bytes_accessed=1000000000, transcendentals=0),
         name="lower",
     )(before, pops, solid, force, sides, walls, face)
 

time: 29.7 us -> 30.7 us (1.034)
  waiting for transfers between devices: 4.46 us -> 6.39 us
  starting transfers between devices: 12.7 us -> 11.8 us
    ppermute x6, waiting for transfers between devices: 1.54 us -> 3.48 us  [send(): return lax.ppermute(value, ('slab', 'col', 'pair'), perm)]
    ppermute x6, starting transfers between devices: 5.41 us -> 4.53 us  [send(): return lax.ppermute(value, ('slab', 'col', 'pair'), perm)]
  transfers between devices with their start and end apart: 7 -> 7, of which waited for: 3 -> 4; matrix products, arithmetic and copies ran while one was open for 0% -> 0% of each run, Pallas kernels for 22% -> 21%
where the time goes in v22:
time: 30.7 us; the launch traced here: 30.5 us
  starting transfers between devices  11.8 us (38%)
  Pallas kernels  10.7 us (35%)
  waiting for transfers between devices  6.39 us (21%)
  local copies, waits for them, and re-layouts  0.91 us (3%)
  between operations  0.71 us (2%)
    all_to_all x1, starting transfers between devices, shards(): messages = swap(messages)  7.26 us
    ppermute x6, starting transfers between devices, send(): return lax.ppermute(value, ('slab', 'col', 'pair'), perm)  4.53 us
    ppermute x6, waiting for transfers between devices, send(): return lax.ppermute(value, ('slab', 'col', 'pair'), perm)  3.48 us
    all_to_all x1, waiting for transfers between devices, shards(): messages = swap(messages)  2.91 us
    pallas_call x1, Pallas kernels, moments(): pl.pallas_call(moments_kernel, out_shape=[jax.ShapeDtypeStruct((3 * width...  2.86 us
    pallas_call x1, Pallas kernels, stream_upper(): pl.pallas_call(upper_kernel, out_shape=[jax.ShapeDtypeStruct(pops.shape,...  2.35 us
    pallas_call x1, Pallas kernels, pack(): pl.pallas_call(functools.partial(pack_kernel, steps), out_shape=[jax.Shap...  1.86 us
    pallas_call x1, Pallas kernels, couple(): pl.pallas_call(functools.partial(couple_kernel, shape, len(drags)), out_s...  1.23 us
  transfers between devices with their start and end apart: 7, of which 4 were waited for; matrix products, arithmetic and copies ran while one was open for 0% of the time, Pallas kernels for 21%

profile of v22, /device:TPU:0, one launch (start us, length us, event | category | flops | bytes accessed | tf_op | source)
XLA Modules:
  0.0 30.5 jit_solution(3874341645232086293)
XLA Ops:
  0.6 0.0 copy-start
  0.6 1.9 %pack.1 = (s32[1,128]{1,0:T(1,128)}, f32[64,128]{1,0:T(8,128)}) custom-call(s32[1,128]{1,0:T(1,128)} %bitcast.3, s32[3,128]{1,0:T(4,128)} %refs_1_.2, f32[3,128]{1,0:T(4,128)} %refs_2_.2, f32[3,128]{1,0:T(4,128)} %refs_3_.1), custom_call_target="tpu_custom_call" | custom-call | tf_op jit(solution)/shard_map/pack/pallas_call | solution.py:251
  2.5 7.3 %all-to-all-start = ((f32[8,8,128]{2,1,0:T(8,128)}), f32[8,8,128]{2,1,0:T(8,128)S(1)}, u32[]{:S(2)}, u32[]{:S(2)}) async-start(f32[8,8,128]{2,1,0:T(8,128)} %bitcast.2), calls=%async_computation | async-start | bytes 65536 | tf_op jit(solution)/shard_map/all_to_all | solution.py:779
  9.8 0.9 %copy-done.1 = s32[16,16,128]{2,1,0:T(8,128)S(1)} copy-done((s32[16,16,128]{2,1,0:T(8,128)S(1)}, s32[16,16,128]{2,1,0:T(8,128)}, u32[]{:S(2)}) %copy-start.1) | copy-done | bytes 131096
  10.7 2.9 %moments.1 = (bf16[384,256]{1,0:T(8,128)(2,1)S(1)}, bf16[384,256]{1,0:T(8,128)(2,1)S(1)}, f32[20,16,128]{2,1,0:T(8,128)S(1)}, f32[19,2,16,128]{3,2,1,0:T(8,128)S(1)}, s32[2,16,128]{2,1,0:T(8,128)S(1)}) custom-call(f32[19,16,16,128]{3,2,1,0:T(8,128)} %pops_ref.5, s32[16,16,128]{2,1,0:T(8,128)S(1)} %copy-done.1), custom_call_target="tpu_custom_call" | custom-call | flops 3000000 | bytes 4000000 | tf_op jit(solution)/shard_map/moments/pallas_call | solution.py:306
  13.6 2.9 %all-to-all-done.beads_ref = f32[8,8,128]{2,1,0:T(8,128)S(1)} async-done(((f32[8,8,128]{2,1,0:T(8,128)}), f32[8,8,128]{2,1,0:T(8,128)S(1)}, u32[]{:S(2)}, u32[]{:S(2)}) %all-to-all-start) | async-done | bytes 32800 | tf_op jit(solution)/shard_map/all_to_all | solution.py:779
  16.5 0.0 copy-done
  16.5 1.2 %couple.1 = (f32[3,16,16,128]{3,2,1,0:T(8,128)S(1)}, f32[2,16,128]{2,1,0:T(8,128)S(1)}, f32[88,128]{1,0:T(8,128)S(1)}, f32[88,128]{1,0:T(8,128)S(1)}, f32[4,8,12...) custom-call(f32[8,8,128]{2,1,0:T(8,128)S(1)} %all-to-all-done.beads_ref, ...), custom_call_target="tpu_custom_call" | custom-call | tf_op jit(solution)/shard_map/couple/pallas_call | solution.py:440
  17.7 0.0 collective-permute-start
  17.7 0.6 %collective-permute-start.3 = (f32[8,128]{1,0:T(8,128)S(1)}, f32[8,128]{1,0:T(8,128)S(1)}, u32[]{:S(2)}, u32[]{:S(2)}) collective-permute-start(f32[8,128]{1,0:T(8,128)S(1)} %get-tuple-element.40), channel_id=1, source_target_pairs={{0,8},{1,9},{2,10},{3,11},{4,12},{5,13},{6,14},{7,15},{8,0},{9,1},... | collective-permute-start | bytes 12296 | tf_op jit(solution)/shard_map/ppermute | solution.py:140
  18.3 2.2 %collective-permute-start.1 = (f32[88,128]{1,0:T(8,128)S(1)}, f32[88,128]{1,0:T(8,128)S(1)}, u32[]{:S(2)}, u32[]{:S(2)}) collective-permute-start(f32[88,128]{1,0:T(8,128)S(1)} %get-tuple-element.37), channel_id=1, source_target_pairs={{0,12},{1,13},{2,14},{3,15},{4,8},{5,9},{6,10},{7,11},{8,4},{9,5},... | collective-permute-start | bytes 135176 | tf_op jit(solution)/shard_map/ppermute | solution.py:140
  20.5 0.7 %collective-permute-start.2 = (f32[88,128]{1,0:T(8,128)S(1)}, f32[88,128]{1,0:T(8,128)S(1)}, u32[]{:S(2)}, u32[]{:S(2)}) collective-permute-start(f32[88,128]{1,0:T(8,128)S(1)} %get-tuple-element.38), channel_id=1, source_target_pairs={{0,4},{1,5},{2,6},{3,7},{4,0},{5,1},{6,2},{7,3},{8,12},{9,13},{10,... | collective-permute-start | bytes 135176 | tf_op jit(solution)/shard_map/ppermute | solution.py:140
  21.3 0.0 collective-permute-done.face_ref
  21.3 1.2 %lower.1 = (f32[19,8,16,128]{3,2,1,0:T(8,128)S(1)}, f32[160,128]{1,0:T(8,128)S(1)}, f32[8,128]{1,0:T(8,128)S(1)}) custom-call(f32[8,128]{1,0:T(8,128)S(1)} %get-tuple-element.30.before_ref, f32[19,16,16,128]{3,2,1,0:T(8,128)S(1)} %copy-done, s32[16,16,128]{2,1,0:T(8,128)S(1)} %copy-done.2, f32[3,16,16,128]{3,2,1,0:T(8,128)S(1)} %get-tuple-element.31.force_ref, ...), custom_call_target="tpu_custom_call" | custom-call | flops 5000000000 | bytes 1000000000 | tf_op jit(solution)/shard_map/lower/pallas_call | solution.py:614
  22.5 0.0 collective-permute-done.3.refs_1_.refs_3_
  22.5 1.9 %collective-permute-done.1.first_ref = f32[88,128]{1,0:T(8,128)S(1)} collective-permute-done((f32[88,128]{1,0:T(8,128)S(1)}, f32[88,128]{1,0:T(8,128)S(1)}, u32[]{:S(2)}, u32[]{:S(2)}) %collective-permute-start.1) | collective-permute-done | bytes 45088 | tf_op jit(solution)/shard_map/ppermute | solution.py:140
  24.3 0.5 %collective-permute-done.2.second_ref = f32[88,128]{1,0:T(8,128)S(1)} collective-permute-done((f32[88,128]{1,0:T(8,128)S(1)}, f32[88,128]{1,0:T(8,128)S(1)}, u32[]{:S(2)}, u32[]{:S(2)}) %collective-permute-start.2) | collective-permute-done | bytes 45088 | tf_op jit(solution)/shard_map/ppermute | solution.py:140
  24.8 0.1 rows.1
  24.9 0.9 %collective-permute-start.4 = (f32[168,128]{1,0:T(8,128)S(1)}, f32[168,128]{1,0:T(8,128)S(1)}, u32[]{:S(2)}, u32[]{:S(2)}) collective-permute-start(f32[168,128]{1,0:T(8,128)S(1)} %get-tuple-element.48), channel_id=1, source_target_pairs={{0,2},{1,3},{2,0},{3,1},{4,6},{5,7},{6,4},{7,5},{8,10},{9,11},{10,... | collective-permute-start | bytes 258056 | tf_op jit(solution)/shard_map/ppermute | solution.py:140
  25.8 0.0 collective-permute-start.5
  25.9 2.3 %upper.1 = (f32[19,16,16,128]{3,2,1,0:T(8,128)}, f32[10,16,8,128]{3,2,1,0:T(8,128)S(1)}) custom-call(f32[8,128]{1,0:T(8,128)S(1)} %get-tuple-element.43.before_ref, f32[19,8,16,128]{3,2,1,0:T(8,128)S(1)} %get-tuple-element.44.lower_ref, f32[19,16,16,128]{3,2,1,0:T(8,128)S(1)} %copy-done, s32[16,16,128]{2,1,0:T(8,128)S(1)} %copy-done.2, ...), custom_call_target="tpu_custom_call" | custom-call | flops 5000000 | bytes 3000000 | tf_op jit(solution)/shard_map/upper/pallas_call | solution.py:632
  28.2 0.0 collective-permute-done.5.refs_1_
  28.2 1.1 %collective-permute-done.4.refs_0_ = f32[168,128]{1,0:T(8,128)S(1)} collective-permute-done((f32[168,128]{1,0:T(8,128)S(1)}, f32[168,128]{1,0:T(8,128)S(1)}, u32[]{:S(2)}, u32[]{:S(2)}) %collective-permute-start.4) | collective-permute-done | bytes 86048 | tf_op jit(solution)/shard_map/ppermute | solution.py:140
  29.4 1.1 %finish.1 = (f32[19,16,16,128]{3,2,1,0:T(8,128)}, f32[3,128]{1,0:T(4,128)}) custom-call(f32[19,16,16,128]{3,2,1,0:T(8,128)} %get-tuple-element.45.whole_ref, bf16[256,128]{1,0:T(8,128)(2,1)S(1)} %get-tuple-element.46.target_ref, f32[10,16,8,128]{3,2,1,0:T(8,128)S(1)} %get-tuple-element.47.tile_ref, ...), custom_call_target="tpu_custom_call", output_to_operand_aliasing={{0}: (0, {})} | custom-call | tf_op jit(solution)/shard_map/finish/pallas_call | solution.py:749
  (6 shorter events, 0.0 us)
Async XLA Ops:
  0.6 15.8 %copy-start = (f32[19,16,16,128]{3,2,1,0:T(8,128)S(1)}, f32[19,16,16,128]{3,2,1,0:T(8,128)}, u32[]{:S(2)}) copy-start(f32[19,16,16,128]{3,2,1,0:T(8,128)} %pops_ref.5) | copy-start | bytes 7471108
  2.5 14.0 %all-to-all-start = ((f32[8,8,128]{2,1,0:T(8,128)}), f32[8,8,128]{2,1,0:T(8,128)S(1)}, u32[]{:S(2)}, u32[]{:S(2)}) async-start(f32[8,8,128]{2,1,0:T(8,128)} %bitcast.2), calls=%async_computation | async-start | bytes 65536 | tf_op jit(solution)/shard_map/all_to_all | solution.py:779
  9.8 0.9 %copy-start.1 = (s32[16,16,128]{2,1,0:T(8,128)S(1)}, s32[16,16,128]{2,1,0:T(8,128)}, u32[]{:S(2)}) copy-start(s32[16,16,128]{2,1,0:T(8,128)} %solid_ref.5) | copy-start | bytes 393220
  10.7 5.8 %copy-start.2 = (s32[16,16,128]{2,1,0:T(8,128)S(1)}, s32[16,16,128]{2,1,0:T(8,128)}, u32[]{:S(2)}) copy-start(s32[16,16,128]{2,1,0:T(8,128)} %solid_ref.5) | copy-start | bytes 393220
  17.7 3.6 %collective-permute-start = (f32[2,16,128]{2,1,0:T(8,128)S(1)}, f32[2,16,128]{2,1,0:T(8,128)S(1)}, u32[]{:S(2)}, u32[]{:S(2)}) collective-permute-start(f32[2,16,128]{2,1,0:T(8,128)S(1)} %get-tuple-element.34), channel_id=1, source_target_pairs={{0,1},{1,0},{2,3},{3,2},{4,5},{5,4},{6,7},{7,6},{8,9},{9,8},{10,11... | collective-permute-start | bytes 49160 | tf_op jit(solution)/shard_map/ppermute | solution.py:140
  17.7 4.7 %collective-permute-start.3 = (f32[8,128]{1,0:T(8,128)S(1)}, f32[8,128]{1,0:T(8,128)S(1)}, u32[]{:S(2)}, u32[]{:S(2)}) collective-permute-start(f32[8,128]{1,0:T(8,128)S(1)} %get-tuple-element.40), channel_id=1, source_target_pairs={{0,8},{1,9},{2,10},{3,11},{4,12},{5,13},{6,14},{7,15},{8,0},{9,1},... | collective-permute-start | bytes 12296 | tf_op jit(solution)/shard_map/ppermute | solution.py:140
  18.3 6.0 %collective-permute-start.1 = (f32[88,128]{1,0:T(8,128)S(1)}, f32[88,128]{1,0:T(8,128)S(1)}, u32[]{:S(2)}, u32[]{:S(2)}) collective-permute-start(f32[88,128]{1,0:T(8,128)S(1)} %get-tuple-element.37), channel_id=1, source_target_pairs={{0,12},{1,13},{2,14},{3,15},{4,8},{5,9},{6,10},{7,11},{8,4},{9,5},... | collective-permute-start | bytes 135176 | tf_op jit(solution)/shard_map/ppermute | solution.py:140
  20.5 4.3 %collective-permute-start.2 = (f32[88,128]{1,0:T(8,128)S(1)}, f32[88,128]{1,0:T(8,128)S(1)}, u32[]{:S(2)}, u32[]{:S(2)}) collective-permute-start(f32[88,128]{1,0:T(8,128)S(1)} %get-tuple-element.38), channel_id=1, source_target_pairs={{0,4},{1,5},{2,6},{3,7},{4,0},{5,1},{6,2},{7,3},{8,12},{9,13},{10,... | collective-permute-start | bytes 135176 | tf_op jit(solution)/shard_map/ppermute | solution.py:140
  21.3 4.5 %copy-start.3 = (s32[1,128]{1,0:T(1,128)S(1)}, s32[1,128]{1,0:T(1,128)}, u32[]{:S(2)}) copy-start(s32[1,128]{1,0:T(1,128)} %get-tuple-element.42.target_ref) | copy-start | bytes 1540
  24.9 4.5 %collective-permute-start.4 = (f32[168,128]{1,0:T(8,128)S(1)}, f32[168,128]{1,0:T(8,128)S(1)}, u32[]{:S(2)}, u32[]{:S(2)}) collective-permute-start(f32[168,128]{1,0:T(8,128)S(1)} %get-tuple-element.48), channel_id=1, source_target_pairs={{0,2},{1,3},{2,0},{3,1},{4,6},{5,7},{6,4},{7,5},{8,10},{9,11},{10,... | collective-permute-start | bytes 258056 | tf_op jit(solution)/shard_map/ppermute | solution.py:140
  25.8 2.4 %collective-permute-start.5 = (f32[64,128]{1,0:T(8,128)S(1)}, f32[64,128]{1,0:T(8,128)S(1)}, u32[]{:S(2)}, u32[]{:S(2)}) collective-permute-start(f32[64,128]{1,0:T(8,128)S(1)} %get-tuple-element.49), channel_id=1, source_target_pairs={{0,1},{1,0},{2,3},{3,2},{4,5},{5,4},{6,7},{7,6},{8,9},{9,8},{10,11... | collective-permute-start | bytes 98312 | tf_op jit(solution)/shard_map/ppermute | solution.py:140
